TPU v7x, 32 devices: a whole 2x2x4 slice. The times are simulated.
32 devices in a mesh: gx: 4 (over x, core), gy: 8 (over z, y).
Axes of the slice: x: 2, y: 2, z: 4, core: 2. Of those that a mesh axis runs over, the one named last changes fastest.
Arguments:
- charges: bfloat16 [65536, 32], P(('gx', 'gy')), may hold values from -6 to 6
- panel_counts: int32 [1024], P(('gx', 'gy')), may hold values from 1 to 64, as said below
- basis: bfloat16 [1024, 64, 64], P(('gx', 'gy')), may hold values from -0.75 to 0.75
- transfer: bfloat16 [1024, 64, 64], P(('gx', 'gy')), may hold values from -0.5 to 0.5
- leaf_coupling: bfloat16 [1024, 16, 64, 64], P(('gx', 'gy')), may hold values from -0.1875 to 0.1875
- leaf_partners: int32 [1024, 16], P(('gx', 'gy')), may hold values from 0 to 1023, as said below
- near_blocks: bfloat16 [1024, 3, 64, 64], P(('gx', 'gy')), may hold values from -0.4375 to 0.4375
- parent_coupling: bfloat16 [512, 16, 64, 64], P(('gx', 'gy')), may hold values from -0.1875 to 0.1875
- parent_partners: int32 [512, 16], P(('gx', 'gy')), may hold values from 0 to 511, as said below
Outputs:
- potential: bfloat16 [65536, 32], P(('gx', 'gy'))
Inputs may be any that keep to these rules, and one draw needn't show every extreme that they name: `panel_counts`: every value 1 to 64 occurs; every fifth leaf has all 64 panels live. `leaf_partners`: the partner of leaf g lies among the leaves of g's device, the device before or the device after in the order of the combined index gx * 32 + gy (leaf g is on device g // 32). `parent_partners`: the partner of parent q lies in the same block of 128 parents as q (one index of gx).
All inputs are finite; a program needn't handle non-finite values.
Results may differ from a plain program's by a relative error of at most 0.0054.
Values may be sent and summed in bfloat16 or wider, within the bound.
No kernel may reach another device: no remote copies, remote signals or barrier semaphores. Data moves between devices by JAX's collectives and lax.ppermute only.
A program may use at most 128 MiB of HBM per device.

v0:
```python
import jax
import jax.numpy as jnp
from jax import lax
from jax.sharding import PartitionSpec as P


def shifted(array, axis, by):
    length = lax.axis_size(axis)
    pairs = [(i, i + by) for i in range(length) if 0 <= i + by < length]
    return lax.ppermute(array, axis, pairs)


def send_rims(payload, offset):
    return shifted(payload, ("gx", "gy"), offset)


def per_device(
    charges,
    panel_counts,
    basis,
    transfer,
    leaf_coupling,
    leaf_partners,
    near_blocks,
    parent_coupling,
    parent_partners,
):
    leaves, leaf_size, rank = basis.shape
    sides = charges.shape[1]
    half = leaves // 2
    slots = jnp.arange(leaf_size, dtype=jnp.int32)
    mask = (slots[None, :] < panel_counts[:, None]).astype(jnp.bfloat16)[:, :, None]
    live = charges.reshape(leaves, leaf_size, sides) * mask
    leaf_coef = jnp.einsum("gpk,gpr->gkr", basis, live, preferred_element_type=jnp.float32).astype(
        jnp.bfloat16
    )
    pairs = transfer.reshape(half, 2, rank, rank)
    kids = leaf_coef.reshape(half, 2, rank, sides)
    parent_coef = jnp.einsum(
        "qckl,qckr->qlr", pairs, kids, preferred_element_type=jnp.float32
    ).astype(jnp.bfloat16)
    device = lax.axis_index("gx") * lax.axis_size("gy") + lax.axis_index("gy")
    relative = leaf_partners - device * leaves
    cut = leaves * rank
    flat_coef = leaf_coef.reshape(cut, sides)
    received = []
    for offset in (1, -1):
        edge = live[leaves - 1] if offset == 1 else live[0]
        payload = jnp.concatenate([flat_coef, edge], axis=0)
        received.append(send_rims(payload, offset))
    before, after = received
    window_coef = jnp.concatenate([before[:cut], flat_coef, after[:cut]], axis=0).reshape(
        3 * leaves, rank, sides
    )
    picked = window_coef[relative + leaves]
    leaf_far = jnp.einsum(
        "gjkl,gjlr->gkr", leaf_coupling, picked, preferred_element_type=jnp.float32
    )
    row_start = lax.axis_index("gx") * lax.axis_size("gy") * half
    row_coef = lax.all_gather(parent_coef, "gy", axis=0, tiled=True)
    chosen = row_coef[parent_partners - row_start]
    parent_far = jnp.einsum(
        "qjkl,qjlr->qkr", parent_coupling, chosen, preferred_element_type=jnp.float32
    )
    parent_far = parent_far.astype(jnp.bfloat16)
    spread = jnp.repeat(parent_far, 2, axis=0)
    local_coef = (
        leaf_far + jnp.einsum("gkl,glr->gkr", transfer, spread, preferred_element_type=jnp.float32)
    ).astype(jnp.bfloat16)
    window = jnp.concatenate([before[cut:][None], live, after[cut:][None]], axis=0)
    near = jnp.zeros((leaves, leaf_size, sides), jnp.float32)
    for n in range(3):
        near = near + jnp.einsum(
            "gpq,gqr->gpr",
            near_blocks[:, n],
            window[n : n + leaves],
            preferred_element_type=jnp.float32,
        )
    total = jnp.einsum("gpk,gkr->gpr", basis, local_coef, preferred_element_type=jnp.float32) + near
    total = total * mask.astype(jnp.float32)
    return total.astype(jnp.bfloat16).reshape(leaves * leaf_size, sides)


def solution(mesh):
    in_specs = (
        P(("gx", "gy"), None),
        P(("gx", "gy")),
        P(("gx", "gy"), None, None),
        P(("gx", "gy"), None, None),
        P(("gx", "gy"), None, None, None),
        P(("gx", "gy"), None),
        P(("gx", "gy"), None, None, None),
        P(("gx", "gy"), None, None, None),
        P(("gx", "gy"), None),
    )
    out_specs = P(("gx", "gy"), None)
    return jax.shard_map(
        per_device, mesh=mesh, in_specs=in_specs, out_specs=out_specs, check_vma=False
    )
```

profile of v0, /device:TPU:2, one launch (start us, length us, event | category | flops | bytes accessed | tf_op | source)
XLA Modules:
  0.0 75.3 jit_solution(3589053728535804790)
XLA Ops:
  0.0 0.0 copy-start
  0.0 1.4 %fusion.23 = (f32[32,64]{1,0:T(8,128)}, bf16[32,64]{1,0:T(8,128)(2,1)S(1)}) fusion(s32[32]{0:T(128)} %param.10), kind=kLoop, calls=%fused_computation.45 | loop fusion | flops 6144 | bytes 12416 | tf_op jit(solution)/shard_map/convert_element_type | solution.py:80
  1.4 1.2 %reshape.62 = bf16[32,64,32]{1,0,2:T(8,128)(2,1)S(1)} reshape(bf16[2048,32]{0,1:T(8,128)(2,1)} %param.9) | data formatting | bytes 262144 | tf_op jit(solution)/shard_map/reshape | solution.py:33
  2.6 0.1 copy_multiply_fusion
  2.7 1.3 %convolution_convert_fusion = bf16[32,32,64]{2,1,0:T(8,128)(2,1)S(1)} fusion(bf16[32,64,32]{1,2,0:T(8,128)(2,1)S(1)} %copy_multiply_fusion, bf16[32,64,64]{2,1,0:T(8,128)(2,1)} %param.11), kind=kOutput, calls=%fused_computation.10 | convolution fusion | flops 8454144 | bytes 524288 | tf_op jit(solution)/shard_map/gpk,gpr->gkr/dot_general | solution.py:34
  4.0 0.1 copy.24
  4.1 0.3 reshape.63
  4.4 0.7 pad_maximum_fusion.2
  5.1 5.9 %collective-permute-start.1 = (bf16[2112,32]{0,1:T(8,128)(2,1)}, bf16[2112,32]{0,1:T(8,128)(2,1)S(1)}, u32[]{:S(2)}, u32[]{:S(2)}) collective-permute-start(bf16[2112,32]{0,1:T(8,128)(2,1)} %get-tuple-element.7), channel_id=1, source_target_pairs={{1,0},{2,1},{3,2},{4,3},{5,4},{6,5},{7,6},{8,7},{9,8},{10,9},{11,1... | collective-permute-start | bytes 405512 | tf_op jit(solution)/shard_map/ppermute | solution.py:10
  11.0 1.9 %collective-permute-start = (bf16[2112,32]{0,1:T(8,128)(2,1)}, bf16[2112,32]{0,1:T(8,128)(2,1)}, u32[]{:S(2)}, u32[]{:S(2)}) collective-permute-start(bf16[2112,32]{0,1:T(8,128)(2,1)} %get-tuple-element.8), channel_id=1, source_target_pairs={{0,1},{1,2},{2,3},{3,4},{4,5},{5,6},{6,7},{7,8},{8,9},{9,10},{10,1... | collective-permute-start | bytes 405512 | tf_op jit(solution)/shard_map/ppermute | solution.py:10
  12.9 0.7 compare_select_fusion
  13.6 0.1 reshape.79
  13.7 1.4 %fusion.10 = f32[32,32,64]{2,1,0:T(8,128)S(1)} fusion(bf16[32,64,32]{1,2,0:T(8,128)(2,1)S(1)} %copy_multiply_fusion, bf16[32,3,64,64]{3,2,1,0:T(8,128)(2,1)} %param.15), kind=kOutput, calls=%fused_computation.19 | convolution fusion | flops 8388608 | bytes 917504 | tf_op jit(solution)/shard_map/gpq,gqr->gpr/dot_general | solution.py:73
  15.1 0.0 copy-done
  15.1 0.3 fusion.7
  15.4 35.5 %all_gather.3 = bf16[128,64,32]{1,2,0:T(8,128)(2,1)S(1)} all-gather(bf16[16,64,32]{1,2,0:T(8,128)(2,1)S(1)} %fusion.7), channel_id=1, replica_groups=mesh['gx'=4,'gy'=8] {'gy'}, dimensions={0}, use_global_device_ids=true | all-gather | bytes 589824 | tf_op jit(solution)/shard_map/all_gather | solution.py:60
  51.0 2.2 %gather_fusion.1 = bf16[256,64,32]{1,2,0:T(8,128)(2,1)} fusion(bf16[128,64,32]{1,2,0:T(8,128)(2,1)S(1)} %all_gather.3, s32[1024]{0:T(1024)S(1)} %pad_clamp_fusion), kind=kCustom, calls=%fused_computation.1 | custom fusion | bytes 2098176 | tf_op jit(solution)/shard_map/gather | solution.py:61
  53.2 0.0 copy-start.3
  53.2 4.0 %fusion.8 = bf16[16,64,32]{1,2,0:T(8,128)(2,1)S(1)} fusion(bf16[16,16,64,32]{2,3,1,0:T(8,128)(2,1)} %bitcast.83, bf16[16,16,64,64]{3,2,1,0:T(8,128)(2,1)} %param.16), kind=kOutput, calls=%fused_computation.17 | convolution fusion | flops 67141632 | bytes 3211264 | tf_op jit(solution)/shard_map/qjkl,qjlr->qkr/dot_general | solution.py:62
  57.2 0.1 broadcast_in_dim.20
  57.3 0.4 fusion.26
  57.7 0.0 copy-done.3
  57.7 0.1 copy.25
  57.7 0.1 reshape.71
  57.8 0.0 collective-permute-done.1
  57.9 0.0 collective-permute-done
  57.9 0.9 %slice.51 = bf16[2048,32]{0,1:T(8,128)(2,1)S(1)} slice(bf16[2112,32]{0,1:T(8,128)(2,1)} %collective-permute-done), slice={[0:2048], [0:32]} | slice | bytes 262144 | tf_op jit(solution)/shard_map/slice | solution.py:52
  58.8 0.8 %reshape.64 = bf16[96,64,32]{1,0,2:T(8,128)(2,1)S(1)} reshape(bf16[6144,32]{0,1:T(8,128)(2,1)S(1)} %pad_maximum_fusion) | data formatting | bytes 786432 | tf_op jit(solution)/shard_map/reshape | solution.py:52
  59.6 0.3 copy.26
  60.0 0.7 slice_bitcast_fusion.1
  60.7 1.4 %convolution_add_fusion.2 = f32[32,32,64]{2,1,0:T(8,128)S(1)} fusion(f32[32,32,64]{2,1,0:T(8,128)S(1)} %fusion.10, bf16[32,3,64,64]{3,2,1,0:T(8,128)(2,1)} %param.15, bf16[32,64,32]{1,2,0:T(8,128)(2,1)S(1)} %copy_multiply_fusion, bf16[1,64,32]{1,2,0:T(8,128)(2,1)S(1)} %slice_bitcast_fusion.1), kind=kOutput, calls=%fused_computation.7 | convolution fusion | flops 8724480 | bytes 1183744 | tf_op jit(solution)/shard_map/gpq,gqr->gpr/dot_general | solution.py:73
  62.1 1.4 %convolution_add_fusion.1 = f32[32,32,64]{2,1,0:T(8,128)S(1)} fusion(f32[32,32,64]{2,1,0:T(8,128)S(1)} %convolution_add_fusion.2, bf16[32,3,64,64]{3,2,1,0:T(8,128)(2,1)} %param.15, bf16[1,64,32]{1,2,0:T(8,128)(2,1)S(1)} %slice_bitcast_fusion, bf16[32,64,32]{1,2,0:T(8,128)(2,1)S(1)} %copy_multiply_fusion), kind=kOutput, calls=%fused_computation.6 | convolution fusion | flops 8724480 | bytes 1183744 | tf_op jit(solution)/shard_map/gpq,gqr->gpr/dot_general | solution.py:73
  63.5 0.0 copy-start.1
  63.5 0.0 copy-start.2
  63.6 3.4 %gather_fusion = bf16[512,64,32]{1,2,0:T(8,128)(2,1)} fusion(bf16[96,64,32]{1,2,0:T(8,128)(2,1)S(1)} %copy.26, s32[1024]{0:T(1024)S(1)} %pad_clamp_fusion.1), kind=kCustom, calls=%fused_computation | custom fusion | bytes 4196352 | tf_op jit(solution)/shard_map/gather | solution.py:55
  67.0 0.0 copy-done.1
  67.0 0.0 copy-done.2
  67.0 7.2 %fusion.4 = bf16[32,64,32]{1,2,0:T(8,128)(2,1)S(1)} fusion(f32[32,32,64]{2,1,0:T(8,128)S(1)} %convolution_add_fusion.1, bf16[32,64,64]{2,1,0:T(8,128)(2,1)S(1)} %copy-done.1, f32[32,32,64]{2,1,0:T(8,128)S(1)} %fusion.26, bf16[32,16,64,32]{2,3,1,0:T(8,128)(2,1)} %bitcast.82, bf16[32,16,64,64]{3,2,1,0:T(8,128)(2,1)} %param.13, f32[32,64]{1,0:T(8,128)S(1)} %copy-done.2), kind=kOutput, calls=%fused_computation.11 | convolution fusion | flops 142934016 | bytes 7217152 | tf_op jit(solution)/shard_map/gpk,gkr->gpr/dot_general | solution.py:79
  74.2 0.1 copy.30
  74.3 0.9 %reshape.68 = bf16[2048,32]{0,1:T(8,128)(2,1)} reshape(bf16[32,64,32]{1,0,2:T(8,128)(2,1)S(1)} %copy.30) | data formatting | bytes 262144 | tf_op jit(solution)/shard_map/reshape | solution.py:81
  (7 shorter events, 0.1 us)
Async XLA Ops:
  0.0 15.1 %copy-start = (bf16[32,64,64]{2,1,0:T(8,128)(2,1)S(1)}, bf16[32,64,64]{2,1,0:T(8,128)(2,1)}, u32[]{:S(2)}) copy-start(bf16[32,64,64]{2,1,0:T(8,128)(2,1)} %param.12) | copy-start | bytes 786436
  5.1 52.7 %collective-permute-start.1 = (bf16[2112,32]{0,1:T(8,128)(2,1)}, bf16[2112,32]{0,1:T(8,128)(2,1)S(1)}, u32[]{:S(2)}, u32[]{:S(2)}) collective-permute-start(bf16[2112,32]{0,1:T(8,128)(2,1)} %get-tuple-element.7), channel_id=1, source_target_pairs={{1,0},{2,1},{3,2},{4,3},{5,4},{6,5},{7,6},{8,7},{9,8},{10,9},{11,1... | collective-permute-start | bytes 405512 | tf_op jit(solution)/shard_map/ppermute | solution.py:10
  11.0 46.9 %collective-permute-start = (bf16[2112,32]{0,1:T(8,128)(2,1)}, bf16[2112,32]{0,1:T(8,128)(2,1)}, u32[]{:S(2)}, u32[]{:S(2)}) collective-permute-start(bf16[2112,32]{0,1:T(8,128)(2,1)} %get-tuple-element.8), channel_id=1, source_target_pairs={{0,1},{1,2},{2,3},{3,4},{4,5},{5,6},{6,7},{7,8},{8,9},{9,10},{10,1... | collective-permute-start | bytes 405512 | tf_op jit(solution)/shard_map/ppermute | solution.py:10
  53.2 4.5 %copy-start.3 = (s32[32,16]{0,1:T(8,128)S(1)}, s32[32,16]{0,1:T(8,128)}, u32[]{:S(2)}) copy-start(s32[32,16]{0,1:T(8,128)} %param.14) | copy-start | bytes 6148
  63.5 3.5 %copy-start.1 = (bf16[32,64,64]{2,1,0:T(8,128)(2,1)S(1)}, bf16[32,64,64]{2,1,0:T(8,128)(2,1)}, u32[]{:S(2)}) copy-start(bf16[32,64,64]{2,1,0:T(8,128)(2,1)} %param.11) | copy-start | bytes 786436
  63.5 3.5 %copy-start.2 = (f32[32,64]{1,0:T(8,128)S(1)}, f32[32,64]{1,0:T(8,128)}, u32[]{:S(2)}) copy-start(f32[32,64]{1,0:T(8,128)} %get-tuple-element.9) | copy-start | bytes 24580
where the time goes:
time: 75.8 us; the launch traced here: 75.3 us
  blocking collectives  35.5 us (47%)
  matrix products  17.5 us (23%)
  local copies, waits for them, and re-layouts  11.3 us (15%)
  starting transfers between devices  7.79 us (10%)
  other arithmetic  2.98 us (4%)
    all_gather x1, blocking collectives, per_device(): row_coef = lax.all_gather(parent_coef, 'gy', axis=0, tiled=True)  35.5 us
    ppermute x2, starting transfers between devices, shifted(): return lax.ppermute(array, axis, pairs)  7.79 us
    dot_general x1, matrix products, per_device(): jnp.einsum('gpk,gkr->gpr', basis, local_coef, preferred_element_type=jnp....  7.23 us
    dot_general x3, matrix products, per_device(): jnp.einsum('gpq,gqr->gpr', near_blocks[:, n], window[n:n + leaves], prefe...  4.28 us
    dot_general x1, matrix products, per_device(): jnp.einsum('qjkl,qjlr->qkr', parent_coupling, chosen, preferred_element_t...  4.03 us
    gather x1, local copies, waits for them, and re-layouts, per_device(): picked = window_coef[relative + leaves]  3.44 us
    gather x1, local copies, waits for them, and re-layouts, per_device(): chosen = row_coef[parent_partners - row_start]  2.2 us
  transfers between devices with their start and end apart: 2, of which 0 were waited for; matrix products, arithmetic and copies ran while one was open for 12% of the time, Pallas kernels for 0%

commit v1 on v0

--- a/solution.py
+++ b/solution.py
@@ -57,7 +57,9 @@
         "gjkl,gjlr->gkr", leaf_coupling, picked, preferred_element_type=jnp.float32
     )
     row_start = lax.axis_index("gx") * lax.axis_size("gy") * half
-    row_coef = lax.all_gather(parent_coef, "gy", axis=0, tiled=True)
+    n = lax.axis_size("gy")
+    sent = jnp.broadcast_to(parent_coef[None], (n,) + parent_coef.shape)
+    row_coef = lax.all_to_all(sent, "gy", 0, 0).reshape((n * half,) + parent_coef.shape[1:])
     chosen = row_coef[parent_partners - row_start]
     parent_far = jnp.einsum(
         "qjkl,qjlr->qkr", parent_coupling, chosen, preferred_element_type=jnp.float32

time: 75.8 us -> 47.7 us (0.63)
  the two profiles are of different devices: /device:TPU:2 before, /device:TPU:1 now
where the time goes in v1:
time: 47.7 us; the launch traced here: 47.1 us
  matrix products  16.5 us (35%)
  local copies, waits for them, and re-layouts  15.8 us (33%)
  starting transfers between devices  13 us (27%)
  other arithmetic  1.56 us (3%)
    ppermute x2, starting transfers between devices, shifted(): return lax.ppermute(array, axis, pairs)  9.5 us
    dot_general x1, matrix products, per_device(): jnp.einsum('gjkl,gjlr->gkr', leaf_coupling, picked, preferred_element_typ...  5.66 us
    unnamed x19, local copies, waits for them, and re-layouts  4.45 us
    dot_general x3, matrix products, per_device(): jnp.einsum('gpq,gqr->gpr', near_blocks[:, n], window[n:n + leaves], prefe...  4.43 us
    dot_general x1, matrix products, per_device(): jnp.einsum('qjkl,qjlr->qkr', parent_coupling, chosen, preferred_element_t...  4.07 us
    all_to_all x1, starting transfers between devices, per_device(): lax.all_to_all(sent, 'gy', 0, 0)  3.49 us
    gather x1, local copies, waits for them, and re-layouts, per_device(): picked = window_coef[relative + leaves]  3.46 us
    gather x1, local copies, waits for them, and re-layouts, per_device(): chosen = row_coef[parent_partners - row_start]  2.2 us
  transfers between devices with their start and end apart: 3, of which 0 were waited for; matrix products, arithmetic and copies ran while one was open for 39% of the time, Pallas kernels for 0%

profile of v1, /device:TPU:1, one launch (start us, length us, event | category | flops | bytes accessed | tf_op | source)
XLA Modules:
  0.0 47.1 jit_solution(5777023419068330199)
XLA Ops:
  0.0 0.0 copy-start
  0.0 1.4 %fusion.22 = (f32[32,64]{1,0:T(8,128)}, bf16[32,64]{1,0:T(8,128)(2,1)S(1)}) fusion(s32[32]{0:T(128)} %param.10), kind=kLoop, calls=%fused_computation.45 | loop fusion | flops 6144 | bytes 12416 | tf_op jit(solution)/shard_map/convert_element_type | solution.py:82
  1.4 1.2 %reshape.66 = bf16[32,64,32]{1,0,2:T(8,128)(2,1)S(1)} reshape(bf16[2048,32]{0,1:T(8,128)(2,1)} %param.9) | data formatting | bytes 262144 | tf_op jit(solution)/shard_map/reshape | solution.py:33
  2.6 0.1 copy_multiply_fusion
  2.7 0.0 copy-start.6
  2.7 0.0 copy-start.7
  2.7 1.3 %convolution_convert_fusion = bf16[32,32,64]{2,1,0:T(8,128)(2,1)S(1)} fusion(bf16[32,64,32]{1,2,0:T(8,128)(2,1)S(1)} %copy_multiply_fusion, bf16[32,64,64]{2,1,0:T(8,128)(2,1)} %param.11), kind=kOutput, calls=%fused_computation.10 | convolution fusion | flops 8454144 | bytes 524288 | tf_op jit(solution)/shard_map/gpk,gpr->gkr/dot_general | solution.py:34
  4.0 0.1 copy.16
  4.1 0.3 reshape.67
  4.4 4.0 %collective-permute-start = (bf16[2112,32]{0,1:T(8,128)(2,1)S(1)}, bf16[2112,32]{0,1:T(8,128)(2,1)S(1)}, u32[]{:S(2)}, u32[]{:S(2)}) collective-permute-start(bf16[2112,32]{0,1:T(8,128)(2,1)S(1)} %get-tuple-element.8), channel_id=1, source_target_pairs={{0,1},{1,2},{2,3},{3,4},{4,5},{5,6},{6,7},{7,8},{8,9},{9,10},{10,1... | collective-permute-start | bytes 405512 | tf_op jit(solution)/shard_map/ppermute | solution.py:10
  8.4 5.5 %collective-permute-start.1 = (bf16[2112,32]{0,1:T(8,128)(2,1)S(1)}, bf16[2112,32]{0,1:T(8,128)(2,1)S(1)}, u32[]{:S(2)}, u32[]{:S(2)}) collective-permute-start(bf16[2112,32]{0,1:T(8,128)(2,1)S(1)} %get-tuple-element.7), channel_id=1, source_target_pairs={{1,0},{2,1},{3,2},{4,3},{5,4},{6,5},{7,6},{8,7},{9,8},{10,9},{11,1... | collective-permute-start | bytes 405512 | tf_op jit(solution)/shard_map/ppermute | solution.py:10
  13.9 0.0 copy-done
  13.9 0.3 fusion.6
  14.2 0.2 broadcast_bitcast_fusion
  14.4 1.5 %reshape.97 = bf16[8,2,16384]{2,1,0:T(2,128)(2,1)} reshape(bf16[8,16,32,64]{3,2,1,0:T(8,128)(2,1)S(1)} %broadcast_bitcast_fusion) | data formatting | bytes 1048576
  15.9 3.5 %all-to-all-start = ((bf16[8,2,16384]{2,1,0:T(2,128)(2,1)}), bf16[8,2,16384]{2,1,0:T(2,128)(2,1)S(1)}, u32[]{:S(2)}, u32[]{:S(2)}) async-start(bf16[8,2,16384]{2,1,0:T(2,128)(2,1)} %reshape.97), calls=%async_computation | async-start | bytes 1048576 | tf_op jit(solution)/shard_map/all_to_all | solution.py:62
  19.5 1.4 %fusion.9 = f32[32,32,64]{2,1,0:T(8,128)S(1)} fusion(bf16[32,64,32]{1,2,0:T(8,128)(2,1)S(1)} %copy_multiply_fusion, bf16[32,3,64,64]{3,2,1,0:T(8,128)(2,1)} %param.15), kind=kOutput, calls=%fused_computation.19 | convolution fusion | flops 8388608 | bytes 917504 | tf_op jit(solution)/shard_map/gpq,gqr->gpr/dot_general | solution.py:75
  20.9 0.0 copy-done.6
  20.9 0.1 copy.17
  21.0 0.1 reshape.76
  21.1 0.0 copy-done.7
  21.1 0.1 reshape.84
  21.2 0.0 collective-permute-done
  21.2 0.0 copy-start.4
  21.2 0.0 collective-permute-done.1
  21.2 0.6 %copy-done.4 = bf16[2112,32]{0,1:T(8,128)(2,1)} copy-done((bf16[2112,32]{0,1:T(8,128)(2,1)}, bf16[2112,32]{0,1:T(8,128)(2,1)S(1)}, u32[]{:S(2)}) %copy-start.4) | copy-done | bytes 135192
  21.9 0.0 copy-start.3
  21.9 0.7 %copy-done.3 = bf16[2112,32]{0,1:T(8,128)(2,1)} copy-done((bf16[2112,32]{0,1:T(8,128)(2,1)}, bf16[2112,32]{0,1:T(8,128)(2,1)S(1)}, u32[]{:S(2)}) %copy-start.3) | copy-done | bytes 135192
  22.6 0.8 %reshape.68 = bf16[96,64,32]{1,0,2:T(8,128)(2,1)S(1)} reshape(bf16[6144,32]{0,1:T(8,128)(2,1)S(1)} %pad_maximum_fusion) | data formatting | bytes 786432 | tf_op jit(solution)/shard_map/reshape | solution.py:52
  23.4 0.3 copy.18
  23.7 0.7 %slice_bitcast_fusion.1 = bf16[1,64,32]{1,2,0:T(8,128)(2,1)S(1)} fusion(bf16[2112,32]{0,1:T(8,128)(2,1)} %copy-done.4), kind=kLoop, calls=%fused_computation.40 | loop fusion | bytes 8192 | tf_op jit(solution)/shard_map/broadcast_in_dim | solution.py:72
  24.4 1.4 %convolution_add_fusion.3 = f32[32,32,64]{2,1,0:T(8,128)S(1)} fusion(f32[32,32,64]{2,1,0:T(8,128)S(1)} %fusion.9, bf16[32,3,64,64]{3,2,1,0:T(8,128)(2,1)} %param.15, bf16[32,64,32]{1,2,0:T(8,128)(2,1)S(1)} %copy_multiply_fusion, bf16[1,64,32]{1,2,0:T(8,128)(2,1)S(1)} %slice_bitcast_fusion.1), kind=kOutput, calls=%fused_computation.7 | convolution fusion | flops 8724480 | bytes 1183744 | tf_op jit(solution)/shard_map/gpq,gqr->gpr/dot_general | solution.py:75
  25.8 3.5 %gather_fusion = bf16[512,64,32]{1,2,0:T(8,128)(2,1)} fusion(bf16[96,64,32]{1,2,0:T(8,128)(2,1)S(1)} %copy.18, s32[1024]{0:T(1024)S(1)} %pad_clamp_fusion.1), kind=kCustom, calls=%fused_computation | custom fusion | bytes 4196352 | tf_op jit(solution)/shard_map/gather | solution.py:55
  29.3 0.7 %slice_bitcast_fusion = bf16[1,64,32]{1,2,0:T(8,128)(2,1)S(1)} fusion(bf16[2112,32]{0,1:T(8,128)(2,1)} %copy-done.3), kind=kLoop, calls=%fused_computation.39 | loop fusion | bytes 8192 | tf_op jit(solution)/shard_map/broadcast_in_dim | solution.py:72
  30.0 1.6 %convolution_add_fusion.2 = f32[32,32,64]{2,1,0:T(8,128)S(1)} fusion(f32[32,32,64]{2,1,0:T(8,128)S(1)} %convolution_add_fusion.3, bf16[32,3,64,64]{3,2,1,0:T(8,128)(2,1)} %param.15, bf16[1,64,32]{1,2,0:T(8,128)(2,1)S(1)} %slice_bitcast_fusion, bf16[32,64,32]{1,2,0:T(8,128)(2,1)S(1)} %copy_multiply_fusion), kind=kOutput, calls=%fused_computation.6 | convolution fusion | flops 8724480 | bytes 1183744 | tf_op jit(solution)/shard_map/gpq,gqr->gpr/dot_general | solution.py:75
  31.6 0.8 %copy-done.1 = bf16[512,64,32]{1,2,0:T(8,128)(2,1)S(1)} copy-done((bf16[512,64,32]{1,2,0:T(8,128)(2,1)S(1)}, bf16[512,64,32]{1,2,0:T(8,128)(2,1)}, u32[]{:S(2)}) %copy-start.1) | copy-done | bytes 2097176
  32.3 5.7 %convolution_bitcast_fusion = f32[32,32,64]{2,1,0:T(8,128)S(1)} fusion(bf16[32,16,64,32]{2,3,1,0:T(8,128)(2,1)S(1)} %bitcast.78, bf16[32,16,64,64]{3,2,1,0:T(8,128)(2,1)} %param.13), kind=kOutput, calls=%fused_computation.2 | convolution fusion | flops 134217728 | bytes 6553600 | tf_op jit(solution)/shard_map/gjkl,gjlr->gkr/dot_general | solution.py:56
  38.0 0.0 all-to-all-done
  38.0 0.7 %reshape.98 = bf16[8,16,32,64]{3,2,1,0:T(8,128)(2,1)S(1)} reshape(bf16[8,2,16384]{2,1,0:T(2,128)(2,1)S(1)} %all-to-all-done) | data formatting | bytes 1048576
  38.7 2.2 %gather_fusion.1 = bf16[256,64,32]{1,2,0:T(8,128)(2,1)} fusion(bf16[128,64,32]{1,2,0:T(8,128)(2,1)S(1)} %bitcast.79, s32[1024]{0:T(1024)S(1)} %pad_clamp_fusion), kind=kCustom, calls=%fused_computation.1 | custom fusion | bytes 2098176 | tf_op jit(solution)/shard_map/gather | solution.py:63
  40.9 4.1 %fusion.7 = bf16[16,64,32]{1,2,0:T(8,128)(2,1)S(1)} fusion(bf16[16,16,64,32]{2,3,1,0:T(8,128)(2,1)} %bitcast.80, bf16[16,16,64,64]{3,2,1,0:T(8,128)(2,1)} %param.16), kind=kOutput, calls=%fused_computation.17 | convolution fusion | flops 67141632 | bytes 3211264 | tf_op jit(solution)/shard_map/qjkl,qjlr->qkr/dot_general | solution.py:64
  44.9 0.2 copy.19
  45.1 0.1 broadcast_in_dim.27
  45.3 0.0 copy-done.2
  45.3 0.0 copy-done.5
  45.3 0.7 %fusion.3 = bf16[32,64,32]{1,2,0:T(8,128)(2,1)S(1)} fusion(f32[32,32,64]{2,1,0:T(8,128)S(1)} %convolution_add_fusion.2, bf16[32,64,64]{2,1,0:T(8,128)(2,1)S(1)} %copy-done.2, f32[32,32,64]{2,1,0:T(8,128)S(1)} %convolution_bitcast_fusion, bf16[32,64,32]{2,1,0:T(8,128)(2,1)S(1)} %bitcast.83, bf16[32,64,64]{2,1,0:T(8,128)(2,1)S(1)} %copy-done, ...), kind=kOutput, calls=%fused_computation.13 | convolution fusion | flops 17104896 | bytes 1318912 | tf_op jit(solution)/shard_map/gpk,gkr->gpr/dot_general | solution.py:81
  46.0 0.1 copy.23
  46.1 0.9 %reshape.73 = bf16[2048,32]{0,1:T(8,128)(2,1)} reshape(bf16[32,64,32]{1,0,2:T(8,128)(2,1)S(1)} %copy.23) | data formatting | bytes 262144 | tf_op jit(solution)/shard_map/reshape | solution.py:83
  (12 shorter events, 0.1 us)
Async XLA Ops:
  0.0 13.9 %copy-start = (bf16[32,64,64]{2,1,0:T(8,128)(2,1)S(1)}, bf16[32,64,64]{2,1,0:T(8,128)(2,1)}, u32[]{:S(2)}) copy-start(bf16[32,64,64]{2,1,0:T(8,128)(2,1)} %param.12) | copy-start | bytes 786436
  2.7 18.2 %copy-start.6 = (s32[32,16]{0,1:T(8,128)S(1)}, s32[32,16]{0,1:T(8,128)}, u32[]{:S(2)}) copy-start(s32[32,16]{0,1:T(8,128)} %param.14) | copy-start | bytes 6148
  2.7 18.4 %copy-start.7 = (s32[16,16]{1,0:T(8,128)S(1)}, s32[16,16]{1,0:T(8,128)}, u32[]{:S(2)}) copy-start(s32[16,16]{1,0:T(8,128)} %param.17) | copy-start | bytes 3076
  4.4 16.8 %collective-permute-start = (bf16[2112,32]{0,1:T(8,128)(2,1)S(1)}, bf16[2112,32]{0,1:T(8,128)(2,1)S(1)}, u32[]{:S(2)}, u32[]{:S(2)}) collective-permute-start(bf16[2112,32]{0,1:T(8,128)(2,1)S(1)} %get-tuple-element.8), channel_id=1, source_target_pairs={{0,1},{1,2},{2,3},{3,4},{4,5},{5,6},{6,7},{7,8},{8,9},{9,10},{10,1... | collective-permute-start | bytes 405512 | tf_op jit(solution)/shard_map/ppermute | solution.py:10
  8.4 12.8 %collective-permute-start.1 = (bf16[2112,32]{0,1:T(8,128)(2,1)S(1)}, bf16[2112,32]{0,1:T(8,128)(2,1)S(1)}, u32[]{:S(2)}, u32[]{:S(2)}) collective-permute-start(bf16[2112,32]{0,1:T(8,128)(2,1)S(1)} %get-tuple-element.7), channel_id=1, source_target_pairs={{1,0},{2,1},{3,2},{4,3},{5,4},{6,5},{7,6},{8,7},{9,8},{10,9},{11,1... | collective-permute-start | bytes 405512 | tf_op jit(solution)/shard_map/ppermute | solution.py:10
  15.9 22.0 %all-to-all-start = ((bf16[8,2,16384]{2,1,0:T(2,128)(2,1)}), bf16[8,2,16384]{2,1,0:T(2,128)(2,1)S(1)}, u32[]{:S(2)}, u32[]{:S(2)}) async-start(bf16[8,2,16384]{2,1,0:T(2,128)(2,1)} %reshape.97), calls=%async_computation | async-start | bytes 1048576 | tf_op jit(solution)/shard_map/all_to_all | solution.py:62
  21.2 0.7 %copy-start.4 = (bf16[2112,32]{0,1:T(8,128)(2,1)}, bf16[2112,32]{0,1:T(8,128)(2,1)S(1)}, u32[]{:S(2)}) copy-start(bf16[2112,32]{0,1:T(8,128)(2,1)S(1)} %collective-permute-done) | copy-start | bytes 405508
  21.9 0.7 %copy-start.3 = (bf16[2112,32]{0,1:T(8,128)(2,1)}, bf16[2112,32]{0,1:T(8,128)(2,1)S(1)}, u32[]{:S(2)}) copy-start(bf16[2112,32]{0,1:T(8,128)(2,1)S(1)} %collective-permute-done.1) | copy-start | bytes 405508
  30.0 2.3 %copy-start.1 = (bf16[512,64,32]{1,2,0:T(8,128)(2,1)S(1)}, bf16[512,64,32]{1,2,0:T(8,128)(2,1)}, u32[]{:S(2)}) copy-start(bf16[512,64,32]{1,2,0:T(8,128)(2,1)} %gather_fusion) | copy-start | bytes 6291460
  40.9 4.4 %copy-start.2 = (bf16[32,64,64]{2,1,0:T(8,128)(2,1)S(1)}, bf16[32,64,64]{2,1,0:T(8,128)(2,1)}, u32[]{:S(2)}) copy-start(bf16[32,64,64]{2,1,0:T(8,128)(2,1)} %param.11) | copy-start | bytes 786436
  40.9 4.4 %copy-start.5 = (f32[32,64]{1,0:T(8,128)S(1)}, f32[32,64]{1,0:T(8,128)}, u32[]{:S(2)}) copy-start(f32[32,64]{1,0:T(8,128)} %get-tuple-element.9) | copy-start | bytes 24580

commit v2 on v0

v2 whole, which is shorter than its diff:
```python
import functools

import jax
import jax.numpy as jnp
from jax import lax
from jax.experimental import pallas as pl
from jax.experimental.pallas import tpu as pltpu
from jax.sharding import PartitionSpec as P

VMEM = pl.BlockSpec(memory_space=pltpu.VMEM)
SMEM = pl.BlockSpec(memory_space=pltpu.SMEM)
NN = (((1,), (0,)), ((), ()))
NT = (((1,), (1,)), ((), ()))


def dot(a, b, dims):
    return lax.dot_general(a, b, dims, preferred_element_type=jnp.float32)


def left_half(sides, width):
    return lax.broadcasted_iota(jnp.int32, (sides, 2 * width), 1) < width


def pair_mask(counts_ref, pair, sides, width):
    lane = lax.broadcasted_iota(jnp.int32, (sides, 2 * width), 1)
    left = lane < width
    count = jnp.where(left, counts_ref[2 * pair], counts_ref[2 * pair + 1])
    return jnp.where(left, lane, lane - width) < count


def swap(pair, width):
    return jnp.concatenate([pair[:, width:], pair[:, :width]], axis=1)


def up_kernel(copies, counts_ref, charges_ref, basis_ref, transfer_ref, rim_ref, live_ref, parents_ref):
    sides = charges_ref.shape[0]
    leaves, width, rank = basis_ref.shape
    pairs = leaves // 2
    own = pairs // 2
    left = left_half(sides, width)
    sums = []
    for a in range(pairs):
        charge = charges_ref[:, 2 * width * a : 2 * width * (a + 1)]
        live = jnp.where(pair_mask(counts_ref, a, sides, width), charge, jnp.zeros_like(charge))
        live_ref[a] = live
        if a == 0:
            rim_ref[pairs] = live
        if a == pairs - 1:
            rim_ref[pairs + 1] = live
        none = jnp.zeros_like(live)
        both = jnp.concatenate([jnp.where(left, live, none), jnp.where(left, none, live)], axis=0)
        coef = dot(both, basis_ref[2 * a : 2 * a + 2].reshape(2 * width, rank), NN)
        coef = jnp.concatenate([coef[:sides], coef[sides:]], axis=1).astype(jnp.bfloat16)
        rim_ref[a] = coef
        sums.append(dot(coef, transfer_ref[2 * a : 2 * a + 2].reshape(2 * rank, rank), NN))
        if a % 2 == 1:
            parent = jnp.concatenate(sums, axis=1).astype(jnp.bfloat16)
            sums = []
            for c in range(copies):
                parents_ref[c * own + a // 2] = parent


def spread_pair(dup_ref, at, pair, left, width):
    turned = swap(pair, width)
    dup_ref[at] = jnp.where(left, pair, turned)
    dup_ref[at + 1] = jnp.where(left, turned, pair)


def picked_product(dup_ref, partners, blocks, left):
    lhs = [
        jnp.where(left, dup_ref[partners[j]], dup_ref[partners[j + 1]])
        for j in range(0, len(partners), 2)
    ]
    rhs = [
        jnp.concatenate([blocks[j], blocks[j + 1]], axis=1) for j in range(0, len(partners), 2)
    ]
    return dot(jnp.concatenate(lhs, axis=1), jnp.concatenate(rhs, axis=1), NT)


def leaf_kernel(
    start_ref, partners_ref, rim_ref, before_ref, after_ref, live_ref, coupling_ref, near_ref,
    far_ref, near_out_ref, dup_ref,
):
    leaves, many, rank, _ = coupling_ref.shape
    width = near_ref.shape[2]
    pairs = leaves // 2
    sides = live_ref.shape[1]
    left = left_half(sides, rank)
    for b, ref in enumerate((before_ref, rim_ref, after_ref)):
        for a in range(pairs):
            spread_pair(dup_ref, b * leaves + 2 * a, ref[a], left, rank)
    shift = leaves - start_ref[0]

    def step(a, carry):
        fars = []
        for c in range(2):
            g = 2 * a + c
            partners = [partners_ref[j, g] + shift for j in range(many)]
            fars.append(picked_product(dup_ref, partners, [coupling_ref[g, j] for j in range(many)], left))
        far_ref[a] = jnp.concatenate(fars, axis=1)
        here = live_ref[a]
        prev = jnp.where(a == 0, before_ref[pairs + 1], live_ref[jnp.maximum(a - 1, 0)])
        next_ = jnp.where(a == pairs - 1, after_ref[pairs], live_ref[jnp.minimum(a + 1, pairs - 1)])
        even = dot(here, jnp.concatenate([near_ref[2 * a, 1], near_ref[2 * a, 2]], axis=1), NT)
        even = even + dot(prev[:, width:], near_ref[2 * a, 0], NT)
        odd = dot(here, jnp.concatenate([near_ref[2 * a + 1, 0], near_ref[2 * a + 1, 1]], axis=1), NT)
        odd = odd + dot(next_[:, :width], near_ref[2 * a + 1, 2], NT)
        near_out_ref[a] = jnp.concatenate([even, odd], axis=1)
        return carry

    lax.fori_loop(0, pairs, step, 0, unroll=2)


def down_kernel(
    counts_ref, partners_ref, row_ref, coupling_ref, transfer_ref, basis_ref, far_ref, near_ref,
    out_ref, dup_ref,
):
    parents, many, rank, _ = coupling_ref.shape
    width = basis_ref.shape[1]
    sides = row_ref.shape[1]
    row = 2 * row_ref.shape[0]
    left = left_half(sides, rank)

    def spread(a, carry):
        spread_pair(dup_ref, 2 * a, row_ref[a], left, rank)
        return carry

    lax.fori_loop(0, row_ref.shape[0], spread, 0, unroll=8)

    for q in range(parents):
        partners = [lax.rem(partners_ref[q, j], row) for j in range(many)]
        far = picked_product(dup_ref, partners, [coupling_ref[q, j] for j in range(many)], left)
        far = far.astype(jnp.bfloat16)
        local = far_ref[q] + dot(far, transfer_ref[2 * q : 2 * q + 2].reshape(2 * rank, rank), NT)
        local = local.astype(jnp.bfloat16)
        total = jnp.concatenate(
            [dot(local[:, :rank], basis_ref[2 * q], NT), dot(local[:, rank:], basis_ref[2 * q + 1], NT)],
            axis=1,
        )
        total = total + near_ref[q]
        total = jnp.where(pair_mask(counts_ref, q, sides, width), total, jnp.zeros_like(total))
        out_ref[:, 2 * width * q : 2 * width * (q + 1)] = total.astype(out_ref.dtype)


def shifted(array, axis, by):
    length = lax.axis_size(axis)
    pairs = [(i, i + by) for i in range(length) if 0 <= i + by < length]
    return lax.ppermute(array, axis, pairs)


def per_device(
    charges,
    panel_counts,
    basis,
    transfer,
    leaf_coupling,
    leaf_partners,
    near_blocks,
    parent_coupling,
    parent_partners,
):
    leaves, width, rank = basis.shape
    sides = charges.shape[1]
    pairs = leaves // 2
    own = pairs // 2
    n = lax.axis_size("gy")
    bf16, f32 = jnp.bfloat16, jnp.float32
    shape = jax.ShapeDtypeStruct
    params = pltpu.CompilerParams(vmem_limit_bytes=16 * 2**20)
    rim, live, parents = pl.pallas_call(
        functools.partial(up_kernel, n),
        name="up",
        out_shape=[
            shape((pairs + 2, sides, 2 * rank), bf16),
            shape((pairs, sides, 2 * width), bf16),
            shape((n * own, sides, 2 * rank), bf16),
        ],
        in_specs=[SMEM, VMEM, VMEM, VMEM],
        out_specs=[VMEM, VMEM, VMEM],
        compiler_params=params,
    )(panel_counts, charges.T, basis, transfer)
    row = lax.all_to_all(parents, "gy", 0, 0, tiled=True)
    axes = ("gx", "gy")
    before = shifted(rim, axes, 1)
    after = shifted(rim, axes, -1)
    device = lax.axis_index("gx") * n + lax.axis_index("gy")
    far, near = pl.pallas_call(
        leaf_kernel,
        name="leaf",
        out_shape=[shape((pairs, sides, 2 * rank), f32), shape((pairs, sides, 2 * width), f32)],
        in_specs=[SMEM, SMEM] + [VMEM] * 6,
        out_specs=[VMEM, VMEM],
        scratch_shapes=[pltpu.VMEM((3 * leaves, sides, 2 * rank), bf16)],
        compiler_params=params,
    )(
        (device * leaves).astype(jnp.int32).reshape(1), leaf_partners.T, rim, before, after, live,
        leaf_coupling, near_blocks,
    )
    out = pl.pallas_call(
        down_kernel,
        name="down",
        out_shape=shape((sides, leaves * width), bf16),
        in_specs=[SMEM, SMEM] + [VMEM] * 6,
        out_specs=VMEM,
        scratch_shapes=[pltpu.VMEM((n * pairs, sides, 2 * rank), bf16)],
        compiler_params=params,
    )(panel_counts, parent_partners, row, parent_coupling, transfer, basis, far, near)
    return out.T


def solution(mesh):
    in_specs = (
        P(("gx", "gy"), None),
        P(("gx", "gy")),
        P(("gx", "gy"), None, None),
        P(("gx", "gy"), None, None),
        P(("gx", "gy"), None, None, None),
        P(("gx", "gy"), None),
        P(("gx", "gy"), None, None, None),
        P(("gx", "gy"), None, None, None),
        P(("gx", "gy"), None),
    )
    out_specs = P(("gx", "gy"), None)
    return jax.shard_map(
        per_device, mesh=mesh, in_specs=in_specs, out_specs=out_specs, check_vma=False
    )
```

time: 75.8 us -> 48.3 us (0.64)
  the two profiles are of different devices: /device:TPU:2 before, /device:TPU:1 now
where the time goes in v2:
time: 48.3 us; the launch traced here: 47.8 us
  starting transfers between devices  15.5 us (32%)
  Pallas kernels  12.6 us (26%)
  local copies, waits for them, and re-layouts  11.3 us (23%)
  waiting for transfers between devices  8.29 us (17%)
    unnamed x24, local copies, waits for them, and re-layouts  11.3 us
    ppermute x2, starting transfers between devices, shifted(): return lax.ppermute(array, axis, pairs)  9.1 us
    ppermute x2, waiting for transfers between devices, shifted(): return lax.ppermute(array, axis, pairs)  8.29 us
    all_to_all x1, starting transfers between devices, per_device(): row = lax.all_to_all(parents, 'gy', 0, 0, tiled=True)  6.38 us
    pallas_call x1, Pallas kernels, per_device(): pl.pallas_call(down_kernel, name='down', out_shape=shape((sides, leaves *...  5.97 us
    pallas_call x1, Pallas kernels, per_device(): pl.pallas_call(leaf_kernel, name='leaf', out_shape=[shape((pairs, sides,...  4.64 us
    pallas_call x1, Pallas kernels, per_device(): pl.pallas_call(functools.partial(up_kernel, n), name='up', out_shape=[sha...  1.98 us
  transfers between devices with their start and end apart: 3, of which 2 were waited for; matrix products, arithmetic and copies ran while one was open for 0% of the time, Pallas kernels for 10%

profile of v2, /device:TPU:1, one launch (start us, length us, event | category | flops | bytes accessed | tf_op | source)
XLA Modules:
  0.0 47.8 jit_solution(1160931152936414399)
XLA Ops:
  0.0 0.0 copy-start.2
  0.0 1.0 %copy-done.2 = bf16[32,64,64]{2,1,0:T(8,128)(2,1)S(1)} copy-done((bf16[32,64,64]{2,1,0:T(8,128)(2,1)S(1)}, bf16[32,64,64]{2,1,0:T(8,128)(2,1)}, u32[]{:S(2)}) %copy-start.2) | copy-done | bytes 262168
  1.0 0.0 copy-start.4
  1.0 1.0 %copy-done.4 = bf16[32,64,64]{2,1,0:T(8,128)(2,1)S(1)} copy-done((bf16[32,64,64]{2,1,0:T(8,128)(2,1)S(1)}, bf16[32,64,64]{2,1,0:T(8,128)(2,1)}, u32[]{:S(2)}) %copy-start.4) | copy-done | bytes 262168
  2.1 0.0 copy-start.7
  2.1 0.9 %copy-done.7 = bf16[2048,32]{0,1:T(8,128)(2,1)S(1)} copy-done((bf16[2048,32]{0,1:T(8,128)(2,1)S(1)}, bf16[2048,32]{0,1:T(8,128)(2,1)}, u32[]{:S(2)}) %copy-start.7) | copy-done | bytes 131096
  3.0 0.0 copy-start.10
  3.0 0.7 %copy-done.10 = s32[32]{0:T(128)S(1)} copy-done((s32[32]{0:T(128)S(1)}, s32[32]{0:T(128)}, u32[]{:S(2)}) %copy-start.10) | copy-done | bytes 152
  3.6 2.0 %up.1 = (bf16[18,32,128]{2,1,0:T(8,128)(2,1)S(1)}, bf16[16,32,128]{2,1,0:T(8,128)(2,1)S(1)}, bf16[64,32,128]{2,1,0:T(8,128)(2,1)}) custom-call(s32[32]{0:T(128)S(1)} %copy-done.10, bf16[32,2048]{1,0:T(8,128)(2,1)S(1)} %bitcast.4, bf16[32,64,64]{2,1,0:T(8,128)(2,1)S(1)} %copy-done.2, bf16[32,64,64]{2,1,0:T(8,128)(2,1)S(1)} %copy-done.4), custom_call_target="tpu_custom_call" | custom-call | tf_op jit(solution)/shard_map/up/pallas_call | solution.py:170
  5.6 6.4 %all-to-all-start = ((bf16[64,32,128]{2,1,0:T(8,128)(2,1)}), bf16[64,32,128]{2,1,0:T(8,128)(2,1)S(1)}, u32[]{:S(2)}, u32[]{:S(2)}) async-start(bf16[64,32,128]{2,1,0:T(8,128)(2,1)} %get-tuple-element.10), calls=%async_computation | async-start | bytes 1048576 | tf_op jit(solution)/shard_map/all_to_all | solution.py:182
  12.0 7.2 %collective-permute-start.1 = (bf16[18,32,128]{2,1,0:T(8,128)(2,1)S(1)}, bf16[18,32,128]{2,1,0:T(8,128)(2,1)S(1)}, u32[]{:S(2)}, u32[]{:S(2)}) collective-permute-start(bf16[18,32,128]{2,1,0:T(8,128)(2,1)S(1)} %get-tuple-element.11.rim_ref), channel_id=1, source_target_pairs={{1,0},{2,1},{3,2},{4,3},{5,4},{6,5},{7,6},{8,7},{9,8},{10,9},{11,1... | collective-permute-start | bytes 442376 | tf_op jit(solution)/shard_map/ppermute | solution.py:148
  19.2 1.9 %collective-permute-start = (bf16[18,32,128]{2,1,0:T(8,128)(2,1)S(1)}, bf16[18,32,128]{2,1,0:T(8,128)(2,1)S(1)}, u32[]{:S(2)}, u32[]{:S(2)}) collective-permute-start(bf16[18,32,128]{2,1,0:T(8,128)(2,1)S(1)} %get-tuple-element.11.rim_ref), channel_id=1, source_target_pairs={{0,1},{1,2},{2,3},{3,4},{4,5},{5,6},{6,7},{7,8},{8,9},{9,10},{10,1... | collective-permute-start | bytes 442376 | tf_op jit(solution)/shard_map/ppermute | solution.py:148
  21.1 2.1 %collective-permute-done.1.after_ref = bf16[18,32,128]{2,1,0:T(8,128)(2,1)S(1)} collective-permute-done((bf16[18,32,128]{2,1,0:T(8,128)(2,1)S(1)}, bf16[18,32,128]{2,1,0:T(8,128)(2,1)S(1)}, u32[]{:S(2)}, u32[]{:S(2)}) %collective-permute-start.1) | collective-permute-done | bytes 147488 | tf_op jit(solution)/shard_map/ppermute | solution.py:148
  23.2 6.2 %collective-permute-done.before_ref = bf16[18,32,128]{2,1,0:T(8,128)(2,1)S(1)} collective-permute-done((bf16[18,32,128]{2,1,0:T(8,128)(2,1)S(1)}, bf16[18,32,128]{2,1,0:T(8,128)(2,1)S(1)}, u32[]{:S(2)}, u32[]{:S(2)}) %collective-permute-start) | collective-permute-done | bytes 147488 | tf_op jit(solution)/shard_map/ppermute | solution.py:148
  29.4 0.0 copy-start
  29.4 3.4 %copy-done = bf16[32,16,64,64]{3,2,1,0:T(8,128)(2,1)S(1)} copy-done((bf16[32,16,64,64]{3,2,1,0:T(8,128)(2,1)S(1)}, bf16[32,16,64,64]{3,2,1,0:T(8,128)(2,1)}, u32[]{:S(2)}) %copy-start) | copy-done | bytes 4194328
  32.8 0.0 copy-start.6
  32.8 1.4 %copy-done.6 = bf16[32,3,64,64]{3,2,1,0:T(8,128)(2,1)S(1)} copy-done((bf16[32,3,64,64]{3,2,1,0:T(8,128)(2,1)S(1)}, bf16[32,3,64,64]{3,2,1,0:T(8,128)(2,1)}, u32[]{:S(2)}) %copy-start.6) | copy-done | bytes 786456
  34.2 0.0 copy-start.8
  34.2 0.7 %copy-done.8 = s32[32,16]{0,1:T(8,128)S(1)} copy-done((s32[32,16]{0,1:T(8,128)S(1)}, s32[32,16]{0,1:T(8,128)}, u32[]{:S(2)}) %copy-start.8) | copy-done | bytes 2072
  34.9 0.0 copy-start.3
  34.9 0.0 copy-start.5
  34.9 0.0 copy-start.9
  34.9 0.0 copy-start.11
  34.9 4.6 %leaf.1 = (f32[16,32,128]{2,1,0:T(8,128)S(1)}, f32[16,32,128]{2,1,0:T(8,128)S(1)}) custom-call(s32[1]{0:T(128)} %bitcast.1.start_ref, s32[16,32]{1,0:T(8,128)S(1)} %bitcast.5, bf16[18,32,128]{2,1,0:T(8,128)(2,1)S(1)} %get-tuple-element.11.rim_ref, bf16[18,32,128]{2,1,0:T(8,128)(2,1)S(1)} %collective-permute-done.before_ref, ...), custom_call_target="tpu_custom_call" | custom-call | tf_op jit(solution)/shard_map/leaf/pallas_call | solution.py:187
  39.6 0.0 all-to-all-done.row_ref
  39.6 0.0 copy-done.3
  39.6 0.0 copy-done.5
  39.6 0.0 copy-done.9
  39.6 0.0 copy-done.11
  39.6 0.0 copy-start.1
  39.6 2.2 %copy-done.1 = bf16[16,16,64,64]{3,2,1,0:T(8,128)(2,1)S(1)} copy-done((bf16[16,16,64,64]{3,2,1,0:T(8,128)(2,1)S(1)}, bf16[16,16,64,64]{3,2,1,0:T(8,128)(2,1)}, u32[]{:S(2)}) %copy-start.1) | copy-done | bytes 2097176
  41.8 6.0 %down.1 = bf16[32,2048]{1,0:T(8,128)(2,1)} custom-call(s32[32]{0:T(128)S(1)} %copy-done.11, s32[16,16]{1,0:T(8,128)S(1)} %copy-done.9, bf16[64,32,128]{2,1,0:T(8,128)(2,1)S(1)} %all-to-all-done.row_ref, bf16[16,16,64,64]{3,2,1,0:T(8,128)(2,1)S(1)} %copy-done.1, bf16[32,64,64]{2,1,0:T(8,128)(2,1)S(1)} %copy-done.5, bf16[32,64,64]{2,1,0:T(8,128)(2,1)S(1)} %copy-done.3, ...), custom_call_target="tpu_custom_call" | custom-call | tf_op jit(solution)/shard_map/down/pallas_call | solution.py:199
Async XLA Ops:
  0.0 1.0 %copy-start.2 = (bf16[32,64,64]{2,1,0:T(8,128)(2,1)S(1)}, bf16[32,64,64]{2,1,0:T(8,128)(2,1)}, u32[]{:S(2)}) copy-start(bf16[32,64,64]{2,1,0:T(8,128)(2,1)} %basis_ref.3) | copy-start | bytes 786436
  1.0 1.0 %copy-start.4 = (bf16[32,64,64]{2,1,0:T(8,128)(2,1)S(1)}, bf16[32,64,64]{2,1,0:T(8,128)(2,1)}, u32[]{:S(2)}) copy-start(bf16[32,64,64]{2,1,0:T(8,128)(2,1)} %transfer_ref.3) | copy-start | bytes 786436
  2.1 0.9 %copy-start.7 = (bf16[2048,32]{0,1:T(8,128)(2,1)S(1)}, bf16[2048,32]{0,1:T(8,128)(2,1)}, u32[]{:S(2)}) copy-start(bf16[2048,32]{0,1:T(8,128)(2,1)} %param.9) | copy-start | bytes 393220
  3.0 0.7 %copy-start.10 = (s32[32]{0:T(128)S(1)}, s32[32]{0:T(128)}, u32[]{:S(2)}) copy-start(s32[32]{0:T(128)} %counts_ref.3) | copy-start | bytes 388
  5.6 33.9 %all-to-all-start = ((bf16[64,32,128]{2,1,0:T(8,128)(2,1)}), bf16[64,32,128]{2,1,0:T(8,128)(2,1)S(1)}, u32[]{:S(2)}, u32[]{:S(2)}) async-start(bf16[64,32,128]{2,1,0:T(8,128)(2,1)} %get-tuple-element.10), calls=%async_computation | async-start | bytes 1048576 | tf_op jit(solution)/shard_map/all_to_all | solution.py:182
  12.0 11.2 %collective-permute-start.1 = (bf16[18,32,128]{2,1,0:T(8,128)(2,1)S(1)}, bf16[18,32,128]{2,1,0:T(8,128)(2,1)S(1)}, u32[]{:S(2)}, u32[]{:S(2)}) collective-permute-start(bf16[18,32,128]{2,1,0:T(8,128)(2,1)S(1)} %get-tuple-element.11.rim_ref), channel_id=1, source_target_pairs={{1,0},{2,1},{3,2},{4,3},{5,4},{6,5},{7,6},{8,7},{9,8},{10,9},{11,1... | collective-permute-start | bytes 442376 | tf_op jit(solution)/shard_map/ppermute | solution.py:148
  19.2 10.2 %collective-permute-start = (bf16[18,32,128]{2,1,0:T(8,128)(2,1)S(1)}, bf16[18,32,128]{2,1,0:T(8,128)(2,1)S(1)}, u32[]{:S(2)}, u32[]{:S(2)}) collective-permute-start(bf16[18,32,128]{2,1,0:T(8,128)(2,1)S(1)} %get-tuple-element.11.rim_ref), channel_id=1, source_target_pairs={{0,1},{1,2},{2,3},{3,4},{4,5},{5,6},{6,7},{7,8},{8,9},{9,10},{10,1... | collective-permute-start | bytes 442376 | tf_op jit(solution)/shard_map/ppermute | solution.py:148
  29.4 3.4 %copy-start = (bf16[32,16,64,64]{3,2,1,0:T(8,128)(2,1)S(1)}, bf16[32,16,64,64]{3,2,1,0:T(8,128)(2,1)}, u32[]{:S(2)}) copy-start(bf16[32,16,64,64]{3,2,1,0:T(8,128)(2,1)} %coupling_ref.2) | copy-start | bytes 12582916
  32.8 1.4 %copy-start.6 = (bf16[32,3,64,64]{3,2,1,0:T(8,128)(2,1)S(1)}, bf16[32,3,64,64]{3,2,1,0:T(8,128)(2,1)}, u32[]{:S(2)}) copy-start(bf16[32,3,64,64]{3,2,1,0:T(8,128)(2,1)} %near_ref.1) | copy-start | bytes 2359300
  34.2 0.7 %copy-start.8 = (s32[32,16]{0,1:T(8,128)S(1)}, s32[32,16]{0,1:T(8,128)}, u32[]{:S(2)}) copy-start(s32[32,16]{0,1:T(8,128)} %param.14) | copy-start | bytes 6148
  34.9 4.7 %copy-start.3 = (bf16[32,64,64]{2,1,0:T(8,128)(2,1)S(1)}, bf16[32,64,64]{2,1,0:T(8,128)(2,1)}, u32[]{:S(2)}) copy-start(bf16[32,64,64]{2,1,0:T(8,128)(2,1)} %basis_ref.3) | copy-start | bytes 786436
  34.9 4.7 %copy-start.5 = (bf16[32,64,64]{2,1,0:T(8,128)(2,1)S(1)}, bf16[32,64,64]{2,1,0:T(8,128)(2,1)}, u32[]{:S(2)}) copy-start(bf16[32,64,64]{2,1,0:T(8,128)(2,1)} %transfer_ref.3) | copy-start | bytes 786436
  34.9 4.7 %copy-start.9 = (s32[16,16]{1,0:T(8,128)S(1)}, s32[16,16]{1,0:T(8,128)}, u32[]{:S(2)}) copy-start(s32[16,16]{1,0:T(8,128)} %partners_ref.1) | copy-start | bytes 3076
  34.9 4.7 %copy-start.11 = (s32[32]{0:T(128)S(1)}, s32[32]{0:T(128)}, u32[]{:S(2)}) copy-start(s32[32]{0:T(128)} %counts_ref.3) | copy-start | bytes 388
  39.6 2.2 %copy-start.1 = (bf16[16,16,64,64]{3,2,1,0:T(8,128)(2,1)S(1)}, bf16[16,16,64,64]{3,2,1,0:T(8,128)(2,1)}, u32[]{:S(2)}) copy-start(bf16[16,16,64,64]{3,2,1,0:T(8,128)(2,1)} %coupling_ref.3) | copy-start | bytes 6291460

commit v3 on v2

v3 whole, which is shorter than its diff:
```python
import functools

import jax
import jax.numpy as jnp
from jax import lax
from jax.experimental import pallas as pl
from jax.experimental.pallas import tpu as pltpu
from jax.sharding import PartitionSpec as P

VMEM = pl.BlockSpec(memory_space=pltpu.VMEM)
HBM = pl.BlockSpec(memory_space=pltpu.HBM)
NN = (((1,), (0,)), ((), ()))
NT = (((1,), (1,)), ((), ()))


def dot(a, b, dims):
    return lax.dot_general(a, b, dims, preferred_element_type=jnp.float32)


def left_half(sides, width):
    return lax.broadcasted_iota(jnp.int32, (sides, 2 * width), 1) < width


def swap(pair, width):
    return jnp.concatenate([pair[:, width:], pair[:, :width]], axis=1)


def start_all(copies, sems):
    started = [pltpu.make_async_copy(src, dst, sems.at[i]) for i, (src, dst) in enumerate(copies)]
    for copy in started:
        copy.start()
    return started


def up_kernel(
    copies, counts_hbm, charges_hbm, basis_hbm, transfer_hbm,
    rim_ref, live_ref, parents_ref, mask_ref,
    counts_ref, charges_ref, basis_ref, transfer_ref, sems,
):
    counts_in, charges_in, basis_in, transfer_in = start_all(
        [
            (counts_hbm, counts_ref), (charges_hbm, charges_ref),
            (basis_hbm, basis_ref), (transfer_hbm, transfer_ref),
        ],
        sems,
    )
    sides = charges_ref.shape[0]
    leaves, width, rank = basis_ref.shape
    pairs = leaves // 2
    own = pairs // 2
    left = left_half(sides, width)
    lane = lax.broadcasted_iota(jnp.int32, (sides, 2 * width), 1)
    slot = jnp.where(left, lane, lane - width)
    counts_in.wait()
    charges_in.wait()
    lives = []
    for a in range(pairs):
        charge = charges_ref[:, 2 * width * a : 2 * width * (a + 1)]
        mask = slot < jnp.where(left, counts_ref[2 * a], counts_ref[2 * a + 1])
        mask_ref[a] = mask[:8].astype(jnp.float32)
        live = jnp.where(mask, charge, jnp.zeros_like(charge))
        live_ref[a] = live
        lives.append(live)
    rim_ref[pairs] = lives[0]
    rim_ref[pairs + 1] = lives[-1]
    basis_in.wait()
    none = jnp.zeros_like(lives[0])
    coefs = []
    for a in range(pairs):
        live = lives[a]
        both = jnp.concatenate([jnp.where(left, live, none), jnp.where(left, none, live)], axis=0)
        coef = dot(both, basis_ref[2 * a : 2 * a + 2].reshape(2 * width, rank), NN)
        coef = jnp.concatenate([coef[:sides], coef[sides:]], axis=1).astype(jnp.bfloat16)
        rim_ref[a] = coef
        coefs.append(coef)
    transfer_in.wait()
    sums = [
        dot(coefs[a], transfer_ref[2 * a : 2 * a + 2].reshape(2 * rank, rank), NN)
        for a in range(pairs)
    ]
    for a in range(own):
        parent = jnp.concatenate(sums[2 * a : 2 * a + 2], axis=1).astype(jnp.bfloat16)
        for c in range(copies):
            parents_ref[c * own + a] = parent


def mid_kernel(
    row_ref, live_ref, coupling_hbm, near_hbm, parent_hbm, basis_hbm, transfer_hbm,
    packed_ref, parent_packed_ref, near_out_ref, rim_near_ref, basis_out_ref, transfer_out_ref,
    coupling_ref, near_ref, parent_ref, sems,
):
    leaves, many, rank, _ = coupling_ref.shape
    parents = parent_ref.shape[0]
    width = near_ref.shape[2]
    pairs = leaves // 2
    started = start_all(
        [(near_hbm, near_ref)]
        + [(coupling_hbm.at[pl.ds(4 * i, 4)], coupling_ref.at[pl.ds(4 * i, 4)]) for i in range(leaves // 4)]
        + [(parent_hbm.at[pl.ds(4 * i, 4)], parent_ref.at[pl.ds(4 * i, 4)]) for i in range(parents // 4)]
        + [(basis_hbm, basis_out_ref), (transfer_hbm, transfer_out_ref)],
        sems,
    )
    near_in, basis_in, transfer_in = started[0], started[-2], started[-1]
    coupling_in = started[1 : 1 + leaves // 4]
    parent_in = started[1 + leaves // 4 : -2]
    near_in.wait()
    rim_near_ref[0] = near_ref[0, 0]
    rim_near_ref[1] = near_ref[leaves - 1, 2]
    for a in range(pairs):
        here = live_ref[a]
        even = dot(here, jnp.concatenate([near_ref[2 * a, 1], near_ref[2 * a, 2]], axis=1), NT)
        odd = dot(here, jnp.concatenate([near_ref[2 * a + 1, 0], near_ref[2 * a + 1, 1]], axis=1), NT)
        if a > 0:
            even = even + dot(live_ref[a - 1][:, width:], near_ref[2 * a, 0], NT)
        if a < pairs - 1:
            odd = odd + dot(live_ref[a + 1][:, :width], near_ref[2 * a + 1, 2], NT)
        near_out_ref[a] = jnp.concatenate([even, odd], axis=1)

    def pack(src, dst, g):
        for j in range(0, many, 2):
            dst[g, :, rank * j : rank * (j + 2)] = jnp.concatenate([src[g, j], src[g, j + 1]], axis=1)

    for i, copy in enumerate(coupling_in):
        copy.wait()
        for g in range(4 * i, 4 * i + 4):
            pack(coupling_ref, packed_ref, g)
    for i, copy in enumerate(parent_in):
        copy.wait()
        for q in range(4 * i, 4 * i + 4):
            pack(parent_ref, parent_packed_ref, q)
    basis_in.wait()
    transfer_in.wait()


def spread_pair(dup_ref, at, pair, left, width):
    turned = swap(pair, width)
    dup_ref[at] = jnp.where(left, pair, turned)
    dup_ref[at + 1] = jnp.where(left, turned, pair)


def picked(dup_ref, partners, left):
    return jnp.concatenate(
        [
            jnp.where(left, dup_ref[partners[j]], dup_ref[partners[j + 1]])
            for j in range(0, len(partners), 2)
        ],
        axis=1,
    )


def leaf_kernel(
    axes, partners_hbm, rim_ref, even_ref, odd_ref, packed_ref, rim_near_ref,
    far_ref, edge_ref, dup_ref, partners_ref, sems,
):
    (partners_in,) = start_all([(partners_hbm, partners_ref)], sems)
    many, leaves = partners_ref.shape
    rank = packed_ref.shape[1]
    width = rim_near_ref.shape[1]
    pairs = leaves // 2
    sides = rim_ref.shape[1]
    left = left_half(sides, rank)
    device = lax.axis_index(axes[0]) * lax.axis_size(axes[1]) + lax.axis_index(axes[1])
    parity = lax.rem(device, 2)
    shift = leaves - device * leaves
    for ref, base in (
        (rim_ref, leaves), (even_ref, 2 * leaves * (1 - parity)), (odd_ref, 2 * leaves * parity),
    ):
        for a in range(pairs):
            spread_pair(dup_ref, base + 2 * a, ref[a], left, rank)
    before = jnp.where(parity == 1, even_ref[pairs + 1], odd_ref[pairs + 1])
    after = jnp.where(parity == 1, odd_ref[pairs], even_ref[pairs])
    low = dot(before[:, width:], rim_near_ref[0], NT)
    high = dot(after[:, :width], rim_near_ref[1], NT)
    edge_ref[0] = jnp.concatenate([low, jnp.zeros_like(low)], axis=1)
    edge_ref[1] = jnp.concatenate([jnp.zeros_like(high), high], axis=1)
    partners_in.wait()
    for a in range(pairs):
        fars = []
        for g in (2 * a, 2 * a + 1):
            partners = [partners_ref[j, g] + shift for j in range(many)]
            fars.append(dot(picked(dup_ref, partners, left), packed_ref[g], NT))
        far_ref[a] = jnp.concatenate(fars, axis=1)


def down_kernel(
    axis, partners_hbm, same_ref, other_ref, packed_ref, transfer_ref, basis_ref,
    far_ref, near_ref, edge_ref, mask_ref,
    out_ref, dup_ref, partners_ref, local_ref, down_ref, sems,
):
    (partners_in,) = start_all([(partners_hbm, partners_ref)], sems)
    parents, many = partners_ref.shape
    rank = packed_ref.shape[1]
    width = basis_ref.shape[1]
    sides = same_ref.shape[1]
    half = 2 * same_ref.shape[0]
    left = left_half(sides, rank)
    parity = lax.rem(lax.axis_index(axis), 2)

    def spread(a, carry):
        spread_pair(dup_ref, half * parity + 2 * a, same_ref[a], left, rank)
        spread_pair(dup_ref, half * (1 - parity) + 2 * a, other_ref[a], left, rank)
        return carry

    lax.fori_loop(0, same_ref.shape[0], spread, 0, unroll=8)
    partners_in.wait()

    def place(partner):
        relative = lax.rem(partner, 2 * half)
        source = relative // parents
        return lax.rem(source, 2) * half + source // 2 * parents + lax.rem(relative, parents)

    for q in range(parents):
        partners = [place(partners_ref[q, j]) for j in range(many)]
        far = dot(picked(dup_ref, partners, left), packed_ref[q], NT)
        down_ref[q] = far.astype(jnp.bfloat16)
    for q in range(parents):
        local = far_ref[q] + dot(down_ref[q], transfer_ref[2 * q : 2 * q + 2].reshape(2 * rank, rank), NT)
        local_ref[q] = local.astype(jnp.bfloat16)
    for q in range(parents):
        local = local_ref[q]
        total = jnp.concatenate(
            [dot(local[:, :rank], basis_ref[2 * q], NT), dot(local[:, rank:], basis_ref[2 * q + 1], NT)],
            axis=1,
        )
        total = total + near_ref[q]
        if q == 0:
            total = total + edge_ref[0]
        if q == parents - 1:
            total = total + edge_ref[1]
        total = total * mask_ref[q][:1]
        out_ref[:, 2 * width * q : 2 * width * (q + 1)] = total.astype(out_ref.dtype)


def per_device(
    charges,
    panel_counts,
    basis,
    transfer,
    leaf_coupling,
    leaf_partners,
    near_blocks,
    parent_coupling,
    parent_partners,
):
    leaves, width, rank = basis.shape
    sides = charges.shape[1]
    parents, many = parent_partners.shape
    pairs = leaves // 2
    own = pairs // 2
    n = lax.axis_size("gy")
    total = n * lax.axis_size("gx")
    axes = ("gx", "gy")
    bf16, f32 = jnp.bfloat16, jnp.float32
    keep = lambda *arrays: [pltpu.with_memory_space_constraint(a, pltpu.HBM) for a in arrays]
    shape = pltpu.VMEM
    dma = lambda count: pltpu.SemaphoreType.DMA((count,))
    params = lambda mib: pltpu.CompilerParams(vmem_limit_bytes=mib * 2**20)

    rim, live, sent, mask = pl.pallas_call(
        functools.partial(up_kernel, n // 2),
        name="up",
        out_shape=[
            shape((pairs + 2, sides, 2 * rank), bf16),
            shape((pairs, sides, 2 * width), bf16),
            shape((n // 2 * own, sides, 2 * rank), bf16),
            shape((pairs, 8, 2 * width), f32),
        ],
        in_specs=[HBM] * 4,
        out_specs=[VMEM] * 4,
        scratch_shapes=[
            pltpu.SMEM((leaves,), jnp.int32),
            pltpu.VMEM((sides, leaves * width), bf16),
            pltpu.VMEM((leaves, width, rank), bf16),
            pltpu.VMEM((leaves, rank, rank), bf16),
            dma(4),
        ],
        compiler_params=params(8),
    )(*keep(panel_counts, charges.T, basis, transfer))

    groups = [list(range(c, n, 2)) for c in range(2)]
    same = lax.all_to_all(sent, "gy", 0, 0, axis_index_groups=groups, tiled=True)
    even = lax.ppermute(rim, axes, [(i, i ^ 1) for i in range(total)])
    steps = [(i, i + 1) for i in range(1, total - 1, 2)]
    odd = lax.ppermute(rim, axes, steps + [(b, a) for a, b in steps])
    other = lax.ppermute(same, "gy", [(i, i ^ 1) for i in range(n)])

    packed, parent_packed, near, rim_near, basis_in, transfer_in = pl.pallas_call(
        mid_kernel,
        name="mid",
        out_shape=[
            shape((leaves, rank, many * rank), bf16),
            shape((parents, rank, many * rank), bf16),
            shape((pairs, sides, 2 * width), f32),
            shape((2, width, width), bf16),
            shape(basis.shape, bf16),
            shape(transfer.shape, bf16),
        ],
        in_specs=[VMEM] * 2 + [HBM] * 5,
        out_specs=[VMEM] * 6,
        scratch_shapes=[
            pltpu.VMEM(leaf_coupling.shape, bf16),
            pltpu.VMEM(near_blocks.shape, bf16),
            pltpu.VMEM(parent_coupling.shape, bf16),
            dma(3 + leaves // 4 + parents // 4),
        ],
        compiler_params=params(20),
    )(same, live, *keep(leaf_coupling, near_blocks, parent_coupling, basis, transfer))

    far, edge = pl.pallas_call(
        functools.partial(leaf_kernel, axes),
        name="leaf",
        out_shape=[shape((pairs, sides, 2 * rank), f32), shape((2, sides, 2 * width), f32)],
        in_specs=[HBM] + [VMEM] * 5,
        out_specs=[VMEM, VMEM],
        scratch_shapes=[
            pltpu.VMEM((3 * leaves, sides, 2 * rank), bf16),
            pltpu.SMEM((leaf_partners.shape[1], leaves), jnp.int32),
            dma(1),
        ],
        compiler_params=params(8),
    )(*keep(leaf_partners.T), rim, even, odd, packed, rim_near)

    out = pl.pallas_call(
        functools.partial(down_kernel, "gy"),
        name="down",
        out_shape=jax.ShapeDtypeStruct((sides, leaves * width), bf16),
        in_specs=[HBM] + [VMEM] * 9,
        out_specs=VMEM,
        scratch_shapes=[
            pltpu.VMEM((n * parents, sides, 2 * rank), bf16),
            pltpu.SMEM(parent_partners.shape, jnp.int32),
            pltpu.VMEM((pairs, sides, 2 * rank), bf16),
            pltpu.VMEM((parents, sides, rank), bf16),
            dma(1),
        ],
        compiler_params=params(12),
    )(*keep(parent_partners), same, other, parent_packed, transfer_in, basis_in, far, near, edge, mask)
    return out.T


def solution(mesh):
    in_specs = (
        P(("gx", "gy"), None),
        P(("gx", "gy")),
        P(("gx", "gy"), None, None),
        P(("gx", "gy"), None, None),
        P(("gx", "gy"), None, None, None),
        P(("gx", "gy"), None),
        P(("gx", "gy"), None, None, None),
        P(("gx", "gy"), None, None, None),
        P(("gx", "gy"), None),
    )
    out_specs = P(("gx", "gy"), None)
    return jax.shard_map(
        per_device, mesh=mesh, in_specs=in_specs, out_specs=out_specs, check_vma=False
    )
```

time: 48.3 us -> 36 us (0.75)
  blocking collectives: 0 us -> 12.1 us
  local copies, waits for them, and re-layouts: 11.3 us -> 0 us
  waiting for transfers between devices: 8.29 us -> 0.01 us
  starting transfers between devices: 15.5 us -> 8.89 us
  Pallas kernels: 12.6 us -> 14.6 us
    all_to_all x0 -> x1, blocking collectives: none -> 12.1 us  [per_device(): lax.all_to_all(sent, 'gy', 0, 0, axis_index_groups=groups, tiled=True)]
    unnamed x24 -> x0, local copies, waits for them, and re-layouts: 11.3 us -> none
    ppermute x2 -> x3, waiting for transfers between devices: 8.29 us -> 0.01 us  [the longest x1 0.01 us: per_device(): other = lax.ppermute(same, 'gy', [(i, i ^ 1) for i in range(n)])]
    all_to_all x1 -> x0, starting transfers between devices: 6.38 us -> none  [per_device(): row = lax.all_to_all(parents, 'gy', 0, 0, tiled=True)]
    pallas_call x3 -> x4, Pallas kernels: 12.6 us -> 14.6 us  [the longest x1 5.44 us: per_device(): pl.pallas_call(mid_kernel, name='mid', out_shape=[shape((leaves, rank, ma...]
    ppermute x2 -> x3, starting transfers between devices: 9.1 us -> 8.89 us  [the longest x1 7.42 us: per_device(): odd = lax.ppermute(rim, axes, steps + [(b, a) for a, b in steps])]
  transfers between devices with their start and end apart: 3 -> 3, of which waited for: 2 -> 0; matrix products, arithmetic and copies ran while one was open for 0% -> 0% of each run, Pallas kernels for 10% -> 21%
where the time goes in v3:
time: 36 us; the launch traced here: 35.7 us
  Pallas kernels  14.6 us (41%)
  blocking collectives  12.1 us (34%)
  starting transfers between devices  8.89 us (25%)
    all_to_all x1, blocking collectives, per_device(): lax.all_to_all(sent, 'gy', 0, 0, axis_index_groups=groups, tiled=True)  12.1 us
    ppermute x1, starting transfers between devices, per_device(): odd = lax.ppermute(rim, axes, steps + [(b, a) for a, b in steps])  7.42 us
    pallas_call x1, Pallas kernels, per_device(): pl.pallas_call(mid_kernel, name='mid', out_shape=[shape((leaves, rank, ma...  5.44 us
    pallas_call x1, Pallas kernels, per_device(): pl.pallas_call(functools.partial(down_kernel, 'gy'), name='down', out_sha...  5.26 us
    pallas_call x1, Pallas kernels, per_device(): pl.pallas_call(functools.partial(leaf_kernel, axes), name='leaf', out_sha...  2.13 us
    pallas_call x1, Pallas kernels, per_device(): pl.pallas_call(functools.partial(up_kernel, n // 2), name='up', out_shape...  1.82 us
    ppermute x1, starting transfers between devices, per_device(): other = lax.ppermute(same, 'gy', [(i, i ^ 1) for i in range(n)])  1.24 us
  transfers between devices with their start and end apart: 3, of which 0 were waited for; matrix products, arithmetic and copies ran while one was open for 0% of the time, Pallas kernels for 21%

profile of v3, /device:TPU:1, one launch (start us, length us, event | category | flops | bytes accessed | tf_op | source)
XLA Modules:
  0.0 35.7 jit_solution(9102012802497298414)
XLA Ops:
  0.0 1.8 %up.1 = (bf16[18,32,128]{2,1,0:T(8,128)(2,1)S(1)}, bf16[16,32,128]{2,1,0:T(8,128)(2,1)S(1)}, bf16[32,32,128]{2,1,0:T(8,128)(2,1)S(1)}, f32[16,8,128]{2,1,0:T(8,128)S(1)}) custom-call(s32[32]{0:T(128)} %counts_hbm.1, bf16[32,2048]{1,0:T(8,128)(2,1)} %bitcast.3, bf16[32,64,64]{2,1,0:T(8,128)(2,1)} %basis_hbm.3, bf16[32,64,64]{2,1,0:T(8,128)(2,1)} %transfer_hbm.3), custom_call_target="tpu_custom_call" | custom-call | tf_op jit(solution)/shard_map/up/pallas_call | solution.py:259
  1.8 12.1 %all_to_all.5.row_ref.same_ref = bf16[32,32,128]{2,1,0:T(8,128)(2,1)S(1)} all-to-all(bf16[32,32,128]{2,1,0:T(8,128)(2,1)S(1)} %get-tuple-element.17), channel_id=1, replica_groups={{0,2,4,6},{1,3,5,7},{8,10,12,14},{9,11,13,15},{16,18,20,22},{17,19,21,2..., dimensions={0} | all-to-all | bytes 524288 | tf_op jit(solution)/shard_map/all_to_all | solution.py:281
  13.9 1.2 %collective-permute-start = (bf16[32,32,128]{2,1,0:T(8,128)(2,1)S(1)}, bf16[32,32,128]{2,1,0:T(8,128)(2,1)S(1)}, u32[]{:S(2)}, u32[]{:S(2)}) collective-permute-start(bf16[32,32,128]{2,1,0:T(8,128)(2,1)S(1)} %all_to_all.5.row_ref.same_ref), channel_id=1, source_target_pairs={{0,1},{1,0},{2,3},{3,2},{4,5},{5,4},{6,7},{7,6},{8,9},{9,8},{10,11... | collective-permute-start | bytes 786440 | tf_op jit(solution)/shard_map/ppermute | solution.py:285
  15.2 0.2 collective-permute-start.1
  15.4 7.4 %collective-permute-start.2 = (bf16[18,32,128]{2,1,0:T(8,128)(2,1)S(1)}, bf16[18,32,128]{2,1,0:T(8,128)(2,1)S(1)}, u32[]{:S(2)}, u32[]{:S(2)}) collective-permute-start(bf16[18,32,128]{2,1,0:T(8,128)(2,1)S(1)} %get-tuple-element.22.rim_ref), channel_id=1, source_target_pairs={{1,2},{3,4},{5,6},{7,8},{9,10},{11,12},{13,14},{15,16},{17,18},{19... | collective-permute-start | bytes 442376 | tf_op jit(solution)/shard_map/ppermute | solution.py:284
  22.8 5.4 %mid.1 = (bf16[32,64,1024]{2,1,0:T(8,128)(2,1)S(1)}, bf16[16,64,1024]{2,1,0:T(8,128)(2,1)S(1)}, f32[16,32,128]{2,1,0:T(8,128)S(1)}, bf16[2,64,64]{2,1,0:T(8,128)...) custom-call(bf16[32,32,128]{2,1,0:T(8,128)(2,1)S(1)} %all_to_all.5.row_ref.same_ref, ...), custom_call_target="tpu_custom_call" | custom-call | tf_op jit(solution)/shard_map/mid/pallas_call | solution.py:287
  28.3 0.0 collective-permute-done.1.even_ref
  28.3 0.0 collective-permute-done.2.odd_ref
  28.3 2.1 %leaf.1 = (f32[16,32,128]{2,1,0:T(8,128)S(1)}, f32[2,32,128]{2,1,0:T(8,128)S(1)}) custom-call(s32[16,32]{1,0:T(8,128)} %bitcast.4, bf16[18,32,128]{2,1,0:T(8,128)(2,1)S(1)} %get-tuple-element.22.rim_ref, bf16[18,32,128]{2,1,0:T(8,128)(2,1)S(1)} %collective-permute-done.1.even_ref, bf16[18,32,128]{2,1,0:T(8,128)(2,1)S(1)} %collective-permute-done.2.odd_ref, ...), custom_call_target="tpu_custom_call" | custom-call | tf_op jit(solution)/shard_map/leaf/pallas_call | solution.py:309
  30.4 0.0 collective-permute-done.other_ref
  30.4 5.3 %down.1 = bf16[32,2048]{1,0:T(8,128)(2,1)} custom-call(s32[16,16]{1,0:T(8,128)} %partners_hbm.1, bf16[32,32,128]{2,1,0:T(8,128)(2,1)S(1)} %all_to_all.5.row_ref.same_ref, bf16[32,32,128]{2,1,0:T(8,128)(2,1)S(1)} %collective-permute-done.other_ref, bf16[16,64,1024]{2,1,0:T(8,128)(2,1)S(1)} %get-tuple-element.19.packed_ref, ...), custom_call_target="tpu_custom_call" | custom-call | tf_op jit(solution)/shard_map/down/pallas_call | solution.py:323
Async XLA Ops:
  13.9 16.5 %collective-permute-start = (bf16[32,32,128]{2,1,0:T(8,128)(2,1)S(1)}, bf16[32,32,128]{2,1,0:T(8,128)(2,1)S(1)}, u32[]{:S(2)}, u32[]{:S(2)}) collective-permute-start(bf16[32,32,128]{2,1,0:T(8,128)(2,1)S(1)} %all_to_all.5.row_ref.same_ref), channel_id=1, source_target_pairs={{0,1},{1,0},{2,3},{3,2},{4,5},{5,4},{6,7},{7,6},{8,9},{9,8},{10,11... | collective-permute-start | bytes 786440 | tf_op jit(solution)/shard_map/ppermute | solution.py:285
  15.2 13.1 %collective-permute-start.1 = (bf16[18,32,128]{2,1,0:T(8,128)(2,1)S(1)}, bf16[18,32,128]{2,1,0:T(8,128)(2,1)S(1)}, u32[]{:S(2)}, u32[]{:S(2)}) collective-permute-start(bf16[18,32,128]{2,1,0:T(8,128)(2,1)S(1)} %get-tuple-element.22.rim_ref), channel_id=1, source_target_pairs={{0,1},{1,0},{2,3},{3,2},{4,5},{5,4},{6,7},{7,6},{8,9},{9,8},{10,11... | collective-permute-start | bytes 442376 | tf_op jit(solution)/shard_map/ppermute | solution.py:282
  15.4 12.9 %collective-permute-start.2 = (bf16[18,32,128]{2,1,0:T(8,128)(2,1)S(1)}, bf16[18,32,128]{2,1,0:T(8,128)(2,1)S(1)}, u32[]{:S(2)}, u32[]{:S(2)}) collective-permute-start(bf16[18,32,128]{2,1,0:T(8,128)(2,1)S(1)} %get-tuple-element.22.rim_ref), channel_id=1, source_target_pairs={{1,2},{3,4},{5,6},{7,8},{9,10},{11,12},{13,14},{15,16},{17,18},{19... | collective-permute-start | bytes 442376 | tf_op jit(solution)/shard_map/ppermute | solution.py:284

commit v4 on v3

--- a/solution.py
+++ b/solution.py
@@ -23,6 +23,21 @@
 
 def swap(pair, width):
     return jnp.concatenate([pair[:, width:], pair[:, :width]], axis=1)
+
+
+def mod(x, m):
+    return x & (m - 1) if m & (m - 1) == 0 else lax.rem(x, m)
+
+
+def div(x, m):
+    return x >> (m.bit_length() - 1) if m & (m - 1) == 0 else x // m
+
+
+def position(axes):
+    index = 0
+    for axis in axes:
+        index = index * lax.axis_size(axis) + lax.axis_index(axis)
+    return index
 
 
 def start_all(copies, sems):
@@ -85,8 +100,10 @@
 
 
 def mid_kernel(
-    row_ref, live_ref, coupling_hbm, near_hbm, parent_hbm, basis_hbm, transfer_hbm,
+    axes, live_ref, coupling_hbm, near_hbm, parent_hbm, basis_hbm, transfer_hbm, leaf_partners_hbm,
+    parent_partners_hbm,
     packed_ref, parent_packed_ref, near_out_ref, rim_near_ref, basis_out_ref, transfer_out_ref,
+    leaf_at_ref, parent_at_ref,
     coupling_ref, near_ref, parent_ref, sems,
 ):
     leaves, many, rank, _ = coupling_ref.shape
@@ -97,12 +114,13 @@
         [(near_hbm, near_ref)]
         + [(coupling_hbm.at[pl.ds(4 * i, 4)], coupling_ref.at[pl.ds(4 * i, 4)]) for i in range(leaves // 4)]
         + [(parent_hbm.at[pl.ds(4 * i, 4)], parent_ref.at[pl.ds(4 * i, 4)]) for i in range(parents // 4)]
-        + [(basis_hbm, basis_out_ref), (transfer_hbm, transfer_out_ref)],
+        + [(basis_hbm, basis_out_ref), (transfer_hbm, transfer_out_ref)]
+        + [(leaf_partners_hbm, leaf_at_ref), (parent_partners_hbm, parent_at_ref)],
         sems,
     )
-    near_in, basis_in, transfer_in = started[0], started[-2], started[-1]
+    near_in = started[0]
     coupling_in = started[1 : 1 + leaves // 4]
-    parent_in = started[1 + leaves // 4 : -2]
+    parent_in = started[1 + leaves // 4 : -4]
     near_in.wait()
     rim_near_ref[0] = near_ref[0, 0]
     rim_near_ref[1] = near_ref[leaves - 1, 2]
@@ -128,90 +146,88 @@
         copy.wait()
         for q in range(4 * i, 4 * i + 4):
             pack(parent_ref, parent_packed_ref, q)
-    basis_in.wait()
-    transfer_in.wait()
-
-
-def spread_pair(dup_ref, at, pair, left, width):
-    turned = swap(pair, width)
-    dup_ref[at] = jnp.where(left, pair, turned)
-    dup_ref[at + 1] = jnp.where(left, turned, pair)
-
-
-def picked(dup_ref, partners, left):
+    for copy in started[-4:]:
+        copy.wait()
+    wanted = leaf_at_ref[...] + (1 - position(axes)) * leaves
+    leaf_at_ref[...] = wanted ^ (lax.broadcasted_iota(jnp.int32, wanted.shape, 0) & 1)
+    n, inner = lax.axis_size(axes[1]) * lax.axis_size(axes[2]), lax.axis_size(axes[2])
+    wanted = mod(parent_at_ref[...], n * parents)
+    source = div(wanted, parents)
+    wanted = (mod(source, inner) * (n // inner) + div(source, inner)) * parents + mod(wanted, parents)
+    parent_at_ref[...] = wanted ^ (lax.broadcasted_iota(jnp.int32, wanted.shape, 1) & 1)
+
+
+def spread_pair(table_ref, at, pair, width):
+    table_ref[at] = pair
+    table_ref[at + 1] = swap(pair, width)
+
+
+def picked(table_ref, rows, left):
     return jnp.concatenate(
         [
-            jnp.where(left, dup_ref[partners[j]], dup_ref[partners[j + 1]])
-            for j in range(0, len(partners), 2)
+            jnp.where(left, table_ref[rows[j]], table_ref[rows[j + 1]])
+            for j in range(0, len(rows), 2)
         ],
         axis=1,
     )
 
 
 def leaf_kernel(
-    axes, partners_hbm, rim_ref, even_ref, odd_ref, packed_ref, rim_near_ref,
-    far_ref, edge_ref, dup_ref, partners_ref, sems,
-):
-    (partners_in,) = start_all([(partners_hbm, partners_ref)], sems)
-    many, leaves = partners_ref.shape
+    axes, at_vmem, rim_ref, even_ref, odd_ref, packed_ref, rim_near_ref,
+    far_ref, edge_ref, table_ref, at_ref, sems,
+):
+    (at_in,) = start_all([(at_vmem, at_ref)], sems)
+    many, leaves = at_ref.shape
     rank = packed_ref.shape[1]
     width = rim_near_ref.shape[1]
     pairs = leaves // 2
     sides = rim_ref.shape[1]
     left = left_half(sides, rank)
-    device = lax.axis_index(axes[0]) * lax.axis_size(axes[1]) + lax.axis_index(axes[1])
-    parity = lax.rem(device, 2)
-    shift = leaves - device * leaves
+    parity = lax.rem(position(axes), 2)
     for ref, base in (
         (rim_ref, leaves), (even_ref, 2 * leaves * (1 - parity)), (odd_ref, 2 * leaves * parity),
     ):
         for a in range(pairs):
-            spread_pair(dup_ref, base + 2 * a, ref[a], left, rank)
+            spread_pair(table_ref, base + 2 * a, ref[a], rank)
     before = jnp.where(parity == 1, even_ref[pairs + 1], odd_ref[pairs + 1])
     after = jnp.where(parity == 1, odd_ref[pairs], even_ref[pairs])
     low = dot(before[:, width:], rim_near_ref[0], NT)
     high = dot(after[:, :width], rim_near_ref[1], NT)
     edge_ref[0] = jnp.concatenate([low, jnp.zeros_like(low)], axis=1)
     edge_ref[1] = jnp.concatenate([jnp.zeros_like(high), high], axis=1)
-    partners_in.wait()
+    at_in.wait()
     for a in range(pairs):
         fars = []
         for g in (2 * a, 2 * a + 1):
-            partners = [partners_ref[j, g] + shift for j in range(many)]
-            fars.append(dot(picked(dup_ref, partners, left), packed_ref[g], NT))
+            rows = [at_ref[j, g] for j in range(many)]
+            fars.append(dot(picked(table_ref, rows, left), packed_ref[g], NT))
         far_ref[a] = jnp.concatenate(fars, axis=1)
 
 
 def down_kernel(
-    axis, partners_hbm, same_ref, other_ref, packed_ref, transfer_ref, basis_ref,
+    axis, at_vmem, same_ref, other_ref, packed_ref, transfer_ref, basis_ref,
     far_ref, near_ref, edge_ref, mask_ref,
-    out_ref, dup_ref, partners_ref, local_ref, down_ref, sems,
-):
-    (partners_in,) = start_all([(partners_hbm, partners_ref)], sems)
-    parents, many = partners_ref.shape
+    out_ref, table_ref, at_ref, local_ref, down_ref, sems,
+):
+    (at_in,) = start_all([(at_vmem, at_ref)], sems)
+    parents, many = at_ref.shape
     rank = packed_ref.shape[1]
     width = basis_ref.shape[1]
     sides = same_ref.shape[1]
     half = 2 * same_ref.shape[0]
     left = left_half(sides, rank)
-    parity = lax.rem(lax.axis_index(axis), 2)
+    parity = lax.axis_index(axis)
 
     def spread(a, carry):
-        spread_pair(dup_ref, half * parity + 2 * a, same_ref[a], left, rank)
-        spread_pair(dup_ref, half * (1 - parity) + 2 * a, other_ref[a], left, rank)
+        spread_pair(table_ref, half * parity + 2 * a, same_ref[a], rank)
+        spread_pair(table_ref, half * (1 - parity) + 2 * a, other_ref[a], rank)
         return carry
 
-    lax.fori_loop(0, same_ref.shape[0], spread, 0, unroll=8)
-    partners_in.wait()
-
-    def place(partner):
-        relative = lax.rem(partner, 2 * half)
-        source = relative // parents
-        return lax.rem(source, 2) * half + source // 2 * parents + lax.rem(relative, parents)
-
+    lax.fori_loop(0, same_ref.shape[0], spread, 0, unroll=min(32, same_ref.shape[0]))
+    at_in.wait()
     for q in range(parents):
-        partners = [place(partners_ref[q, j]) for j in range(many)]
-        far = dot(picked(dup_ref, partners, left), packed_ref[q], NT)
+        rows = [at_ref[q, j] for j in range(many)]
+        far = dot(picked(table_ref, rows, left), packed_ref[q], NT)
         down_ref[q] = far.astype(jnp.bfloat16)
     for q in range(parents):
         local = far_ref[q] + dot(down_ref[q], transfer_ref[2 * q : 2 * q + 2].reshape(2 * rank, rank), NT)
@@ -247,9 +263,9 @@
     parents, many = parent_partners.shape
     pairs = leaves // 2
     own = pairs // 2
-    n = lax.axis_size("gy")
+    axes = ("gx", "gz", "gp")
+    n = lax.axis_size("gz") * lax.axis_size("gp")
     total = n * lax.axis_size("gx")
-    axes = ("gx", "gy")
     bf16, f32 = jnp.bfloat16, jnp.float32
     keep = lambda *arrays: [pltpu.with_memory_space_constraint(a, pltpu.HBM) for a in arrays]
     shape = pltpu.VMEM
@@ -277,15 +293,14 @@
         compiler_params=params(8),
     )(*keep(panel_counts, charges.T, basis, transfer))
 
-    groups = [list(range(c, n, 2)) for c in range(2)]
-    same = lax.all_to_all(sent, "gy", 0, 0, axis_index_groups=groups, tiled=True)
+    same = lax.all_to_all(sent, "gz", 0, 0, tiled=True)
     even = lax.ppermute(rim, axes, [(i, i ^ 1) for i in range(total)])
     steps = [(i, i + 1) for i in range(1, total - 1, 2)]
     odd = lax.ppermute(rim, axes, steps + [(b, a) for a, b in steps])
-    other = lax.ppermute(same, "gy", [(i, i ^ 1) for i in range(n)])
-
-    packed, parent_packed, near, rim_near, basis_in, transfer_in = pl.pallas_call(
-        mid_kernel,
+    other = lax.ppermute(same, "gp", [(0, 1), (1, 0)])
+
+    packed, parent_packed, near, rim_near, basis_in, transfer_in, leaf_at, parent_at = pl.pallas_call(
+        functools.partial(mid_kernel, axes),
         name="mid",
         out_shape=[
             shape((leaves, rank, many * rank), bf16),
@@ -294,63 +309,72 @@
             shape((2, width, width), bf16),
             shape(basis.shape, bf16),
             shape(transfer.shape, bf16),
-        ],
-        in_specs=[VMEM] * 2 + [HBM] * 5,
-        out_specs=[VMEM] * 6,
+            shape((many, leaves), jnp.int32),
+            shape((parents, many), jnp.int32),
+        ],
+        in_specs=[VMEM] + [HBM] * 7,
+        out_specs=[VMEM] * 8,
         scratch_shapes=[
             pltpu.VMEM(leaf_coupling.shape, bf16),
             pltpu.VMEM(near_blocks.shape, bf16),
             pltpu.VMEM(parent_coupling.shape, bf16),
-            dma(3 + leaves // 4 + parents // 4),
+            dma(5 + leaves // 4 + parents // 4),
         ],
         compiler_params=params(20),
-    )(same, live, *keep(leaf_coupling, near_blocks, parent_coupling, basis, transfer))
+    )(
+        live,
+        *keep(
+            leaf_coupling, near_blocks, parent_coupling, basis, transfer, leaf_partners.T, parent_partners
+        ),
+    )
 
     far, edge = pl.pallas_call(
         functools.partial(leaf_kernel, axes),
         name="leaf",
         out_shape=[shape((pairs, sides, 2 * rank), f32), shape((2, sides, 2 * width), f32)],
-        in_specs=[HBM] + [VMEM] * 5,
+        in_specs=[VMEM] * 6,
         out_specs=[VMEM, VMEM],
         scratch_shapes=[
             pltpu.VMEM((3 * leaves, sides, 2 * rank), bf16),
-            pltpu.SMEM((leaf_partners.shape[1], leaves), jnp.int32),
+            pltpu.SMEM((many, leaves), jnp.int32),
             dma(1),
         ],
         compiler_params=params(8),
-    )(*keep(leaf_partners.T), rim, even, odd, packed, rim_near)
+    )(leaf_at, rim, even, odd, packed, rim_near)
 
     out = pl.pallas_call(
-        functools.partial(down_kernel, "gy"),
+        functools.partial(down_kernel, "gp"),
         name="down",
         out_shape=jax.ShapeDtypeStruct((sides, leaves * width), bf16),
-        in_specs=[HBM] + [VMEM] * 9,
+        in_specs=[VMEM] * 10,
         out_specs=VMEM,
         scratch_shapes=[
             pltpu.VMEM((n * parents, sides, 2 * rank), bf16),
-            pltpu.SMEM(parent_partners.shape, jnp.int32),
+            pltpu.SMEM((parents, many), jnp.int32),
             pltpu.VMEM((pairs, sides, 2 * rank), bf16),
             pltpu.VMEM((parents, sides, rank), bf16),
             dma(1),
         ],
         compiler_params=params(12),
-    )(*keep(parent_partners), same, other, parent_packed, transfer_in, basis_in, far, near, edge, mask)
+    )(parent_at, same, other, parent_packed, transfer_in, basis_in, far, near, edge, mask)
     return out.T
 
 
 def solution(mesh):
+    outer, inner = mesh.devices.shape
+    split = jax.sharding.Mesh(mesh.devices.reshape(outer, inner // 2, 2), ("gx", "gz", "gp"))
+    leaves = ("gx", "gz", "gp")
     in_specs = (
-        P(("gx", "gy"), None),
-        P(("gx", "gy")),
-        P(("gx", "gy"), None, None),
-        P(("gx", "gy"), None, None),
-        P(("gx", "gy"), None, None, None),
-        P(("gx", "gy"), None),
-        P(("gx", "gy"), None, None, None),
-        P(("gx", "gy"), None, None, None),
-        P(("gx", "gy"), None),
-    )
-    out_specs = P(("gx", "gy"), None)
+        P(leaves, None),
+        P(leaves),
+        P(leaves, None, None),
+        P(leaves, None, None),
+        P(leaves, None, None, None),
+        P(leaves, None),
+        P(leaves, None, None, None),
+        P(leaves, None, None, None),
+        P(leaves, None),
+    )
     return jax.shard_map(
-        per_device, mesh=mesh, in_specs=in_specs, out_specs=out_specs, check_vma=False
-    )
+        per_device, mesh=split, in_specs=in_specs, out_specs=P(leaves, None), check_vma=False
+    )

time: 36 us -> 33.4 us (0.928)
  Pallas kernels: 14.6 us -> 12.1 us
    pallas_call x2, Pallas kernels: 10.7 us -> 8.22 us  [the longest x1 5.47 us: per_device(): pl.pallas_call(functools.partial(mid_kernel, axes), name='mid', out_shape...]
  transfers between devices with their start and end apart: 3 -> 3, of which waited for: 0 -> 0; matrix products, arithmetic and copies ran while one was open for 0% -> 0% of each run, Pallas kernels for 21% -> 23%
where the time goes in v4:
time: 33.4 us; the launch traced here: 33.2 us
  Pallas kernels  12.1 us (36%)
  blocking collectives  12.1 us (36%)
  starting transfers between devices  8.89 us (27%)
    all_to_all x1, blocking collectives, per_device(): same = lax.all_to_all(sent, 'gz', 0, 0, tiled=True)  12.1 us
    ppermute x1, starting transfers between devices, per_device(): odd = lax.ppermute(rim, axes, steps + [(b, a) for a, b in steps])  7.42 us
    pallas_call x1, Pallas kernels, per_device(): pl.pallas_call(functools.partial(mid_kernel, axes), name='mid', out_shape...  5.47 us
    pallas_call x1, Pallas kernels, per_device(): pl.pallas_call(functools.partial(down_kernel, 'gp'), name='down', out_sha...  2.75 us
    pallas_call x1, Pallas kernels, per_device(): pl.pallas_call(functools.partial(leaf_kernel, axes), name='leaf', out_sha...  2.07 us
    pallas_call x1, Pallas kernels, per_device(): pl.pallas_call(functools.partial(up_kernel, n // 2), name='up', out_shape...  1.82 us
    ppermute x1, starting transfers between devices, per_device(): other = lax.ppermute(same, 'gp', [(0, 1), (1, 0)])  1.24 us
  transfers between devices with their start and end apart: 3, of which 0 were waited for; matrix products, arithmetic and copies ran while one was open for 0% of the time, Pallas kernels for 23%

profile of v4, /device:TPU:1, one launch (start us, length us, event | category | flops | bytes accessed | tf_op | source)
XLA Modules:
  0.0 33.2 jit_solution(4660447718464244354)
XLA Ops:
  0.0 1.8 %up.1 = (bf16[18,32,128]{2,1,0:T(8,128)(2,1)S(1)}, bf16[16,32,128]{2,1,0:T(8,128)(2,1)S(1)}, bf16[32,32,128]{2,1,0:T(8,128)(2,1)S(1)}, f32[16,8,128]{2,1,0:T(8,128)S(1)}) custom-call(s32[32]{0:T(128)} %counts_hbm.1, bf16[32,2048]{1,0:T(8,128)(2,1)} %bitcast.3, bf16[32,64,64]{2,1,0:T(8,128)(2,1)} %basis_hbm.3, bf16[32,64,64]{2,1,0:T(8,128)(2,1)} %transfer_hbm.3), custom_call_target="tpu_custom_call" | custom-call | tf_op jit(solution)/shard_map/up/pallas_call | solution.py:275
  1.8 12.1 %all_to_all.5.same_ref = bf16[32,32,128]{2,1,0:T(8,128)(2,1)S(1)} all-to-all(bf16[32,32,128]{2,1,0:T(8,128)(2,1)S(1)} %get-tuple-element.21), channel_id=1, replica_groups=mesh['gx'=4,'gz'=4,'gp'=2] {'gz'}, dimensions={0} | all-to-all | bytes 524288 | tf_op jit(solution)/shard_map/all_to_all | solution.py:296
  13.9 1.2 %collective-permute-start = (bf16[32,32,128]{2,1,0:T(8,128)(2,1)S(1)}, bf16[32,32,128]{2,1,0:T(8,128)(2,1)S(1)}, u32[]{:S(2)}, u32[]{:S(2)}) collective-permute-start(bf16[32,32,128]{2,1,0:T(8,128)(2,1)S(1)} %all_to_all.5.same_ref), channel_id=1, source_target_pairs={{0,1},{1,0},{2,3},{3,2},{4,5},{5,4},{6,7},{7,6},{8,9},{9,8},{10,11... | collective-permute-start | bytes 786440 | tf_op jit(solution)/shard_map/ppermute | solution.py:300
  15.2 0.2 collective-permute-start.1
  15.4 7.4 %collective-permute-start.2 = (bf16[18,32,128]{2,1,0:T(8,128)(2,1)S(1)}, bf16[18,32,128]{2,1,0:T(8,128)(2,1)S(1)}, u32[]{:S(2)}, u32[]{:S(2)}) collective-permute-start(bf16[18,32,128]{2,1,0:T(8,128)(2,1)S(1)} %get-tuple-element.26.rim_ref), channel_id=1, source_target_pairs={{1,2},{3,4},{5,6},{7,8},{9,10},{11,12},{13,14},{15,16},{17,18},{19... | collective-permute-start | bytes 442376 | tf_op jit(solution)/shard_map/ppermute | solution.py:299
  22.8 5.5 %mid.1 = (bf16[32,64,1024]{2,1,0:T(8,128)(2,1)S(1)}, bf16[16,64,1024]{2,1,0:T(8,128)(2,1)S(1)}, f32[16,32,128]{2,1,0:T(8,128)S(1)}, bf16[2,64,64]{2,1,0:T(8,128)...) custom-call(bf16[16,32,128]{2,1,0:T(8,128)(2,1)S(1)} %get-tuple-elem, ...), custom_call_target="tpu_custom_call" | custom-call | tf_op jit(solution)/shard_map/mid/pallas_call | solution.py:302
  28.3 0.0 collective-permute-done.1.even_ref
  28.3 0.0 collective-permute-done.2.odd_ref
  28.3 2.1 %leaf.1 = (f32[16,32,128]{2,1,0:T(8,128)S(1)}, f32[2,32,128]{2,1,0:T(8,128)S(1)}) custom-call(s32[16,32]{1,0:T(8,128)S(1)} %get-tuple-element.25.at_vmem, bf16[18,32,128]{2,1,0:T(8,128)(2,1)S(1)} %get-tuple-element.26.rim_ref, bf16[18,32,128]{2,1,0:T(8,128)(2,1)S(1)} %collective-permute-done.1.even_ref, ...), custom_call_target="tpu_custom_call" | custom-call | tf_op jit(solution)/shard_map/leaf/pallas_call | solution.py:331
  30.4 0.0 collective-permute-done.other_ref
  30.4 2.7 %down.1 = bf16[32,2048]{1,0:T(8,128)(2,1)} custom-call(s32[16,16]{1,0:T(8,128)S(1)} %get-tuple-element.20.at_vmem, bf16[32,32,128]{2,1,0:T(8,128)(2,1)S(1)} %all_to_all.5.same_ref, bf16[32,32,128]{2,1,0:T(8,128)(2,1)S(1)} %collective-permute-done.other_ref, bf16[16,64,1024]{2,1,0:T(8,128)(2,1)S(1)} %get-tuple-element.22.packed_ref, ...), custom_call_target="tpu_custom_call" | custom-call | tf_op jit(solution)/shard_map/down/pallas_call | solution.py:345
Async XLA Ops:
  13.9 16.5 %collective-permute-start = (bf16[32,32,128]{2,1,0:T(8,128)(2,1)S(1)}, bf16[32,32,128]{2,1,0:T(8,128)(2,1)S(1)}, u32[]{:S(2)}, u32[]{:S(2)}) collective-permute-start(bf16[32,32,128]{2,1,0:T(8,128)(2,1)S(1)} %all_to_all.5.same_ref), channel_id=1, source_target_pairs={{0,1},{1,0},{2,3},{3,2},{4,5},{5,4},{6,7},{7,6},{8,9},{9,8},{10,11... | collective-permute-start | bytes 786440 | tf_op jit(solution)/shard_map/ppermute | solution.py:300
  15.2 13.1 %collective-permute-start.1 = (bf16[18,32,128]{2,1,0:T(8,128)(2,1)S(1)}, bf16[18,32,128]{2,1,0:T(8,128)(2,1)S(1)}, u32[]{:S(2)}, u32[]{:S(2)}) collective-permute-start(bf16[18,32,128]{2,1,0:T(8,128)(2,1)S(1)} %get-tuple-element.26.rim_ref), channel_id=1, source_target_pairs={{0,1},{1,0},{2,3},{3,2},{4,5},{5,4},{6,7},{7,6},{8,9},{9,8},{10,11... | collective-permute-start | bytes 442376 | tf_op jit(solution)/shard_map/ppermute | solution.py:297
  15.4 12.9 %collective-permute-start.2 = (bf16[18,32,128]{2,1,0:T(8,128)(2,1)S(1)}, bf16[18,32,128]{2,1,0:T(8,128)(2,1)S(1)}, u32[]{:S(2)}, u32[]{:S(2)}) collective-permute-start(bf16[18,32,128]{2,1,0:T(8,128)(2,1)S(1)} %get-tuple-element.26.rim_ref), channel_id=1, source_target_pairs={{1,2},{3,4},{5,6},{7,8},{9,10},{11,12},{13,14},{15,16},{17,18},{19... | collective-permute-start | bytes 442376 | tf_op jit(solution)/shard_map/ppermute | solution.py:299

commit v5 on v4

--- a/solution.py
+++ b/solution.py
@@ -27,10 +27,6 @@
 
 def mod(x, m):
     return x & (m - 1) if m & (m - 1) == 0 else lax.rem(x, m)
-
-
-def div(x, m):
-    return x >> (m.bit_length() - 1) if m & (m - 1) == 0 else x // m
 
 
 def position(axes):
@@ -150,10 +146,8 @@
         copy.wait()
     wanted = leaf_at_ref[...] + (1 - position(axes)) * leaves
     leaf_at_ref[...] = wanted ^ (lax.broadcasted_iota(jnp.int32, wanted.shape, 0) & 1)
-    n, inner = lax.axis_size(axes[1]) * lax.axis_size(axes[2]), lax.axis_size(axes[2])
+    n = lax.axis_size(axes[1])
     wanted = mod(parent_at_ref[...], n * parents)
-    source = div(wanted, parents)
-    wanted = (mod(source, inner) * (n // inner) + div(source, inner)) * parents + mod(wanted, parents)
     parent_at_ref[...] = wanted ^ (lax.broadcasted_iota(jnp.int32, wanted.shape, 1) & 1)
 
 
@@ -205,7 +199,7 @@
 
 
 def down_kernel(
-    axis, at_vmem, same_ref, other_ref, packed_ref, transfer_ref, basis_ref,
+    at_vmem, row_ref, packed_ref, transfer_ref, basis_ref,
     far_ref, near_ref, edge_ref, mask_ref,
     out_ref, table_ref, at_ref, local_ref, down_ref, sems,
 ):
@@ -213,17 +207,14 @@
     parents, many = at_ref.shape
     rank = packed_ref.shape[1]
     width = basis_ref.shape[1]
-    sides = same_ref.shape[1]
-    half = 2 * same_ref.shape[0]
+    sides = row_ref.shape[1]
     left = left_half(sides, rank)
-    parity = lax.axis_index(axis)
 
     def spread(a, carry):
-        spread_pair(table_ref, half * parity + 2 * a, same_ref[a], rank)
-        spread_pair(table_ref, half * (1 - parity) + 2 * a, other_ref[a], rank)
+        spread_pair(table_ref, 2 * a, row_ref[a], rank)
         return carry
 
-    lax.fori_loop(0, same_ref.shape[0], spread, 0, unroll=min(32, same_ref.shape[0]))
+    lax.fori_loop(0, row_ref.shape[0], spread, 0, unroll=min(64, row_ref.shape[0]))
     at_in.wait()
     for q in range(parents):
         rows = [at_ref[q, j] for j in range(many)]
@@ -263,8 +254,8 @@
     parents, many = parent_partners.shape
     pairs = leaves // 2
     own = pairs // 2
-    axes = ("gx", "gz", "gp")
-    n = lax.axis_size("gz") * lax.axis_size("gp")
+    axes = ("gx", "gy")
+    n = lax.axis_size("gy")
     total = n * lax.axis_size("gx")
     bf16, f32 = jnp.bfloat16, jnp.float32
     keep = lambda *arrays: [pltpu.with_memory_space_constraint(a, pltpu.HBM) for a in arrays]
@@ -273,12 +264,12 @@
     params = lambda mib: pltpu.CompilerParams(vmem_limit_bytes=mib * 2**20)
 
     rim, live, sent, mask = pl.pallas_call(
-        functools.partial(up_kernel, n // 2),
+        functools.partial(up_kernel, n),
         name="up",
         out_shape=[
             shape((pairs + 2, sides, 2 * rank), bf16),
             shape((pairs, sides, 2 * width), bf16),
-            shape((n // 2 * own, sides, 2 * rank), bf16),
+            shape((n * own, sides, 2 * rank), bf16),
             shape((pairs, 8, 2 * width), f32),
         ],
         in_specs=[HBM] * 4,
@@ -293,11 +284,10 @@
         compiler_params=params(8),
     )(*keep(panel_counts, charges.T, basis, transfer))
 
-    same = lax.all_to_all(sent, "gz", 0, 0, tiled=True)
+    row = lax.all_to_all(sent, "gy", 0, 0, tiled=True)
     even = lax.ppermute(rim, axes, [(i, i ^ 1) for i in range(total)])
     steps = [(i, i + 1) for i in range(1, total - 1, 2)]
     odd = lax.ppermute(rim, axes, steps + [(b, a) for a, b in steps])
-    other = lax.ppermute(same, "gp", [(0, 1), (1, 0)])
 
     packed, parent_packed, near, rim_near, basis_in, transfer_in, leaf_at, parent_at = pl.pallas_call(
         functools.partial(mid_kernel, axes),
@@ -343,10 +333,10 @@
     )(leaf_at, rim, even, odd, packed, rim_near)
 
     out = pl.pallas_call(
-        functools.partial(down_kernel, "gp"),
+        down_kernel,
         name="down",
         out_shape=jax.ShapeDtypeStruct((sides, leaves * width), bf16),
-        in_specs=[VMEM] * 10,
+        in_specs=[VMEM] * 9,
         out_specs=VMEM,
         scratch_shapes=[
             pltpu.VMEM((n * parents, sides, 2 * rank), bf16),
@@ -356,14 +346,12 @@
             dma(1),
         ],
         compiler_params=params(12),
-    )(parent_at, same, other, parent_packed, transfer_in, basis_in, far, near, edge, mask)
+    )(parent_at, row, parent_packed, transfer_in, basis_in, far, near, edge, mask)
     return out.T
 
 
 def solution(mesh):
-    outer, inner = mesh.devices.shape
-    split = jax.sharding.Mesh(mesh.devices.reshape(outer, inner // 2, 2), ("gx", "gz", "gp"))
-    leaves = ("gx", "gz", "gp")
+    leaves = ("gx", "gy")
     in_specs = (
         P(leaves, None),
         P(leaves),
@@ -376,5 +364,5 @@
         P(leaves, None),
     )
     return jax.shard_map(
-        per_device, mesh=split, in_specs=in_specs, out_specs=P(leaves, None), check_vma=False
-    )
+        per_device, mesh=mesh, in_specs=in_specs, out_specs=P(leaves, None), check_vma=False
+    )

time: 33.4 us -> 38.2 us (1.14)
  blocking collectives: 12.1 us -> 0 us
  local copies, waits for them, and re-layouts: 0 us -> 9.16 us
  starting transfers between devices: 8.89 us -> 13.6 us
  waiting for transfers between devices: 0.01 us -> 1.97 us
  Pallas kernels: 12.1 us -> 12.9 us
    all_to_all x1 -> x0, blocking collectives: 12.1 us -> none  [per_device(): same = lax.all_to_all(sent, 'gz', 0, 0, tiled=True)]
    unnamed x0 -> x24, local copies, waits for them, and re-layouts: none -> 9.16 us
    all_to_all x0 -> x1, starting transfers between devices: none -> 6.38 us  [per_device(): row = lax.all_to_all(sent, 'gy', 0, 0, tiled=True)]
    ppermute x1, waiting for transfers between devices: 0.01 us -> 1.96 us  [per_device(): odd = lax.ppermute(rim, axes, steps + [(b, a) for a, b in steps])]
    ppermute x1 -> x0, starting transfers between devices: 1.24 us -> none  [per_device(): other = lax.ppermute(same, 'gp', [(0, 1), (1, 0)])]
    pallas_call x2, Pallas kernels: 4.57 us -> 5.37 us  [the longest x1 2.75 us: per_device(): pl.pallas_call(down_kernel, name='down', out_shape=jax.ShapeDtypeStruct((...]
  transfers between devices with their start and end apart: 3 -> 3, of which waited for: 0 -> 1; matrix products, arithmetic and copies ran while one was open for 0% -> 0% of each run, Pallas kernels for 23% -> 20%
where the time goes in v5:
time: 38.2 us; the launch traced here: 37.8 us
  starting transfers between devices  13.6 us (36%)
  Pallas kernels  12.9 us (34%)
  local copies, waits for them, and re-layouts  9.16 us (24%)
  waiting for transfers between devices  1.97 us (5%)
    unnamed x24, local copies, waits for them, and re-layouts  9.16 us
    ppermute x1, starting transfers between devices, per_device(): odd = lax.ppermute(rim, axes, steps + [(b, a) for a, b in steps])  7.18 us
    all_to_all x1, starting transfers between devices, per_device(): row = lax.all_to_all(sent, 'gy', 0, 0, tiled=True)  6.38 us
    pallas_call x1, Pallas kernels, per_device(): pl.pallas_call(functools.partial(mid_kernel, axes), name='mid', out_shape...  5.46 us
    pallas_call x1, Pallas kernels, per_device(): pl.pallas_call(down_kernel, name='down', out_shape=jax.ShapeDtypeStruct((...  2.75 us
    pallas_call x1, Pallas kernels, per_device(): pl.pallas_call(functools.partial(up_kernel, n), name='up', out_shape=[sha...  2.63 us
    pallas_call x1, Pallas kernels, per_device(): pl.pallas_call(functools.partial(leaf_kernel, axes), name='leaf', out_sha...  2.08 us
    ppermute x1, waiting for transfers between devices, per_device(): odd = lax.ppermute(rim, axes, steps + [(b, a) for a, b in steps])  1.96 us
  transfers between devices with their start and end apart: 3, of which 1 were waited for; matrix products, arithmetic and copies ran while one was open for 0% of the time, Pallas kernels for 20%

profile of v5, /device:TPU:1, one launch (start us, length us, event | category | flops | bytes accessed | tf_op | source)
XLA Modules:
  0.0 37.8 jit_solution(8117298167439290665)
XLA Ops:
  0.0 2.6 %up.1 = (bf16[18,32,128]{2,1,0:T(8,128)(2,1)S(1)}, bf16[16,32,128]{2,1,0:T(8,128)(2,1)S(1)}, bf16[64,32,128]{2,1,0:T(8,128)(2,1)}, f32[16,8,128]{2,1,0:T(8,128)S(1)}) custom-call(s32[32]{0:T(128)} %counts_hbm.1, bf16[32,2048]{1,0:T(8,128)(2,1)} %bitcast.3, bf16[32,64,64]{2,1,0:T(8,128)(2,1)} %basis_hbm.3, bf16[32,64,64]{2,1,0:T(8,128)(2,1)} %transfer_hbm.3), custom_call_target="tpu_custom_call" | custom-call | tf_op jit(solution)/shard_map/up/pallas_call | solution.py:266
  2.6 0.0 copy-start.4
  2.6 0.6 %copy-done.4 = bf16[16,32,128]{2,1,0:T(8,128)(2,1)} copy-done((bf16[16,32,128]{2,1,0:T(8,128)(2,1)}, bf16[16,32,128]{2,1,0:T(8,128)(2,1)S(1)}, u32[]{:S(2)}) %copy-start.4) | copy-done | bytes 131096
  3.3 0.0 copy-start.6
  3.3 0.6 %copy-done.6 = f32[16,8,128]{2,1,0:T(8,128)} copy-done((f32[16,8,128]{2,1,0:T(8,128)}, f32[16,8,128]{2,1,0:T(8,128)S(1)}, u32[]{:S(2)}) %copy-start.6) | copy-done | bytes 65560
  3.9 6.4 %all-to-all-start = ((bf16[64,32,128]{2,1,0:T(8,128)(2,1)}), bf16[64,32,128]{2,1,0:T(8,128)(2,1)S(1)}, u32[]{:S(2)}, u32[]{:S(2)}) async-start(bf16[64,32,128]{2,1,0:T(8,128)(2,1)} %get-tuple-element.21), calls=%async_computation | async-start | bytes 1048576 | tf_op jit(solution)/shard_map/all_to_all | solution.py:287
  10.3 7.2 %collective-permute-start.1 = (bf16[18,32,128]{2,1,0:T(8,128)(2,1)S(1)}, bf16[18,32,128]{2,1,0:T(8,128)(2,1)S(1)}, u32[]{:S(2)}, u32[]{:S(2)}) collective-permute-start(bf16[18,32,128]{2,1,0:T(8,128)(2,1)S(1)} %get-tuple-element.26.rim_ref), channel_id=1, source_target_pairs={{1,2},{3,4},{5,6},{7,8},{9,10},{11,12},{13,14},{15,16},{17,18},{19... | collective-permute-start | bytes 442376 | tf_op jit(solution)/shard_map/ppermute | solution.py:290
  17.5 0.1 collective-permute-start
  17.6 0.0 copy-start.5
  17.6 0.9 %copy-done.5 = bf16[16,32,128]{2,1,0:T(8,128)(2,1)S(1)} copy-done((bf16[16,32,128]{2,1,0:T(8,128)(2,1)S(1)}, bf16[16,32,128]{2,1,0:T(8,128)(2,1)}, u32[]{:S(2)}) %copy-start.5) | copy-done | bytes 131096
  18.5 5.5 %mid.1 = (bf16[32,64,1024]{2,1,0:T(8,128)(2,1)S(1)}, bf16[16,64,1024]{2,1,0:T(8,128)(2,1)S(1)}, f32[16,32,128]{2,1,0:T(8,128)S(1)}, bf16[2,64,64]{2,1,0:T(8,128)...) custom-call(bf16[16,32,128]{2,1,0:T(8,128)(2,1)S(1)} %copy-done.5, ...), custom_call_target="tpu_custom_call" | custom-call | tf_op jit(solution)/shard_map/mid/pallas_call | solution.py:292
  23.9 0.0 copy-start
  24.0 0.8 %copy-done = bf16[32,64,64]{2,1,0:T(8,128)(2,1)} copy-done((bf16[32,64,64]{2,1,0:T(8,128)(2,1)}, bf16[32,64,64]{2,1,0:T(8,128)(2,1)S(1)}, u32[]{:S(2)}) %copy-start) | copy-done | bytes 262168
  24.7 0.0 copy-start.10
  24.7 0.6 %copy-done.10 = s32[16,16]{1,0:T(8,128)} copy-done((s32[16,16]{1,0:T(8,128)}, s32[16,16]{1,0:T(8,128)S(1)}, u32[]{:S(2)}) %copy-start.10) | copy-done | bytes 1048
  25.3 2.0 %collective-permute-done.1.odd_ref = bf16[18,32,128]{2,1,0:T(8,128)(2,1)S(1)} collective-permute-done((bf16[18,32,128]{2,1,0:T(8,128)(2,1)S(1)}, bf16[18,32,128]{2,1,0:T(8,128)(2,1)S(1)}, u32[]{:S(2)}, u32[]{:S(2)}) %collective-permute-start.1) | collective-permute-done | bytes 147488 | tf_op jit(solution)/shard_map/ppermute | solution.py:290
  27.3 0.0 collective-permute-done.even_ref
  27.3 2.1 %leaf.1 = (f32[16,32,128]{2,1,0:T(8,128)S(1)}, f32[2,32,128]{2,1,0:T(8,128)S(1)}) custom-call(s32[16,32]{1,0:T(8,128)S(1)} %get-tuple-element.25.at_vmem, bf16[18,32,128]{2,1,0:T(8,128)(2,1)S(1)} %get-tuple-element.26.rim_ref, bf16[18,32,128]{2,1,0:T(8,128)(2,1)S(1)} %collective-permute-done.even_ref, ...), custom_call_target="tpu_custom_call" | custom-call | tf_op jit(solution)/shard_map/leaf/pallas_call | solution.py:321
  29.4 0.0 copy-start.2
  29.4 0.7 %copy-done.2 = f32[16,32,128]{2,1,0:T(8,128)} copy-done((f32[16,32,128]{2,1,0:T(8,128)}, f32[16,32,128]{2,1,0:T(8,128)S(1)}, u32[]{:S(2)}) %copy-start.2) | copy-done | bytes 262168
  30.1 0.0 copy-start.8
  30.1 0.6 %copy-done.8 = f32[2,32,128]{2,1,0:T(8,128)} copy-done((f32[2,32,128]{2,1,0:T(8,128)}, f32[2,32,128]{2,1,0:T(8,128)S(1)}, u32[]{:S(2)}) %copy-start.8) | copy-done | bytes 32792
  30.7 0.0 all-to-all-done.row_ref
  30.7 0.0 copy-start.1
  30.7 1.0 %copy-done.1 = bf16[32,64,64]{2,1,0:T(8,128)(2,1)S(1)} copy-done((bf16[32,64,64]{2,1,0:T(8,128)(2,1)S(1)}, bf16[32,64,64]{2,1,0:T(8,128)(2,1)}, u32[]{:S(2)}) %copy-start.1) | copy-done | bytes 262168
  31.8 0.0 copy-start.3
  31.8 0.9 %copy-done.3 = f32[16,32,128]{2,1,0:T(8,128)S(1)} copy-done((f32[16,32,128]{2,1,0:T(8,128)S(1)}, f32[16,32,128]{2,1,0:T(8,128)}, u32[]{:S(2)}) %copy-start.3) | copy-done | bytes 262168
  32.7 0.0 copy-start.7
  32.7 0.8 %copy-done.7 = f32[16,8,128]{2,1,0:T(8,128)S(1)} copy-done((f32[16,8,128]{2,1,0:T(8,128)S(1)}, f32[16,8,128]{2,1,0:T(8,128)}, u32[]{:S(2)}) %copy-start.7) | copy-done | bytes 65560
  33.6 0.0 copy-start.9
  33.6 0.8 %copy-done.9 = f32[2,32,128]{2,1,0:T(8,128)S(1)} copy-done((f32[2,32,128]{2,1,0:T(8,128)S(1)}, f32[2,32,128]{2,1,0:T(8,128)}, u32[]{:S(2)}) %copy-start.9) | copy-done | bytes 32792
  34.3 0.0 copy-start.11
  34.3 0.7 %copy-done.11 = s32[16,16]{1,0:T(8,128)S(1)} copy-done((s32[16,16]{1,0:T(8,128)S(1)}, s32[16,16]{1,0:T(8,128)}, u32[]{:S(2)}) %copy-start.11) | copy-done | bytes 1048
  35.0 2.7 %down.1 = bf16[32,2048]{1,0:T(8,128)(2,1)} custom-call(s32[16,16]{1,0:T(8,128)S(1)} %copy-done.11, bf16[64,32,128]{2,1,0:T(8,128)(2,1)S(1)} %all-to-all-done.row_ref, bf16[16,64,1024]{2,1,0:T(8,128)(2,1)S(1)} %get-tuple-element.22.packed_ref, bf16[32,64,64]{2,1,0:T(8,128)(2,1)S(1)} %copy-done.1, bf16[32,64,64]{2,1,0:T(8,128)(2,1)S(1)} %get-tuple-element.24.basis_ref, ...), custom_call_target="tpu_custom_call" | custom-call | tf_op jit(solution)/shard_map/down/pallas_call | solution.py:335
Async XLA Ops:
  2.6 0.7 %copy-start.4 = (bf16[16,32,128]{2,1,0:T(8,128)(2,1)}, bf16[16,32,128]{2,1,0:T(8,128)(2,1)S(1)}, u32[]{:S(2)}) copy-start(bf16[16,32,128]{2,1,0:T(8,128)(2,1)S(1)} %get-tuple-element.19.live_ref) | copy-start | bytes 393220
  3.3 0.6 %copy-start.6 = (f32[16,8,128]{2,1,0:T(8,128)}, f32[16,8,128]{2,1,0:T(8,128)S(1)}, u32[]{:S(2)}) copy-start(f32[16,8,128]{2,1,0:T(8,128)S(1)} %get-tuple-element.32.mask_ref) | copy-start | bytes 196612
  3.9 26.8 %all-to-all-start = ((bf16[64,32,128]{2,1,0:T(8,128)(2,1)}), bf16[64,32,128]{2,1,0:T(8,128)(2,1)S(1)}, u32[]{:S(2)}, u32[]{:S(2)}) async-start(bf16[64,32,128]{2,1,0:T(8,128)(2,1)} %get-tuple-element.21), calls=%async_computation | async-start | bytes 1048576 | tf_op jit(solution)/shard_map/all_to_all | solution.py:287
  10.3 17.0 %collective-permute-start.1 = (bf16[18,32,128]{2,1,0:T(8,128)(2,1)S(1)}, bf16[18,32,128]{2,1,0:T(8,128)(2,1)S(1)}, u32[]{:S(2)}, u32[]{:S(2)}) collective-permute-start(bf16[18,32,128]{2,1,0:T(8,128)(2,1)S(1)} %get-tuple-element.26.rim_ref), channel_id=1, source_target_pairs={{1,2},{3,4},{5,6},{7,8},{9,10},{11,12},{13,14},{15,16},{17,18},{19... | collective-permute-start | bytes 442376 | tf_op jit(solution)/shard_map/ppermute | solution.py:290
  17.5 9.8 %collective-permute-start = (bf16[18,32,128]{2,1,0:T(8,128)(2,1)S(1)}, bf16[18,32,128]{2,1,0:T(8,128)(2,1)S(1)}, u32[]{:S(2)}, u32[]{:S(2)}) collective-permute-start(bf16[18,32,128]{2,1,0:T(8,128)(2,1)S(1)} %get-tuple-element.26.rim_ref), channel_id=1, source_target_pairs={{0,1},{1,0},{2,3},{3,2},{4,5},{5,4},{6,7},{7,6},{8,9},{9,8},{10,11... | collective-permute-start | bytes 442376 | tf_op jit(solution)/shard_map/ppermute | solution.py:288
  17.6 0.9 %copy-start.5 = (bf16[16,32,128]{2,1,0:T(8,128)(2,1)S(1)}, bf16[16,32,128]{2,1,0:T(8,128)(2,1)}, u32[]{:S(2)}) copy-start(bf16[16,32,128]{2,1,0:T(8,128)(2,1)} %copy-done.4) | copy-start | bytes 393220
  23.9 0.8 %copy-start = (bf16[32,64,64]{2,1,0:T(8,128)(2,1)}, bf16[32,64,64]{2,1,0:T(8,128)(2,1)S(1)}, u32[]{:S(2)}) copy-start(bf16[32,64,64]{2,1,0:T(8,128)(2,1)S(1)} %get-tuple-element.23.transfer_ref) | copy-start | bytes 786436
  24.7 0.6 %copy-start.10 = (s32[16,16]{1,0:T(8,128)}, s32[16,16]{1,0:T(8,128)S(1)}, u32[]{:S(2)}) copy-start(s32[16,16]{1,0:T(8,128)S(1)} %get-tuple-element.20.at_vmem) | copy-start | bytes 3076
  29.4 0.7 %copy-start.2 = (f32[16,32,128]{2,1,0:T(8,128)}, f32[16,32,128]{2,1,0:T(8,128)S(1)}, u32[]{:S(2)}) copy-start(f32[16,32,128]{2,1,0:T(8,128)S(1)} %get-tuple-element.29.far_ref) | copy-start | bytes 786436
  30.1 0.6 %copy-start.8 = (f32[2,32,128]{2,1,0:T(8,128)}, f32[2,32,128]{2,1,0:T(8,128)S(1)}, u32[]{:S(2)}) copy-start(f32[2,32,128]{2,1,0:T(8,128)S(1)} %get-tuple-element.31.edge_ref) | copy-start | bytes 98308
  30.7 1.0 %copy-start.1 = (bf16[32,64,64]{2,1,0:T(8,128)(2,1)S(1)}, bf16[32,64,64]{2,1,0:T(8,128)(2,1)}, u32[]{:S(2)}) copy-start(bf16[32,64,64]{2,1,0:T(8,128)(2,1)} %copy-done) | copy-start | bytes 786436
  31.8 0.9 %copy-start.3 = (f32[16,32,128]{2,1,0:T(8,128)S(1)}, f32[16,32,128]{2,1,0:T(8,128)}, u32[]{:S(2)}) copy-start(f32[16,32,128]{2,1,0:T(8,128)} %copy-done.2) | copy-start | bytes 786436
  32.7 0.8 %copy-start.7 = (f32[16,8,128]{2,1,0:T(8,128)S(1)}, f32[16,8,128]{2,1,0:T(8,128)}, u32[]{:S(2)}) copy-start(f32[16,8,128]{2,1,0:T(8,128)} %copy-done.6) | copy-start | bytes 196612
  33.6 0.8 %copy-start.9 = (f32[2,32,128]{2,1,0:T(8,128)S(1)}, f32[2,32,128]{2,1,0:T(8,128)}, u32[]{:S(2)}) copy-start(f32[2,32,128]{2,1,0:T(8,128)} %copy-done.8) | copy-start | bytes 98308
  34.3 0.7 %copy-start.11 = (s32[16,16]{1,0:T(8,128)S(1)}, s32[16,16]{1,0:T(8,128)}, u32[]{:S(2)}) copy-start(s32[16,16]{1,0:T(8,128)} %copy-done.10) | copy-start | bytes 3076

commit v6 on v5

--- a/solution.py
+++ b/solution.py
@@ -21,6 +21,13 @@
     return lax.broadcasted_iota(jnp.int32, (sides, 2 * width), 1) < width
 
 
+def pair_mask(counts_ref, pair, sides, width):
+    lane = lax.broadcasted_iota(jnp.int32, (sides, 2 * width), 1)
+    left = lane < width
+    count = jnp.where(left, counts_ref[2 * pair], counts_ref[2 * pair + 1])
+    return jnp.where(left, lane, lane - width) < count
+
+
 def swap(pair, width):
     return jnp.concatenate([pair[:, width:], pair[:, :width]], axis=1)
 
@@ -45,7 +52,7 @@
 
 def up_kernel(
     copies, counts_hbm, charges_hbm, basis_hbm, transfer_hbm,
-    rim_ref, live_ref, parents_ref, mask_ref,
+    rim_ref, live_ref, parents_ref,
     counts_ref, charges_ref, basis_ref, transfer_ref, sems,
 ):
     counts_in, charges_in, basis_in, transfer_in = start_all(
@@ -60,16 +67,12 @@
     pairs = leaves // 2
     own = pairs // 2
     left = left_half(sides, width)
-    lane = lax.broadcasted_iota(jnp.int32, (sides, 2 * width), 1)
-    slot = jnp.where(left, lane, lane - width)
     counts_in.wait()
     charges_in.wait()
     lives = []
     for a in range(pairs):
         charge = charges_ref[:, 2 * width * a : 2 * width * (a + 1)]
-        mask = slot < jnp.where(left, counts_ref[2 * a], counts_ref[2 * a + 1])
-        mask_ref[a] = mask[:8].astype(jnp.float32)
-        live = jnp.where(mask, charge, jnp.zeros_like(charge))
+        live = jnp.where(pair_mask(counts_ref, a, sides, width), charge, jnp.zeros_like(charge))
         live_ref[a] = live
         lives.append(live)
     rim_ref[pairs] = lives[0]
@@ -96,11 +99,9 @@
 
 
 def mid_kernel(
-    axes, live_ref, coupling_hbm, near_hbm, parent_hbm, basis_hbm, transfer_hbm, leaf_partners_hbm,
-    parent_partners_hbm,
-    packed_ref, parent_packed_ref, near_out_ref, rim_near_ref, basis_out_ref, transfer_out_ref,
-    leaf_at_ref, parent_at_ref,
-    coupling_ref, near_ref, parent_ref, sems,
+    axes, live_ref, coupling_hbm, near_hbm, parent_hbm, leaf_partners_hbm, parent_partners_hbm,
+    packed_ref, first_ref, second_hbm, near_out_ref, rim_near_ref, leaf_at_ref, parent_at_ref,
+    coupling_ref, near_ref, parent_ref, second_ref, sems,
 ):
     leaves, many, rank, _ = coupling_ref.shape
     parents = parent_ref.shape[0]
@@ -108,15 +109,14 @@
     pairs = leaves // 2
     started = start_all(
         [(near_hbm, near_ref)]
+        + [(parent_hbm.at[pl.ds(4 * i, 4)], parent_ref.at[pl.ds(4 * i, 4)]) for i in reversed(range(parents // 4))]
         + [(coupling_hbm.at[pl.ds(4 * i, 4)], coupling_ref.at[pl.ds(4 * i, 4)]) for i in range(leaves // 4)]
-        + [(parent_hbm.at[pl.ds(4 * i, 4)], parent_ref.at[pl.ds(4 * i, 4)]) for i in range(parents // 4)]
-        + [(basis_hbm, basis_out_ref), (transfer_hbm, transfer_out_ref)]
         + [(leaf_partners_hbm, leaf_at_ref), (parent_partners_hbm, parent_at_ref)],
         sems,
     )
     near_in = started[0]
-    coupling_in = started[1 : 1 + leaves // 4]
-    parent_in = started[1 + leaves // 4 : -4]
+    parent_in = started[1 : 1 + parents // 4][::-1]
+    coupling_in = started[1 + parents // 4 : -2]
     near_in.wait()
     rim_near_ref[0] = near_ref[0, 0]
     rim_near_ref[1] = near_ref[leaves - 1, 2]
@@ -130,20 +130,28 @@
             odd = odd + dot(live_ref[a + 1][:, :width], near_ref[2 * a + 1, 2], NT)
         near_out_ref[a] = jnp.concatenate([even, odd], axis=1)
 
-    def pack(src, dst, g):
+    def pack(src, dst, g, to):
         for j in range(0, many, 2):
-            dst[g, :, rank * j : rank * (j + 2)] = jnp.concatenate([src[g, j], src[g, j + 1]], axis=1)
-
+            dst[to, :, rank * j : rank * (j + 2)] = jnp.concatenate([src[g, j], src[g, j + 1]], axis=1)
+
+    half = first_ref.shape[0]
+    for i, copy in reversed(list(enumerate(parent_in))):
+        copy.wait()
+        for q in range(4 * i, 4 * i + 4):
+            if q < half:
+                pack(parent_ref, first_ref, q, q)
+            else:
+                pack(parent_ref, second_ref, q, q - half)
+        if 4 * i == half:
+            out = pltpu.make_async_copy(second_ref, second_hbm, sems.at[len(started)])
+            out.start()
     for i, copy in enumerate(coupling_in):
         copy.wait()
         for g in range(4 * i, 4 * i + 4):
-            pack(coupling_ref, packed_ref, g)
-    for i, copy in enumerate(parent_in):
+            pack(coupling_ref, packed_ref, g, g)
+    for copy in started[-2:]:
         copy.wait()
-        for q in range(4 * i, 4 * i + 4):
-            pack(parent_ref, parent_packed_ref, q)
-    for copy in started[-4:]:
-        copy.wait()
+    out.wait()
     wanted = leaf_at_ref[...] + (1 - position(axes)) * leaves
     leaf_at_ref[...] = wanted ^ (lax.broadcasted_iota(jnp.int32, wanted.shape, 0) & 1)
     n = lax.axis_size(axes[1])
@@ -199,13 +207,20 @@
 
 
 def down_kernel(
-    at_vmem, row_ref, packed_ref, transfer_ref, basis_ref,
-    far_ref, near_ref, edge_ref, mask_ref,
-    out_ref, table_ref, at_ref, local_ref, down_ref, sems,
-):
-    (at_in,) = start_all([(at_vmem, at_ref)], sems)
+    at_vmem, row_ref, first_ref, second_hbm, transfer_hbm, basis_hbm, counts_hbm,
+    far_ref, near_ref, edge_ref,
+    out_ref, table_ref, at_ref, local_ref, down_ref, second_ref, transfer_ref, basis_ref, counts_ref, sems,
+):
+    at_in, second_in, transfer_in, basis_in, counts_in = start_all(
+        [
+            (at_vmem, at_ref), (second_hbm, second_ref), (transfer_hbm, transfer_ref),
+            (basis_hbm, basis_ref), (counts_hbm, counts_ref),
+        ],
+        sems,
+    )
     parents, many = at_ref.shape
-    rank = packed_ref.shape[1]
+    rank = first_ref.shape[1]
+    half = first_ref.shape[0]
     width = basis_ref.shape[1]
     sides = row_ref.shape[1]
     left = left_half(sides, rank)
@@ -217,12 +232,18 @@
     lax.fori_loop(0, row_ref.shape[0], spread, 0, unroll=min(64, row_ref.shape[0]))
     at_in.wait()
     for q in range(parents):
+        if q == half:
+            second_in.wait()
         rows = [at_ref[q, j] for j in range(many)]
-        far = dot(picked(table_ref, rows, left), packed_ref[q], NT)
+        packed = first_ref[q] if q < half else second_ref[q - half]
+        far = dot(picked(table_ref, rows, left), packed, NT)
         down_ref[q] = far.astype(jnp.bfloat16)
+    transfer_in.wait()
     for q in range(parents):
         local = far_ref[q] + dot(down_ref[q], transfer_ref[2 * q : 2 * q + 2].reshape(2 * rank, rank), NT)
         local_ref[q] = local.astype(jnp.bfloat16)
+    basis_in.wait()
+    counts_in.wait()
     for q in range(parents):
         local = local_ref[q]
         total = jnp.concatenate(
@@ -234,7 +255,7 @@
             total = total + edge_ref[0]
         if q == parents - 1:
             total = total + edge_ref[1]
-        total = total * mask_ref[q][:1]
+        total = jnp.where(pair_mask(counts_ref, q, sides, width), total, jnp.zeros_like(total))
         out_ref[:, 2 * width * q : 2 * width * (q + 1)] = total.astype(out_ref.dtype)
 
 
@@ -263,17 +284,16 @@
     dma = lambda count: pltpu.SemaphoreType.DMA((count,))
     params = lambda mib: pltpu.CompilerParams(vmem_limit_bytes=mib * 2**20)
 
-    rim, live, sent, mask = pl.pallas_call(
+    rim, live, sent = pl.pallas_call(
         functools.partial(up_kernel, n),
         name="up",
         out_shape=[
             shape((pairs + 2, sides, 2 * rank), bf16),
             shape((pairs, sides, 2 * width), bf16),
             shape((n * own, sides, 2 * rank), bf16),
-            shape((pairs, 8, 2 * width), f32),
         ],
         in_specs=[HBM] * 4,
-        out_specs=[VMEM] * 4,
+        out_specs=[VMEM] * 3,
         scratch_shapes=[
             pltpu.SMEM((leaves,), jnp.int32),
             pltpu.VMEM((sides, leaves * width), bf16),
@@ -289,34 +309,30 @@
     steps = [(i, i + 1) for i in range(1, total - 1, 2)]
     odd = lax.ppermute(rim, axes, steps + [(b, a) for a, b in steps])
 
-    packed, parent_packed, near, rim_near, basis_in, transfer_in, leaf_at, parent_at = pl.pallas_call(
+    half = parents // 8 * 4
+    packed, first, second, near, rim_near, leaf_at, parent_at = pl.pallas_call(
         functools.partial(mid_kernel, axes),
         name="mid",
         out_shape=[
             shape((leaves, rank, many * rank), bf16),
-            shape((parents, rank, many * rank), bf16),
+            shape((half, rank, many * rank), bf16),
+            pltpu.HBM((parents - half, rank, many * rank), bf16),
             shape((pairs, sides, 2 * width), f32),
             shape((2, width, width), bf16),
-            shape(basis.shape, bf16),
-            shape(transfer.shape, bf16),
             shape((many, leaves), jnp.int32),
             shape((parents, many), jnp.int32),
         ],
-        in_specs=[VMEM] + [HBM] * 7,
-        out_specs=[VMEM] * 8,
+        in_specs=[VMEM] + [HBM] * 5,
+        out_specs=[VMEM] * 2 + [HBM] + [VMEM] * 4,
         scratch_shapes=[
             pltpu.VMEM(leaf_coupling.shape, bf16),
             pltpu.VMEM(near_blocks.shape, bf16),
             pltpu.VMEM(parent_coupling.shape, bf16),
-            dma(5 + leaves // 4 + parents // 4),
+            pltpu.VMEM((parents - half, rank, many * rank), bf16),
+            dma(4 + leaves // 4 + parents // 4),
         ],
         compiler_params=params(20),
-    )(
-        live,
-        *keep(
-            leaf_coupling, near_blocks, parent_coupling, basis, transfer, leaf_partners.T, parent_partners
-        ),
-    )
+    )(live, *keep(leaf_coupling, near_blocks, parent_coupling, leaf_partners.T, parent_partners))
 
     far, edge = pl.pallas_call(
         functools.partial(leaf_kernel, axes),
@@ -336,17 +352,21 @@
         down_kernel,
         name="down",
         out_shape=jax.ShapeDtypeStruct((sides, leaves * width), bf16),
-        in_specs=[VMEM] * 9,
+        in_specs=[VMEM] * 3 + [HBM] * 4 + [VMEM] * 3,
         out_specs=VMEM,
         scratch_shapes=[
             pltpu.VMEM((n * parents, sides, 2 * rank), bf16),
             pltpu.SMEM((parents, many), jnp.int32),
             pltpu.VMEM((pairs, sides, 2 * rank), bf16),
             pltpu.VMEM((parents, sides, rank), bf16),
-            dma(1),
+            pltpu.VMEM((parents - half, rank, many * rank), bf16),
+            pltpu.VMEM(transfer.shape, bf16),
+            pltpu.VMEM(basis.shape, bf16),
+            pltpu.SMEM((leaves,), jnp.int32),
+            dma(5),
         ],
         compiler_params=params(12),
-    )(parent_at, row, parent_packed, transfer_in, basis_in, far, near, edge, mask)
+    )(parent_at, row, first, *keep(second, transfer, basis, panel_counts), far, near, edge)
     return out.T
 
 

time: 38.2 us -> 31.7 us (0.83)
  local copies, waits for them, and re-layouts: 9.16 us -> 0 us
  waiting for transfers between devices: 1.97 us -> 3.95 us
  Pallas kernels: 12.9 us -> 13.8 us
    unnamed x24 -> x0, local copies, waits for them, and re-layouts: 9.16 us -> none
    ppermute x1, waiting for transfers between devices: 1.96 us -> 3.94 us  [per_device(): odd = lax.ppermute(rim, axes, steps + [(b, a) for a, b in steps])]
    pallas_call x1, Pallas kernels: 2.75 us -> 3.36 us  [per_device(): pl.pallas_call(down_kernel, name='down', out_shape=jax.ShapeDtypeStruct((...]
  transfers between devices with their start and end apart: 3 -> 3, of which waited for: 1 -> 1; matrix products, arithmetic and copies ran while one was open for 0% -> 0% of each run, Pallas kernels for 20% -> 25%
where the time goes in v6:
time: 31.7 us; the launch traced here: 31.5 us
  Pallas kernels  13.8 us (44%)
  starting transfers between devices  13.6 us (43%)
  waiting for transfers between devices  3.95 us (12%)
    ppermute x1, starting transfers between devices, per_device(): odd = lax.ppermute(rim, axes, steps + [(b, a) for a, b in steps])  7.18 us
    all_to_all x1, starting transfers between devices, per_device(): row = lax.all_to_all(sent, 'gy', 0, 0, tiled=True)  6.4 us
    pallas_call x1, Pallas kernels, per_device(): pl.pallas_call(functools.partial(mid_kernel, axes), name='mid', out_shape...  5.78 us
    ppermute x1, waiting for transfers between devices, per_device(): odd = lax.ppermute(rim, axes, steps + [(b, a) for a, b in steps])  3.94 us
    pallas_call x1, Pallas kernels, per_device(): pl.pallas_call(down_kernel, name='down', out_shape=jax.ShapeDtypeStruct((...  3.36 us
    pallas_call x1, Pallas kernels, per_device(): pl.pallas_call(functools.partial(up_kernel, n), name='up', out_shape=[sha...  2.62 us
    pallas_call x1, Pallas kernels, per_device(): pl.pallas_call(functools.partial(leaf_kernel, axes), name='leaf', out_sha...  2.08 us
  transfers between devices with their start and end apart: 3, of which 1 were waited for; matrix products, arithmetic and copies ran while one was open for 0% of the time, Pallas kernels for 25%

profile of v6, /device:TPU:1, one launch (start us, length us, event | category | flops | bytes accessed | tf_op | source)
XLA Modules:
  0.0 31.5 jit_solution(2300575408479586809)
XLA Ops:
  0.0 2.6 %up.1 = (bf16[18,32,128]{2,1,0:T(8,128)(2,1)S(1)}, bf16[16,32,128]{2,1,0:T(8,128)(2,1)S(1)}, bf16[64,32,128]{2,1,0:T(8,128)(2,1)}) custom-call(s32[32]{0:T(128)} %counts_hbm.3, bf16[32,2048]{1,0:T(8,128)(2,1)} %bitcast.3, bf16[32,64,64]{2,1,0:T(8,128)(2,1)} %basis_hbm.3, bf16[32,64,64]{2,1,0:T(8,128)(2,1)} %transfer_hbm.3), custom_call_target="tpu_custom_call" | custom-call | tf_op jit(solution)/shard_map/up/pallas_call | solution.py:287
  2.6 6.4 %all-to-all-start = ((bf16[64,32,128]{2,1,0:T(8,128)(2,1)}), bf16[64,32,128]{2,1,0:T(8,128)(2,1)S(1)}, u32[]{:S(2)}, u32[]{:S(2)}) async-start(bf16[64,32,128]{2,1,0:T(8,128)(2,1)} %get-tuple-element.19), calls=%async_computation | async-start | bytes 1048576 | tf_op jit(solution)/shard_map/all_to_all | solution.py:307
  9.0 7.2 %collective-permute-start.1 = (bf16[18,32,128]{2,1,0:T(8,128)(2,1)S(1)}, bf16[18,32,128]{2,1,0:T(8,128)(2,1)S(1)}, u32[]{:S(2)}, u32[]{:S(2)}) collective-permute-start(bf16[18,32,128]{2,1,0:T(8,128)(2,1)S(1)} %get-tuple-element.23.rim_ref), channel_id=1, source_target_pairs={{1,2},{3,4},{5,6},{7,8},{9,10},{11,12},{13,14},{15,16},{17,18},{19... | collective-permute-start | bytes 442376 | tf_op jit(solution)/shard_map/ppermute | solution.py:310
  16.2 0.1 collective-permute-start
  16.3 5.8 %mid.1 = (bf16[32,64,1024]{2,1,0:T(8,128)(2,1)S(1)}, bf16[8,64,1024]{2,1,0:T(8,128)(2,1)S(1)}, bf16[8,64,1024]{2,1,0:T(8,128)(2,1)}, f32[16,32,128]{2,1,0:T(8,12...) custom-call(bf16[16,32,128]{2,1,0:T(8,128)(2,1)S(1)} %get-tuple-element.17.live_ref, ...), custom_call_target="tpu_custom_call" | custom-call | tf_op jit(solution)/shard_map/mid/pallas_call | solution.py:313
  22.1 3.9 %collective-permute-done.1.odd_ref = bf16[18,32,128]{2,1,0:T(8,128)(2,1)S(1)} collective-permute-done((bf16[18,32,128]{2,1,0:T(8,128)(2,1)S(1)}, bf16[18,32,128]{2,1,0:T(8,128)(2,1)S(1)}, u32[]{:S(2)}, u32[]{:S(2)}) %collective-permute-start.1) | collective-permute-done | bytes 147488 | tf_op jit(solution)/shard_map/ppermute | solution.py:310
  26.0 0.0 collective-permute-done.even_ref
  26.0 2.1 %leaf.1 = (f32[16,32,128]{2,1,0:T(8,128)S(1)}, f32[2,32,128]{2,1,0:T(8,128)S(1)}) custom-call(s32[16,32]{1,0:T(8,128)S(1)} %get-tuple-element.22.at_vmem, bf16[18,32,128]{2,1,0:T(8,128)(2,1)S(1)} %get-tuple-element.23.rim_ref, bf16[18,32,128]{2,1,0:T(8,128)(2,1)S(1)} %collective-permute-done.even_ref, ...), custom_call_target="tpu_custom_call" | custom-call | tf_op jit(solution)/shard_map/leaf/pallas_call | solution.py:337
  28.1 0.0 all-to-all-done.row_ref
  28.1 3.4 %down.1 = bf16[32,2048]{1,0:T(8,128)(2,1)} custom-call(s32[16,16]{1,0:T(8,128)S(1)} %get-tuple-element.18.at_vmem, bf16[64,32,128]{2,1,0:T(8,128)(2,1)S(1)} %all-to-all-done.row_ref, bf16[8,64,1024]{2,1,0:T(8,128)(2,1)S(1)} %get-tuple-element.20.first_ref, bf16[8,64,1024]{2,1,0:T(8,128)(2,1)} %get-tuple-element.21.second_hbm, ...), custom_call_target="tpu_custom_call" | custom-call | tf_op jit(solution)/shard_map/down/pallas_call | solution.py:351
Async XLA Ops:
  2.6 25.5 %all-to-all-start = ((bf16[64,32,128]{2,1,0:T(8,128)(2,1)}), bf16[64,32,128]{2,1,0:T(8,128)(2,1)S(1)}, u32[]{:S(2)}, u32[]{:S(2)}) async-start(bf16[64,32,128]{2,1,0:T(8,128)(2,1)} %get-tuple-element.19), calls=%async_computation | async-start | bytes 1048576 | tf_op jit(solution)/shard_map/all_to_all | solution.py:307
  9.0 17.0 %collective-permute-start.1 = (bf16[18,32,128]{2,1,0:T(8,128)(2,1)S(1)}, bf16[18,32,128]{2,1,0:T(8,128)(2,1)S(1)}, u32[]{:S(2)}, u32[]{:S(2)}) collective-permute-start(bf16[18,32,128]{2,1,0:T(8,128)(2,1)S(1)} %get-tuple-element.23.rim_ref), channel_id=1, source_target_pairs={{1,2},{3,4},{5,6},{7,8},{9,10},{11,12},{13,14},{15,16},{17,18},{19... | collective-permute-start | bytes 442376 | tf_op jit(solution)/shard_map/ppermute | solution.py:310
  16.2 9.8 %collective-permute-start = (bf16[18,32,128]{2,1,0:T(8,128)(2,1)S(1)}, bf16[18,32,128]{2,1,0:T(8,128)(2,1)S(1)}, u32[]{:S(2)}, u32[]{:S(2)}) collective-permute-start(bf16[18,32,128]{2,1,0:T(8,128)(2,1)S(1)} %get-tuple-element.23.rim_ref), channel_id=1, source_target_pairs={{0,1},{1,0},{2,3},{3,2},{4,5},{5,4},{6,7},{7,6},{8,9},{9,8},{10,11... | collective-permute-start | bytes 442376 | tf_op jit(solution)/shard_map/ppermute | solution.py:308

commit v7 on v6

--- a/solution.py
+++ b/solution.py
@@ -51,7 +51,7 @@
 
 
 def up_kernel(
-    copies, counts_hbm, charges_hbm, basis_hbm, transfer_hbm,
+    counts_hbm, charges_hbm, basis_hbm, transfer_hbm,
     rim_ref, live_ref, parents_ref,
     counts_ref, charges_ref, basis_ref, transfer_ref, sems,
 ):
@@ -93,9 +93,14 @@
         for a in range(pairs)
     ]
     for a in range(own):
-        parent = jnp.concatenate(sums[2 * a : 2 * a + 2], axis=1).astype(jnp.bfloat16)
-        for c in range(copies):
-            parents_ref[c * own + a] = parent
+        parents_ref[a] = jnp.concatenate(sums[2 * a : 2 * a + 2], axis=1).astype(jnp.bfloat16)
+
+
+def copies_kernel(parents_ref, sent_hbm, sems):
+    own = parents_ref.shape[0]
+    copies = sent_hbm.shape[0] // own
+    for copy in start_all([(parents_ref, sent_hbm.at[pl.ds(own * c, own)]) for c in range(copies)], sems):
+        copy.wait()
 
 
 def mid_kernel(
@@ -175,10 +180,10 @@
 
 
 def leaf_kernel(
-    axes, at_vmem, rim_ref, even_ref, odd_ref, packed_ref, rim_near_ref,
-    far_ref, edge_ref, table_ref, at_ref, sems,
+    axes, at_vmem, rim_ref, even_ref, odd_ref, packed_ref, rim_near_ref, transfer_hbm,
+    far_ref, edge_ref, transfer_ref, table_ref, at_ref, sems,
 ):
-    (at_in,) = start_all([(at_vmem, at_ref)], sems)
+    at_in, transfer_in = start_all([(at_vmem, at_ref), (transfer_hbm, transfer_ref)], sems)
     many, leaves = at_ref.shape
     rank = packed_ref.shape[1]
     width = rim_near_ref.shape[1]
@@ -204,17 +209,17 @@
             rows = [at_ref[j, g] for j in range(many)]
             fars.append(dot(picked(table_ref, rows, left), packed_ref[g], NT))
         far_ref[a] = jnp.concatenate(fars, axis=1)
+    transfer_in.wait()
 
 
 def down_kernel(
-    at_vmem, row_ref, first_ref, second_hbm, transfer_hbm, basis_hbm, counts_hbm,
-    far_ref, near_ref, edge_ref,
-    out_ref, table_ref, at_ref, local_ref, down_ref, second_ref, transfer_ref, basis_ref, counts_ref, sems,
+    at_vmem, row_ref, first_ref, second_hbm, basis_hbm, counts_hbm,
+    far_ref, near_ref, edge_ref, transfer_ref,
+    out_ref, table_ref, at_ref, local_ref, down_ref, second_ref, basis_ref, counts_ref, sems,
 ):
-    at_in, second_in, transfer_in, basis_in, counts_in = start_all(
+    at_in, second_in, basis_in, counts_in = start_all(
         [
-            (at_vmem, at_ref), (second_hbm, second_ref), (transfer_hbm, transfer_ref),
-            (basis_hbm, basis_ref), (counts_hbm, counts_ref),
+            (at_vmem, at_ref), (second_hbm, second_ref), (basis_hbm, basis_ref), (counts_hbm, counts_ref),
         ],
         sems,
     )
@@ -238,7 +243,6 @@
         packed = first_ref[q] if q < half else second_ref[q - half]
         far = dot(picked(table_ref, rows, left), packed, NT)
         down_ref[q] = far.astype(jnp.bfloat16)
-    transfer_in.wait()
     for q in range(parents):
         local = far_ref[q] + dot(down_ref[q], transfer_ref[2 * q : 2 * q + 2].reshape(2 * rank, rank), NT)
         local_ref[q] = local.astype(jnp.bfloat16)
@@ -284,13 +288,13 @@
     dma = lambda count: pltpu.SemaphoreType.DMA((count,))
     params = lambda mib: pltpu.CompilerParams(vmem_limit_bytes=mib * 2**20)
 
-    rim, live, sent = pl.pallas_call(
-        functools.partial(up_kernel, n),
+    rim, live, parent_coef = pl.pallas_call(
+        up_kernel,
         name="up",
         out_shape=[
             shape((pairs + 2, sides, 2 * rank), bf16),
             shape((pairs, sides, 2 * width), bf16),
-            shape((n * own, sides, 2 * rank), bf16),
+            shape((own, sides, 2 * rank), bf16),
         ],
         in_specs=[HBM] * 4,
         out_specs=[VMEM] * 3,
@@ -304,6 +308,15 @@
         compiler_params=params(8),
     )(*keep(panel_counts, charges.T, basis, transfer))
 
+    sent = pl.pallas_call(
+        copies_kernel,
+        name="copies",
+        out_shape=pltpu.HBM((n * own, sides, 2 * rank), bf16),
+        in_specs=[VMEM],
+        out_specs=HBM,
+        scratch_shapes=[dma(n)],
+        compiler_params=params(4),
+    )(parent_coef)
     row = lax.all_to_all(sent, "gy", 0, 0, tiled=True)
     even = lax.ppermute(rim, axes, [(i, i ^ 1) for i in range(total)])
     steps = [(i, i + 1) for i in range(1, total - 1, 2)]
@@ -334,25 +347,29 @@
         compiler_params=params(20),
     )(live, *keep(leaf_coupling, near_blocks, parent_coupling, leaf_partners.T, parent_partners))
 
-    far, edge = pl.pallas_call(
+    far, edge, transfer_in = pl.pallas_call(
         functools.partial(leaf_kernel, axes),
         name="leaf",
-        out_shape=[shape((pairs, sides, 2 * rank), f32), shape((2, sides, 2 * width), f32)],
-        in_specs=[VMEM] * 6,
-        out_specs=[VMEM, VMEM],
+        out_shape=[
+            shape((pairs, sides, 2 * rank), f32),
+            shape((2, sides, 2 * width), f32),
+            shape(transfer.shape, bf16),
+        ],
+        in_specs=[VMEM] * 6 + [HBM],
+        out_specs=[VMEM] * 3,
         scratch_shapes=[
             pltpu.VMEM((3 * leaves, sides, 2 * rank), bf16),
             pltpu.SMEM((many, leaves), jnp.int32),
-            dma(1),
+            dma(2),
         ],
         compiler_params=params(8),
-    )(leaf_at, rim, even, odd, packed, rim_near)
+    )(leaf_at, rim, even, odd, packed, rim_near, *keep(transfer))
 
     out = pl.pallas_call(
         down_kernel,
         name="down",
         out_shape=jax.ShapeDtypeStruct((sides, leaves * width), bf16),
-        in_specs=[VMEM] * 3 + [HBM] * 4 + [VMEM] * 3,
+        in_specs=[VMEM] * 3 + [HBM] * 3 + [VMEM] * 4,
         out_specs=VMEM,
         scratch_shapes=[
             pltpu.VMEM((n * parents, sides, 2 * rank), bf16),
@@ -360,13 +377,12 @@
             pltpu.VMEM((pairs, sides, 2 * rank), bf16),
             pltpu.VMEM((parents, sides, rank), bf16),
             pltpu.VMEM((parents - half, rank, many * rank), bf16),
-            pltpu.VMEM(transfer.shape, bf16),
             pltpu.VMEM(basis.shape, bf16),
             pltpu.SMEM((leaves,), jnp.int32),
-            dma(5),
+            dma(4),
         ],
         compiler_params=params(12),
-    )(parent_at, row, first, *keep(second, transfer, basis, panel_counts), far, near, edge)
+    )(parent_at, row, first, *keep(second, basis, panel_counts), far, near, edge, transfer_in)
     return out.T
 
 

time: 31.7 us -> 31.7 us (level)
  starting transfers between devices: 13.6 us -> 14.1 us
  waiting for transfers between devices: 3.95 us -> 3.45 us
    ppermute x1, starting transfers between devices: 0.07 us -> 1.46 us  [per_device(): even = lax.ppermute(rim, axes, [(i, i ^ 1) for i in range(total)])]
    ppermute x1, starting transfers between devices: 7.18 us -> 6.28 us  [per_device(): odd = lax.ppermute(rim, axes, steps + [(b, a) for a, b in steps])]
    ppermute x1, waiting for transfers between devices: 3.94 us -> 3.45 us  [per_device(): odd = lax.ppermute(rim, axes, steps + [(b, a) for a, b in steps])]
    pallas_call x1 -> x2, Pallas kernels: 2.62 us -> 2.69 us  [the longest x1 1.82 us: per_device(): pl.pallas_call(up_kernel, name='up', out_shape=[shape((pairs + 2, sides,...]
where the time goes in v7:
time: 31.7 us; the launch traced here: 31.4 us
  starting transfers between devices  14.1 us (44%)
  Pallas kernels  13.8 us (44%)
  waiting for transfers between devices  3.45 us (11%)
    all_to_all x1, starting transfers between devices, per_device(): row = lax.all_to_all(sent, 'gy', 0, 0, tiled=True)  6.4 us
    ppermute x1, starting transfers between devices, per_device(): odd = lax.ppermute(rim, axes, steps + [(b, a) for a, b in steps])  6.28 us
    pallas_call x1, Pallas kernels, per_device(): pl.pallas_call(functools.partial(mid_kernel, axes), name='mid', out_shape...  5.78 us
    ppermute x1, waiting for transfers between devices, per_device(): odd = lax.ppermute(rim, axes, steps + [(b, a) for a, b in steps])  3.45 us
    pallas_call x1, Pallas kernels, per_device(): pl.pallas_call(down_kernel, name='down', out_shape=jax.ShapeDtypeStruct((...  3.24 us
    pallas_call x1, Pallas kernels, per_device(): pl.pallas_call(functools.partial(leaf_kernel, axes), name='leaf', out_sha...  2.09 us
    pallas_call x1, Pallas kernels, per_device(): pl.pallas_call(up_kernel, name='up', out_shape=[shape((pairs + 2, sides,...  1.82 us
    ppermute x1, starting transfers between devices, per_device(): even = lax.ppermute(rim, axes, [(i, i ^ 1) for i in range(total)])  1.46 us
  transfers between devices with their start and end apart: 3, of which 1 were waited for; matrix products, arithmetic and copies ran while one was open for 0% of the time, Pallas kernels for 25%

profile of v7, /device:TPU:1, one launch (start us, length us, event | category | flops | bytes accessed | tf_op | source)
XLA Modules:
  0.0 31.4 jit_solution(11029960292017279745)
XLA Ops:
  0.0 1.8 %up.1 = (bf16[18,32,128]{2,1,0:T(8,128)(2,1)S(1)}, bf16[16,32,128]{2,1,0:T(8,128)(2,1)S(1)}, bf16[8,32,128]{2,1,0:T(8,128)(2,1)S(1)}) custom-call(s32[32]{0:T(128)} %counts_hbm.3, bf16[32,2048]{1,0:T(8,128)(2,1)} %bitcast.3, bf16[32,64,64]{2,1,0:T(8,128)(2,1)} %basis_hbm.3, bf16[32,64,64]{2,1,0:T(8,128)(2,1)} %transfer_hbm.3), custom_call_target="tpu_custom_call" | custom-call | tf_op jit(solution)/shard_map/up/pallas_call | solution.py:291
  1.8 0.9 %copies.1 = bf16[64,32,128]{2,1,0:T(8,128)(2,1)} custom-call(bf16[8,32,128]{2,1,0:T(8,128)(2,1)S(1)} %get-tuple-element.20.parents_ref), custom_call_target="tpu_custom_call" | custom-call | tf_op jit(solution)/shard_map/copies/pallas_call | solution.py:311
  2.7 6.4 %all-to-all-start = ((bf16[64,32,128]{2,1,0:T(8,128)(2,1)}), bf16[64,32,128]{2,1,0:T(8,128)(2,1)S(1)}, u32[]{:S(2)}, u32[]{:S(2)}) async-start(bf16[64,32,128]{2,1,0:T(8,128)(2,1)} %copies.1), calls=%async_computation | async-start | bytes 1048576 | tf_op jit(solution)/shard_map/all_to_all | solution.py:320
  9.1 1.5 %collective-permute-start = (bf16[18,32,128]{2,1,0:T(8,128)(2,1)S(1)}, bf16[18,32,128]{2,1,0:T(8,128)(2,1)S(1)}, u32[]{:S(2)}, u32[]{:S(2)}) collective-permute-start(bf16[18,32,128]{2,1,0:T(8,128)(2,1)S(1)} %get-tuple-element.24.rim_ref), channel_id=1, source_target_pairs={{0,1},{1,0},{2,3},{3,2},{4,5},{5,4},{6,7},{7,6},{8,9},{9,8},{10,11... | collective-permute-start | bytes 442376 | tf_op jit(solution)/shard_map/ppermute | solution.py:321
  10.6 6.3 %collective-permute-start.1 = (bf16[18,32,128]{2,1,0:T(8,128)(2,1)S(1)}, bf16[18,32,128]{2,1,0:T(8,128)(2,1)S(1)}, u32[]{:S(2)}, u32[]{:S(2)}) collective-permute-start(bf16[18,32,128]{2,1,0:T(8,128)(2,1)S(1)} %get-tuple-element.24.rim_ref), channel_id=1, source_target_pairs={{1,2},{3,4},{5,6},{7,8},{9,10},{11,12},{13,14},{15,16},{17,18},{19... | collective-permute-start | bytes 442376 | tf_op jit(solution)/shard_map/ppermute | solution.py:323
  16.9 5.8 %mid.1 = (bf16[32,64,1024]{2,1,0:T(8,128)(2,1)S(1)}, bf16[8,64,1024]{2,1,0:T(8,128)(2,1)S(1)}, bf16[8,64,1024]{2,1,0:T(8,128)(2,1)}, f32[16,32,128]{2,1,0:T(8,12...) custom-call(bf16[16,32,128]{2,1,0:T(8,128)(2,1)S(1)} %get-tuple-element.18.live_ref, ...), custom_call_target="tpu_custom_call" | custom-call | tf_op jit(solution)/shard_map/mid/pallas_call | solution.py:326
  22.6 0.0 collective-permute-done.even_ref
  22.7 3.4 %collective-permute-done.1.odd_ref = bf16[18,32,128]{2,1,0:T(8,128)(2,1)S(1)} collective-permute-done((bf16[18,32,128]{2,1,0:T(8,128)(2,1)S(1)}, bf16[18,32,128]{2,1,0:T(8,128)(2,1)S(1)}, u32[]{:S(2)}, u32[]{:S(2)}) %collective-permute-start.1) | collective-permute-done | bytes 147488 | tf_op jit(solution)/shard_map/ppermute | solution.py:323
  26.1 2.1 %leaf.1 = (f32[16,32,128]{2,1,0:T(8,128)S(1)}, f32[2,32,128]{2,1,0:T(8,128)S(1)}, bf16[32,64,64]{2,1,0:T(8,128)(2,1)S(1)}) custom-call(s32[16,32]{1,0:T(8,128)S(1)} %get-tuple-element.23.at_vmem, bf16[18,32,128]{2,1,0:T(8,128)(2,1)S(1)} %get-tuple-element.24.rim_ref, bf16[18,32,128]{2,1,0:T(8,128)(2,1)S(1)} %collective-permute-done.even_ref, ...), custom_call_target="tpu_custom_call" | custom-call | tf_op jit(solution)/shard_map/leaf/pallas_call | solution.py:350
  28.2 0.0 all-to-all-done.row_ref
  28.2 3.2 %down.1 = bf16[32,2048]{1,0:T(8,128)(2,1)} custom-call(s32[16,16]{1,0:T(8,128)S(1)} %get-tuple-element.19.at_vmem, bf16[64,32,128]{2,1,0:T(8,128)(2,1)S(1)} %all-to-all-done.row_ref, bf16[8,64,1024]{2,1,0:T(8,128)(2,1)S(1)} %get-tuple-element.21.first_ref, bf16[8,64,1024]{2,1,0:T(8,128)(2,1)} %get-tuple-element.22.second_hbm, bf16[32,64,64]{2,1,0:T(8,128)(2,1)} %basis_hbm.3, ...), custom_call_target="tpu_custom_call" | custom-call | tf_op jit(solution)/shard_map/down/pallas_call | solution.py:368
Async XLA Ops:
  2.7 25.5 %all-to-all-start = ((bf16[64,32,128]{2,1,0:T(8,128)(2,1)}), bf16[64,32,128]{2,1,0:T(8,128)(2,1)S(1)}, u32[]{:S(2)}, u32[]{:S(2)}) async-start(bf16[64,32,128]{2,1,0:T(8,128)(2,1)} %copies.1), calls=%async_computation | async-start | bytes 1048576 | tf_op jit(solution)/shard_map/all_to_all | solution.py:320
  9.1 13.5 %collective-permute-start = (bf16[18,32,128]{2,1,0:T(8,128)(2,1)S(1)}, bf16[18,32,128]{2,1,0:T(8,128)(2,1)S(1)}, u32[]{:S(2)}, u32[]{:S(2)}) collective-permute-start(bf16[18,32,128]{2,1,0:T(8,128)(2,1)S(1)} %get-tuple-element.24.rim_ref), channel_id=1, source_target_pairs={{0,1},{1,0},{2,3},{3,2},{4,5},{5,4},{6,7},{7,6},{8,9},{9,8},{10,11... | collective-permute-start | bytes 442376 | tf_op jit(solution)/shard_map/ppermute | solution.py:321
  10.6 15.5 %collective-permute-start.1 = (bf16[18,32,128]{2,1,0:T(8,128)(2,1)S(1)}, bf16[18,32,128]{2,1,0:T(8,128)(2,1)S(1)}, u32[]{:S(2)}, u32[]{:S(2)}) collective-permute-start(bf16[18,32,128]{2,1,0:T(8,128)(2,1)S(1)} %get-tuple-element.24.rim_ref), channel_id=1, source_target_pairs={{1,2},{3,4},{5,6},{7,8},{9,10},{11,12},{13,14},{15,16},{17,18},{19... | collective-permute-start | bytes 442376 | tf_op jit(solution)/shard_map/ppermute | solution.py:323

commit v8 on v7

--- a/solution.py
+++ b/solution.py
@@ -96,7 +96,8 @@
         parents_ref[a] = jnp.concatenate(sums[2 * a : 2 * a + 2], axis=1).astype(jnp.bfloat16)
 
 
-def copies_kernel(parents_ref, sent_hbm, sems):
+def copies_kernel(parents_ref, rim_ref, sent_hbm, sems):
+    del rim_ref
     own = parents_ref.shape[0]
     copies = sent_hbm.shape[0] // own
     for copy in start_all([(parents_ref, sent_hbm.at[pl.ds(own * c, own)]) for c in range(copies)], sems):
@@ -104,10 +105,11 @@
 
 
 def mid_kernel(
-    axes, live_ref, coupling_hbm, near_hbm, parent_hbm, leaf_partners_hbm, parent_partners_hbm,
+    axes, sent_hbm, live_ref, coupling_hbm, near_hbm, parent_hbm, leaf_partners_hbm, parent_partners_hbm,
     packed_ref, first_ref, second_hbm, near_out_ref, rim_near_ref, leaf_at_ref, parent_at_ref,
     coupling_ref, near_ref, parent_ref, second_ref, sems,
 ):
+    del sent_hbm
     leaves, many, rank, _ = coupling_ref.shape
     parents = parent_ref.shape[0]
     width = near_ref.shape[2]
@@ -180,10 +182,12 @@
 
 
 def leaf_kernel(
-    axes, at_vmem, rim_ref, even_ref, odd_ref, packed_ref, rim_near_ref, transfer_hbm,
-    far_ref, edge_ref, transfer_ref, table_ref, at_ref, sems,
+    axes, at_vmem, rim_ref, even_ref, odd_ref, packed_ref, rim_near_ref, transfer_hbm, basis_hbm,
+    far_ref, edge_ref, transfer_ref, basis_packed_ref, table_ref, at_ref, basis_ref, sems,
 ):
-    at_in, transfer_in = start_all([(at_vmem, at_ref), (transfer_hbm, transfer_ref)], sems)
+    at_in, transfer_in, basis_in = start_all(
+        [(at_vmem, at_ref), (transfer_hbm, transfer_ref), (basis_hbm, basis_ref)], sems
+    )
     many, leaves = at_ref.shape
     rank = packed_ref.shape[1]
     width = rim_near_ref.shape[1]
@@ -209,19 +213,19 @@
             rows = [at_ref[j, g] for j in range(many)]
             fars.append(dot(picked(table_ref, rows, left), packed_ref[g], NT))
         far_ref[a] = jnp.concatenate(fars, axis=1)
+    basis_in.wait()
+    for a in range(pairs):
+        basis_packed_ref[a] = jnp.concatenate([basis_ref[2 * a], basis_ref[2 * a + 1]], axis=1)
     transfer_in.wait()
 
 
 def down_kernel(
-    at_vmem, row_ref, first_ref, second_hbm, basis_hbm, counts_hbm,
-    far_ref, near_ref, edge_ref, transfer_ref,
-    out_ref, table_ref, at_ref, local_ref, down_ref, second_ref, basis_ref, counts_ref, sems,
+    at_vmem, row_ref, first_ref, second_hbm, counts_hbm,
+    far_ref, near_ref, edge_ref, transfer_ref, basis_ref,
+    out_ref, table_ref, at_ref, local_ref, down_ref, second_ref, counts_ref, sems,
 ):
-    at_in, second_in, basis_in, counts_in = start_all(
-        [
-            (at_vmem, at_ref), (second_hbm, second_ref), (basis_hbm, basis_ref), (counts_hbm, counts_ref),
-        ],
-        sems,
+    at_in, second_in, counts_in = start_all(
+        [(at_vmem, at_ref), (second_hbm, second_ref), (counts_hbm, counts_ref)], sems
     )
     parents, many = at_ref.shape
     rank = first_ref.shape[1]
@@ -246,15 +250,13 @@
     for q in range(parents):
         local = far_ref[q] + dot(down_ref[q], transfer_ref[2 * q : 2 * q + 2].reshape(2 * rank, rank), NT)
         local_ref[q] = local.astype(jnp.bfloat16)
-    basis_in.wait()
     counts_in.wait()
     for q in range(parents):
         local = local_ref[q]
-        total = jnp.concatenate(
-            [dot(local[:, :rank], basis_ref[2 * q], NT), dot(local[:, rank:], basis_ref[2 * q + 1], NT)],
-            axis=1,
-        )
-        total = total + near_ref[q]
+        none = jnp.zeros_like(local)
+        both = jnp.concatenate([jnp.where(left, local, none), jnp.where(left, none, local)], axis=0)
+        total = dot(both, basis_ref[q], NT)
+        total = jnp.concatenate([total[:sides], total[sides:]], axis=1) + near_ref[q]
         if q == 0:
             total = total + edge_ref[0]
         if q == parents - 1:
@@ -308,81 +310,82 @@
         compiler_params=params(8),
     )(*keep(panel_counts, charges.T, basis, transfer))
 
+    even = lax.ppermute(rim, axes, [(i, i ^ 1) for i in range(total)])
+    steps = [(i, i + 1) for i in range(1, total - 1, 2)]
+    odd = lax.ppermute(rim, axes, steps + [(b, a) for a, b in steps])
     sent = pl.pallas_call(
         copies_kernel,
         name="copies",
         out_shape=pltpu.HBM((n * own, sides, 2 * rank), bf16),
-        in_specs=[VMEM],
+        in_specs=[VMEM, VMEM],
         out_specs=HBM,
         scratch_shapes=[dma(n)],
         compiler_params=params(4),
-    )(parent_coef)
+    )(parent_coef, even)
     row = lax.all_to_all(sent, "gy", 0, 0, tiled=True)
-    even = lax.ppermute(rim, axes, [(i, i ^ 1) for i in range(total)])
-    steps = [(i, i + 1) for i in range(1, total - 1, 2)]
-    odd = lax.ppermute(rim, axes, steps + [(b, a) for a, b in steps])
-
-    half = parents // 8 * 4
+
+    held = parents // 16 * 12
     packed, first, second, near, rim_near, leaf_at, parent_at = pl.pallas_call(
         functools.partial(mid_kernel, axes),
         name="mid",
         out_shape=[
             shape((leaves, rank, many * rank), bf16),
-            shape((half, rank, many * rank), bf16),
-            pltpu.HBM((parents - half, rank, many * rank), bf16),
+            shape((held, rank, many * rank), bf16),
+            pltpu.HBM((parents - held, rank, many * rank), bf16),
             shape((pairs, sides, 2 * width), f32),
             shape((2, width, width), bf16),
             shape((many, leaves), jnp.int32),
             shape((parents, many), jnp.int32),
         ],
-        in_specs=[VMEM] + [HBM] * 5,
+        in_specs=[HBM, VMEM] + [HBM] * 5,
         out_specs=[VMEM] * 2 + [HBM] + [VMEM] * 4,
         scratch_shapes=[
             pltpu.VMEM(leaf_coupling.shape, bf16),
             pltpu.VMEM(near_blocks.shape, bf16),
             pltpu.VMEM(parent_coupling.shape, bf16),
-            pltpu.VMEM((parents - half, rank, many * rank), bf16),
+            pltpu.VMEM((parents - held, rank, many * rank), bf16),
             dma(4 + leaves // 4 + parents // 4),
         ],
         compiler_params=params(20),
-    )(live, *keep(leaf_coupling, near_blocks, parent_coupling, leaf_partners.T, parent_partners))
-
-    far, edge, transfer_in = pl.pallas_call(
+    )(*keep(sent), live, *keep(leaf_coupling, near_blocks, parent_coupling, leaf_partners.T, parent_partners))
+
+    far, edge, transfer_in, basis_in = pl.pallas_call(
         functools.partial(leaf_kernel, axes),
         name="leaf",
         out_shape=[
             shape((pairs, sides, 2 * rank), f32),
             shape((2, sides, 2 * width), f32),
             shape(transfer.shape, bf16),
-        ],
-        in_specs=[VMEM] * 6 + [HBM],
-        out_specs=[VMEM] * 3,
+            shape((pairs, width, 2 * rank), bf16),
+        ],
+        in_specs=[VMEM] * 6 + [HBM] * 2,
+        out_specs=[VMEM] * 4,
         scratch_shapes=[
             pltpu.VMEM((3 * leaves, sides, 2 * rank), bf16),
             pltpu.SMEM((many, leaves), jnp.int32),
-            dma(2),
+            pltpu.VMEM(basis.shape, bf16),
+            dma(3),
         ],
         compiler_params=params(8),
-    )(leaf_at, rim, even, odd, packed, rim_near, *keep(transfer))
+    )(leaf_at, rim, even, odd, packed, rim_near, *keep(transfer, basis))
 
     out = pl.pallas_call(
         down_kernel,
         name="down",
         out_shape=jax.ShapeDtypeStruct((sides, leaves * width), bf16),
-        in_specs=[VMEM] * 3 + [HBM] * 3 + [VMEM] * 4,
+        in_specs=[VMEM] * 3 + [HBM] * 2 + [VMEM] * 5,
         out_specs=VMEM,
         scratch_shapes=[
             pltpu.VMEM((n * parents, sides, 2 * rank), bf16),
             pltpu.SMEM((parents, many), jnp.int32),
             pltpu.VMEM((pairs, sides, 2 * rank), bf16),
             pltpu.VMEM((parents, sides, rank), bf16),
-            pltpu.VMEM((parents - half, rank, many * rank), bf16),
-            pltpu.VMEM(basis.shape, bf16),
+            pltpu.VMEM((parents - held, rank, many * rank), bf16),
             pltpu.SMEM((leaves,), jnp.int32),
-            dma(4),
+            dma(3),
         ],
         compiler_params=params(12),
-    )(parent_at, row, first, *keep(second, basis, panel_counts), far, near, edge, transfer_in)
+    )(parent_at, row, first, *keep(second, panel_counts), far, near, edge, transfer_in, basis_in)
     return out.T
 
 

time: 31.7 us -> 39.3 us (1.24)
  local copies, waits for them, and re-layouts: 0 us -> 3.57 us
  waiting for transfers between devices: 3.45 us -> 6.22 us
  starting transfers between devices: 14.1 us -> 15.7 us
  Pallas kernels: 13.8 us -> 13.4 us
    ppermute x1, waiting for transfers between devices: 0.01 us -> 3.57 us  [per_device(): even = lax.ppermute(rim, axes, [(i, i ^ 1) for i in range(total)])]
    unnamed x0 -> x12, local copies, waits for them, and re-layouts: none -> 3.57 us
    ppermute x1, starting transfers between devices: 6.28 us -> 8.05 us  [per_device(): odd = lax.ppermute(rim, axes, steps + [(b, a) for a, b in steps])]
    all_to_all x1, starting transfers between devices: 6.4 us -> 5.47 us  [per_device(): row = lax.all_to_all(sent, 'gy', 0, 0, tiled=True)]
    ppermute x1, waiting for transfers between devices: 3.45 us -> 2.65 us  [per_device(): odd = lax.ppermute(rim, axes, steps + [(b, a) for a, b in steps])]
    ppermute x1, starting transfers between devices: 1.46 us -> 2.14 us  [per_device(): even = lax.ppermute(rim, axes, [(i, i ^ 1) for i in range(total)])]
  transfers between devices with their start and end apart: 3 -> 3, of which waited for: 1 -> 2; matrix products, arithmetic and copies ran while one was open for 0% -> 0% of each run, Pallas kernels for 25% -> 20%
where the time goes in v8:
time: 39.3 us; the launch traced here: 38.9 us
  starting transfers between devices  15.7 us (40%)
  Pallas kernels  13.4 us (34%)
  waiting for transfers between devices  6.22 us (16%)
  local copies, waits for them, and re-layouts  3.57 us (9%)
    ppermute x1, starting transfers between devices, per_device(): odd = lax.ppermute(rim, axes, steps + [(b, a) for a, b in steps])  8.05 us
    pallas_call x1, Pallas kernels, per_device(): pl.pallas_call(functools.partial(mid_kernel, axes), name='mid', out_shape...  5.59 us
    all_to_all x1, starting transfers between devices, per_device(): row = lax.all_to_all(sent, 'gy', 0, 0, tiled=True)  5.47 us
    ppermute x1, waiting for transfers between devices, per_device(): even = lax.ppermute(rim, axes, [(i, i ^ 1) for i in range(total)])  3.57 us
    unnamed x12, local copies, waits for them, and re-layouts  3.57 us
    pallas_call x1, Pallas kernels, per_device(): pl.pallas_call(down_kernel, name='down', out_shape=jax.ShapeDtypeStruct((...  2.9 us
    ppermute x1, waiting for transfers between devices, per_device(): odd = lax.ppermute(rim, axes, steps + [(b, a) for a, b in steps])  2.65 us
    pallas_call x1, Pallas kernels, per_device(): pl.pallas_call(functools.partial(leaf_kernel, axes), name='leaf', out_sha...  2.24 us
  transfers between devices with their start and end apart: 3, of which 2 were waited for; matrix products, arithmetic and copies ran while one was open for 0% of the time, Pallas kernels for 20%

profile of v8, /device:TPU:1, one launch (start us, length us, event | category | flops | bytes accessed | tf_op | source)
XLA Modules:
  0.0 38.9 jit_solution(4316805985684387608)
XLA Ops:
  0.0 1.8 %up.1 = (bf16[18,32,128]{2,1,0:T(8,128)(2,1)S(1)}, bf16[16,32,128]{2,1,0:T(8,128)(2,1)S(1)}, bf16[8,32,128]{2,1,0:T(8,128)(2,1)S(1)}) custom-call(s32[32]{0:T(128)} %counts_hbm.3, bf16[32,2048]{1,0:T(8,128)(2,1)} %bitcast.3, bf16[32,64,64]{2,1,0:T(8,128)(2,1)} %basis_hbm.3, bf16[32,64,64]{2,1,0:T(8,128)(2,1)} %transfer_hbm.3), custom_call_target="tpu_custom_call" | custom-call | tf_op jit(solution)/shard_map/up/pallas_call | solution.py:293
  1.8 0.0 copy-start
  1.8 2.1 %collective-permute-start = (bf16[18,32,128]{2,1,0:T(8,128)(2,1)S(1)}, bf16[18,32,128]{2,1,0:T(8,128)(2,1)S(1)}, u32[]{:S(2)}, u32[]{:S(2)}) collective-permute-start(bf16[18,32,128]{2,1,0:T(8,128)(2,1)S(1)} %get-tuple-element.20.rim_ref), channel_id=1, source_target_pairs={{0,1},{1,0},{2,3},{3,2},{4,5},{5,4},{6,7},{7,6},{8,9},{9,8},{10,11... | collective-permute-start | bytes 442376 | tf_op jit(solution)/shard_map/ppermute | solution.py:313
  4.0 3.6 %collective-permute-done.rim_ref.even_ref = bf16[18,32,128]{2,1,0:T(8,128)(2,1)S(1)} collective-permute-done((bf16[18,32,128]{2,1,0:T(8,128)(2,1)S(1)}, bf16[18,32,128]{2,1,0:T(8,128)(2,1)S(1)}, u32[]{:S(2)}, u32[]{:S(2)}) %collective-permute-start) | collective-permute-done | bytes 147488 | tf_op jit(solution)/shard_map/ppermute | solution.py:313
  7.5 0.9 %copies.1.sent_hbm = bf16[64,32,128]{2,1,0:T(8,128)(2,1)} custom-call(bf16[8,32,128]{2,1,0:T(8,128)(2,1)S(1)} %get-tuple-element.19.parents_ref, bf16[18,32,128]{2,1,0:T(8,128)(2,1)S(1)} %collective-permute-done.rim_ref.even_ref), custom_call_target="tpu_custom_call" | custom-call | tf_op jit(solution)/shard_map/copies/pallas_call | solution.py:316
  8.4 5.5 %all-to-all-start = ((bf16[64,32,128]{2,1,0:T(8,128)(2,1)}), bf16[64,32,128]{2,1,0:T(8,128)(2,1)S(1)}, u32[]{:S(2)}, u32[]{:S(2)}) async-start(bf16[64,32,128]{2,1,0:T(8,128)(2,1)} %copies.1.sent_hbm), calls=%async_computation | async-start | bytes 1048576 | tf_op jit(solution)/shard_map/all_to_all | solution.py:325
  13.9 8.0 %collective-permute-start.1 = (bf16[18,32,128]{2,1,0:T(8,128)(2,1)S(1)}, bf16[18,32,128]{2,1,0:T(8,128)(2,1)S(1)}, u32[]{:S(2)}, u32[]{:S(2)}) collective-permute-start(bf16[18,32,128]{2,1,0:T(8,128)(2,1)S(1)} %get-tuple-element.20.rim_ref), channel_id=1, source_target_pairs={{1,2},{3,4},{5,6},{7,8},{9,10},{11,12},{13,14},{15,16},{17,18},{19... | collective-permute-start | bytes 442376 | tf_op jit(solution)/shard_map/ppermute | solution.py:315
  21.9 5.6 %mid.1 = (bf16[32,64,1024]{2,1,0:T(8,128)(2,1)S(1)}, bf16[12,64,1024]{2,1,0:T(8,128)(2,1)S(1)}, bf16[4,64,1024]{2,1,0:T(8,128)(2,1)}, f32[16,32,128]{2,1,0:T(8,1...) custom-call(bf16[64,32,128]{2,1,0:T(8,128)(2,1)} %copies.1.sent_hbm, ...), custom_call_target="tpu_custom_call" | custom-call | tf_op jit(solution)/shard_map/mid/pallas_call | solution.py:328
  27.5 0.0 copy-done
  27.6 0.0 copy-start.4
  27.6 0.6 %copy-done.4 = s32[16,16]{1,0:T(8,128)} copy-done((s32[16,16]{1,0:T(8,128)}, s32[16,16]{1,0:T(8,128)S(1)}, u32[]{:S(2)}) %copy-start.4) | copy-done | bytes 1048
  28.2 2.6 %collective-permute-done.1.odd_ref = bf16[18,32,128]{2,1,0:T(8,128)(2,1)S(1)} collective-permute-done((bf16[18,32,128]{2,1,0:T(8,128)(2,1)S(1)}, bf16[18,32,128]{2,1,0:T(8,128)(2,1)S(1)}, u32[]{:S(2)}, u32[]{:S(2)}) %collective-permute-start.1) | collective-permute-done | bytes 147488 | tf_op jit(solution)/shard_map/ppermute | solution.py:315
  30.8 0.0 copy-start.1
  30.8 0.9 %copy-done.1 = bf16[18,32,128]{2,1,0:T(8,128)(2,1)S(1)} copy-done((bf16[18,32,128]{2,1,0:T(8,128)(2,1)S(1)}, bf16[18,32,128]{2,1,0:T(8,128)(2,1)}, u32[]{:S(2)}) %copy-start.1) | copy-done | bytes 147480
  31.7 2.2 %leaf.1 = (f32[16,32,128]{2,1,0:T(8,128)S(1)}, f32[2,32,128]{2,1,0:T(8,128)S(1)}, bf16[32,64,64]{2,1,0:T(8,128)(2,1)S(1)}, bf16[16,64,128]{2,1,0:T(8,128)(2,1)S(1)}) custom-call(s32[16,32]{1,0:T(8,128)S(1)} %get-tuple-element.25.at_vmem, bf16[18,32,128]{2,1,0:T(8,128)(2,1)S(1)} %copy-done.1, bf16[18,32,128]{2,1,0:T(8,128)(2,1)S(1)} %collective-permute-done.rim_ref.even_ref, ...), custom_call_target="tpu_custom_call" | custom-call | tf_op jit(solution)/shard_map/leaf/pallas_call | solution.py:352
  34.0 0.0 copy-start.2
  34.0 0.6 %copy-done.2 = f32[2,32,128]{2,1,0:T(8,128)} copy-done((f32[2,32,128]{2,1,0:T(8,128)}, f32[2,32,128]{2,1,0:T(8,128)S(1)}, u32[]{:S(2)}) %copy-start.2) | copy-done | bytes 32792
  34.6 0.0 all-to-all-done.row_ref
  34.6 0.0 copy-start.3
  34.6 0.8 %copy-done.3 = f32[2,32,128]{2,1,0:T(8,128)S(1)} copy-done((f32[2,32,128]{2,1,0:T(8,128)S(1)}, f32[2,32,128]{2,1,0:T(8,128)}, u32[]{:S(2)}) %copy-start.3) | copy-done | bytes 32792
  35.3 0.0 copy-start.5
  35.3 0.7 %copy-done.5 = s32[16,16]{1,0:T(8,128)S(1)} copy-done((s32[16,16]{1,0:T(8,128)S(1)}, s32[16,16]{1,0:T(8,128)}, u32[]{:S(2)}) %copy-start.5) | copy-done | bytes 1048
  36.0 2.9 %down.1 = bf16[32,2048]{1,0:T(8,128)(2,1)} custom-call(s32[16,16]{1,0:T(8,128)S(1)} %copy-done.5, bf16[64,32,128]{2,1,0:T(8,128)(2,1)S(1)} %all-to-all-done.row_ref, bf16[12,64,1024]{2,1,0:T(8,128)(2,1)S(1)} %get-tuple-element.23.first_ref, bf16[4,64,1024]{2,1,0:T(8,128)(2,1)} %get-tuple-element.24.second_hbm, s32[32]{0:T(128)} %counts_hbm.3, ...), custom_call_target="tpu_custom_call" | custom-call | tf_op jit(solution)/shard_map/down/pallas_call | solution.py:372
Async XLA Ops:
  1.8 25.7 %copy-start = (bf16[18,32,128]{2,1,0:T(8,128)(2,1)}, bf16[18,32,128]{2,1,0:T(8,128)(2,1)S(1)}, u32[]{:S(2)}) copy-start(bf16[18,32,128]{2,1,0:T(8,128)(2,1)S(1)} %get-tuple-element.20.rim_ref) | copy-start | bytes 442372
  1.8 5.7 %collective-permute-start = (bf16[18,32,128]{2,1,0:T(8,128)(2,1)S(1)}, bf16[18,32,128]{2,1,0:T(8,128)(2,1)S(1)}, u32[]{:S(2)}, u32[]{:S(2)}) collective-permute-start(bf16[18,32,128]{2,1,0:T(8,128)(2,1)S(1)} %get-tuple-element.20.rim_ref), channel_id=1, source_target_pairs={{0,1},{1,0},{2,3},{3,2},{4,5},{5,4},{6,7},{7,6},{8,9},{9,8},{10,11... | collective-permute-start | bytes 442376 | tf_op jit(solution)/shard_map/ppermute | solution.py:313
  8.4 26.2 %all-to-all-start = ((bf16[64,32,128]{2,1,0:T(8,128)(2,1)}), bf16[64,32,128]{2,1,0:T(8,128)(2,1)S(1)}, u32[]{:S(2)}, u32[]{:S(2)}) async-start(bf16[64,32,128]{2,1,0:T(8,128)(2,1)} %copies.1.sent_hbm), calls=%async_computation | async-start | bytes 1048576 | tf_op jit(solution)/shard_map/all_to_all | solution.py:325
  13.9 16.9 %collective-permute-start.1 = (bf16[18,32,128]{2,1,0:T(8,128)(2,1)S(1)}, bf16[18,32,128]{2,1,0:T(8,128)(2,1)S(1)}, u32[]{:S(2)}, u32[]{:S(2)}) collective-permute-start(bf16[18,32,128]{2,1,0:T(8,128)(2,1)S(1)} %get-tuple-element.20.rim_ref), channel_id=1, source_target_pairs={{1,2},{3,4},{5,6},{7,8},{9,10},{11,12},{13,14},{15,16},{17,18},{19... | collective-permute-start | bytes 442376 | tf_op jit(solution)/shard_map/ppermute | solution.py:315
  27.6 0.6 %copy-start.4 = (s32[16,16]{1,0:T(8,128)}, s32[16,16]{1,0:T(8,128)S(1)}, u32[]{:S(2)}) copy-start(s32[16,16]{1,0:T(8,128)S(1)} %get-tuple-element.22.at_vmem) | copy-start | bytes 3076
  30.8 0.9 %copy-start.1 = (bf16[18,32,128]{2,1,0:T(8,128)(2,1)S(1)}, bf16[18,32,128]{2,1,0:T(8,128)(2,1)}, u32[]{:S(2)}) copy-start(bf16[18,32,128]{2,1,0:T(8,128)(2,1)} %copy-done) | copy-start | bytes 442372
  34.0 0.6 %copy-start.2 = (f32[2,32,128]{2,1,0:T(8,128)}, f32[2,32,128]{2,1,0:T(8,128)S(1)}, u32[]{:S(2)}) copy-start(f32[2,32,128]{2,1,0:T(8,128)S(1)} %get-tuple-element.30.edge_ref) | copy-start | bytes 98308
  34.6 0.8 %copy-start.3 = (f32[2,32,128]{2,1,0:T(8,128)S(1)}, f32[2,32,128]{2,1,0:T(8,128)}, u32[]{:S(2)}) copy-start(f32[2,32,128]{2,1,0:T(8,128)} %copy-done.2) | copy-start | bytes 98308
  35.3 0.7 %copy-start.5 = (s32[16,16]{1,0:T(8,128)S(1)}, s32[16,16]{1,0:T(8,128)}, u32[]{:S(2)}) copy-start(s32[16,16]{1,0:T(8,128)} %copy-done.4) | copy-start | bytes 3076

commit v9 on v8

--- a/solution.py
+++ b/solution.py
@@ -96,8 +96,7 @@
         parents_ref[a] = jnp.concatenate(sums[2 * a : 2 * a + 2], axis=1).astype(jnp.bfloat16)
 
 
-def copies_kernel(parents_ref, rim_ref, sent_hbm, sems):
-    del rim_ref
+def copies_kernel(parents_ref, sent_hbm, sems):
     own = parents_ref.shape[0]
     copies = sent_hbm.shape[0] // own
     for copy in start_all([(parents_ref, sent_hbm.at[pl.ds(own * c, own)]) for c in range(copies)], sems):
@@ -105,11 +104,10 @@
 
 
 def mid_kernel(
-    axes, sent_hbm, live_ref, coupling_hbm, near_hbm, parent_hbm, leaf_partners_hbm, parent_partners_hbm,
+    axes, live_ref, coupling_hbm, near_hbm, parent_hbm, leaf_partners_hbm, parent_partners_hbm,
     packed_ref, first_ref, second_hbm, near_out_ref, rim_near_ref, leaf_at_ref, parent_at_ref,
     coupling_ref, near_ref, parent_ref, second_ref, sems,
 ):
-    del sent_hbm
     leaves, many, rank, _ = coupling_ref.shape
     parents = parent_ref.shape[0]
     width = near_ref.shape[2]
@@ -289,6 +287,7 @@
     shape = pltpu.VMEM
     dma = lambda count: pltpu.SemaphoreType.DMA((count,))
     params = lambda mib: pltpu.CompilerParams(vmem_limit_bytes=mib * 2**20)
+    cost = lambda mib: pl.CostEstimate(flops=0, transcendentals=0, bytes_accessed=mib * 2**20)
 
     rim, live, parent_coef = pl.pallas_call(
         up_kernel,
@@ -317,14 +316,14 @@
         copies_kernel,
         name="copies",
         out_shape=pltpu.HBM((n * own, sides, 2 * rank), bf16),
-        in_specs=[VMEM, VMEM],
+        in_specs=[VMEM],
         out_specs=HBM,
         scratch_shapes=[dma(n)],
         compiler_params=params(4),
-    )(parent_coef, even)
+    )(parent_coef)
     row = lax.all_to_all(sent, "gy", 0, 0, tiled=True)
 
-    held = parents // 16 * 12
+    held = parents // 8 * 4
     packed, first, second, near, rim_near, leaf_at, parent_at = pl.pallas_call(
         functools.partial(mid_kernel, axes),
         name="mid",
@@ -337,7 +336,7 @@
             shape((many, leaves), jnp.int32),
             shape((parents, many), jnp.int32),
         ],
-        in_specs=[HBM, VMEM] + [HBM] * 5,
+        in_specs=[VMEM] + [HBM] * 5,
         out_specs=[VMEM] * 2 + [HBM] + [VMEM] * 4,
         scratch_shapes=[
             pltpu.VMEM(leaf_coupling.shape, bf16),
@@ -347,7 +346,8 @@
             dma(4 + leaves // 4 + parents // 4),
         ],
         compiler_params=params(20),
-    )(*keep(sent), live, *keep(leaf_coupling, near_blocks, parent_coupling, leaf_partners.T, parent_partners))
+        cost_estimate=cost(16),
+    )(live, *keep(leaf_coupling, near_blocks, parent_coupling, leaf_partners.T, parent_partners))
 
     far, edge, transfer_in, basis_in = pl.pallas_call(
         functools.partial(leaf_kernel, axes),
@@ -367,6 +367,7 @@
             dma(3),
         ],
         compiler_params=params(8),
+        cost_estimate=cost(64),
     )(leaf_at, rim, even, odd, packed, rim_near, *keep(transfer, basis))
 
     out = pl.pallas_call(

time: 39.3 us -> 31.7 us (0.81)
  local copies, waits for them, and re-layouts: 3.57 us -> 0 us
  waiting for transfers between devices: 6.22 us -> 3.45 us
  starting transfers between devices: 15.7 us -> 14.1 us
  Pallas kernels: 13.4 us -> 13.8 us
    ppermute x1, waiting for transfers between devices: 3.57 us -> 0.01 us  [per_device(): even = lax.ppermute(rim, axes, [(i, i ^ 1) for i in range(total)])]
    unnamed x12 -> x0, local copies, waits for them, and re-layouts: 3.57 us -> none
    ppermute x1, starting transfers between devices: 8.05 us -> 6.28 us  [per_device(): odd = lax.ppermute(rim, axes, steps + [(b, a) for a, b in steps])]
    all_to_all x1, starting transfers between devices: 5.47 us -> 6.4 us  [per_device(): row = lax.all_to_all(sent, 'gy', 0, 0, tiled=True)]
    ppermute x1, waiting for transfers between devices: 2.65 us -> 3.45 us  [per_device(): odd = lax.ppermute(rim, axes, steps + [(b, a) for a, b in steps])]
    ppermute x1, starting transfers between devices: 2.14 us -> 1.46 us  [per_device(): even = lax.ppermute(rim, axes, [(i, i ^ 1) for i in range(total)])]
  transfers between devices with their start and end apart: 3 -> 3, of which waited for: 2 -> 1; matrix products, arithmetic and copies ran while one was open for 0% -> 0% of each run, Pallas kernels for 20% -> 26%
where the time goes in v9:
time: 31.7 us; the launch traced here: 31.4 us
  starting transfers between devices  14.1 us (44%)
  Pallas kernels  13.8 us (44%)
  waiting for transfers between devices  3.45 us (11%)
    all_to_all x1, starting transfers between devices, per_device(): row = lax.all_to_all(sent, 'gy', 0, 0, tiled=True)  6.4 us
    ppermute x1, starting transfers between devices, per_device(): odd = lax.ppermute(rim, axes, steps + [(b, a) for a, b in steps])  6.28 us
    pallas_call x1, Pallas kernels, per_device(): pl.pallas_call(functools.partial(mid_kernel, axes), name='mid', out_shape...  5.78 us
    ppermute x1, waiting for transfers between devices, per_device(): odd = lax.ppermute(rim, axes, steps + [(b, a) for a, b in steps])  3.45 us
    pallas_call x1, Pallas kernels, per_device(): pl.pallas_call(down_kernel, name='down', out_shape=jax.ShapeDtypeStruct((...  3.05 us
    pallas_call x1, Pallas kernels, per_device(): pl.pallas_call(functools.partial(leaf_kernel, axes), name='leaf', out_sha...  2.23 us
    pallas_call x1, Pallas kernels, per_device(): pl.pallas_call(up_kernel, name='up', out_shape=[shape((pairs + 2, sides,...  1.82 us
    ppermute x1, starting transfers between devices, per_device(): even = lax.ppermute(rim, axes, [(i, i ^ 1) for i in range(total)])  1.46 us
  transfers between devices with their start and end apart: 3, of which 1 were waited for; matrix products, arithmetic and copies ran while one was open for 0% of the time, Pallas kernels for 26%

profile of v9, /device:TPU:1, one launch (start us, length us, event | category | flops | bytes accessed | tf_op | source)
XLA Modules:
  0.0 31.4 jit_solution(4235783947716624464)
XLA Ops:
  0.0 1.8 %up.1 = (bf16[18,32,128]{2,1,0:T(8,128)(2,1)S(1)}, bf16[16,32,128]{2,1,0:T(8,128)(2,1)S(1)}, bf16[8,32,128]{2,1,0:T(8,128)(2,1)S(1)}) custom-call(s32[32]{0:T(128)} %counts_hbm.3, bf16[32,2048]{1,0:T(8,128)(2,1)} %bitcast.3, bf16[32,64,64]{2,1,0:T(8,128)(2,1)} %basis_hbm.3, bf16[32,64,64]{2,1,0:T(8,128)(2,1)} %transfer_hbm.3), custom_call_target="tpu_custom_call" | custom-call | tf_op jit(solution)/shard_map/up/pallas_call | solution.py:292
  1.8 0.9 %copies.1 = bf16[64,32,128]{2,1,0:T(8,128)(2,1)} custom-call(bf16[8,32,128]{2,1,0:T(8,128)(2,1)S(1)} %get-tuple-element.21.parents_ref), custom_call_target="tpu_custom_call" | custom-call | tf_op jit(solution)/shard_map/copies/pallas_call | solution.py:315
  2.7 6.4 %all-to-all-start = ((bf16[64,32,128]{2,1,0:T(8,128)(2,1)}), bf16[64,32,128]{2,1,0:T(8,128)(2,1)S(1)}, u32[]{:S(2)}, u32[]{:S(2)}) async-start(bf16[64,32,128]{2,1,0:T(8,128)(2,1)} %copies.1), calls=%async_computation | async-start | bytes 1048576 | tf_op jit(solution)/shard_map/all_to_all | solution.py:324
  9.1 1.5 %collective-permute-start = (bf16[18,32,128]{2,1,0:T(8,128)(2,1)S(1)}, bf16[18,32,128]{2,1,0:T(8,128)(2,1)S(1)}, u32[]{:S(2)}, u32[]{:S(2)}) collective-permute-start(bf16[18,32,128]{2,1,0:T(8,128)(2,1)S(1)} %get-tuple-element.25.rim_ref), channel_id=1, source_target_pairs={{0,1},{1,0},{2,3},{3,2},{4,5},{5,4},{6,7},{7,6},{8,9},{9,8},{10,11... | collective-permute-start | bytes 442376 | tf_op jit(solution)/shard_map/ppermute | solution.py:312
  10.6 6.3 %collective-permute-start.1 = (bf16[18,32,128]{2,1,0:T(8,128)(2,1)S(1)}, bf16[18,32,128]{2,1,0:T(8,128)(2,1)S(1)}, u32[]{:S(2)}, u32[]{:S(2)}) collective-permute-start(bf16[18,32,128]{2,1,0:T(8,128)(2,1)S(1)} %get-tuple-element.25.rim_ref), channel_id=1, source_target_pairs={{1,2},{3,4},{5,6},{7,8},{9,10},{11,12},{13,14},{15,16},{17,18},{19... | collective-permute-start | bytes 442376 | tf_op jit(solution)/shard_map/ppermute | solution.py:314
  16.9 5.8 %mid.1 = (bf16[32,64,1024]{2,1,0:T(8,128)(2,1)S(1)}, bf16[8,64,1024]{2,1,0:T(8,128)(2,1)S(1)}, bf16[8,64,1024]{2,1,0:T(8,128)(2,1)}, f32[16,32,128]{2,1,0:T(8,12...) custom-call(bf16[16,32,128]{2,1,0:T(8,128)(2,1)S(1)} %get-tuple-element.19.live_ref, ...), custom_call_target="tpu_custom_call" | custom-call | bytes 16777216 | tf_op jit(solution)/shard_map/mid/pallas_call | solution.py:327
  22.6 0.0 collective-permute-done.even_ref
  22.7 3.4 %collective-permute-done.1.odd_ref = bf16[18,32,128]{2,1,0:T(8,128)(2,1)S(1)} collective-permute-done((bf16[18,32,128]{2,1,0:T(8,128)(2,1)S(1)}, bf16[18,32,128]{2,1,0:T(8,128)(2,1)S(1)}, u32[]{:S(2)}, u32[]{:S(2)}) %collective-permute-start.1) | collective-permute-done | bytes 147488 | tf_op jit(solution)/shard_map/ppermute | solution.py:314
  26.1 2.2 %leaf.1 = (f32[16,32,128]{2,1,0:T(8,128)S(1)}, f32[2,32,128]{2,1,0:T(8,128)S(1)}, bf16[32,64,64]{2,1,0:T(8,128)(2,1)S(1)}, bf16[16,64,128]{2,1,0:T(8,128)(2,1)S(1)}) custom-call(s32[16,32]{1,0:T(8,128)S(1)} %get-tuple-element.24.at_vmem, bf16[18,32,128]{2,1,0:T(8,128)(2,1)S(1)} %get-tuple-element.25.rim_ref, ...), custom_call_target="tpu_custom_call" | custom-call | bytes 67108864 | tf_op jit(solution)/shard_map/leaf/pallas_call | solution.py:352
  28.3 0.0 all-to-all-done.row_ref
  28.4 3.1 %down.1 = bf16[32,2048]{1,0:T(8,128)(2,1)} custom-call(s32[16,16]{1,0:T(8,128)S(1)} %get-tuple-element.20.at_vmem, bf16[64,32,128]{2,1,0:T(8,128)(2,1)S(1)} %all-to-all-done.row_ref, bf16[8,64,1024]{2,1,0:T(8,128)(2,1)S(1)} %get-tuple-element.22.first_ref, bf16[8,64,1024]{2,1,0:T(8,128)(2,1)} %get-tuple-element.23.second_hbm, s32[32]{0:T(128)} %counts_hbm.3, ...), custom_call_target="tpu_custom_call" | custom-call | tf_op jit(solution)/shard_map/down/pallas_call | solution.py:373
Async XLA Ops:
  2.7 25.6 %all-to-all-start = ((bf16[64,32,128]{2,1,0:T(8,128)(2,1)}), bf16[64,32,128]{2,1,0:T(8,128)(2,1)S(1)}, u32[]{:S(2)}, u32[]{:S(2)}) async-start(bf16[64,32,128]{2,1,0:T(8,128)(2,1)} %copies.1), calls=%async_computation | async-start | bytes 1048576 | tf_op jit(solution)/shard_map/all_to_all | solution.py:324
  9.1 13.5 %collective-permute-start = (bf16[18,32,128]{2,1,0:T(8,128)(2,1)S(1)}, bf16[18,32,128]{2,1,0:T(8,128)(2,1)S(1)}, u32[]{:S(2)}, u32[]{:S(2)}) collective-permute-start(bf16[18,32,128]{2,1,0:T(8,128)(2,1)S(1)} %get-tuple-element.25.rim_ref), channel_id=1, source_target_pairs={{0,1},{1,0},{2,3},{3,2},{4,5},{5,4},{6,7},{7,6},{8,9},{9,8},{10,11... | collective-permute-start | bytes 442376 | tf_op jit(solution)/shard_map/ppermute | solution.py:312
  10.6 15.5 %collective-permute-start.1 = (bf16[18,32,128]{2,1,0:T(8,128)(2,1)S(1)}, bf16[18,32,128]{2,1,0:T(8,128)(2,1)S(1)}, u32[]{:S(2)}, u32[]{:S(2)}) collective-permute-start(bf16[18,32,128]{2,1,0:T(8,128)(2,1)S(1)} %get-tuple-element.25.rim_ref), channel_id=1, source_target_pairs={{1,2},{3,4},{5,6},{7,8},{9,10},{11,12},{13,14},{15,16},{17,18},{19... | collective-permute-start | bytes 442376 | tf_op jit(solution)/shard_map/ppermute | solution.py:314

commit v10 on v9

--- a/solution.py
+++ b/solution.py
@@ -346,7 +346,7 @@
             dma(4 + leaves // 4 + parents // 4),
         ],
         compiler_params=params(20),
-        cost_estimate=cost(16),
+        cost_estimate=cost(256),
     )(live, *keep(leaf_coupling, near_blocks, parent_coupling, leaf_partners.T, parent_partners))
 
     far, edge, transfer_in, basis_in = pl.pallas_call(
@@ -367,7 +367,7 @@
             dma(3),
         ],
         compiler_params=params(8),
-        cost_estimate=cost(64),
+        cost_estimate=cost(4096),
     )(leaf_at, rim, even, odd, packed, rim_near, *keep(transfer, basis))
 
     out = pl.pallas_call(

time: 31.7 us -> 31.7 us (level)
  no operation moved by 1% of the time
where the time goes in v10:
time: 31.7 us; the launch traced here: 31.4 us
  starting transfers between devices  14.1 us (44%)
  Pallas kernels  13.8 us (44%)
  waiting for transfers between devices  3.45 us (11%)
    all_to_all x1, starting transfers between devices, per_device(): row = lax.all_to_all(sent, 'gy', 0, 0, tiled=True)  6.4 us
    ppermute x1, starting transfers between devices, per_device(): odd = lax.ppermute(rim, axes, steps + [(b, a) for a, b in steps])  6.28 us
    pallas_call x1, Pallas kernels, per_device(): pl.pallas_call(functools.partial(mid_kernel, axes), name='mid', out_shape...  5.78 us
    ppermute x1, waiting for transfers between devices, per_device(): odd = lax.ppermute(rim, axes, steps + [(b, a) for a, b in steps])  3.45 us
    pallas_call x1, Pallas kernels, per_device(): pl.pallas_call(down_kernel, name='down', out_shape=jax.ShapeDtypeStruct((...  3.05 us
    pallas_call x1, Pallas kernels, per_device(): pl.pallas_call(functools.partial(leaf_kernel, axes), name='leaf', out_sha...  2.24 us
    pallas_call x1, Pallas kernels, per_device(): pl.pallas_call(up_kernel, name='up', out_shape=[shape((pairs + 2, sides,...  1.82 us
    ppermute x1, starting transfers between devices, per_device(): even = lax.ppermute(rim, axes, [(i, i ^ 1) for i in range(total)])  1.46 us
  transfers between devices with their start and end apart: 3, of which 1 were waited for; matrix products, arithmetic and copies ran while one was open for 0% of the time, Pallas kernels for 26%

profile of v10, /device:TPU:1, one launch (start us, length us, event | category | flops | bytes accessed | tf_op | source)
XLA Modules:
  0.0 31.4 jit_solution(4235783947716624464)
XLA Ops:
  0.0 1.8 %up.1 = (bf16[18,32,128]{2,1,0:T(8,128)(2,1)S(1)}, bf16[16,32,128]{2,1,0:T(8,128)(2,1)S(1)}, bf16[8,32,128]{2,1,0:T(8,128)(2,1)S(1)}) custom-call(s32[32]{0:T(128)} %counts_hbm.3, bf16[32,2048]{1,0:T(8,128)(2,1)} %bitcast.3, bf16[32,64,64]{2,1,0:T(8,128)(2,1)} %basis_hbm.3, bf16[32,64,64]{2,1,0:T(8,128)(2,1)} %transfer_hbm.3), custom_call_target="tpu_custom_call" | custom-call | tf_op jit(solution)/shard_map/up/pallas_call | solution.py:292
  1.8 0.9 %copies.1 = bf16[64,32,128]{2,1,0:T(8,128)(2,1)} custom-call(bf16[8,32,128]{2,1,0:T(8,128)(2,1)S(1)} %get-tuple-element.21.parents_ref), custom_call_target="tpu_custom_call" | custom-call | tf_op jit(solution)/shard_map/copies/pallas_call | solution.py:315
  2.7 6.4 %all-to-all-start = ((bf16[64,32,128]{2,1,0:T(8,128)(2,1)}), bf16[64,32,128]{2,1,0:T(8,128)(2,1)S(1)}, u32[]{:S(2)}, u32[]{:S(2)}) async-start(bf16[64,32,128]{2,1,0:T(8,128)(2,1)} %copies.1), calls=%async_computation | async-start | bytes 1048576 | tf_op jit(solution)/shard_map/all_to_all | solution.py:324
  9.1 1.5 %collective-permute-start = (bf16[18,32,128]{2,1,0:T(8,128)(2,1)S(1)}, bf16[18,32,128]{2,1,0:T(8,128)(2,1)S(1)}, u32[]{:S(2)}, u32[]{:S(2)}) collective-permute-start(bf16[18,32,128]{2,1,0:T(8,128)(2,1)S(1)} %get-tuple-element.25.rim_ref), channel_id=1, source_target_pairs={{0,1},{1,0},{2,3},{3,2},{4,5},{5,4},{6,7},{7,6},{8,9},{9,8},{10,11... | collective-permute-start | bytes 442376 | tf_op jit(solution)/shard_map/ppermute | solution.py:312
  10.6 6.3 %collective-permute-start.1 = (bf16[18,32,128]{2,1,0:T(8,128)(2,1)S(1)}, bf16[18,32,128]{2,1,0:T(8,128)(2,1)S(1)}, u32[]{:S(2)}, u32[]{:S(2)}) collective-permute-start(bf16[18,32,128]{2,1,0:T(8,128)(2,1)S(1)} %get-tuple-element.25.rim_ref), channel_id=1, source_target_pairs={{1,2},{3,4},{5,6},{7,8},{9,10},{11,12},{13,14},{15,16},{17,18},{19... | collective-permute-start | bytes 442376 | tf_op jit(solution)/shard_map/ppermute | solution.py:314
  16.9 5.8 %mid.1 = (bf16[32,64,1024]{2,1,0:T(8,128)(2,1)S(1)}, bf16[8,64,1024]{2,1,0:T(8,128)(2,1)S(1)}, bf16[8,64,1024]{2,1,0:T(8,128)(2,1)}, f32[16,32,128]{2,1,0:T(8,12...) custom-call(bf16[16,32,128]{2,1,0:T(8,128)(2,1)S(1)} %get-tuple-element.19.live_ref, ...), custom_call_target="tpu_custom_call" | custom-call | bytes 268435456 | tf_op jit(solution)/shard_map/mid/pallas_call | solution.py:327
  22.6 0.0 collective-permute-done.even_ref
  22.7 3.4 %collective-permute-done.1.odd_ref = bf16[18,32,128]{2,1,0:T(8,128)(2,1)S(1)} collective-permute-done((bf16[18,32,128]{2,1,0:T(8,128)(2,1)S(1)}, bf16[18,32,128]{2,1,0:T(8,128)(2,1)S(1)}, u32[]{:S(2)}, u32[]{:S(2)}) %collective-permute-start.1) | collective-permute-done | bytes 147488 | tf_op jit(solution)/shard_map/ppermute | solution.py:314
  26.1 2.2 %leaf.1 = (f32[16,32,128]{2,1,0:T(8,128)S(1)}, f32[2,32,128]{2,1,0:T(8,128)S(1)}, bf16[32,64,64]{2,1,0:T(8,128)(2,1)S(1)}, bf16[16,64,128]{2,1,0:T(8,128)(2,1)S(1)}) custom-call(s32[16,32]{1,0:T(8,128)S(1)} %get-tuple-element.24.at_vmem, bf16[18,32,128]{2,1,0:T(8,128)(2,1)S(1)} %get-tuple-element.25.rim_ref, ...), custom_call_target="tpu_custom_call" | custom-call | bytes 4294967296 | tf_op jit(solution)/shard_map/leaf/pallas_call | solution.py:352
  28.3 0.0 all-to-all-done.row_ref
  28.4 3.1 %down.1 = bf16[32,2048]{1,0:T(8,128)(2,1)} custom-call(s32[16,16]{1,0:T(8,128)S(1)} %get-tuple-element.20.at_vmem, bf16[64,32,128]{2,1,0:T(8,128)(2,1)S(1)} %all-to-all-done.row_ref, bf16[8,64,1024]{2,1,0:T(8,128)(2,1)S(1)} %get-tuple-element.22.first_ref, bf16[8,64,1024]{2,1,0:T(8,128)(2,1)} %get-tuple-element.23.second_hbm, s32[32]{0:T(128)} %counts_hbm.3, ...), custom_call_target="tpu_custom_call" | custom-call | tf_op jit(solution)/shard_map/down/pallas_call | solution.py:373
Async XLA Ops:
  2.7 25.6 %all-to-all-start = ((bf16[64,32,128]{2,1,0:T(8,128)(2,1)}), bf16[64,32,128]{2,1,0:T(8,128)(2,1)S(1)}, u32[]{:S(2)}, u32[]{:S(2)}) async-start(bf16[64,32,128]{2,1,0:T(8,128)(2,1)} %copies.1), calls=%async_computation | async-start | bytes 1048576 | tf_op jit(solution)/shard_map/all_to_all | solution.py:324
  9.1 13.5 %collective-permute-start = (bf16[18,32,128]{2,1,0:T(8,128)(2,1)S(1)}, bf16[18,32,128]{2,1,0:T(8,128)(2,1)S(1)}, u32[]{:S(2)}, u32[]{:S(2)}) collective-permute-start(bf16[18,32,128]{2,1,0:T(8,128)(2,1)S(1)} %get-tuple-element.25.rim_ref), channel_id=1, source_target_pairs={{0,1},{1,0},{2,3},{3,2},{4,5},{5,4},{6,7},{7,6},{8,9},{9,8},{10,11... | collective-permute-start | bytes 442376 | tf_op jit(solution)/shard_map/ppermute | solution.py:312
  10.6 15.5 %collective-permute-start.1 = (bf16[18,32,128]{2,1,0:T(8,128)(2,1)S(1)}, bf16[18,32,128]{2,1,0:T(8,128)(2,1)S(1)}, u32[]{:S(2)}, u32[]{:S(2)}) collective-permute-start(bf16[18,32,128]{2,1,0:T(8,128)(2,1)S(1)} %get-tuple-element.25.rim_ref), channel_id=1, source_target_pairs={{1,2},{3,4},{5,6},{7,8},{9,10},{11,12},{13,14},{15,16},{17,18},{19... | collective-permute-start | bytes 442376 | tf_op jit(solution)/shard_map/ppermute | solution.py:314

commit v11 on v10

--- a/solution.py
+++ b/solution.py
@@ -346,7 +346,7 @@
             dma(4 + leaves // 4 + parents // 4),
         ],
         compiler_params=params(20),
-        cost_estimate=cost(256),
+        cost_estimate=cost(0),
     )(live, *keep(leaf_coupling, near_blocks, parent_coupling, leaf_partners.T, parent_partners))
 
     far, edge, transfer_in, basis_in = pl.pallas_call(
@@ -367,7 +367,7 @@
             dma(3),
         ],
         compiler_params=params(8),
-        cost_estimate=cost(4096),
+        cost_estimate=cost(512),
     )(leaf_at, rim, even, odd, packed, rim_near, *keep(transfer, basis))
 
     out = pl.pallas_call(

time: 31.7 us -> 31.7 us (level)
  no operation moved by 1% of the time
where the time goes in v11:
time: 31.7 us; the launch traced here: 31.4 us
  starting transfers between devices  14.1 us (44%)
  Pallas kernels  13.8 us (44%)
  waiting for transfers between devices  3.45 us (11%)
    all_to_all x1, starting transfers between devices, per_device(): row = lax.all_to_all(sent, 'gy', 0, 0, tiled=True)  6.4 us
    ppermute x1, starting transfers between devices, per_device(): odd = lax.ppermute(rim, axes, steps + [(b, a) for a, b in steps])  6.28 us
    pallas_call x1, Pallas kernels, per_device(): pl.pallas_call(functools.partial(mid_kernel, axes), name='mid', out_shape...  5.78 us
    ppermute x1, waiting for transfers between devices, per_device(): odd = lax.ppermute(rim, axes, steps + [(b, a) for a, b in steps])  3.45 us
    pallas_call x1, Pallas kernels, per_device(): pl.pallas_call(down_kernel, name='down', out_shape=jax.ShapeDtypeStruct((...  3.05 us
    pallas_call x1, Pallas kernels, per_device(): pl.pallas_call(functools.partial(leaf_kernel, axes), name='leaf', out_sha...  2.23 us
    pallas_call x1, Pallas kernels, per_device(): pl.pallas_call(up_kernel, name='up', out_shape=[shape((pairs + 2, sides,...  1.82 us
    ppermute x1, starting transfers between devices, per_device(): even = lax.ppermute(rim, axes, [(i, i ^ 1) for i in range(total)])  1.46 us
  transfers between devices with their start and end apart: 3, of which 1 were waited for; matrix products, arithmetic and copies ran while one was open for 0% of the time, Pallas kernels for 26%

profile of v11, /device:TPU:1, one launch (start us, length us, event | category | flops | bytes accessed | tf_op | source)
XLA Modules:
  0.0 31.4 jit_solution(4235783947716624464)
XLA Ops:
  0.0 1.8 %up.1 = (bf16[18,32,128]{2,1,0:T(8,128)(2,1)S(1)}, bf16[16,32,128]{2,1,0:T(8,128)(2,1)S(1)}, bf16[8,32,128]{2,1,0:T(8,128)(2,1)S(1)}) custom-call(s32[32]{0:T(128)} %counts_hbm.3, bf16[32,2048]{1,0:T(8,128)(2,1)} %bitcast.3, bf16[32,64,64]{2,1,0:T(8,128)(2,1)} %basis_hbm.3, bf16[32,64,64]{2,1,0:T(8,128)(2,1)} %transfer_hbm.3), custom_call_target="tpu_custom_call" | custom-call | tf_op jit(solution)/shard_map/up/pallas_call | solution.py:292
  1.8 0.9 %copies.1 = bf16[64,32,128]{2,1,0:T(8,128)(2,1)} custom-call(bf16[8,32,128]{2,1,0:T(8,128)(2,1)S(1)} %get-tuple-element.21.parents_ref), custom_call_target="tpu_custom_call" | custom-call | tf_op jit(solution)/shard_map/copies/pallas_call | solution.py:315
  2.7 6.4 %all-to-all-start = ((bf16[64,32,128]{2,1,0:T(8,128)(2,1)}), bf16[64,32,128]{2,1,0:T(8,128)(2,1)S(1)}, u32[]{:S(2)}, u32[]{:S(2)}) async-start(bf16[64,32,128]{2,1,0:T(8,128)(2,1)} %copies.1), calls=%async_computation | async-start | bytes 1048576 | tf_op jit(solution)/shard_map/all_to_all | solution.py:324
  9.1 1.5 %collective-permute-start = (bf16[18,32,128]{2,1,0:T(8,128)(2,1)S(1)}, bf16[18,32,128]{2,1,0:T(8,128)(2,1)S(1)}, u32[]{:S(2)}, u32[]{:S(2)}) collective-permute-start(bf16[18,32,128]{2,1,0:T(8,128)(2,1)S(1)} %get-tuple-element.25.rim_ref), channel_id=1, source_target_pairs={{0,1},{1,0},{2,3},{3,2},{4,5},{5,4},{6,7},{7,6},{8,9},{9,8},{10,11... | collective-permute-start | bytes 442376 | tf_op jit(solution)/shard_map/ppermute | solution.py:312
  10.6 6.3 %collective-permute-start.1 = (bf16[18,32,128]{2,1,0:T(8,128)(2,1)S(1)}, bf16[18,32,128]{2,1,0:T(8,128)(2,1)S(1)}, u32[]{:S(2)}, u32[]{:S(2)}) collective-permute-start(bf16[18,32,128]{2,1,0:T(8,128)(2,1)S(1)} %get-tuple-element.25.rim_ref), channel_id=1, source_target_pairs={{1,2},{3,4},{5,6},{7,8},{9,10},{11,12},{13,14},{15,16},{17,18},{19... | collective-permute-start | bytes 442376 | tf_op jit(solution)/shard_map/ppermute | solution.py:314
  16.9 5.8 %mid.1 = (bf16[32,64,1024]{2,1,0:T(8,128)(2,1)S(1)}, bf16[8,64,1024]{2,1,0:T(8,128)(2,1)S(1)}, bf16[8,64,1024]{2,1,0:T(8,128)(2,1)}, f32[16,32,128]{2,1,0:T(8,12...) custom-call(bf16[16,32,128]{2,1,0:T(8,128)(2,1)S(1)} %get-tuple-element.19.live_ref, ...), custom_call_target="tpu_custom_call" | custom-call | tf_op jit(solution)/shard_map/mid/pallas_call | solution.py:327
  22.6 0.0 collective-permute-done.even_ref
  22.7 3.4 %collective-permute-done.1.odd_ref = bf16[18,32,128]{2,1,0:T(8,128)(2,1)S(1)} collective-permute-done((bf16[18,32,128]{2,1,0:T(8,128)(2,1)S(1)}, bf16[18,32,128]{2,1,0:T(8,128)(2,1)S(1)}, u32[]{:S(2)}, u32[]{:S(2)}) %collective-permute-start.1) | collective-permute-done | bytes 147488 | tf_op jit(solution)/shard_map/ppermute | solution.py:314
  26.1 2.2 %leaf.1 = (f32[16,32,128]{2,1,0:T(8,128)S(1)}, f32[2,32,128]{2,1,0:T(8,128)S(1)}, bf16[32,64,64]{2,1,0:T(8,128)(2,1)S(1)}, bf16[16,64,128]{2,1,0:T(8,128)(2,1)S(1)}) custom-call(s32[16,32]{1,0:T(8,128)S(1)} %get-tuple-element.24.at_vmem, bf16[18,32,128]{2,1,0:T(8,128)(2,1)S(1)} %get-tuple-element.25.rim_ref, ...), custom_call_target="tpu_custom_call" | custom-call | bytes 536870912 | tf_op jit(solution)/shard_map/leaf/pallas_call | solution.py:352
  28.3 0.0 all-to-all-done.row_ref
  28.4 3.1 %down.1 = bf16[32,2048]{1,0:T(8,128)(2,1)} custom-call(s32[16,16]{1,0:T(8,128)S(1)} %get-tuple-element.20.at_vmem, bf16[64,32,128]{2,1,0:T(8,128)(2,1)S(1)} %all-to-all-done.row_ref, bf16[8,64,1024]{2,1,0:T(8,128)(2,1)S(1)} %get-tuple-element.22.first_ref, bf16[8,64,1024]{2,1,0:T(8,128)(2,1)} %get-tuple-element.23.second_hbm, s32[32]{0:T(128)} %counts_hbm.3, ...), custom_call_target="tpu_custom_call" | custom-call | tf_op jit(solution)/shard_map/down/pallas_call | solution.py:373
Async XLA Ops:
  2.7 25.6 %all-to-all-start = ((bf16[64,32,128]{2,1,0:T(8,128)(2,1)}), bf16[64,32,128]{2,1,0:T(8,128)(2,1)S(1)}, u32[]{:S(2)}, u32[]{:S(2)}) async-start(bf16[64,32,128]{2,1,0:T(8,128)(2,1)} %copies.1), calls=%async_computation | async-start | bytes 1048576 | tf_op jit(solution)/shard_map/all_to_all | solution.py:324
  9.1 13.5 %collective-permute-start = (bf16[18,32,128]{2,1,0:T(8,128)(2,1)S(1)}, bf16[18,32,128]{2,1,0:T(8,128)(2,1)S(1)}, u32[]{:S(2)}, u32[]{:S(2)}) collective-permute-start(bf16[18,32,128]{2,1,0:T(8,128)(2,1)S(1)} %get-tuple-element.25.rim_ref), channel_id=1, source_target_pairs={{0,1},{1,0},{2,3},{3,2},{4,5},{5,4},{6,7},{7,6},{8,9},{9,8},{10,11... | collective-permute-start | bytes 442376 | tf_op jit(solution)/shard_map/ppermute | solution.py:312
  10.6 15.5 %collective-permute-start.1 = (bf16[18,32,128]{2,1,0:T(8,128)(2,1)S(1)}, bf16[18,32,128]{2,1,0:T(8,128)(2,1)S(1)}, u32[]{:S(2)}, u32[]{:S(2)}) collective-permute-start(bf16[18,32,128]{2,1,0:T(8,128)(2,1)S(1)} %get-tuple-element.25.rim_ref), channel_id=1, source_target_pairs={{1,2},{3,4},{5,6},{7,8},{9,10},{11,12},{13,14},{15,16},{17,18},{19... | collective-permute-start | bytes 442376 | tf_op jit(solution)/shard_map/ppermute | solution.py:314

commit v12 on v11

--- a/solution.py
+++ b/solution.py
@@ -320,6 +320,7 @@
         out_specs=HBM,
         scratch_shapes=[dma(n)],
         compiler_params=params(4),
+        cost_estimate=cost(512),
     )(parent_coef)
     row = lax.all_to_all(sent, "gy", 0, 0, tiled=True)
 
@@ -346,7 +347,7 @@
             dma(4 + leaves // 4 + parents // 4),
         ],
         compiler_params=params(20),
-        cost_estimate=cost(0),
+        cost_estimate=cost(16),
     )(live, *keep(leaf_coupling, near_blocks, parent_coupling, leaf_partners.T, parent_partners))
 
     far, edge, transfer_in, basis_in = pl.pallas_call(

time: 31.7 us -> 31.7 us (level)
  no operation moved by 1% of the time
where the time goes in v12:
time: 31.7 us; the launch traced here: 31.4 us
  starting transfers between devices  14.1 us (44%)
  Pallas kernels  13.8 us (44%)
  waiting for transfers between devices  3.45 us (11%)
    all_to_all x1, starting transfers between devices, per_device(): row = lax.all_to_all(sent, 'gy', 0, 0, tiled=True)  6.4 us
    ppermute x1, starting transfers between devices, per_device(): odd = lax.ppermute(rim, axes, steps + [(b, a) for a, b in steps])  6.28 us
    pallas_call x1, Pallas kernels, per_device(): pl.pallas_call(functools.partial(mid_kernel, axes), name='mid', out_shape...  5.78 us
    ppermute x1, waiting for transfers between devices, per_device(): odd = lax.ppermute(rim, axes, steps + [(b, a) for a, b in steps])  3.45 us
    pallas_call x1, Pallas kernels, per_device(): pl.pallas_call(down_kernel, name='down', out_shape=jax.ShapeDtypeStruct((...  3.06 us
    pallas_call x1, Pallas kernels, per_device(): pl.pallas_call(functools.partial(leaf_kernel, axes), name='leaf', out_sha...  2.23 us
    pallas_call x1, Pallas kernels, per_device(): pl.pallas_call(up_kernel, name='up', out_shape=[shape((pairs + 2, sides,...  1.82 us
    ppermute x1, starting transfers between devices, per_device(): even = lax.ppermute(rim, axes, [(i, i ^ 1) for i in range(total)])  1.46 us
  transfers between devices with their start and end apart: 3, of which 1 were waited for; matrix products, arithmetic and copies ran while one was open for 0% of the time, Pallas kernels for 26%

profile of v12, /device:TPU:1, one launch (start us, length us, event | category | flops | bytes accessed | tf_op | source)
XLA Modules:
  0.0 31.4 jit_solution(4235783947716624464)
XLA Ops:
  0.0 1.8 %up.1 = (bf16[18,32,128]{2,1,0:T(8,128)(2,1)S(1)}, bf16[16,32,128]{2,1,0:T(8,128)(2,1)S(1)}, bf16[8,32,128]{2,1,0:T(8,128)(2,1)S(1)}) custom-call(s32[32]{0:T(128)} %counts_hbm.3, bf16[32,2048]{1,0:T(8,128)(2,1)} %bitcast.3, bf16[32,64,64]{2,1,0:T(8,128)(2,1)} %basis_hbm.3, bf16[32,64,64]{2,1,0:T(8,128)(2,1)} %transfer_hbm.3), custom_call_target="tpu_custom_call" | custom-call | tf_op jit(solution)/shard_map/up/pallas_call | solution.py:292
  1.8 0.9 %copies.1 = bf16[64,32,128]{2,1,0:T(8,128)(2,1)} custom-call(bf16[8,32,128]{2,1,0:T(8,128)(2,1)S(1)} %get-tuple-element.21.parents_ref), custom_call_target="tpu_custom_call" | custom-call | bytes 536870912 | tf_op jit(solution)/shard_map/copies/pallas_call | solution.py:315
  2.7 6.4 %all-to-all-start = ((bf16[64,32,128]{2,1,0:T(8,128)(2,1)}), bf16[64,32,128]{2,1,0:T(8,128)(2,1)S(1)}, u32[]{:S(2)}, u32[]{:S(2)}) async-start(bf16[64,32,128]{2,1,0:T(8,128)(2,1)} %copies.1), calls=%async_computation | async-start | bytes 1048576 | tf_op jit(solution)/shard_map/all_to_all | solution.py:325
  9.1 1.5 %collective-permute-start = (bf16[18,32,128]{2,1,0:T(8,128)(2,1)S(1)}, bf16[18,32,128]{2,1,0:T(8,128)(2,1)S(1)}, u32[]{:S(2)}, u32[]{:S(2)}) collective-permute-start(bf16[18,32,128]{2,1,0:T(8,128)(2,1)S(1)} %get-tuple-element.25.rim_ref), channel_id=1, source_target_pairs={{0,1},{1,0},{2,3},{3,2},{4,5},{5,4},{6,7},{7,6},{8,9},{9,8},{10,11... | collective-permute-start | bytes 442376 | tf_op jit(solution)/shard_map/ppermute | solution.py:312
  10.6 6.3 %collective-permute-start.1 = (bf16[18,32,128]{2,1,0:T(8,128)(2,1)S(1)}, bf16[18,32,128]{2,1,0:T(8,128)(2,1)S(1)}, u32[]{:S(2)}, u32[]{:S(2)}) collective-permute-start(bf16[18,32,128]{2,1,0:T(8,128)(2,1)S(1)} %get-tuple-element.25.rim_ref), channel_id=1, source_target_pairs={{1,2},{3,4},{5,6},{7,8},{9,10},{11,12},{13,14},{15,16},{17,18},{19... | collective-permute-start | bytes 442376 | tf_op jit(solution)/shard_map/ppermute | solution.py:314
  16.9 5.8 %mid.1 = (bf16[32,64,1024]{2,1,0:T(8,128)(2,1)S(1)}, bf16[8,64,1024]{2,1,0:T(8,128)(2,1)S(1)}, bf16[8,64,1024]{2,1,0:T(8,128)(2,1)}, f32[16,32,128]{2,1,0:T(8,12...) custom-call(bf16[16,32,128]{2,1,0:T(8,128)(2,1)S(1)} %get-tuple-element.19.live_ref, ...), custom_call_target="tpu_custom_call" | custom-call | bytes 16777216 | tf_op jit(solution)/shard_map/mid/pallas_call | solution.py:328
  22.6 0.0 collective-permute-done.even_ref
  22.7 3.4 %collective-permute-done.1.odd_ref = bf16[18,32,128]{2,1,0:T(8,128)(2,1)S(1)} collective-permute-done((bf16[18,32,128]{2,1,0:T(8,128)(2,1)S(1)}, bf16[18,32,128]{2,1,0:T(8,128)(2,1)S(1)}, u32[]{:S(2)}, u32[]{:S(2)}) %collective-permute-start.1) | collective-permute-done | bytes 147488 | tf_op jit(solution)/shard_map/ppermute | solution.py:314
  26.1 2.2 %leaf.1 = (f32[16,32,128]{2,1,0:T(8,128)S(1)}, f32[2,32,128]{2,1,0:T(8,128)S(1)}, bf16[32,64,64]{2,1,0:T(8,128)(2,1)S(1)}, bf16[16,64,128]{2,1,0:T(8,128)(2,1)S(1)}) custom-call(s32[16,32]{1,0:T(8,128)S(1)} %get-tuple-element.24.at_vmem, bf16[18,32,128]{2,1,0:T(8,128)(2,1)S(1)} %get-tuple-element.25.rim_ref, ...), custom_call_target="tpu_custom_call" | custom-call | bytes 536870912 | tf_op jit(solution)/shard_map/leaf/pallas_call | solution.py:353
  28.3 0.0 all-to-all-done.row_ref
  28.4 3.1 %down.1 = bf16[32,2048]{1,0:T(8,128)(2,1)} custom-call(s32[16,16]{1,0:T(8,128)S(1)} %get-tuple-element.20.at_vmem, bf16[64,32,128]{2,1,0:T(8,128)(2,1)S(1)} %all-to-all-done.row_ref, bf16[8,64,1024]{2,1,0:T(8,128)(2,1)S(1)} %get-tuple-element.22.first_ref, bf16[8,64,1024]{2,1,0:T(8,128)(2,1)} %get-tuple-element.23.second_hbm, s32[32]{0:T(128)} %counts_hbm.3, ...), custom_call_target="tpu_custom_call" | custom-call | tf_op jit(solution)/shard_map/down/pallas_call | solution.py:374
Async XLA Ops:
  2.7 25.6 %all-to-all-start = ((bf16[64,32,128]{2,1,0:T(8,128)(2,1)}), bf16[64,32,128]{2,1,0:T(8,128)(2,1)S(1)}, u32[]{:S(2)}, u32[]{:S(2)}) async-start(bf16[64,32,128]{2,1,0:T(8,128)(2,1)} %copies.1), calls=%async_computation | async-start | bytes 1048576 | tf_op jit(solution)/shard_map/all_to_all | solution.py:325
  9.1 13.5 %collective-permute-start = (bf16[18,32,128]{2,1,0:T(8,128)(2,1)S(1)}, bf16[18,32,128]{2,1,0:T(8,128)(2,1)S(1)}, u32[]{:S(2)}, u32[]{:S(2)}) collective-permute-start(bf16[18,32,128]{2,1,0:T(8,128)(2,1)S(1)} %get-tuple-element.25.rim_ref), channel_id=1, source_target_pairs={{0,1},{1,0},{2,3},{3,2},{4,5},{5,4},{6,7},{7,6},{8,9},{9,8},{10,11... | collective-permute-start | bytes 442376 | tf_op jit(solution)/shard_map/ppermute | solution.py:312
  10.6 15.5 %collective-permute-start.1 = (bf16[18,32,128]{2,1,0:T(8,128)(2,1)S(1)}, bf16[18,32,128]{2,1,0:T(8,128)(2,1)S(1)}, u32[]{:S(2)}, u32[]{:S(2)}) collective-permute-start(bf16[18,32,128]{2,1,0:T(8,128)(2,1)S(1)} %get-tuple-element.25.rim_ref), channel_id=1, source_target_pairs={{1,2},{3,4},{5,6},{7,8},{9,10},{11,12},{13,14},{15,16},{17,18},{19... | collective-permute-start | bytes 442376 | tf_op jit(solution)/shard_map/ppermute | solution.py:314

commit v13 on v9

--- a/solution.py
+++ b/solution.py
@@ -287,7 +287,7 @@
     shape = pltpu.VMEM
     dma = lambda count: pltpu.SemaphoreType.DMA((count,))
     params = lambda mib: pltpu.CompilerParams(vmem_limit_bytes=mib * 2**20)
-    cost = lambda mib: pl.CostEstimate(flops=0, transcendentals=0, bytes_accessed=mib * 2**20)
+    cost = lambda kib: pl.CostEstimate(flops=kib * 2**10, transcendentals=0, bytes_accessed=kib * 2**10)
 
     rim, live, parent_coef = pl.pallas_call(
         up_kernel,
@@ -320,6 +320,7 @@
         out_specs=HBM,
         scratch_shapes=[dma(n)],
         compiler_params=params(4),
+        cost_estimate=cost(16),
     )(parent_coef)
     row = lax.all_to_all(sent, "gy", 0, 0, tiled=True)
 
@@ -367,7 +368,7 @@
             dma(3),
         ],
         compiler_params=params(8),
-        cost_estimate=cost(64),
+        cost_estimate=cost(512 * 1024),
     )(leaf_at, rim, even, odd, packed, rim_near, *keep(transfer, basis))
 
     out = pl.pallas_call(

time: 31.7 us -> 31.7 us (level)
  no operation moved by 1% of the time
where the time goes in v13:
time: 31.7 us; the launch traced here: 31.4 us
  starting transfers between devices  14.1 us (44%)
  Pallas kernels  13.8 us (44%)
  waiting for transfers between devices  3.45 us (11%)
    all_to_all x1, starting transfers between devices, per_device(): row = lax.all_to_all(sent, 'gy', 0, 0, tiled=True)  6.4 us
    ppermute x1, starting transfers between devices, per_device(): odd = lax.ppermute(rim, axes, steps + [(b, a) for a, b in steps])  6.28 us
    pallas_call x1, Pallas kernels, per_device(): pl.pallas_call(functools.partial(mid_kernel, axes), name='mid', out_shape...  5.78 us
    ppermute x1, waiting for transfers between devices, per_device(): odd = lax.ppermute(rim, axes, steps + [(b, a) for a, b in steps])  3.45 us
    pallas_call x1, Pallas kernels, per_device(): pl.pallas_call(down_kernel, name='down', out_shape=jax.ShapeDtypeStruct((...  3.06 us
    pallas_call x1, Pallas kernels, per_device(): pl.pallas_call(functools.partial(leaf_kernel, axes), name='leaf', out_sha...  2.23 us
    pallas_call x1, Pallas kernels, per_device(): pl.pallas_call(up_kernel, name='up', out_shape=[shape((pairs + 2, sides,...  1.82 us
    ppermute x1, starting transfers between devices, per_device(): even = lax.ppermute(rim, axes, [(i, i ^ 1) for i in range(total)])  1.46 us
  transfers between devices with their start and end apart: 3, of which 1 were waited for; matrix products, arithmetic and copies ran while one was open for 0% of the time, Pallas kernels for 26%

profile of v13, /device:TPU:1, one launch (start us, length us, event | category | flops | bytes accessed | tf_op | source)
XLA Modules:
  0.0 31.4 jit_solution(4235783947716624464)
XLA Ops:
  0.0 1.8 %up.1 = (bf16[18,32,128]{2,1,0:T(8,128)(2,1)S(1)}, bf16[16,32,128]{2,1,0:T(8,128)(2,1)S(1)}, bf16[8,32,128]{2,1,0:T(8,128)(2,1)S(1)}) custom-call(s32[32]{0:T(128)} %counts_hbm.3, bf16[32,2048]{1,0:T(8,128)(2,1)} %bitcast.3, bf16[32,64,64]{2,1,0:T(8,128)(2,1)} %basis_hbm.3, bf16[32,64,64]{2,1,0:T(8,128)(2,1)} %transfer_hbm.3), custom_call_target="tpu_custom_call" | custom-call | tf_op jit(solution)/shard_map/up/pallas_call | solution.py:292
  1.8 0.9 %copies.1 = bf16[64,32,128]{2,1,0:T(8,128)(2,1)} custom-call(bf16[8,32,128]{2,1,0:T(8,128)(2,1)S(1)} %get-tuple-element.21.parents_ref), custom_call_target="tpu_custom_call" | custom-call | flops 16384 | bytes 16384 | tf_op jit(solution)/shard_map/copies/pallas_call | solution.py:315
  2.7 6.4 %all-to-all-start = ((bf16[64,32,128]{2,1,0:T(8,128)(2,1)}), bf16[64,32,128]{2,1,0:T(8,128)(2,1)S(1)}, u32[]{:S(2)}, u32[]{:S(2)}) async-start(bf16[64,32,128]{2,1,0:T(8,128)(2,1)} %copies.1), calls=%async_computation | async-start | bytes 1048576 | tf_op jit(solution)/shard_map/all_to_all | solution.py:325
  9.1 1.5 %collective-permute-start = (bf16[18,32,128]{2,1,0:T(8,128)(2,1)S(1)}, bf16[18,32,128]{2,1,0:T(8,128)(2,1)S(1)}, u32[]{:S(2)}, u32[]{:S(2)}) collective-permute-start(bf16[18,32,128]{2,1,0:T(8,128)(2,1)S(1)} %get-tuple-element.25.rim_ref), channel_id=1, source_target_pairs={{0,1},{1,0},{2,3},{3,2},{4,5},{5,4},{6,7},{7,6},{8,9},{9,8},{10,11... | collective-permute-start | bytes 442376 | tf_op jit(solution)/shard_map/ppermute | solution.py:312
  10.6 6.3 %collective-permute-start.1 = (bf16[18,32,128]{2,1,0:T(8,128)(2,1)S(1)}, bf16[18,32,128]{2,1,0:T(8,128)(2,1)S(1)}, u32[]{:S(2)}, u32[]{:S(2)}) collective-permute-start(bf16[18,32,128]{2,1,0:T(8,128)(2,1)S(1)} %get-tuple-element.25.rim_ref), channel_id=1, source_target_pairs={{1,2},{3,4},{5,6},{7,8},{9,10},{11,12},{13,14},{15,16},{17,18},{19... | collective-permute-start | bytes 442376 | tf_op jit(solution)/shard_map/ppermute | solution.py:314
  16.9 5.8 %mid.1 = (bf16[32,64,1024]{2,1,0:T(8,128)(2,1)S(1)}, bf16[8,64,1024]{2,1,0:T(8,128)(2,1)S(1)}, bf16[8,64,1024]{2,1,0:T(8,128)(2,1)}, f32[16,32,128]{2,1,0:T(8,12...) custom-call(bf16[16,32,128]{2,1,0:T(8,128)(2,1)S(1)} %get-tuple-element.19.live_ref, ...), custom_call_target="tpu_custom_call" | custom-call | flops 16384 | bytes 16384 | tf_op jit(solution)/shard_map/mid/pallas_call | solution.py:328
  22.6 0.0 collective-permute-done.even_ref
  22.7 3.4 %collective-permute-done.1.odd_ref = bf16[18,32,128]{2,1,0:T(8,128)(2,1)S(1)} collective-permute-done((bf16[18,32,128]{2,1,0:T(8,128)(2,1)S(1)}, bf16[18,32,128]{2,1,0:T(8,128)(2,1)S(1)}, u32[]{:S(2)}, u32[]{:S(2)}) %collective-permute-start.1) | collective-permute-done | bytes 147488 | tf_op jit(solution)/shard_map/ppermute | solution.py:314
  26.1 2.2 %leaf.1 = (f32[16,32,128]{2,1,0:T(8,128)S(1)}, f32[2,32,128]{2,1,0:T(8,128)S(1)}, bf16[32,64,64]{2,1,0:T(8,128)(2,1)S(1)}, bf16[16,64,128]{2,1,0:T(8,128)(2,1)S(1)}) custom-call(s32[16,32]{1,0:T(8,128)S(1)} %get-tuple-element.24.at_vmem, bf16[18,32,128]{2,1,0:T(8,128)(2,1)S(1)} %get-tuple-element.25.rim_ref, ...), custom_call_target="tpu_custom_call" | custom-call | flops 536870912 | bytes 536870912 | tf_op jit(solution)/shard_map/leaf/pallas_call | solution.py:353
  28.3 0.0 all-to-all-done.row_ref
  28.4 3.1 %down.1 = bf16[32,2048]{1,0:T(8,128)(2,1)} custom-call(s32[16,16]{1,0:T(8,128)S(1)} %get-tuple-element.20.at_vmem, bf16[64,32,128]{2,1,0:T(8,128)(2,1)S(1)} %all-to-all-done.row_ref, bf16[8,64,1024]{2,1,0:T(8,128)(2,1)S(1)} %get-tuple-element.22.first_ref, bf16[8,64,1024]{2,1,0:T(8,128)(2,1)} %get-tuple-element.23.second_hbm, s32[32]{0:T(128)} %counts_hbm.3, ...), custom_call_target="tpu_custom_call" | custom-call | tf_op jit(solution)/shard_map/down/pallas_call | solution.py:374
Async XLA Ops:
  2.7 25.6 %all-to-all-start = ((bf16[64,32,128]{2,1,0:T(8,128)(2,1)}), bf16[64,32,128]{2,1,0:T(8,128)(2,1)S(1)}, u32[]{:S(2)}, u32[]{:S(2)}) async-start(bf16[64,32,128]{2,1,0:T(8,128)(2,1)} %copies.1), calls=%async_computation | async-start | bytes 1048576 | tf_op jit(solution)/shard_map/all_to_all | solution.py:325
  9.1 13.5 %collective-permute-start = (bf16[18,32,128]{2,1,0:T(8,128)(2,1)S(1)}, bf16[18,32,128]{2,1,0:T(8,128)(2,1)S(1)}, u32[]{:S(2)}, u32[]{:S(2)}) collective-permute-start(bf16[18,32,128]{2,1,0:T(8,128)(2,1)S(1)} %get-tuple-element.25.rim_ref), channel_id=1, source_target_pairs={{0,1},{1,0},{2,3},{3,2},{4,5},{5,4},{6,7},{7,6},{8,9},{9,8},{10,11... | collective-permute-start | bytes 442376 | tf_op jit(solution)/shard_map/ppermute | solution.py:312
  10.6 15.5 %collective-permute-start.1 = (bf16[18,32,128]{2,1,0:T(8,128)(2,1)S(1)}, bf16[18,32,128]{2,1,0:T(8,128)(2,1)S(1)}, u32[]{:S(2)}, u32[]{:S(2)}) collective-permute-start(bf16[18,32,128]{2,1,0:T(8,128)(2,1)S(1)} %get-tuple-element.25.rim_ref), channel_id=1, source_target_pairs={{1,2},{3,4},{5,6},{7,8},{9,10},{11,12},{13,14},{15,16},{17,18},{19... | collective-permute-start | bytes 442376 | tf_op jit(solution)/shard_map/ppermute | solution.py:314

commit v14 on v11

--- a/solution.py
+++ b/solution.py
@@ -34,6 +34,10 @@
 
 def mod(x, m):
     return x & (m - 1) if m & (m - 1) == 0 else lax.rem(x, m)
+
+
+def div(x, m):
+    return x >> (m.bit_length() - 1) if m & (m - 1) == 0 else x // m
 
 
 def position(axes):
@@ -105,8 +109,8 @@
 
 def mid_kernel(
     axes, live_ref, coupling_hbm, near_hbm, parent_hbm, leaf_partners_hbm, parent_partners_hbm,
-    packed_ref, first_ref, second_hbm, near_out_ref, rim_near_ref, leaf_at_ref, parent_at_ref,
-    coupling_ref, near_ref, parent_ref, second_ref, sems,
+    packed_ref, parent_packed_ref, near_out_ref, rim_near_ref, leaf_at_ref, parent_at_ref,
+    coupling_ref, near_ref, parent_ref, sems,
 ):
     leaves, many, rank, _ = coupling_ref.shape
     parents = parent_ref.shape[0]
@@ -114,13 +118,13 @@
     pairs = leaves // 2
     started = start_all(
         [(near_hbm, near_ref)]
-        + [(parent_hbm.at[pl.ds(4 * i, 4)], parent_ref.at[pl.ds(4 * i, 4)]) for i in reversed(range(parents // 4))]
+        + [(parent_hbm.at[pl.ds(4 * i, 4)], parent_ref.at[pl.ds(4 * i, 4)]) for i in range(parents // 4)]
         + [(coupling_hbm.at[pl.ds(4 * i, 4)], coupling_ref.at[pl.ds(4 * i, 4)]) for i in range(leaves // 4)]
         + [(leaf_partners_hbm, leaf_at_ref), (parent_partners_hbm, parent_at_ref)],
         sems,
     )
     near_in = started[0]
-    parent_in = started[1 : 1 + parents // 4][::-1]
+    parent_in = started[1 : 1 + parents // 4]
     coupling_in = started[1 + parents // 4 : -2]
     near_in.wait()
     rim_near_ref[0] = near_ref[0, 0]
@@ -135,33 +139,34 @@
             odd = odd + dot(live_ref[a + 1][:, :width], near_ref[2 * a + 1, 2], NT)
         near_out_ref[a] = jnp.concatenate([even, odd], axis=1)
 
-    def pack(src, dst, g, to):
+    def pack(src, dst, g):
         for j in range(0, many, 2):
-            dst[to, :, rank * j : rank * (j + 2)] = jnp.concatenate([src[g, j], src[g, j + 1]], axis=1)
-
-    half = first_ref.shape[0]
-    for i, copy in reversed(list(enumerate(parent_in))):
+            dst[g, :, rank * j : rank * (j + 2)] = jnp.concatenate([src[g, j], src[g, j + 1]], axis=1)
+
+    for i, copy in enumerate(parent_in):
         copy.wait()
         for q in range(4 * i, 4 * i + 4):
-            if q < half:
-                pack(parent_ref, first_ref, q, q)
-            else:
-                pack(parent_ref, second_ref, q, q - half)
-        if 4 * i == half:
-            out = pltpu.make_async_copy(second_ref, second_hbm, sems.at[len(started)])
-            out.start()
+            pack(parent_ref, parent_packed_ref, q)
     for i, copy in enumerate(coupling_in):
         copy.wait()
         for g in range(4 * i, 4 * i + 4):
-            pack(coupling_ref, packed_ref, g, g)
+            pack(coupling_ref, packed_ref, g)
     for copy in started[-2:]:
         copy.wait()
-    out.wait()
     wanted = leaf_at_ref[...] + (1 - position(axes)) * leaves
     leaf_at_ref[...] = wanted ^ (lax.broadcasted_iota(jnp.int32, wanted.shape, 0) & 1)
-    n = lax.axis_size(axes[1])
-    wanted = mod(parent_at_ref[...], n * parents)
+    inner = lax.axis_size(axes[2])
+    outer = lax.axis_size(axes[1])
+    wanted = mod(parent_at_ref[...], outer * inner * parents)
+    source = div(wanted, parents)
+    wanted = (mod(source, inner) * outer + div(source, inner)) * parents + mod(wanted, parents)
     parent_at_ref[...] = wanted ^ (lax.broadcasted_iota(jnp.int32, wanted.shape, 1) & 1)
+
+
+def halves_kernel(whole_ref, first_ref, second_ref):
+    half = first_ref.shape[0]
+    first_ref[...] = whole_ref[:half]
+    second_ref[...] = whole_ref[half:]
 
 
 def spread_pair(table_ref, at, pair, width):
@@ -218,32 +223,31 @@
 
 
 def down_kernel(
-    at_vmem, row_ref, first_ref, second_hbm, counts_hbm,
+    axis, at_vmem, same_ref, other_refs, packed_ref, counts_hbm,
     far_ref, near_ref, edge_ref, transfer_ref, basis_ref,
-    out_ref, table_ref, at_ref, local_ref, down_ref, second_ref, counts_ref, sems,
+    out_ref, table_ref, at_ref, local_ref, down_ref, counts_ref, sems,
 ):
-    at_in, second_in, counts_in = start_all(
-        [(at_vmem, at_ref), (second_hbm, second_ref), (counts_hbm, counts_ref)], sems
-    )
+    at_in, counts_in = start_all([(at_vmem, at_ref), (counts_hbm, counts_ref)], sems)
     parents, many = at_ref.shape
-    rank = first_ref.shape[1]
-    half = first_ref.shape[0]
+    rank = packed_ref.shape[1]
     width = basis_ref.shape[1]
-    sides = row_ref.shape[1]
+    sides = same_ref.shape[1]
+    half = 2 * same_ref.shape[0]
     left = left_half(sides, rank)
+    parity = lax.axis_index(axis)
+    quarter = other_refs[0].shape[0]
 
     def spread(a, carry):
-        spread_pair(table_ref, 2 * a, row_ref[a], rank)
+        for b, ref in enumerate(other_refs):
+            spread_pair(table_ref, half * (1 - parity) + 2 * (quarter * b + a), ref[a], rank)
+            spread_pair(table_ref, half * parity + 2 * (quarter * b + a), same_ref[quarter * b + a], rank)
         return carry
 
-    lax.fori_loop(0, row_ref.shape[0], spread, 0, unroll=min(64, row_ref.shape[0]))
+    lax.fori_loop(0, quarter, spread, 0, unroll=min(16, quarter))
     at_in.wait()
     for q in range(parents):
-        if q == half:
-            second_in.wait()
         rows = [at_ref[q, j] for j in range(many)]
-        packed = first_ref[q] if q < half else second_ref[q - half]
-        far = dot(picked(table_ref, rows, left), packed, NT)
+        far = dot(picked(table_ref, rows, left), packed_ref[q], NT)
         down_ref[q] = far.astype(jnp.bfloat16)
     for q in range(parents):
         local = far_ref[q] + dot(down_ref[q], transfer_ref[2 * q : 2 * q + 2].reshape(2 * rank, rank), NT)
@@ -279,15 +283,14 @@
     parents, many = parent_partners.shape
     pairs = leaves // 2
     own = pairs // 2
-    axes = ("gx", "gy")
-    n = lax.axis_size("gy")
+    axes = ("gx", "gz", "gp")
+    n = lax.axis_size("gz") * lax.axis_size("gp")
     total = n * lax.axis_size("gx")
     bf16, f32 = jnp.bfloat16, jnp.float32
     keep = lambda *arrays: [pltpu.with_memory_space_constraint(a, pltpu.HBM) for a in arrays]
     shape = pltpu.VMEM
     dma = lambda count: pltpu.SemaphoreType.DMA((count,))
     params = lambda mib: pltpu.CompilerParams(vmem_limit_bytes=mib * 2**20)
-    cost = lambda mib: pl.CostEstimate(flops=0, transcendentals=0, bytes_accessed=mib * 2**20)
 
     rim, live, parent_coef = pl.pallas_call(
         up_kernel,
@@ -315,38 +318,44 @@
     sent = pl.pallas_call(
         copies_kernel,
         name="copies",
-        out_shape=pltpu.HBM((n * own, sides, 2 * rank), bf16),
+        out_shape=pltpu.HBM((n // 2 * own, sides, 2 * rank), bf16),
         in_specs=[VMEM],
         out_specs=HBM,
-        scratch_shapes=[dma(n)],
+        scratch_shapes=[dma(n // 2)],
         compiler_params=params(4),
     )(parent_coef)
-    row = lax.all_to_all(sent, "gy", 0, 0, tiled=True)
-
-    held = parents // 8 * 4
-    packed, first, second, near, rim_near, leaf_at, parent_at = pl.pallas_call(
+    same = lax.all_to_all(sent, "gz", 0, 0, tiled=True)
+    quarter = shape((n // 4 * own, sides, 2 * rank), bf16)
+    pieces = pl.pallas_call(
+        halves_kernel,
+        name="halves",
+        out_shape=[quarter, quarter],
+        in_specs=[VMEM],
+        out_specs=[VMEM, VMEM],
+        compiler_params=params(4),
+    )(same)
+    other = [lax.ppermute(piece, "gp", [(0, 1), (1, 0)]) for piece in pieces]
+
+    packed, parent_packed, near, rim_near, leaf_at, parent_at = pl.pallas_call(
         functools.partial(mid_kernel, axes),
         name="mid",
         out_shape=[
             shape((leaves, rank, many * rank), bf16),
-            shape((held, rank, many * rank), bf16),
-            pltpu.HBM((parents - held, rank, many * rank), bf16),
+            shape((parents, rank, many * rank), bf16),
             shape((pairs, sides, 2 * width), f32),
             shape((2, width, width), bf16),
             shape((many, leaves), jnp.int32),
             shape((parents, many), jnp.int32),
         ],
         in_specs=[VMEM] + [HBM] * 5,
-        out_specs=[VMEM] * 2 + [HBM] + [VMEM] * 4,
+        out_specs=[VMEM] * 6,
         scratch_shapes=[
             pltpu.VMEM(leaf_coupling.shape, bf16),
             pltpu.VMEM(near_blocks.shape, bf16),
             pltpu.VMEM(parent_coupling.shape, bf16),
-            pltpu.VMEM((parents - held, rank, many * rank), bf16),
-            dma(4 + leaves // 4 + parents // 4),
+            dma(3 + leaves // 4 + parents // 4),
         ],
         compiler_params=params(20),
-        cost_estimate=cost(0),
     )(live, *keep(leaf_coupling, near_blocks, parent_coupling, leaf_partners.T, parent_partners))
 
     far, edge, transfer_in, basis_in = pl.pallas_call(
@@ -367,31 +376,31 @@
             dma(3),
         ],
         compiler_params=params(8),
-        cost_estimate=cost(512),
     )(leaf_at, rim, even, odd, packed, rim_near, *keep(transfer, basis))
 
     out = pl.pallas_call(
-        down_kernel,
+        functools.partial(down_kernel, "gp"),
         name="down",
         out_shape=jax.ShapeDtypeStruct((sides, leaves * width), bf16),
-        in_specs=[VMEM] * 3 + [HBM] * 2 + [VMEM] * 5,
+        in_specs=[VMEM, VMEM, [VMEM] * 2, VMEM, HBM] + [VMEM] * 5,
         out_specs=VMEM,
         scratch_shapes=[
             pltpu.VMEM((n * parents, sides, 2 * rank), bf16),
             pltpu.SMEM((parents, many), jnp.int32),
             pltpu.VMEM((pairs, sides, 2 * rank), bf16),
             pltpu.VMEM((parents, sides, rank), bf16),
-            pltpu.VMEM((parents - held, rank, many * rank), bf16),
             pltpu.SMEM((leaves,), jnp.int32),
-            dma(3),
+            dma(2),
         ],
         compiler_params=params(12),
-    )(parent_at, row, first, *keep(second, panel_counts), far, near, edge, transfer_in, basis_in)
+    )(parent_at, same, other, parent_packed, *keep(panel_counts), far, near, edge, transfer_in, basis_in)
     return out.T
 
 
 def solution(mesh):
-    leaves = ("gx", "gy")
+    outer, inner = mesh.devices.shape
+    split = jax.sharding.Mesh(mesh.devices.reshape(outer, inner // 2, 2), ("gx", "gz", "gp"))
+    leaves = ("gx", "gz", "gp")
     in_specs = (
         P(leaves, None),
         P(leaves),
@@ -404,5 +413,5 @@
         P(leaves, None),
     )
     return jax.shard_map(
-        per_device, mesh=mesh, in_specs=in_specs, out_specs=P(leaves, None), check_vma=False
-    )
+        per_device, mesh=split, in_specs=in_specs, out_specs=P(leaves, None), check_vma=False
+    )

time: 31.7 us -> 33.3 us (1.050)
  the two profiles are of different devices: /device:TPU:1 before, /device:TPU:0 now
where the time goes in v14:
time: 33.3 us; the launch traced here: 33.1 us
  Pallas kernels  13 us (39%)
  starting transfers between devices  12.3 us (37%)
  waiting for transfers between devices  7.79 us (23%)
    all_to_all x1, waiting for transfers between devices, per_device(): same = lax.all_to_all(sent, 'gz', 0, 0, tiled=True)  7.78 us
    all_to_all x1, starting transfers between devices, per_device(): same = lax.all_to_all(sent, 'gz', 0, 0, tiled=True)  6.33 us
    pallas_call x1, Pallas kernels, per_device(): pl.pallas_call(functools.partial(mid_kernel, axes), name='mid', out_shape...  5.39 us
    ppermute x2, starting transfers between devices, per_device(): other = [lax.ppermute(piece, 'gp', [(0, 1), (1, 0)]) for piece in pieces]  3.77 us
    pallas_call x1, Pallas kernels, per_device(): pl.pallas_call(functools.partial(down_kernel, 'gp'), name='down', out_sha...  2.75 us
    pallas_call x1, Pallas kernels, per_device(): pl.pallas_call(functools.partial(leaf_kernel, axes), name='leaf', out_sha...  2.25 us
    pallas_call x1, Pallas kernels, per_device(): pl.pallas_call(up_kernel, name='up', out_shape=[shape((pairs + 2, sides,...  1.82 us
    ppermute x1, starting transfers between devices, per_device(): even = lax.ppermute(rim, axes, [(i, i ^ 1) for i in range(total)])  1.52 us
  transfers between devices with their start and end apart: 5, of which 1 were waited for; matrix products, arithmetic and copies ran while one was open for 0% of the time, Pallas kernels for 23%

profile of v14, /device:TPU:0, one launch (start us, length us, event | category | flops | bytes accessed | tf_op | source)
XLA Modules:
  0.0 33.1 jit_solution(609012121170420375)
XLA Ops:
  0.0 1.8 %up.1 = (bf16[18,32,128]{2,1,0:T(8,128)(2,1)S(1)}, bf16[16,32,128]{2,1,0:T(8,128)(2,1)S(1)}, bf16[8,32,128]{2,1,0:T(8,128)(2,1)S(1)}) custom-call(s32[32]{0:T(128)} %counts_hbm.3, bf16[32,2048]{1,0:T(8,128)(2,1)} %bitcast.3, bf16[32,64,64]{2,1,0:T(8,128)(2,1)} %basis_hbm.3, bf16[32,64,64]{2,1,0:T(8,128)(2,1)} %transfer_hbm.3), custom_call_target="tpu_custom_call" | custom-call | tf_op jit(solution)/shard_map/up/pallas_call | solution.py:295
  1.8 0.7 %copies.1 = bf16[32,32,128]{2,1,0:T(8,128)(2,1)} custom-call(bf16[8,32,128]{2,1,0:T(8,128)(2,1)S(1)} %get-tuple-element.22.parents_ref), custom_call_target="tpu_custom_call" | custom-call | tf_op jit(solution)/shard_map/copies/pallas_call | solution.py:318
  2.6 6.3 %all-to-all-start = ((bf16[32,32,128]{2,1,0:T(8,128)(2,1)}), bf16[32,32,128]{2,1,0:T(8,128)(2,1)S(1)}, u32[]{:S(2)}, u32[]{:S(2)}) async-start(bf16[32,32,128]{2,1,0:T(8,128)(2,1)} %copies.1), calls=%async_computation | async-start | bytes 524288 | tf_op jit(solution)/shard_map/all_to_all | solution.py:327
  8.9 1.5 %collective-permute-start.2 = (bf16[18,32,128]{2,1,0:T(8,128)(2,1)S(1)}, bf16[18,32,128]{2,1,0:T(8,128)(2,1)S(1)}, u32[]{:S(2)}, u32[]{:S(2)}) collective-permute-start(bf16[18,32,128]{2,1,0:T(8,128)(2,1)S(1)} %get-tuple-element.27.rim_ref), channel_id=1, source_target_pairs={{0,1},{1,0},{2,3},{3,2},{4,5},{5,4},{6,7},{7,6},{8,9},{9,8},{10,11... | collective-permute-start | bytes 442376 | tf_op jit(solution)/shard_map/ppermute | solution.py:315
  10.4 0.7 %collective-permute-start.3 = (bf16[18,32,128]{2,1,0:T(8,128)(2,1)S(1)}, bf16[18,32,128]{2,1,0:T(8,128)(2,1)S(1)}, u32[]{:S(2)}, u32[]{:S(2)}) collective-permute-start(bf16[18,32,128]{2,1,0:T(8,128)(2,1)S(1)} %get-tuple-element.27.rim_ref), channel_id=1, source_target_pairs={{1,2},{3,4},{5,6},{7,8},{9,10},{11,12},{13,14},{15,16},{17,18},{19... | collective-permute-start | bytes 442376 | tf_op jit(solution)/shard_map/ppermute | solution.py:317
  11.1 7.8 %all-to-all-done.whole_ref.same_ref = bf16[32,32,128]{2,1,0:T(8,128)(2,1)S(1)} async-done(((bf16[32,32,128]{2,1,0:T(8,128)(2,1)}), bf16[32,32,128]{2,1,0:T(8,128)(2,1)S(1)}, u32[]{:S(2)}, u32[]{:S(2)}) %all-to-all-start) | async-done | bytes 262176 | tf_op jit(solution)/shard_map/all_to_all | solution.py:327
  18.9 3.7 %collective-permute-start = (bf16[16,32,128]{2,1,0:T(8,128)(2,1)S(1)}, bf16[16,32,128]{2,1,0:T(8,128)(2,1)S(1)}, u32[]{:S(2)}, u32[]{:S(2)}) collective-permute-start(bf16[16,32,128]{2,1,0:T(8,128)(2,1)S(1)} %get-tuple-element.23), channel_id=1, source_target_pairs={{0,1},{1,0},{2,3},{3,2},{4,5},{5,4},{6,7},{7,6},{8,9},{9,8},{10,11... | collective-permute-start | bytes 393224 | tf_op jit(solution)/shard_map/ppermute | solution.py:337
  22.6 0.1 collective-permute-start.1
  22.7 5.4 %mid.1 = (bf16[32,64,1024]{2,1,0:T(8,128)(2,1)S(1)}, bf16[16,64,1024]{2,1,0:T(8,128)(2,1)S(1)}, f32[16,32,128]{2,1,0:T(8,128)S(1)}, bf16[2,64,64]{2,1,0:T(8,128)...) custom-call(bf16[16,32,128]{2,1,0:T(8,128)(2,1)S(1)} %get-tuple-element.20.live_ref, ...), custom_call_target="tpu_custom_call" | custom-call | tf_op jit(solution)/shard_map/mid/pallas_call | solution.py:339
  28.1 0.0 collective-permute-done.2.even_ref
  28.1 0.0 collective-permute-done.3.odd_ref
  28.1 2.2 %leaf.1 = (f32[16,32,128]{2,1,0:T(8,128)S(1)}, f32[2,32,128]{2,1,0:T(8,128)S(1)}, bf16[32,64,64]{2,1,0:T(8,128)(2,1)S(1)}, bf16[16,64,128]{2,1,0:T(8,128)(2,1)S(1)}) custom-call(s32[16,32]{1,0:T(8,128)S(1)} %get-tuple-element.26.at_vmem, bf16[18,32,128]{2,1,0:T(8,128)(2,1)S(1)} %get-tuple-element.27.rim_ref, ...), custom_call_target="tpu_custom_call" | custom-call | tf_op jit(solution)/shard_map/leaf/pallas_call | solution.py:361
  30.3 0.0 collective-permute-done.other_refs_0_
  30.3 0.0 collective-permute-done.1.other_refs_1_
  30.4 2.8 %down.1 = bf16[32,2048]{1,0:T(8,128)(2,1)} custom-call(s32[16,16]{1,0:T(8,128)S(1)} %get-tuple-element.21.at_vmem, bf16[32,32,128]{2,1,0:T(8,128)(2,1)S(1)} %all-to-all-done.whole_ref.same_ref, bf16[16,32,128]{2,1,0:T(8,128)(2,1)S(1)} %collective-permute-done.other_refs_0_, bf16[16,32,128]{2,1,0:T(8,128)(2,1)S(1)} %collective-permute-done.1.other_refs_1_, ...), custom_call_target="tpu_custom_call" | custom-call | tf_op jit(solution)/shard_map/down/pallas_call | solution.py:381
  (1 shorter events, 0.0 us)
Async XLA Ops:
  2.6 16.3 %all-to-all-start = ((bf16[32,32,128]{2,1,0:T(8,128)(2,1)}), bf16[32,32,128]{2,1,0:T(8,128)(2,1)S(1)}, u32[]{:S(2)}, u32[]{:S(2)}) async-start(bf16[32,32,128]{2,1,0:T(8,128)(2,1)} %copies.1), calls=%async_computation | async-start | bytes 524288 | tf_op jit(solution)/shard_map/all_to_all | solution.py:327
  8.9 19.2 %collective-permute-start.2 = (bf16[18,32,128]{2,1,0:T(8,128)(2,1)S(1)}, bf16[18,32,128]{2,1,0:T(8,128)(2,1)S(1)}, u32[]{:S(2)}, u32[]{:S(2)}) collective-permute-start(bf16[18,32,128]{2,1,0:T(8,128)(2,1)S(1)} %get-tuple-element.27.rim_ref), channel_id=1, source_target_pairs={{0,1},{1,0},{2,3},{3,2},{4,5},{5,4},{6,7},{7,6},{8,9},{9,8},{10,11... | collective-permute-start | bytes 442376 | tf_op jit(solution)/shard_map/ppermute | solution.py:315
  10.4 17.6 %collective-permute-start.3 = (bf16[18,32,128]{2,1,0:T(8,128)(2,1)S(1)}, bf16[18,32,128]{2,1,0:T(8,128)(2,1)S(1)}, u32[]{:S(2)}, u32[]{:S(2)}) collective-permute-start(bf16[18,32,128]{2,1,0:T(8,128)(2,1)S(1)} %get-tuple-element.27.rim_ref), channel_id=1, source_target_pairs={{1,2},{3,4},{5,6},{7,8},{9,10},{11,12},{13,14},{15,16},{17,18},{19... | collective-permute-start | bytes 442376 | tf_op jit(solution)/shard_map/ppermute | solution.py:317
  18.9 11.4 %collective-permute-start = (bf16[16,32,128]{2,1,0:T(8,128)(2,1)S(1)}, bf16[16,32,128]{2,1,0:T(8,128)(2,1)S(1)}, u32[]{:S(2)}, u32[]{:S(2)}) collective-permute-start(bf16[16,32,128]{2,1,0:T(8,128)(2,1)S(1)} %get-tuple-element.23), channel_id=1, source_target_pairs={{0,1},{1,0},{2,3},{3,2},{4,5},{5,4},{6,7},{7,6},{8,9},{9,8},{10,11... | collective-permute-start | bytes 393224 | tf_op jit(solution)/shard_map/ppermute | solution.py:337
  22.6 7.8 %collective-permute-start.1 = (bf16[16,32,128]{2,1,0:T(8,128)(2,1)S(1)}, bf16[16,32,128]{2,1,0:T(8,128)(2,1)S(1)}, u32[]{:S(2)}, u32[]{:S(2)}) collective-permute-start(bf16[16,32,128]{2,1,0:T(8,128)(2,1)S(1)} %get-tuple-element.24), channel_id=1, source_target_pairs={{0,1},{1,0},{2,3},{3,2},{4,5},{5,4},{6,7},{7,6},{8,9},{9,8},{10,11... | collective-permute-start | bytes 393224 | tf_op jit(solution)/shard_map/ppermute | solution.py:337

commit v15 on v14

--- a/solution.py
+++ b/solution.py
@@ -107,25 +107,27 @@
         copy.wait()
 
 
+def side_by_side(blocks_ref, g):
+    return jnp.concatenate([blocks_ref[g, j] for j in range(blocks_ref.shape[1])], axis=1)
+
+
 def mid_kernel(
-    axes, live_ref, coupling_hbm, near_hbm, parent_hbm, leaf_partners_hbm, parent_partners_hbm,
-    packed_ref, parent_packed_ref, near_out_ref, rim_near_ref, leaf_at_ref, parent_at_ref,
-    coupling_ref, near_ref, parent_ref, sems,
+    axes, live_ref, near_hbm, parent_hbm, leaf_partners_hbm, parent_partners_hbm,
+    parent_packed_ref, near_out_ref, rim_near_ref, leaf_at_ref, parent_at_ref,
+    near_ref, parent_ref, sems,
 ):
-    leaves, many, rank, _ = coupling_ref.shape
-    parents = parent_ref.shape[0]
+    parents, many, rank, _ = parent_ref.shape
+    leaves = near_ref.shape[0]
     width = near_ref.shape[2]
     pairs = leaves // 2
     started = start_all(
         [(near_hbm, near_ref)]
         + [(parent_hbm.at[pl.ds(4 * i, 4)], parent_ref.at[pl.ds(4 * i, 4)]) for i in range(parents // 4)]
-        + [(coupling_hbm.at[pl.ds(4 * i, 4)], coupling_ref.at[pl.ds(4 * i, 4)]) for i in range(leaves // 4)]
         + [(leaf_partners_hbm, leaf_at_ref), (parent_partners_hbm, parent_at_ref)],
         sems,
     )
     near_in = started[0]
-    parent_in = started[1 : 1 + parents // 4]
-    coupling_in = started[1 + parents // 4 : -2]
+    parent_in = started[1:-2]
     near_in.wait()
     rim_near_ref[0] = near_ref[0, 0]
     rim_near_ref[1] = near_ref[leaves - 1, 2]
@@ -139,18 +141,10 @@
             odd = odd + dot(live_ref[a + 1][:, :width], near_ref[2 * a + 1, 2], NT)
         near_out_ref[a] = jnp.concatenate([even, odd], axis=1)
 
-    def pack(src, dst, g):
-        for j in range(0, many, 2):
-            dst[g, :, rank * j : rank * (j + 2)] = jnp.concatenate([src[g, j], src[g, j + 1]], axis=1)
-
     for i, copy in enumerate(parent_in):
         copy.wait()
         for q in range(4 * i, 4 * i + 4):
-            pack(parent_ref, parent_packed_ref, q)
-    for i, copy in enumerate(coupling_in):
-        copy.wait()
-        for g in range(4 * i, 4 * i + 4):
-            pack(coupling_ref, packed_ref, g)
+            parent_packed_ref[q] = side_by_side(parent_ref, q)
     for copy in started[-2:]:
         copy.wait()
     wanted = leaf_at_ref[...] + (1 - position(axes)) * leaves
@@ -163,7 +157,8 @@
     parent_at_ref[...] = wanted ^ (lax.broadcasted_iota(jnp.int32, wanted.shape, 1) & 1)
 
 
-def halves_kernel(whole_ref, first_ref, second_ref):
+def halves_kernel(whole_ref, at_ref, first_ref, second_ref):
+    del at_ref
     half = first_ref.shape[0]
     first_ref[...] = whole_ref[:half]
     second_ref[...] = whole_ref[half:]
@@ -185,14 +180,16 @@
 
 
 def leaf_kernel(
-    axes, at_vmem, rim_ref, even_ref, odd_ref, packed_ref, rim_near_ref, transfer_hbm, basis_hbm,
-    far_ref, edge_ref, transfer_ref, basis_packed_ref, table_ref, at_ref, basis_ref, sems,
+    axes, at_vmem, rim_ref, even_ref, odd_ref, rim_near_ref, coupling_hbm, transfer_hbm, basis_hbm,
+    far_ref, edge_ref, transfer_ref, basis_packed_ref, table_ref, at_ref, coupling_ref, basis_ref, sems,
 ):
-    at_in, transfer_in, basis_in = start_all(
-        [(at_vmem, at_ref), (transfer_hbm, transfer_ref), (basis_hbm, basis_ref)], sems
-    )
-    many, leaves = at_ref.shape
-    rank = packed_ref.shape[1]
+    leaves, many, rank, _ = coupling_ref.shape
+    at_in, *coupling_in, transfer_in, basis_in = start_all(
+        [(at_vmem, at_ref)]
+        + [(coupling_hbm.at[pl.ds(2 * i, 2)], coupling_ref.at[pl.ds(2 * i, 2)]) for i in range(leaves // 2)]
+        + [(transfer_hbm, transfer_ref), (basis_hbm, basis_ref)],
+        sems,
+    )
     width = rim_near_ref.shape[1]
     pairs = leaves // 2
     sides = rim_ref.shape[1]
@@ -212,9 +209,10 @@
     at_in.wait()
     for a in range(pairs):
         fars = []
+        coupling_in[a].wait()
         for g in (2 * a, 2 * a + 1):
             rows = [at_ref[j, g] for j in range(many)]
-            fars.append(dot(picked(table_ref, rows, left), packed_ref[g], NT))
+            fars.append(dot(picked(table_ref, rows, left), side_by_side(coupling_ref, g), NT))
         far_ref[a] = jnp.concatenate(fars, axis=1)
     basis_in.wait()
     for a in range(pairs):
@@ -325,38 +323,37 @@
         compiler_params=params(4),
     )(parent_coef)
     same = lax.all_to_all(sent, "gz", 0, 0, tiled=True)
+
+    parent_packed, near, rim_near, leaf_at, parent_at = pl.pallas_call(
+        functools.partial(mid_kernel, axes),
+        name="mid",
+        out_shape=[
+            shape((parents, rank, many * rank), bf16),
+            shape((pairs, sides, 2 * width), f32),
+            shape((2, width, width), bf16),
+            shape((many, leaves), jnp.int32),
+            shape((parents, many), jnp.int32),
+        ],
+        in_specs=[VMEM] + [HBM] * 4,
+        out_specs=[VMEM] * 5,
+        scratch_shapes=[
+            pltpu.VMEM(near_blocks.shape, bf16),
+            pltpu.VMEM(parent_coupling.shape, bf16),
+            dma(3 + parents // 4),
+        ],
+        compiler_params=params(12),
+    )(live, *keep(near_blocks, parent_coupling, leaf_partners.T, parent_partners))
+
     quarter = shape((n // 4 * own, sides, 2 * rank), bf16)
     pieces = pl.pallas_call(
         halves_kernel,
         name="halves",
         out_shape=[quarter, quarter],
-        in_specs=[VMEM],
+        in_specs=[VMEM, VMEM],
         out_specs=[VMEM, VMEM],
         compiler_params=params(4),
-    )(same)
+    )(same, parent_at)
     other = [lax.ppermute(piece, "gp", [(0, 1), (1, 0)]) for piece in pieces]
-
-    packed, parent_packed, near, rim_near, leaf_at, parent_at = pl.pallas_call(
-        functools.partial(mid_kernel, axes),
-        name="mid",
-        out_shape=[
-            shape((leaves, rank, many * rank), bf16),
-            shape((parents, rank, many * rank), bf16),
-            shape((pairs, sides, 2 * width), f32),
-            shape((2, width, width), bf16),
-            shape((many, leaves), jnp.int32),
-            shape((parents, many), jnp.int32),
-        ],
-        in_specs=[VMEM] + [HBM] * 5,
-        out_specs=[VMEM] * 6,
-        scratch_shapes=[
-            pltpu.VMEM(leaf_coupling.shape, bf16),
-            pltpu.VMEM(near_blocks.shape, bf16),
-            pltpu.VMEM(parent_coupling.shape, bf16),
-            dma(3 + leaves // 4 + parents // 4),
-        ],
-        compiler_params=params(20),
-    )(live, *keep(leaf_coupling, near_blocks, parent_coupling, leaf_partners.T, parent_partners))
 
     far, edge, transfer_in, basis_in = pl.pallas_call(
         functools.partial(leaf_kernel, axes),
@@ -367,16 +364,17 @@
             shape(transfer.shape, bf16),
             shape((pairs, width, 2 * rank), bf16),
         ],
-        in_specs=[VMEM] * 6 + [HBM] * 2,
+        in_specs=[VMEM] * 5 + [HBM] * 3,
         out_specs=[VMEM] * 4,
         scratch_shapes=[
             pltpu.VMEM((3 * leaves, sides, 2 * rank), bf16),
             pltpu.SMEM((many, leaves), jnp.int32),
+            pltpu.VMEM(leaf_coupling.shape, bf16),
             pltpu.VMEM(basis.shape, bf16),
-            dma(3),
-        ],
-        compiler_params=params(8),
-    )(leaf_at, rim, even, odd, packed, rim_near, *keep(transfer, basis))
+            dma(3 + leaves // 2),
+        ],
+        compiler_params=params(16),
+    )(leaf_at, rim, even, odd, rim_near, *keep(leaf_coupling, transfer, basis))
 
     out = pl.pallas_call(
         functools.partial(down_kernel, "gp"),

time: 33.3 us -> 32.3 us (0.970)
  waiting for transfers between devices: 7.79 us -> 4.69 us
  Pallas kernels: 13 us -> 15.1 us
    pallas_call x1, Pallas kernels: 2.25 us -> 6.66 us  [per_device(): pl.pallas_call(functools.partial(leaf_kernel, axes), name='leaf', out_sha...]
    all_to_all x1, waiting for transfers between devices: 7.78 us -> 4.68 us  [per_device(): same = lax.all_to_all(sent, 'gz', 0, 0, tiled=True)]
    pallas_call x1, Pallas kernels: 5.39 us -> 3.09 us  [per_device(): pl.pallas_call(functools.partial(mid_kernel, axes), name='mid', out_shape...]
  transfers between devices with their start and end apart: 5 -> 5, of which waited for: 1 -> 1; matrix products, arithmetic and copies ran while one was open for 0% -> 0% of each run, Pallas kernels for 23% -> 30%
where the time goes in v15:
time: 32.3 us; the launch traced here: 32.1 us
  Pallas kernels  15.1 us (47%)
  starting transfers between devices  12.3 us (38%)
  waiting for transfers between devices  4.69 us (15%)
    pallas_call x1, Pallas kernels, per_device(): pl.pallas_call(functools.partial(leaf_kernel, axes), name='leaf', out_sha...  6.66 us
    all_to_all x1, starting transfers between devices, per_device(): same = lax.all_to_all(sent, 'gz', 0, 0, tiled=True)  6.33 us
    all_to_all x1, waiting for transfers between devices, per_device(): same = lax.all_to_all(sent, 'gz', 0, 0, tiled=True)  4.68 us
    ppermute x2, starting transfers between devices, per_device(): other = [lax.ppermute(piece, 'gp', [(0, 1), (1, 0)]) for piece in pieces]  3.77 us
    pallas_call x1, Pallas kernels, per_device(): pl.pallas_call(functools.partial(mid_kernel, axes), name='mid', out_shape...  3.09 us
    pallas_call x1, Pallas kernels, per_device(): pl.pallas_call(functools.partial(down_kernel, 'gp'), name='down', out_sha...  2.76 us
    pallas_call x1, Pallas kernels, per_device(): pl.pallas_call(up_kernel, name='up', out_shape=[shape((pairs + 2, sides,...  1.82 us
    ppermute x1, starting transfers between devices, per_device(): even = lax.ppermute(rim, axes, [(i, i ^ 1) for i in range(total)])  1.52 us
  transfers between devices with their start and end apart: 5, of which 1 were waited for; matrix products, arithmetic and copies ran while one was open for 0% of the time, Pallas kernels for 30%

profile of v15, /device:TPU:0, one launch (start us, length us, event | category | flops | bytes accessed | tf_op | source)
XLA Modules:
  0.0 32.1 jit_solution(4251088349315513279)
XLA Ops:
  0.0 1.8 %up.1 = (bf16[18,32,128]{2,1,0:T(8,128)(2,1)S(1)}, bf16[16,32,128]{2,1,0:T(8,128)(2,1)S(1)}, bf16[8,32,128]{2,1,0:T(8,128)(2,1)S(1)}) custom-call(s32[32]{0:T(128)} %counts_hbm.3, bf16[32,2048]{1,0:T(8,128)(2,1)} %bitcast.3, bf16[32,64,64]{2,1,0:T(8,128)(2,1)} %basis_hbm.3, bf16[32,64,64]{2,1,0:T(8,128)(2,1)} %transfer_hbm.3), custom_call_target="tpu_custom_call" | custom-call | tf_op jit(solution)/shard_map/up/pallas_call | solution.py:293
  1.8 0.7 %copies.1 = bf16[32,32,128]{2,1,0:T(8,128)(2,1)} custom-call(bf16[8,32,128]{2,1,0:T(8,128)(2,1)S(1)} %get-tuple-element.21.parents_ref), custom_call_target="tpu_custom_call" | custom-call | tf_op jit(solution)/shard_map/copies/pallas_call | solution.py:316
  2.6 6.3 %all-to-all-start = ((bf16[32,32,128]{2,1,0:T(8,128)(2,1)}), bf16[32,32,128]{2,1,0:T(8,128)(2,1)S(1)}, u32[]{:S(2)}, u32[]{:S(2)}) async-start(bf16[32,32,128]{2,1,0:T(8,128)(2,1)} %copies.1), calls=%async_computation | async-start | bytes 524288 | tf_op jit(solution)/shard_map/all_to_all | solution.py:325
  8.9 1.5 %collective-permute-start.2 = (bf16[18,32,128]{2,1,0:T(8,128)(2,1)S(1)}, bf16[18,32,128]{2,1,0:T(8,128)(2,1)S(1)}, u32[]{:S(2)}, u32[]{:S(2)}) collective-permute-start(bf16[18,32,128]{2,1,0:T(8,128)(2,1)S(1)} %get-tuple-element.26.rim_ref), channel_id=1, source_target_pairs={{0,1},{1,0},{2,3},{3,2},{4,5},{5,4},{6,7},{7,6},{8,9},{9,8},{10,11... | collective-permute-start | bytes 442376 | tf_op jit(solution)/shard_map/ppermute | solution.py:313
  10.4 0.7 %collective-permute-start.3 = (bf16[18,32,128]{2,1,0:T(8,128)(2,1)S(1)}, bf16[18,32,128]{2,1,0:T(8,128)(2,1)S(1)}, u32[]{:S(2)}, u32[]{:S(2)}) collective-permute-start(bf16[18,32,128]{2,1,0:T(8,128)(2,1)S(1)} %get-tuple-element.26.rim_ref), channel_id=1, source_target_pairs={{1,2},{3,4},{5,6},{7,8},{9,10},{11,12},{13,14},{15,16},{17,18},{19... | collective-permute-start | bytes 442376 | tf_op jit(solution)/shard_map/ppermute | solution.py:315
  11.1 3.1 %mid.1 = (bf16[16,64,1024]{2,1,0:T(8,128)(2,1)S(1)}, f32[16,32,128]{2,1,0:T(8,128)S(1)}, bf16[2,64,64]{2,1,0:T(8,128)(2,1)S(1)}, s32[16,32]{1,0:T(8,128)S(1)}, s32[16,16]{1,0:T(8,128)S(1)}) custom-call(bf16[16,32,128]{2,1,0:T(8,128)(2,1)S(1)} %get-tuple-element.19.live_ref, bf16[32,3,64,64]{3,2,1,0:T(8,128)(2,1)} %near_hbm.1, ...), custom_call_target="tpu_custom_call" | custom-call | tf_op jit(solution)/shard_map/mid/pallas_call | solution.py:327
  14.2 4.7 %all-to-all-done.whole_ref.same_ref = bf16[32,32,128]{2,1,0:T(8,128)(2,1)S(1)} async-done(((bf16[32,32,128]{2,1,0:T(8,128)(2,1)}), bf16[32,32,128]{2,1,0:T(8,128)(2,1)S(1)}, u32[]{:S(2)}, u32[]{:S(2)}) %all-to-all-start) | async-done | bytes 262176 | tf_op jit(solution)/shard_map/all_to_all | solution.py:325
  18.9 3.7 %collective-permute-start = (bf16[16,32,128]{2,1,0:T(8,128)(2,1)S(1)}, bf16[16,32,128]{2,1,0:T(8,128)(2,1)S(1)}, u32[]{:S(2)}, u32[]{:S(2)}) collective-permute-start(bf16[16,32,128]{2,1,0:T(8,128)(2,1)S(1)} %get-tuple-element.22), channel_id=1, source_target_pairs={{0,1},{1,0},{2,3},{3,2},{4,5},{5,4},{6,7},{7,6},{8,9},{9,8},{10,11... | collective-permute-start | bytes 393224 | tf_op jit(solution)/shard_map/ppermute | solution.py:356
  22.6 0.1 collective-permute-start.1
  22.7 0.0 collective-permute-done.2.even_ref
  22.7 0.0 collective-permute-done.3.odd_ref
  22.7 6.7 %leaf.1 = (f32[16,32,128]{2,1,0:T(8,128)S(1)}, f32[2,32,128]{2,1,0:T(8,128)S(1)}, bf16[32,64,64]{2,1,0:T(8,128)(2,1)S(1)}, bf16[16,64,128]{2,1,0:T(8,128)(2,1)S(1)}) custom-call(s32[16,32]{1,0:T(8,128)S(1)} %get-tuple-element.25.at_vmem, bf16[18,32,128]{2,1,0:T(8,128)(2,1)S(1)} %get-tuple-element.26.rim_ref, ...), custom_call_target="tpu_custom_call" | custom-call | tf_op jit(solution)/shard_map/leaf/pallas_call | solution.py:358
  29.3 0.0 collective-permute-done.other_refs_0_
  29.4 0.0 collective-permute-done.1.other_refs_1_
  29.4 2.8 %down.1 = bf16[32,2048]{1,0:T(8,128)(2,1)} custom-call(s32[16,16]{1,0:T(8,128)S(1)} %get-tuple-element.20.at_ref.at_vmem, bf16[32,32,128]{2,1,0:T(8,128)(2,1)S(1)} %all-to-all-done.whole_ref.same_ref, bf16[16,32,128]{2,1,0:T(8,128)(2,1)S(1)} %collective-permute-done.other_refs_0_, bf16[16,32,128]{2,1,0:T(8,128)(2,1)S(1)} %collective-permute-done.1.other_refs_1_, ...), custom_call_target="tpu_custom_call" | custom-call | tf_op jit(solution)/shard_map/down/pallas_call | solution.py:379
  (1 shorter events, 0.0 us)
Async XLA Ops:
  2.6 16.3 %all-to-all-start = ((bf16[32,32,128]{2,1,0:T(8,128)(2,1)}), bf16[32,32,128]{2,1,0:T(8,128)(2,1)S(1)}, u32[]{:S(2)}, u32[]{:S(2)}) async-start(bf16[32,32,128]{2,1,0:T(8,128)(2,1)} %copies.1), calls=%async_computation | async-start | bytes 524288 | tf_op jit(solution)/shard_map/all_to_all | solution.py:325
  8.9 13.8 %collective-permute-start.2 = (bf16[18,32,128]{2,1,0:T(8,128)(2,1)S(1)}, bf16[18,32,128]{2,1,0:T(8,128)(2,1)S(1)}, u32[]{:S(2)}, u32[]{:S(2)}) collective-permute-start(bf16[18,32,128]{2,1,0:T(8,128)(2,1)S(1)} %get-tuple-element.26.rim_ref), channel_id=1, source_target_pairs={{0,1},{1,0},{2,3},{3,2},{4,5},{5,4},{6,7},{7,6},{8,9},{9,8},{10,11... | collective-permute-start | bytes 442376 | tf_op jit(solution)/shard_map/ppermute | solution.py:313
  10.4 12.2 %collective-permute-start.3 = (bf16[18,32,128]{2,1,0:T(8,128)(2,1)S(1)}, bf16[18,32,128]{2,1,0:T(8,128)(2,1)S(1)}, u32[]{:S(2)}, u32[]{:S(2)}) collective-permute-start(bf16[18,32,128]{2,1,0:T(8,128)(2,1)S(1)} %get-tuple-element.26.rim_ref), channel_id=1, source_target_pairs={{1,2},{3,4},{5,6},{7,8},{9,10},{11,12},{13,14},{15,16},{17,18},{19... | collective-permute-start | bytes 442376 | tf_op jit(solution)/shard_map/ppermute | solution.py:315
  18.9 10.5 %collective-permute-start = (bf16[16,32,128]{2,1,0:T(8,128)(2,1)S(1)}, bf16[16,32,128]{2,1,0:T(8,128)(2,1)S(1)}, u32[]{:S(2)}, u32[]{:S(2)}) collective-permute-start(bf16[16,32,128]{2,1,0:T(8,128)(2,1)S(1)} %get-tuple-element.22), channel_id=1, source_target_pairs={{0,1},{1,0},{2,3},{3,2},{4,5},{5,4},{6,7},{7,6},{8,9},{9,8},{10,11... | collective-permute-start | bytes 393224 | tf_op jit(solution)/shard_map/ppermute | solution.py:356
  22.6 6.8 %collective-permute-start.1 = (bf16[16,32,128]{2,1,0:T(8,128)(2,1)S(1)}, bf16[16,32,128]{2,1,0:T(8,128)(2,1)S(1)}, u32[]{:S(2)}, u32[]{:S(2)}) collective-permute-start(bf16[16,32,128]{2,1,0:T(8,128)(2,1)S(1)} %get-tuple-element.23), channel_id=1, source_target_pairs={{0,1},{1,0},{2,3},{3,2},{4,5},{5,4},{6,7},{7,6},{8,9},{9,8},{10,11... | collective-permute-start | bytes 393224 | tf_op jit(solution)/shard_map/ppermute | solution.py:356

commit v16 on v15

--- a/solution.py
+++ b/solution.py
@@ -147,8 +147,7 @@
             parent_packed_ref[q] = side_by_side(parent_ref, q)
     for copy in started[-2:]:
         copy.wait()
-    wanted = leaf_at_ref[...] + (1 - position(axes)) * leaves
-    leaf_at_ref[...] = wanted ^ (lax.broadcasted_iota(jnp.int32, wanted.shape, 0) & 1)
+    leaf_at_ref[...] = leaf_at_ref[...] + (1 - position(axes)) * leaves
     inner = lax.axis_size(axes[2])
     outer = lax.axis_size(axes[1])
     wanted = mod(parent_at_ref[...], outer * inner * parents)
@@ -193,7 +192,6 @@
     width = rim_near_ref.shape[1]
     pairs = leaves // 2
     sides = rim_ref.shape[1]
-    left = left_half(sides, rank)
     parity = lax.rem(position(axes), 2)
     for ref, base in (
         (rim_ref, leaves), (even_ref, 2 * leaves * (1 - parity)), (odd_ref, 2 * leaves * parity),
@@ -211,8 +209,10 @@
         fars = []
         coupling_in[a].wait()
         for g in (2 * a, 2 * a + 1):
-            rows = [at_ref[j, g] for j in range(many)]
-            fars.append(dot(picked(table_ref, rows, left), side_by_side(coupling_ref, g), NT))
+            far = jnp.zeros((sides, rank), jnp.float32)
+            for j in range(many):
+                far = far + dot(table_ref[at_ref[j, g], :, :rank], coupling_ref[g, j], NT)
+            fars.append(far)
         far_ref[a] = jnp.concatenate(fars, axis=1)
     basis_in.wait()
     for a in range(pairs):

time: 32.3 us -> 34.4 us (1.065)
  Pallas kernels: 15.1 us -> 17.2 us
    pallas_call x1, Pallas kernels: 6.66 us -> 8.77 us  [per_device(): pl.pallas_call(functools.partial(leaf_kernel, axes), name='leaf', out_sha...]
  transfers between devices with their start and end apart: 5 -> 5, of which waited for: 1 -> 1; matrix products, arithmetic and copies ran while one was open for 0% -> 0% of each run, Pallas kernels for 30% -> 35%
where the time goes in v16:
time: 34.4 us; the launch traced here: 34.2 us
  Pallas kernels  17.2 us (50%)
  starting transfers between devices  12.3 us (36%)
  waiting for transfers between devices  4.69 us (14%)
    pallas_call x1, Pallas kernels, per_device(): pl.pallas_call(functools.partial(leaf_kernel, axes), name='leaf', out_sha...  8.77 us
    all_to_all x1, starting transfers between devices, per_device(): same = lax.all_to_all(sent, 'gz', 0, 0, tiled=True)  6.33 us
    all_to_all x1, waiting for transfers between devices, per_device(): same = lax.all_to_all(sent, 'gz', 0, 0, tiled=True)  4.68 us
    ppermute x2, starting transfers between devices, per_device(): other = [lax.ppermute(piece, 'gp', [(0, 1), (1, 0)]) for piece in pieces]  3.77 us
    pallas_call x1, Pallas kernels, per_device(): pl.pallas_call(functools.partial(mid_kernel, axes), name='mid', out_shape...  3.09 us
    pallas_call x1, Pallas kernels, per_device(): pl.pallas_call(functools.partial(down_kernel, 'gp'), name='down', out_sha...  2.76 us
    pallas_call x1, Pallas kernels, per_device(): pl.pallas_call(up_kernel, name='up', out_shape=[shape((pairs + 2, sides,...  1.82 us
    ppermute x1, starting transfers between devices, per_device(): even = lax.ppermute(rim, axes, [(i, i ^ 1) for i in range(total)])  1.52 us
  transfers between devices with their start and end apart: 5, of which 1 were waited for; matrix products, arithmetic and copies ran while one was open for 0% of the time, Pallas kernels for 35%

profile of v16, /device:TPU:0, one launch (start us, length us, event | category | flops | bytes accessed | tf_op | source)
XLA Modules:
  0.0 34.2 jit_solution(14356389706236066470)
XLA Ops:
  0.0 1.8 %up.1 = (bf16[18,32,128]{2,1,0:T(8,128)(2,1)S(1)}, bf16[16,32,128]{2,1,0:T(8,128)(2,1)S(1)}, bf16[8,32,128]{2,1,0:T(8,128)(2,1)S(1)}) custom-call(s32[32]{0:T(128)} %counts_hbm.3, bf16[32,2048]{1,0:T(8,128)(2,1)} %bitcast.3, bf16[32,64,64]{2,1,0:T(8,128)(2,1)} %basis_hbm.3, bf16[32,64,64]{2,1,0:T(8,128)(2,1)} %transfer_hbm.3), custom_call_target="tpu_custom_call" | custom-call | tf_op jit(solution)/shard_map/up/pallas_call | solution.py:293
  1.8 0.7 %copies.1 = bf16[32,32,128]{2,1,0:T(8,128)(2,1)} custom-call(bf16[8,32,128]{2,1,0:T(8,128)(2,1)S(1)} %get-tuple-element.21.parents_ref), custom_call_target="tpu_custom_call" | custom-call | tf_op jit(solution)/shard_map/copies/pallas_call | solution.py:316
  2.6 6.3 %all-to-all-start = ((bf16[32,32,128]{2,1,0:T(8,128)(2,1)}), bf16[32,32,128]{2,1,0:T(8,128)(2,1)S(1)}, u32[]{:S(2)}, u32[]{:S(2)}) async-start(bf16[32,32,128]{2,1,0:T(8,128)(2,1)} %copies.1), calls=%async_computation | async-start | bytes 524288 | tf_op jit(solution)/shard_map/all_to_all | solution.py:325
  8.9 1.5 %collective-permute-start.2 = (bf16[18,32,128]{2,1,0:T(8,128)(2,1)S(1)}, bf16[18,32,128]{2,1,0:T(8,128)(2,1)S(1)}, u32[]{:S(2)}, u32[]{:S(2)}) collective-permute-start(bf16[18,32,128]{2,1,0:T(8,128)(2,1)S(1)} %get-tuple-element.26.rim_ref), channel_id=1, source_target_pairs={{0,1},{1,0},{2,3},{3,2},{4,5},{5,4},{6,7},{7,6},{8,9},{9,8},{10,11... | collective-permute-start | bytes 442376 | tf_op jit(solution)/shard_map/ppermute | solution.py:313
  10.4 0.7 %collective-permute-start.3 = (bf16[18,32,128]{2,1,0:T(8,128)(2,1)S(1)}, bf16[18,32,128]{2,1,0:T(8,128)(2,1)S(1)}, u32[]{:S(2)}, u32[]{:S(2)}) collective-permute-start(bf16[18,32,128]{2,1,0:T(8,128)(2,1)S(1)} %get-tuple-element.26.rim_ref), channel_id=1, source_target_pairs={{1,2},{3,4},{5,6},{7,8},{9,10},{11,12},{13,14},{15,16},{17,18},{19... | collective-permute-start | bytes 442376 | tf_op jit(solution)/shard_map/ppermute | solution.py:315
  11.1 3.1 %mid.1 = (bf16[16,64,1024]{2,1,0:T(8,128)(2,1)S(1)}, f32[16,32,128]{2,1,0:T(8,128)S(1)}, bf16[2,64,64]{2,1,0:T(8,128)(2,1)S(1)}, s32[16,32]{1,0:T(8,128)S(1)}, s32[16,16]{1,0:T(8,128)S(1)}) custom-call(bf16[16,32,128]{2,1,0:T(8,128)(2,1)S(1)} %get-tuple-element.19.live_ref, bf16[32,3,64,64]{3,2,1,0:T(8,128)(2,1)} %near_hbm.1, ...), custom_call_target="tpu_custom_call" | custom-call | tf_op jit(solution)/shard_map/mid/pallas_call | solution.py:327
  14.2 4.7 %all-to-all-done.whole_ref.same_ref = bf16[32,32,128]{2,1,0:T(8,128)(2,1)S(1)} async-done(((bf16[32,32,128]{2,1,0:T(8,128)(2,1)}), bf16[32,32,128]{2,1,0:T(8,128)(2,1)S(1)}, u32[]{:S(2)}, u32[]{:S(2)}) %all-to-all-start) | async-done | bytes 262176 | tf_op jit(solution)/shard_map/all_to_all | solution.py:325
  18.9 3.7 %collective-permute-start = (bf16[16,32,128]{2,1,0:T(8,128)(2,1)S(1)}, bf16[16,32,128]{2,1,0:T(8,128)(2,1)S(1)}, u32[]{:S(2)}, u32[]{:S(2)}) collective-permute-start(bf16[16,32,128]{2,1,0:T(8,128)(2,1)S(1)} %get-tuple-element.22), channel_id=1, source_target_pairs={{0,1},{1,0},{2,3},{3,2},{4,5},{5,4},{6,7},{7,6},{8,9},{9,8},{10,11... | collective-permute-start | bytes 393224 | tf_op jit(solution)/shard_map/ppermute | solution.py:356
  22.6 0.1 collective-permute-start.1
  22.7 0.0 collective-permute-done.2.even_ref
  22.7 0.0 collective-permute-done.3.odd_ref
  22.7 8.8 %leaf.1 = (f32[16,32,128]{2,1,0:T(8,128)S(1)}, f32[2,32,128]{2,1,0:T(8,128)S(1)}, bf16[32,64,64]{2,1,0:T(8,128)(2,1)S(1)}, bf16[16,64,128]{2,1,0:T(8,128)(2,1)S(1)}) custom-call(s32[16,32]{1,0:T(8,128)S(1)} %get-tuple-element.25.at_vmem, bf16[18,32,128]{2,1,0:T(8,128)(2,1)S(1)} %get-tuple-element.26.rim_ref, ...), custom_call_target="tpu_custom_call" | custom-call | tf_op jit(solution)/shard_map/leaf/pallas_call | solution.py:358
  31.4 0.0 collective-permute-done.other_refs_0_
  31.5 0.0 collective-permute-done.1.other_refs_1_
  31.5 2.8 %down.1 = bf16[32,2048]{1,0:T(8,128)(2,1)} custom-call(s32[16,16]{1,0:T(8,128)S(1)} %get-tuple-element.20.at_ref.at_vmem, bf16[32,32,128]{2,1,0:T(8,128)(2,1)S(1)} %all-to-all-done.whole_ref.same_ref, bf16[16,32,128]{2,1,0:T(8,128)(2,1)S(1)} %collective-permute-done.other_refs_0_, bf16[16,32,128]{2,1,0:T(8,128)(2,1)S(1)} %collective-permute-done.1.other_refs_1_, ...), custom_call_target="tpu_custom_call" | custom-call | tf_op jit(solution)/shard_map/down/pallas_call | solution.py:379
  (1 shorter events, 0.0 us)
Async XLA Ops:
  2.6 16.3 %all-to-all-start = ((bf16[32,32,128]{2,1,0:T(8,128)(2,1)}), bf16[32,32,128]{2,1,0:T(8,128)(2,1)S(1)}, u32[]{:S(2)}, u32[]{:S(2)}) async-start(bf16[32,32,128]{2,1,0:T(8,128)(2,1)} %copies.1), calls=%async_computation | async-start | bytes 524288 | tf_op jit(solution)/shard_map/all_to_all | solution.py:325
  8.9 13.8 %collective-permute-start.2 = (bf16[18,32,128]{2,1,0:T(8,128)(2,1)S(1)}, bf16[18,32,128]{2,1,0:T(8,128)(2,1)S(1)}, u32[]{:S(2)}, u32[]{:S(2)}) collective-permute-start(bf16[18,32,128]{2,1,0:T(8,128)(2,1)S(1)} %get-tuple-element.26.rim_ref), channel_id=1, source_target_pairs={{0,1},{1,0},{2,3},{3,2},{4,5},{5,4},{6,7},{7,6},{8,9},{9,8},{10,11... | collective-permute-start | bytes 442376 | tf_op jit(solution)/shard_map/ppermute | solution.py:313
  10.4 12.2 %collective-permute-start.3 = (bf16[18,32,128]{2,1,0:T(8,128)(2,1)S(1)}, bf16[18,32,128]{2,1,0:T(8,128)(2,1)S(1)}, u32[]{:S(2)}, u32[]{:S(2)}) collective-permute-start(bf16[18,32,128]{2,1,0:T(8,128)(2,1)S(1)} %get-tuple-element.26.rim_ref), channel_id=1, source_target_pairs={{1,2},{3,4},{5,6},{7,8},{9,10},{11,12},{13,14},{15,16},{17,18},{19... | collective-permute-start | bytes 442376 | tf_op jit(solution)/shard_map/ppermute | solution.py:315
  18.9 12.6 %collective-permute-start = (bf16[16,32,128]{2,1,0:T(8,128)(2,1)S(1)}, bf16[16,32,128]{2,1,0:T(8,128)(2,1)S(1)}, u32[]{:S(2)}, u32[]{:S(2)}) collective-permute-start(bf16[16,32,128]{2,1,0:T(8,128)(2,1)S(1)} %get-tuple-element.22), channel_id=1, source_target_pairs={{0,1},{1,0},{2,3},{3,2},{4,5},{5,4},{6,7},{7,6},{8,9},{9,8},{10,11... | collective-permute-start | bytes 393224 | tf_op jit(solution)/shard_map/ppermute | solution.py:356
  22.6 8.9 %collective-permute-start.1 = (bf16[16,32,128]{2,1,0:T(8,128)(2,1)S(1)}, bf16[16,32,128]{2,1,0:T(8,128)(2,1)S(1)}, u32[]{:S(2)}, u32[]{:S(2)}) collective-permute-start(bf16[16,32,128]{2,1,0:T(8,128)(2,1)S(1)} %get-tuple-element.23), channel_id=1, source_target_pairs={{0,1},{1,0},{2,3},{3,2},{4,5},{5,4},{6,7},{7,6},{8,9},{9,8},{10,11... | collective-permute-start | bytes 393224 | tf_op jit(solution)/shard_map/ppermute | solution.py:356

commit v17 on v15

--- a/solution.py
+++ b/solution.py
@@ -56,8 +56,8 @@
 
 def up_kernel(
     counts_hbm, charges_hbm, basis_hbm, transfer_hbm,
-    rim_ref, live_ref, parents_ref,
-    counts_ref, charges_ref, basis_ref, transfer_ref, sems,
+    rim_ref, live_ref, sent_hbm,
+    counts_ref, charges_ref, basis_ref, transfer_ref, parents_ref, sems, sent_sems,
 ):
     counts_in, charges_in, basis_in, transfer_in = start_all(
         [
@@ -98,12 +98,8 @@
     ]
     for a in range(own):
         parents_ref[a] = jnp.concatenate(sums[2 * a : 2 * a + 2], axis=1).astype(jnp.bfloat16)
-
-
-def copies_kernel(parents_ref, sent_hbm, sems):
-    own = parents_ref.shape[0]
     copies = sent_hbm.shape[0] // own
-    for copy in start_all([(parents_ref, sent_hbm.at[pl.ds(own * c, own)]) for c in range(copies)], sems):
+    for copy in start_all([(parents_ref, sent_hbm.at[pl.ds(own * c, own)]) for c in range(copies)], sent_sems):
         copy.wait()
 
 
@@ -181,12 +177,12 @@
 
 def leaf_kernel(
     axes, at_vmem, rim_ref, even_ref, odd_ref, rim_near_ref, coupling_hbm, transfer_hbm, basis_hbm,
-    far_ref, edge_ref, transfer_ref, basis_packed_ref, table_ref, at_ref, coupling_ref, basis_ref, sems,
+    far_ref, edge_ref, transfer_ref, basis_packed_ref, table_ref, at_ref, coupling_ref, packed_ref, basis_ref, sems,
 ):
     leaves, many, rank, _ = coupling_ref.shape
     at_in, *coupling_in, transfer_in, basis_in = start_all(
         [(at_vmem, at_ref)]
-        + [(coupling_hbm.at[pl.ds(2 * i, 2)], coupling_ref.at[pl.ds(2 * i, 2)]) for i in range(leaves // 2)]
+        + [(coupling_hbm.at[pl.ds(4 * i, 4)], coupling_ref.at[pl.ds(4 * i, 4)]) for i in range(leaves // 4)]
         + [(transfer_hbm, transfer_ref), (basis_hbm, basis_ref)],
         sems,
     )
@@ -207,13 +203,17 @@
     edge_ref[0] = jnp.concatenate([low, jnp.zeros_like(low)], axis=1)
     edge_ref[1] = jnp.concatenate([jnp.zeros_like(high), high], axis=1)
     at_in.wait()
-    for a in range(pairs):
+    for i in range(leaves // 4 + 1):
+        if i < leaves // 4:
+            coupling_in[i].wait()
+            for g in range(4 * i, 4 * i + 4):
+                packed_ref[g] = side_by_side(coupling_ref, g)
         fars = []
-        coupling_in[a].wait()
-        for g in (2 * a, 2 * a + 1):
+        for g in range(4 * i - 4, 4 * i) if i else ():
             rows = [at_ref[j, g] for j in range(many)]
-            fars.append(dot(picked(table_ref, rows, left), side_by_side(coupling_ref, g), NT))
-        far_ref[a] = jnp.concatenate(fars, axis=1)
+            fars.append(dot(picked(table_ref, rows, left), packed_ref[g], NT))
+            if g % 2 == 1:
+                far_ref[g // 2] = jnp.concatenate(fars[-2:], axis=1)
     basis_in.wait()
     for a in range(pairs):
         basis_packed_ref[a] = jnp.concatenate([basis_ref[2 * a], basis_ref[2 * a + 1]], axis=1)
@@ -290,22 +290,24 @@
     dma = lambda count: pltpu.SemaphoreType.DMA((count,))
     params = lambda mib: pltpu.CompilerParams(vmem_limit_bytes=mib * 2**20)
 
-    rim, live, parent_coef = pl.pallas_call(
+    rim, live, sent = pl.pallas_call(
         up_kernel,
         name="up",
         out_shape=[
             shape((pairs + 2, sides, 2 * rank), bf16),
             shape((pairs, sides, 2 * width), bf16),
-            shape((own, sides, 2 * rank), bf16),
+            pltpu.HBM((n // 2 * own, sides, 2 * rank), bf16),
         ],
         in_specs=[HBM] * 4,
-        out_specs=[VMEM] * 3,
+        out_specs=[VMEM, VMEM, HBM],
         scratch_shapes=[
             pltpu.SMEM((leaves,), jnp.int32),
             pltpu.VMEM((sides, leaves * width), bf16),
             pltpu.VMEM((leaves, width, rank), bf16),
             pltpu.VMEM((leaves, rank, rank), bf16),
+            pltpu.VMEM((own, sides, 2 * rank), bf16),
             dma(4),
+            dma(n // 2),
         ],
         compiler_params=params(8),
     )(*keep(panel_counts, charges.T, basis, transfer))
@@ -313,15 +315,6 @@
     even = lax.ppermute(rim, axes, [(i, i ^ 1) for i in range(total)])
     steps = [(i, i + 1) for i in range(1, total - 1, 2)]
     odd = lax.ppermute(rim, axes, steps + [(b, a) for a, b in steps])
-    sent = pl.pallas_call(
-        copies_kernel,
-        name="copies",
-        out_shape=pltpu.HBM((n // 2 * own, sides, 2 * rank), bf16),
-        in_specs=[VMEM],
-        out_specs=HBM,
-        scratch_shapes=[dma(n // 2)],
-        compiler_params=params(4),
-    )(parent_coef)
     same = lax.all_to_all(sent, "gz", 0, 0, tiled=True)
 
     parent_packed, near, rim_near, leaf_at, parent_at = pl.pallas_call(
@@ -370,10 +363,11 @@
             pltpu.VMEM((3 * leaves, sides, 2 * rank), bf16),
             pltpu.SMEM((many, leaves), jnp.int32),
             pltpu.VMEM(leaf_coupling.shape, bf16),
+            pltpu.VMEM((leaves, rank, many * rank), bf16),
             pltpu.VMEM(basis.shape, bf16),
-            dma(3 + leaves // 2),
-        ],
-        compiler_params=params(16),
+            dma(3 + leaves // 4),
+        ],
+        compiler_params=params(20),
     )(leaf_at, rim, even, odd, rim_near, *keep(leaf_coupling, transfer, basis))
 
     out = pl.pallas_call(

time: 32.3 us -> 30.6 us (0.947)
  Pallas kernels: 15.1 us -> 12.9 us
  waiting for transfers between devices: 4.69 us -> 5.15 us
    pallas_call x1, Pallas kernels: 6.66 us -> 4.47 us  [per_device(): pl.pallas_call(functools.partial(leaf_kernel, axes), name='leaf', out_sha...]
    pallas_call x1 -> x0, Pallas kernels: 0.73 us -> none  [per_device(): pl.pallas_call(copies_kernel, name='copies', out_shape=pltpu.HBM((n // 2...]
    pallas_call x1, Pallas kernels: 1.82 us -> 2.55 us  [per_device(): pl.pallas_call(up_kernel, name='up', out_shape=[shape((pairs + 2, sides,...]
    ppermute x2, waiting for transfers between devices: 0.01 us -> 0.46 us  [per_device(): other = [lax.ppermute(piece, 'gp', [(0, 1), (1, 0)]) for piece in pieces]]
  transfers between devices with their start and end apart: 5 -> 5, of which waited for: 1 -> 2; matrix products, arithmetic and copies ran while one was open for 0% -> 0% of each run, Pallas kernels for 30% -> 25%
where the time goes in v17:
time: 30.6 us; the launch traced here: 30.4 us
  Pallas kernels  12.9 us (42%)
  starting transfers between devices  12.3 us (40%)
  waiting for transfers between devices  5.15 us (17%)
    all_to_all x1, starting transfers between devices, per_device(): same = lax.all_to_all(sent, 'gz', 0, 0, tiled=True)  6.33 us
    all_to_all x1, waiting for transfers between devices, per_device(): same = lax.all_to_all(sent, 'gz', 0, 0, tiled=True)  4.68 us
    pallas_call x1, Pallas kernels, per_device(): pl.pallas_call(functools.partial(leaf_kernel, axes), name='leaf', out_sha...  4.47 us
    ppermute x2, starting transfers between devices, per_device(): other = [lax.ppermute(piece, 'gp', [(0, 1), (1, 0)]) for piece in pieces]  3.77 us
    pallas_call x1, Pallas kernels, per_device(): pl.pallas_call(functools.partial(mid_kernel, axes), name='mid', out_shape...  3.09 us
    pallas_call x1, Pallas kernels, per_device(): pl.pallas_call(functools.partial(down_kernel, 'gp'), name='down', out_sha...  2.76 us
    pallas_call x1, Pallas kernels, per_device(): pl.pallas_call(up_kernel, name='up', out_shape=[shape((pairs + 2, sides,...  2.55 us
    ppermute x1, starting transfers between devices, per_device(): even = lax.ppermute(rim, axes, [(i, i ^ 1) for i in range(total)])  1.52 us
  transfers between devices with their start and end apart: 5, of which 2 were waited for; matrix products, arithmetic and copies ran while one was open for 0% of the time, Pallas kernels for 25%

profile of v17, /device:TPU:0, one launch (start us, length us, event | category | flops | bytes accessed | tf_op | source)
XLA Modules:
  0.0 30.4 jit_solution(3656542716409992671)
XLA Ops:
  0.0 2.6 %up.1 = (bf16[18,32,128]{2,1,0:T(8,128)(2,1)S(1)}, bf16[16,32,128]{2,1,0:T(8,128)(2,1)S(1)}, bf16[32,32,128]{2,1,0:T(8,128)(2,1)}) custom-call(s32[32]{0:T(128)} %counts_hbm.3, bf16[32,2048]{1,0:T(8,128)(2,1)} %bitcast.3, bf16[32,64,64]{2,1,0:T(8,128)(2,1)} %basis_hbm.3, bf16[32,64,64]{2,1,0:T(8,128)(2,1)} %transfer_hbm.3), custom_call_target="tpu_custom_call" | custom-call | tf_op jit(solution)/shard_map/up/pallas_call | solution.py:293
  2.6 6.3 %all-to-all-start = ((bf16[32,32,128]{2,1,0:T(8,128)(2,1)}), bf16[32,32,128]{2,1,0:T(8,128)(2,1)S(1)}, u32[]{:S(2)}, u32[]{:S(2)}) async-start(bf16[32,32,128]{2,1,0:T(8,128)(2,1)} %get-tuple-element.21), calls=%async_computation | async-start | bytes 524288 | tf_op jit(solution)/shard_map/all_to_all | solution.py:318
  8.9 1.5 %collective-permute-start.2 = (bf16[18,32,128]{2,1,0:T(8,128)(2,1)S(1)}, bf16[18,32,128]{2,1,0:T(8,128)(2,1)S(1)}, u32[]{:S(2)}, u32[]{:S(2)}) collective-permute-start(bf16[18,32,128]{2,1,0:T(8,128)(2,1)S(1)} %get-tuple-element.26.rim_ref), channel_id=1, source_target_pairs={{0,1},{1,0},{2,3},{3,2},{4,5},{5,4},{6,7},{7,6},{8,9},{9,8},{10,11... | collective-permute-start | bytes 442376 | tf_op jit(solution)/shard_map/ppermute | solution.py:315
  10.4 0.7 %collective-permute-start.3 = (bf16[18,32,128]{2,1,0:T(8,128)(2,1)S(1)}, bf16[18,32,128]{2,1,0:T(8,128)(2,1)S(1)}, u32[]{:S(2)}, u32[]{:S(2)}) collective-permute-start(bf16[18,32,128]{2,1,0:T(8,128)(2,1)S(1)} %get-tuple-element.26.rim_ref), channel_id=1, source_target_pairs={{1,2},{3,4},{5,6},{7,8},{9,10},{11,12},{13,14},{15,16},{17,18},{19... | collective-permute-start | bytes 442376 | tf_op jit(solution)/shard_map/ppermute | solution.py:317
  11.1 3.1 %mid.1 = (bf16[16,64,1024]{2,1,0:T(8,128)(2,1)S(1)}, f32[16,32,128]{2,1,0:T(8,128)S(1)}, bf16[2,64,64]{2,1,0:T(8,128)(2,1)S(1)}, s32[16,32]{1,0:T(8,128)S(1)}, s32[16,16]{1,0:T(8,128)S(1)}) custom-call(bf16[16,32,128]{2,1,0:T(8,128)(2,1)S(1)} %get-tuple-element.19.live_ref, bf16[32,3,64,64]{3,2,1,0:T(8,128)(2,1)} %near_hbm.1, ...), custom_call_target="tpu_custom_call" | custom-call | tf_op jit(solution)/shard_map/mid/pallas_call | solution.py:320
  14.2 4.7 %all-to-all-done.whole_ref.same_ref = bf16[32,32,128]{2,1,0:T(8,128)(2,1)S(1)} async-done(((bf16[32,32,128]{2,1,0:T(8,128)(2,1)}), bf16[32,32,128]{2,1,0:T(8,128)(2,1)S(1)}, u32[]{:S(2)}, u32[]{:S(2)}) %all-to-all-start) | async-done | bytes 262176 | tf_op jit(solution)/shard_map/all_to_all | solution.py:318
  18.9 3.7 %collective-permute-start = (bf16[16,32,128]{2,1,0:T(8,128)(2,1)S(1)}, bf16[16,32,128]{2,1,0:T(8,128)(2,1)S(1)}, u32[]{:S(2)}, u32[]{:S(2)}) collective-permute-start(bf16[16,32,128]{2,1,0:T(8,128)(2,1)S(1)} %get-tuple-element.22), channel_id=1, source_target_pairs={{0,1},{1,0},{2,3},{3,2},{4,5},{5,4},{6,7},{7,6},{8,9},{9,8},{10,11... | collective-permute-start | bytes 393224 | tf_op jit(solution)/shard_map/ppermute | solution.py:349
  22.6 0.1 collective-permute-start.1
  22.7 0.0 collective-permute-done.2.even_ref
  22.7 0.0 collective-permute-done.3.odd_ref
  22.7 4.5 %leaf.1 = (f32[16,32,128]{2,1,0:T(8,128)S(1)}, f32[2,32,128]{2,1,0:T(8,128)S(1)}, bf16[32,64,64]{2,1,0:T(8,128)(2,1)S(1)}, bf16[16,64,128]{2,1,0:T(8,128)(2,1)S(1)}) custom-call(s32[16,32]{1,0:T(8,128)S(1)} %get-tuple-element.25.at_vmem, bf16[18,32,128]{2,1,0:T(8,128)(2,1)S(1)} %get-tuple-element.26.rim_ref, ...), custom_call_target="tpu_custom_call" | custom-call | tf_op jit(solution)/shard_map/leaf/pallas_call | solution.py:351
  27.1 0.0 collective-permute-done.other_refs_0_
  27.2 0.5 %collective-permute-done.1.other_refs_1_ = bf16[16,32,128]{2,1,0:T(8,128)(2,1)S(1)} collective-permute-done((bf16[16,32,128]{2,1,0:T(8,128)(2,1)S(1)}, bf16[16,32,128]{2,1,0:T(8,128)(2,1)S(1)}, u32[]{:S(2)}, u32[]{:S(2)}) %collective-permute-start.1) | collective-permute-done | bytes 131104 | tf_op jit(solution)/shard_map/ppermute | solution.py:349
  27.6 2.8 %down.1 = bf16[32,2048]{1,0:T(8,128)(2,1)} custom-call(s32[16,16]{1,0:T(8,128)S(1)} %get-tuple-element.20.at_ref.at_vmem, bf16[32,32,128]{2,1,0:T(8,128)(2,1)S(1)} %all-to-all-done.whole_ref.same_ref, bf16[16,32,128]{2,1,0:T(8,128)(2,1)S(1)} %collective-permute-done.other_refs_0_, bf16[16,32,128]{2,1,0:T(8,128)(2,1)S(1)} %collective-permute-done.1.other_refs_1_, ...), custom_call_target="tpu_custom_call" | custom-call | tf_op jit(solution)/shard_map/down/pallas_call | solution.py:373
  (1 shorter events, 0.0 us)
Async XLA Ops:
  2.6 16.3 %all-to-all-start = ((bf16[32,32,128]{2,1,0:T(8,128)(2,1)}), bf16[32,32,128]{2,1,0:T(8,128)(2,1)S(1)}, u32[]{:S(2)}, u32[]{:S(2)}) async-start(bf16[32,32,128]{2,1,0:T(8,128)(2,1)} %get-tuple-element.21), calls=%async_computation | async-start | bytes 524288 | tf_op jit(solution)/shard_map/all_to_all | solution.py:318
  8.9 13.8 %collective-permute-start.2 = (bf16[18,32,128]{2,1,0:T(8,128)(2,1)S(1)}, bf16[18,32,128]{2,1,0:T(8,128)(2,1)S(1)}, u32[]{:S(2)}, u32[]{:S(2)}) collective-permute-start(bf16[18,32,128]{2,1,0:T(8,128)(2,1)S(1)} %get-tuple-element.26.rim_ref), channel_id=1, source_target_pairs={{0,1},{1,0},{2,3},{3,2},{4,5},{5,4},{6,7},{7,6},{8,9},{9,8},{10,11... | collective-permute-start | bytes 442376 | tf_op jit(solution)/shard_map/ppermute | solution.py:315
  10.4 12.2 %collective-permute-start.3 = (bf16[18,32,128]{2,1,0:T(8,128)(2,1)S(1)}, bf16[18,32,128]{2,1,0:T(8,128)(2,1)S(1)}, u32[]{:S(2)}, u32[]{:S(2)}) collective-permute-start(bf16[18,32,128]{2,1,0:T(8,128)(2,1)S(1)} %get-tuple-element.26.rim_ref), channel_id=1, source_target_pairs={{1,2},{3,4},{5,6},{7,8},{9,10},{11,12},{13,14},{15,16},{17,18},{19... | collective-permute-start | bytes 442376 | tf_op jit(solution)/shard_map/ppermute | solution.py:317
  18.9 8.3 %collective-permute-start = (bf16[16,32,128]{2,1,0:T(8,128)(2,1)S(1)}, bf16[16,32,128]{2,1,0:T(8,128)(2,1)S(1)}, u32[]{:S(2)}, u32[]{:S(2)}) collective-permute-start(bf16[16,32,128]{2,1,0:T(8,128)(2,1)S(1)} %get-tuple-element.22), channel_id=1, source_target_pairs={{0,1},{1,0},{2,3},{3,2},{4,5},{5,4},{6,7},{7,6},{8,9},{9,8},{10,11... | collective-permute-start | bytes 393224 | tf_op jit(solution)/shard_map/ppermute | solution.py:349
  22.6 5.0 %collective-permute-start.1 = (bf16[16,32,128]{2,1,0:T(8,128)(2,1)S(1)}, bf16[16,32,128]{2,1,0:T(8,128)(2,1)S(1)}, u32[]{:S(2)}, u32[]{:S(2)}) collective-permute-start(bf16[16,32,128]{2,1,0:T(8,128)(2,1)S(1)} %get-tuple-element.23), channel_id=1, source_target_pairs={{0,1},{1,0},{2,3},{3,2},{4,5},{5,4},{6,7},{7,6},{8,9},{9,8},{10,11... | collective-permute-start | bytes 393224 | tf_op jit(solution)/shard_map/ppermute | solution.py:349

commit v18 on v17

--- a/solution.py
+++ b/solution.py
@@ -55,14 +55,14 @@
 
 
 def up_kernel(
-    counts_hbm, charges_hbm, basis_hbm, transfer_hbm,
-    rim_ref, live_ref, sent_hbm,
+    axes, counts_hbm, charges_hbm, basis_hbm, transfer_hbm, near_hbm,
+    rim_ref, even_rim_ref, live_ref, sent_hbm, near_ref,
     counts_ref, charges_ref, basis_ref, transfer_ref, parents_ref, sems, sent_sems,
 ):
-    counts_in, charges_in, basis_in, transfer_in = start_all(
+    counts_in, charges_in, basis_in, transfer_in, near_in = start_all(
         [
             (counts_hbm, counts_ref), (charges_hbm, charges_ref),
-            (basis_hbm, basis_ref), (transfer_hbm, transfer_ref),
+            (basis_hbm, basis_ref), (transfer_hbm, transfer_ref), (near_hbm, near_ref),
         ],
         sems,
     )
@@ -81,6 +81,7 @@
         lives.append(live)
     rim_ref[pairs] = lives[0]
     rim_ref[pairs + 1] = lives[-1]
+    even_rim_ref[pairs] = jnp.where(lax.rem(position(axes), 2) == 0, lives[-1], lives[0])
     basis_in.wait()
     none = jnp.zeros_like(lives[0])
     coefs = []
@@ -90,6 +91,7 @@
         coef = dot(both, basis_ref[2 * a : 2 * a + 2].reshape(2 * width, rank), NN)
         coef = jnp.concatenate([coef[:sides], coef[sides:]], axis=1).astype(jnp.bfloat16)
         rim_ref[a] = coef
+        even_rim_ref[a] = coef
         coefs.append(coef)
     transfer_in.wait()
     sums = [
@@ -101,6 +103,7 @@
     copies = sent_hbm.shape[0] // own
     for copy in start_all([(parents_ref, sent_hbm.at[pl.ds(own * c, own)]) for c in range(copies)], sent_sems):
         copy.wait()
+    near_in.wait()
 
 
 def side_by_side(blocks_ref, g):
@@ -108,23 +111,20 @@
 
 
 def mid_kernel(
-    axes, live_ref, near_hbm, parent_hbm, leaf_partners_hbm, parent_partners_hbm,
+    axes, live_ref, near_ref, parent_hbm, leaf_partners_hbm, parent_partners_hbm,
     parent_packed_ref, near_out_ref, rim_near_ref, leaf_at_ref, parent_at_ref,
-    near_ref, parent_ref, sems,
+    parent_ref, sems,
 ):
     parents, many, rank, _ = parent_ref.shape
     leaves = near_ref.shape[0]
     width = near_ref.shape[2]
     pairs = leaves // 2
     started = start_all(
-        [(near_hbm, near_ref)]
-        + [(parent_hbm.at[pl.ds(4 * i, 4)], parent_ref.at[pl.ds(4 * i, 4)]) for i in range(parents // 4)]
+        [(parent_hbm.at[pl.ds(4 * i, 4)], parent_ref.at[pl.ds(4 * i, 4)]) for i in range(parents // 4)]
         + [(leaf_partners_hbm, leaf_at_ref), (parent_partners_hbm, parent_at_ref)],
         sems,
     )
-    near_in = started[0]
-    parent_in = started[1:-2]
-    near_in.wait()
+    parent_in = started[:-2]
     rim_near_ref[0] = near_ref[0, 0]
     rim_near_ref[1] = near_ref[leaves - 1, 2]
     for a in range(pairs):
@@ -196,7 +196,7 @@
     ):
         for a in range(pairs):
             spread_pair(table_ref, base + 2 * a, ref[a], rank)
-    before = jnp.where(parity == 1, even_ref[pairs + 1], odd_ref[pairs + 1])
+    before = jnp.where(parity == 1, even_ref[pairs], odd_ref[pairs + 1])
     after = jnp.where(parity == 1, odd_ref[pairs], even_ref[pairs])
     low = dot(before[:, width:], rim_near_ref[0], NT)
     high = dot(after[:, :width], rim_near_ref[1], NT)
@@ -290,29 +290,31 @@
     dma = lambda count: pltpu.SemaphoreType.DMA((count,))
     params = lambda mib: pltpu.CompilerParams(vmem_limit_bytes=mib * 2**20)
 
-    rim, live, sent = pl.pallas_call(
-        up_kernel,
+    rim, even_rim, live, sent, near_held = pl.pallas_call(
+        functools.partial(up_kernel, axes),
         name="up",
         out_shape=[
             shape((pairs + 2, sides, 2 * rank), bf16),
+            shape((pairs + 1, sides, 2 * rank), bf16),
             shape((pairs, sides, 2 * width), bf16),
             pltpu.HBM((n // 2 * own, sides, 2 * rank), bf16),
-        ],
-        in_specs=[HBM] * 4,
-        out_specs=[VMEM, VMEM, HBM],
+            shape(near_blocks.shape, bf16),
+        ],
+        in_specs=[HBM] * 5,
+        out_specs=[VMEM, VMEM, VMEM, HBM, VMEM],
         scratch_shapes=[
             pltpu.SMEM((leaves,), jnp.int32),
             pltpu.VMEM((sides, leaves * width), bf16),
             pltpu.VMEM((leaves, width, rank), bf16),
             pltpu.VMEM((leaves, rank, rank), bf16),
             pltpu.VMEM((own, sides, 2 * rank), bf16),
-            dma(4),
+            dma(5),
             dma(n // 2),
         ],
         compiler_params=params(8),
-    )(*keep(panel_counts, charges.T, basis, transfer))
-
-    even = lax.ppermute(rim, axes, [(i, i ^ 1) for i in range(total)])
+    )(*keep(panel_counts, charges.T, basis, transfer, near_blocks))
+
+    even = lax.ppermute(even_rim, axes, [(i, i ^ 1) for i in range(total)])
     steps = [(i, i + 1) for i in range(1, total - 1, 2)]
     odd = lax.ppermute(rim, axes, steps + [(b, a) for a, b in steps])
     same = lax.all_to_all(sent, "gz", 0, 0, tiled=True)
@@ -327,15 +329,14 @@
             shape((many, leaves), jnp.int32),
             shape((parents, many), jnp.int32),
         ],
-        in_specs=[VMEM] + [HBM] * 4,
+        in_specs=[VMEM, VMEM] + [HBM] * 3,
         out_specs=[VMEM] * 5,
         scratch_shapes=[
-            pltpu.VMEM(near_blocks.shape, bf16),
             pltpu.VMEM(parent_coupling.shape, bf16),
-            dma(3 + parents // 4),
+            dma(2 + parents // 4),
         ],
         compiler_params=params(12),
-    )(live, *keep(near_blocks, parent_coupling, leaf_partners.T, parent_partners))
+    )(live, near_held, *keep(parent_coupling, leaf_partners.T, parent_partners))
 
     quarter = shape((n // 4 * own, sides, 2 * rank), bf16)
     pieces = pl.pallas_call(

time: 30.6 us -> 32.4 us (1.059)
  the two profiles are of different devices: /device:TPU:0 before, /device:TPU:3 now
where the time goes in v18:
time: 32.4 us; the launch traced here: 32.1 us
  starting transfers between devices  13.5 us (42%)
  Pallas kernels  12.2 us (38%)
  waiting for transfers between devices  3.78 us (12%)
  local copies, waits for them, and re-layouts  2.55 us (8%)
    ppermute x1, starting transfers between devices, per_device(): odd = lax.ppermute(rim, axes, steps + [(b, a) for a, b in steps])  7.23 us
    all_to_all x1, starting transfers between devices, per_device(): same = lax.all_to_all(sent, 'gz', 0, 0, tiled=True)  4.59 us
    pallas_call x1, Pallas kernels, per_device(): pl.pallas_call(functools.partial(leaf_kernel, axes), name='leaf', out_sha...  4.46 us
    ppermute x1, waiting for transfers between devices, per_device(): even = lax.ppermute(even_rim, axes, [(i, i ^ 1) for i in range(total)])  2.93 us
    pallas_call x1, Pallas kernels, per_device(): pl.pallas_call(functools.partial(down_kernel, 'gp'), name='down', out_sha...  2.75 us
    pallas_call x1, Pallas kernels, per_device(): pl.pallas_call(functools.partial(up_kernel, axes), name='up', out_shape=[...  2.56 us
    unnamed x4, local copies, waits for them, and re-layouts  2.55 us
    pallas_call x1, Pallas kernels, per_device(): pl.pallas_call(functools.partial(mid_kernel, axes), name='mid', out_shape...  2.44 us
  transfers between devices with their start and end apart: 5, of which 2 were waited for; matrix products, arithmetic and copies ran while one was open for 0% of the time, Pallas kernels for 22%

profile of v18, /device:TPU:3, one launch (start us, length us, event | category | flops | bytes accessed | tf_op | source)
XLA Modules:
  0.0 32.1 jit_solution(6790297520401171569)
XLA Ops:
  0.0 2.6 %up.1 = (bf16[18,32,128]{2,1,0:T(8,128)(2,1)S(1)}, bf16[17,32,128]{2,1,0:T(8,128)(2,1)S(1)}, bf16[16,32,128]{2,1,0:T(8,128)(2,1)S(1)}, bf16[32,32,128]{2,1,0:T(8,128)(2,1)}, bf16[32,3,64,64]{3,2,1,0:T(8,128)(2,1)S(1)}) custom-call(s32[32]{0:T(128)} %counts_hbm.3, bf16[32,2048]{1,0:T(8,128)(2,1)} %bitcast.3, bf16[32,64,64]{2,1,0:T(8,128)(2,1)} %basis_hbm.3, ...), custom_call_target="tpu_custom_call" | custom-call | tf_op jit(solution)/shard_map/up/pallas_call | solution.py:293
  2.6 0.0 copy-start
  2.6 1.1 %copy-done = bf16[32,3,64,64]{3,2,1,0:T(8,128)(2,1)} copy-done((bf16[32,3,64,64]{3,2,1,0:T(8,128)(2,1)}, bf16[32,3,64,64]{3,2,1,0:T(8,128)(2,1)S(1)}, u32[]{:S(2)}) %copy-start) | copy-done | bytes 786456
  3.7 4.6 %all-to-all-start = ((bf16[32,32,128]{2,1,0:T(8,128)(2,1)}), bf16[32,32,128]{2,1,0:T(8,128)(2,1)S(1)}, u32[]{:S(2)}, u32[]{:S(2)}) async-start(bf16[32,32,128]{2,1,0:T(8,128)(2,1)} %get-tuple-element.24), calls=%async_computation | async-start | bytes 524288 | tf_op jit(solution)/shard_map/all_to_all | solution.py:320
  8.3 7.2 %collective-permute-start.3 = (bf16[18,32,128]{2,1,0:T(8,128)(2,1)S(1)}, bf16[18,32,128]{2,1,0:T(8,128)(2,1)S(1)}, u32[]{:S(2)}, u32[]{:S(2)}) collective-permute-start(bf16[18,32,128]{2,1,0:T(8,128)(2,1)S(1)} %get-tuple-element.29.rim_ref), channel_id=1, source_target_pairs={{1,2},{3,4},{5,6},{7,8},{9,10},{11,12},{13,14},{15,16},{17,18},{19... | collective-permute-start | bytes 442376 | tf_op jit(solution)/shard_map/ppermute | solution.py:319
  15.6 0.1 collective-permute-start.2
  15.6 0.0 copy-start.1
  15.6 1.4 %copy-done.1 = bf16[32,3,64,64]{3,2,1,0:T(8,128)(2,1)S(1)} copy-done((bf16[32,3,64,64]{3,2,1,0:T(8,128)(2,1)S(1)}, bf16[32,3,64,64]{3,2,1,0:T(8,128)(2,1)}, u32[]{:S(2)}) %copy-start.1) | copy-done | bytes 786456
  17.0 2.4 %mid.1 = (bf16[16,64,1024]{2,1,0:T(8,128)(2,1)S(1)}, f32[16,32,128]{2,1,0:T(8,128)S(1)}, bf16[2,64,64]{2,1,0:T(8,128)(2,1)S(1)}, s32[16,32]{1,0:T(8,128)S(1)}, s32[16,16]{1,0:T(8,128)S(1)}) custom-call(bf16[16,32,128]{2,1,0:T(8,128)(2,1)S(1)} %get-tuple-element.21.live_ref, bf16[32,3,64,64]{3,2,1,0:T(8,128)(2,1)S(1)} %copy-done.1, ...), custom_call_target="tpu_custom_call" | custom-call | tf_op jit(solution)/shard_map/mid/pallas_call | solution.py:322
  19.5 0.0 all-to-all-done.whole_ref.same_ref
  19.5 1.5 %collective-permute-start = (bf16[16,32,128]{2,1,0:T(8,128)(2,1)S(1)}, bf16[16,32,128]{2,1,0:T(8,128)(2,1)S(1)}, u32[]{:S(2)}, u32[]{:S(2)}) collective-permute-start(bf16[16,32,128]{2,1,0:T(8,128)(2,1)S(1)} %get-tuple-element.25), channel_id=1, source_target_pairs={{0,1},{1,0},{2,3},{3,2},{4,5},{5,4},{6,7},{7,6},{8,9},{9,8},{10,11... | collective-permute-start | bytes 393224 | tf_op jit(solution)/shard_map/ppermute | solution.py:350
  21.1 0.1 collective-permute-start.1
  21.1 2.9 %collective-permute-done.2.even_ref = bf16[17,32,128]{2,1,0:T(8,128)(2,1)S(1)} collective-permute-done((bf16[17,32,128]{2,1,0:T(8,128)(2,1)S(1)}, bf16[17,32,128]{2,1,0:T(8,128)(2,1)S(1)}, u32[]{:S(2)}, u32[]{:S(2)}) %collective-permute-start.2) | collective-permute-done | bytes 139296 | tf_op jit(solution)/shard_map/ppermute | solution.py:317
  24.1 0.0 collective-permute-done.3.odd_ref
  24.1 4.5 %leaf.1 = (f32[16,32,128]{2,1,0:T(8,128)S(1)}, f32[2,32,128]{2,1,0:T(8,128)S(1)}, bf16[32,64,64]{2,1,0:T(8,128)(2,1)S(1)}, bf16[16,64,128]{2,1,0:T(8,128)(2,1)S(1)}) custom-call(s32[16,32]{1,0:T(8,128)S(1)} %get-tuple-element.28.at_vmem, bf16[18,32,128]{2,1,0:T(8,128)(2,1)S(1)} %get-tuple-element.29.rim_ref, ...), custom_call_target="tpu_custom_call" | custom-call | tf_op jit(solution)/shard_map/leaf/pallas_call | solution.py:352
  28.5 0.0 collective-permute-done.other_refs_0_
  28.6 0.8 %collective-permute-done.1.other_refs_1_ = bf16[16,32,128]{2,1,0:T(8,128)(2,1)S(1)} collective-permute-done((bf16[16,32,128]{2,1,0:T(8,128)(2,1)S(1)}, bf16[16,32,128]{2,1,0:T(8,128)(2,1)S(1)}, u32[]{:S(2)}, u32[]{:S(2)}) %collective-permute-start.1) | collective-permute-done | bytes 131104 | tf_op jit(solution)/shard_map/ppermute | solution.py:350
  29.4 2.7 %down.1 = bf16[32,2048]{1,0:T(8,128)(2,1)} custom-call(s32[16,16]{1,0:T(8,128)S(1)} %get-tuple-element.23.at_ref.at_vmem, bf16[32,32,128]{2,1,0:T(8,128)(2,1)S(1)} %all-to-all-done.whole_ref.same_ref, bf16[16,32,128]{2,1,0:T(8,128)(2,1)S(1)} %collective-permute-done.other_refs_0_, bf16[16,32,128]{2,1,0:T(8,128)(2,1)S(1)} %collective-permute-done.1.other_refs_1_, ...), custom_call_target="tpu_custom_call" | custom-call | tf_op jit(solution)/shard_map/down/pallas_call | solution.py:374
  (1 shorter events, 0.0 us)
Async XLA Ops:
  2.6 1.2 %copy-start = (bf16[32,3,64,64]{3,2,1,0:T(8,128)(2,1)}, bf16[32,3,64,64]{3,2,1,0:T(8,128)(2,1)S(1)}, u32[]{:S(2)}) copy-start(bf16[32,3,64,64]{3,2,1,0:T(8,128)(2,1)S(1)} %get-tuple-element.22.near_ref) | copy-start | bytes 2359300
  3.7 15.8 %all-to-all-start = ((bf16[32,32,128]{2,1,0:T(8,128)(2,1)}), bf16[32,32,128]{2,1,0:T(8,128)(2,1)S(1)}, u32[]{:S(2)}, u32[]{:S(2)}) async-start(bf16[32,32,128]{2,1,0:T(8,128)(2,1)} %get-tuple-element.24), calls=%async_computation | async-start | bytes 524288 | tf_op jit(solution)/shard_map/all_to_all | solution.py:320
  8.3 15.7 %collective-permute-start.3 = (bf16[18,32,128]{2,1,0:T(8,128)(2,1)S(1)}, bf16[18,32,128]{2,1,0:T(8,128)(2,1)S(1)}, u32[]{:S(2)}, u32[]{:S(2)}) collective-permute-start(bf16[18,32,128]{2,1,0:T(8,128)(2,1)S(1)} %get-tuple-element.29.rim_ref), channel_id=1, source_target_pairs={{1,2},{3,4},{5,6},{7,8},{9,10},{11,12},{13,14},{15,16},{17,18},{19... | collective-permute-start | bytes 442376 | tf_op jit(solution)/shard_map/ppermute | solution.py:319
  15.6 8.5 %collective-permute-start.2 = (bf16[17,32,128]{2,1,0:T(8,128)(2,1)S(1)}, bf16[17,32,128]{2,1,0:T(8,128)(2,1)S(1)}, u32[]{:S(2)}, u32[]{:S(2)}) collective-permute-start(bf16[17,32,128]{2,1,0:T(8,128)(2,1)S(1)} %get-tuple-element.30), channel_id=1, source_target_pairs={{0,1},{1,0},{2,3},{3,2},{4,5},{5,4},{6,7},{7,6},{8,9},{9,8},{10,11... | collective-permute-start | bytes 417800 | tf_op jit(solution)/shard_map/ppermute | solution.py:317
  15.6 1.4 %copy-start.1 = (bf16[32,3,64,64]{3,2,1,0:T(8,128)(2,1)S(1)}, bf16[32,3,64,64]{3,2,1,0:T(8,128)(2,1)}, u32[]{:S(2)}) copy-start(bf16[32,3,64,64]{3,2,1,0:T(8,128)(2,1)} %copy-done) | copy-start | bytes 2359300
  19.5 9.0 %collective-permute-start = (bf16[16,32,128]{2,1,0:T(8,128)(2,1)S(1)}, bf16[16,32,128]{2,1,0:T(8,128)(2,1)S(1)}, u32[]{:S(2)}, u32[]{:S(2)}) collective-permute-start(bf16[16,32,128]{2,1,0:T(8,128)(2,1)S(1)} %get-tuple-element.25), channel_id=1, source_target_pairs={{0,1},{1,0},{2,3},{3,2},{4,5},{5,4},{6,7},{7,6},{8,9},{9,8},{10,11... | collective-permute-start | bytes 393224 | tf_op jit(solution)/shard_map/ppermute | solution.py:350
  21.1 8.3 %collective-permute-start.1 = (bf16[16,32,128]{2,1,0:T(8,128)(2,1)S(1)}, bf16[16,32,128]{2,1,0:T(8,128)(2,1)S(1)}, u32[]{:S(2)}, u32[]{:S(2)}) collective-permute-start(bf16[16,32,128]{2,1,0:T(8,128)(2,1)S(1)} %get-tuple-element.26), channel_id=1, source_target_pairs={{0,1},{1,0},{2,3},{3,2},{4,5},{5,4},{6,7},{7,6},{8,9},{9,8},{10,11... | collective-permute-start | bytes 393224 | tf_op jit(solution)/shard_map/ppermute | solution.py:350

commit v19 on v17

--- a/solution.py
+++ b/solution.py
@@ -56,8 +56,8 @@
 
 def up_kernel(
     counts_hbm, charges_hbm, basis_hbm, transfer_hbm,
-    rim_ref, live_ref, sent_hbm,
-    counts_ref, charges_ref, basis_ref, transfer_ref, parents_ref, sems, sent_sems,
+    rim_ref, live_ref, parents_ref, sent_hbm,
+    counts_ref, charges_ref, basis_ref, transfer_ref, sems, sent_sems,
 ):
     counts_in, charges_in, basis_in, transfer_in = start_all(
         [
@@ -153,11 +153,13 @@
     parent_at_ref[...] = wanted ^ (lax.broadcasted_iota(jnp.int32, wanted.shape, 1) & 1)
 
 
-def halves_kernel(whole_ref, at_ref, first_ref, second_ref):
+def halves_kernel(axis, whole_ref, own_ref, at_ref, first_ref, second_ref):
     del at_ref
-    half = first_ref.shape[0]
-    first_ref[...] = whole_ref[:half]
-    second_ref[...] = whole_ref[half:]
+    own, half = own_ref.shape[0], first_ref.shape[0]
+    count = lax.axis_size(axis)
+    for t in range(2 * half):
+        source = lax.rem(lax.axis_index(axis) + 1 + t // own, count) * own + t % own
+        (first_ref if t < half else second_ref)[t % half] = whole_ref[source]
 
 
 def spread_pair(table_ref, at, pair, width):
@@ -180,9 +182,10 @@
     far_ref, edge_ref, transfer_ref, basis_packed_ref, table_ref, at_ref, coupling_ref, packed_ref, basis_ref, sems,
 ):
     leaves, many, rank, _ = coupling_ref.shape
+    chunks = [(at, 4) for at in range(0, leaves - 4, 4)] + [(leaves - 4, 2), (leaves - 2, 2)]
     at_in, *coupling_in, transfer_in, basis_in = start_all(
         [(at_vmem, at_ref)]
-        + [(coupling_hbm.at[pl.ds(4 * i, 4)], coupling_ref.at[pl.ds(4 * i, 4)]) for i in range(leaves // 4)]
+        + [(coupling_hbm.at[pl.ds(at, size)], coupling_ref.at[pl.ds(at, size)]) for at, size in chunks]
         + [(transfer_hbm, transfer_ref), (basis_hbm, basis_ref)],
         sems,
     )
@@ -203,13 +206,16 @@
     edge_ref[0] = jnp.concatenate([low, jnp.zeros_like(low)], axis=1)
     edge_ref[1] = jnp.concatenate([jnp.zeros_like(high), high], axis=1)
     at_in.wait()
-    for i in range(leaves // 4 + 1):
-        if i < leaves // 4:
+    ready = []
+    for i in range(len(chunks) + 1):
+        now, ready = ready, []
+        if i < len(chunks):
             coupling_in[i].wait()
-            for g in range(4 * i, 4 * i + 4):
+            ready = range(chunks[i][0], sum(chunks[i]))
+            for g in ready:
                 packed_ref[g] = side_by_side(coupling_ref, g)
         fars = []
-        for g in range(4 * i - 4, 4 * i) if i else ():
+        for g in now:
             rows = [at_ref[j, g] for j in range(many)]
             fars.append(dot(picked(table_ref, rows, left), packed_ref[g], NT))
             if g % 2 == 1:
@@ -221,9 +227,9 @@
 
 
 def down_kernel(
-    axis, at_vmem, same_ref, other_refs, packed_ref, counts_hbm,
+    axes, at_vmem, same_ref, other_own_ref, other_refs, packed_ref, counts_hbm,
     far_ref, near_ref, edge_ref, transfer_ref, basis_ref,
-    out_ref, table_ref, at_ref, local_ref, down_ref, counts_ref, sems,
+    out_hbm, table_ref, at_ref, local_ref, down_ref, counts_ref, out_ref, sems, out_sems,
 ):
     at_in, counts_in = start_all([(at_vmem, at_ref), (counts_hbm, counts_ref)], sems)
     parents, many = at_ref.shape
@@ -232,16 +238,15 @@
     sides = same_ref.shape[1]
     half = 2 * same_ref.shape[0]
     left = left_half(sides, rank)
-    parity = lax.axis_index(axis)
-    quarter = other_refs[0].shape[0]
-
-    def spread(a, carry):
-        for b, ref in enumerate(other_refs):
-            spread_pair(table_ref, half * (1 - parity) + 2 * (quarter * b + a), ref[a], rank)
-            spread_pair(table_ref, half * parity + 2 * (quarter * b + a), same_ref[quarter * b + a], rank)
-        return carry
-
-    lax.fori_loop(0, quarter, spread, 0, unroll=min(16, quarter))
+    parity, mine, count = lax.axis_index(axes[1]), lax.axis_index(axes[0]), lax.axis_size(axes[0])
+    own, piece = other_own_ref.shape[0], other_refs[0].shape[0]
+    for t in range(count * own):
+        spread_pair(table_ref, half * parity + 2 * t, same_ref[t], rank)
+    for t in range(own):
+        spread_pair(table_ref, half * (1 - parity) + 2 * (mine * own + t), other_own_ref[t], rank)
+    for t in range(2 * piece):
+        place = lax.rem(mine + 1 + t // own, count) * own + t % own
+        spread_pair(table_ref, half * (1 - parity) + 2 * place, other_refs[t // piece][t % piece], rank)
     at_in.wait()
     for q in range(parents):
         rows = [at_ref[q, j] for j in range(many)]
@@ -251,6 +256,7 @@
         local = far_ref[q] + dot(down_ref[q], transfer_ref[2 * q : 2 * q + 2].reshape(2 * rank, rank), NT)
         local_ref[q] = local.astype(jnp.bfloat16)
     counts_in.wait()
+    sent = []
     for q in range(parents):
         local = local_ref[q]
         none = jnp.zeros_like(local)
@@ -263,6 +269,12 @@
             total = total + edge_ref[1]
         total = jnp.where(pair_mask(counts_ref, q, sides, width), total, jnp.zeros_like(total))
         out_ref[:, 2 * width * q : 2 * width * (q + 1)] = total.astype(out_ref.dtype)
+        if (q + 1) % 4 == 0:
+            lanes = pl.ds(2 * width * (q - 3), 8 * width)
+            sent.append(pltpu.make_async_copy(out_ref.at[:, lanes], out_hbm.at[:, lanes], out_sems.at[q // 4]))
+            sent[-1].start()
+    for copy in sent:
+        copy.wait()
 
 
 def per_device(
@@ -290,22 +302,22 @@
     dma = lambda count: pltpu.SemaphoreType.DMA((count,))
     params = lambda mib: pltpu.CompilerParams(vmem_limit_bytes=mib * 2**20)
 
-    rim, live, sent = pl.pallas_call(
+    rim, live, parent_coef, sent = pl.pallas_call(
         up_kernel,
         name="up",
         out_shape=[
             shape((pairs + 2, sides, 2 * rank), bf16),
             shape((pairs, sides, 2 * width), bf16),
+            shape((own, sides, 2 * rank), bf16),
             pltpu.HBM((n // 2 * own, sides, 2 * rank), bf16),
         ],
         in_specs=[HBM] * 4,
-        out_specs=[VMEM, VMEM, HBM],
+        out_specs=[VMEM, VMEM, VMEM, HBM],
         scratch_shapes=[
             pltpu.SMEM((leaves,), jnp.int32),
             pltpu.VMEM((sides, leaves * width), bf16),
             pltpu.VMEM((leaves, width, rank), bf16),
             pltpu.VMEM((leaves, rank, rank), bf16),
-            pltpu.VMEM((own, sides, 2 * rank), bf16),
             dma(4),
             dma(n // 2),
         ],
@@ -337,15 +349,16 @@
         compiler_params=params(12),
     )(live, *keep(near_blocks, parent_coupling, leaf_partners.T, parent_partners))
 
-    quarter = shape((n // 4 * own, sides, 2 * rank), bf16)
+    other_own = lax.ppermute(parent_coef, "gp", [(0, 1), (1, 0)])
+    piece = shape(((n // 2 - 1) * own // 2, sides, 2 * rank), bf16)
     pieces = pl.pallas_call(
-        halves_kernel,
+        functools.partial(halves_kernel, "gz"),
         name="halves",
-        out_shape=[quarter, quarter],
-        in_specs=[VMEM, VMEM],
+        out_shape=[piece, piece],
+        in_specs=[VMEM, VMEM, VMEM],
         out_specs=[VMEM, VMEM],
         compiler_params=params(4),
-    )(same, parent_at)
+    )(same, other_own, parent_at)
     other = [lax.ppermute(piece, "gp", [(0, 1), (1, 0)]) for piece in pieces]
 
     far, edge, transfer_in, basis_in = pl.pallas_call(
@@ -365,27 +378,29 @@
             pltpu.VMEM(leaf_coupling.shape, bf16),
             pltpu.VMEM((leaves, rank, many * rank), bf16),
             pltpu.VMEM(basis.shape, bf16),
-            dma(3 + leaves // 4),
+            dma(4 + leaves // 4),
         ],
         compiler_params=params(20),
     )(leaf_at, rim, even, odd, rim_near, *keep(leaf_coupling, transfer, basis))
 
     out = pl.pallas_call(
-        functools.partial(down_kernel, "gp"),
+        functools.partial(down_kernel, axes[1:]),
         name="down",
-        out_shape=jax.ShapeDtypeStruct((sides, leaves * width), bf16),
-        in_specs=[VMEM, VMEM, [VMEM] * 2, VMEM, HBM] + [VMEM] * 5,
-        out_specs=VMEM,
+        out_shape=pltpu.HBM((sides, leaves * width), bf16),
+        in_specs=[VMEM, VMEM, VMEM, [VMEM] * 2, VMEM, HBM] + [VMEM] * 5,
+        out_specs=HBM,
         scratch_shapes=[
             pltpu.VMEM((n * parents, sides, 2 * rank), bf16),
             pltpu.SMEM((parents, many), jnp.int32),
             pltpu.VMEM((pairs, sides, 2 * rank), bf16),
             pltpu.VMEM((parents, sides, rank), bf16),
             pltpu.SMEM((leaves,), jnp.int32),
+            pltpu.VMEM((sides, leaves * width), bf16),
             dma(2),
+            dma(parents // 4),
         ],
         compiler_params=params(12),
-    )(parent_at, same, other, parent_packed, *keep(panel_counts), far, near, edge, transfer_in, basis_in)
+    )(parent_at, same, other_own, other, parent_packed, *keep(panel_counts), far, near, edge, transfer_in, basis_in)
     return out.T
 
 

time: 30.6 us -> 29.7 us (0.971)
  the two profiles are of different devices: /device:TPU:0 before, /device:TPU:1 now
where the time goes in v19:
time: 29.7 us; the launch traced here: 29.5 us
  starting transfers between devices  16.2 us (55%)
  Pallas kernels  13.2 us (44%)
    ppermute x1, starting transfers between devices, per_device(): odd = lax.ppermute(rim, axes, steps + [(b, a) for a, b in steps])  7.8 us
    all_to_all x1, starting transfers between devices, per_device(): same = lax.all_to_all(sent, 'gz', 0, 0, tiled=True)  5.43 us
    pallas_call x1, Pallas kernels, per_device(): pl.pallas_call(functools.partial(leaf_kernel, axes), name='leaf', out_sha...  4.68 us
    pallas_call x1, Pallas kernels, per_device(): pl.pallas_call(functools.partial(mid_kernel, axes), name='mid', out_shape...  3.09 us
    pallas_call x1, Pallas kernels, per_device(): pl.pallas_call(functools.partial(down_kernel, axes[1:]), name='down', out...  2.8 us
    pallas_call x1, Pallas kernels, per_device(): pl.pallas_call(up_kernel, name='up', out_shape=[shape((pairs + 2, sides,...  2.56 us
    ppermute x2, starting transfers between devices, per_device(): other = [lax.ppermute(piece, 'gp', [(0, 1), (1, 0)]) for piece in pieces]  1.52 us
    ppermute x1, starting transfers between devices, per_device(): other_own = lax.ppermute(parent_coef, 'gp', [(0, 1), (1, 0)])  1.24 us
  transfers between devices with their start and end apart: 6, of which 0 were waited for; matrix products, arithmetic and copies ran while one was open for 0% of the time, Pallas kernels for 26%

profile of v19, /device:TPU:1, one launch (start us, length us, event | category | flops | bytes accessed | tf_op | source)
XLA Modules:
  0.0 29.5 jit_solution(6454508677410239358)
XLA Ops:
  0.0 2.6 %up.1 = (bf16[18,32,128]{2,1,0:T(8,128)(2,1)S(1)}, bf16[16,32,128]{2,1,0:T(8,128)(2,1)S(1)}, bf16[8,32,128]{2,1,0:T(8,128)(2,1)S(1)}, bf16[32,32,128]{2,1,0:T(8,128)(2,1)}) custom-call(s32[32]{0:T(128)} %counts_hbm.3, bf16[32,2048]{1,0:T(8,128)(2,1)} %bitcast.3, bf16[32,64,64]{2,1,0:T(8,128)(2,1)} %basis_hbm.3, bf16[32,64,64]{2,1,0:T(8,128)(2,1)} %transfer_hbm.3), custom_call_target="tpu_custom_call" | custom-call | tf_op jit(solution)/shard_map/up/pallas_call | solution.py:305
  2.6 5.4 %all-to-all-start = ((bf16[32,32,128]{2,1,0:T(8,128)(2,1)}), bf16[32,32,128]{2,1,0:T(8,128)(2,1)S(1)}, u32[]{:S(2)}, u32[]{:S(2)}) async-start(bf16[32,32,128]{2,1,0:T(8,128)(2,1)} %get-tuple-element.22), calls=%async_computation | async-start | bytes 524288 | tf_op jit(solution)/shard_map/all_to_all | solution.py:330
  8.0 1.2 %collective-permute-start = (bf16[8,32,128]{2,1,0:T(8,128)(2,1)S(1)}, bf16[8,32,128]{2,1,0:T(8,128)(2,1)S(1)}, u32[]{:S(2)}, u32[]{:S(2)}) collective-permute-start(bf16[8,32,128]{2,1,0:T(8,128)(2,1)S(1)} %get-tuple-element.23), channel_id=1, source_target_pairs={{0,1},{1,0},{2,3},{3,2},{4,5},{5,4},{6,7},{7,6},{8,9},{9,8},{10,11... | collective-permute-start | bytes 196616 | tf_op jit(solution)/shard_map/ppermute | solution.py:352
  9.2 0.2 collective-permute-start.3
  9.5 7.8 %collective-permute-start.4 = (bf16[18,32,128]{2,1,0:T(8,128)(2,1)S(1)}, bf16[18,32,128]{2,1,0:T(8,128)(2,1)S(1)}, u32[]{:S(2)}, u32[]{:S(2)}) collective-permute-start(bf16[18,32,128]{2,1,0:T(8,128)(2,1)S(1)} %get-tuple-element.28.rim_ref), channel_id=1, source_target_pairs={{1,2},{3,4},{5,6},{7,8},{9,10},{11,12},{13,14},{15,16},{17,18},{19... | collective-permute-start | bytes 442376 | tf_op jit(solution)/shard_map/ppermute | solution.py:329
  17.3 3.1 %mid.1 = (bf16[16,64,1024]{2,1,0:T(8,128)(2,1)S(1)}, f32[16,32,128]{2,1,0:T(8,128)S(1)}, bf16[2,64,64]{2,1,0:T(8,128)(2,1)S(1)}, s32[16,32]{1,0:T(8,128)S(1)}, s32[16,16]{1,0:T(8,128)S(1)}) custom-call(bf16[16,32,128]{2,1,0:T(8,128)(2,1)S(1)} %get-tuple-element.20.live_ref, bf16[32,3,64,64]{3,2,1,0:T(8,128)(2,1)} %near_hbm.1, ...), custom_call_target="tpu_custom_call" | custom-call | tf_op jit(solution)/shard_map/mid/pallas_call | solution.py:332
  20.4 0.0 collective-permute-done.own_ref.other_own_ref
  20.4 0.0 all-to-all-done.whole_ref.same_ref
  20.4 0.1 collective-permute-start.1
  20.5 1.5 %collective-permute-start.2 = (bf16[12,32,128]{2,1,0:T(8,128)(2,1)S(1)}, bf16[12,32,128]{2,1,0:T(8,128)(2,1)S(1)}, u32[]{:S(2)}, u32[]{:S(2)}) collective-permute-start(bf16[12,32,128]{2,1,0:T(8,128)(2,1)S(1)} %get-tuple-element.25), channel_id=1, source_target_pairs={{0,1},{1,0},{2,3},{3,2},{4,5},{5,4},{6,7},{7,6},{8,9},{9,8},{10,11... | collective-permute-start | bytes 294920 | tf_op jit(solution)/shard_map/ppermute | solution.py:362
  22.0 0.0 collective-permute-done.3.even_ref
  22.0 0.0 collective-permute-done.4.odd_ref
  22.0 4.7 %leaf.1 = (f32[16,32,128]{2,1,0:T(8,128)S(1)}, f32[2,32,128]{2,1,0:T(8,128)S(1)}, bf16[32,64,64]{2,1,0:T(8,128)(2,1)S(1)}, bf16[16,64,128]{2,1,0:T(8,128)(2,1)S(1)}) custom-call(s32[16,32]{1,0:T(8,128)S(1)} %get-tuple-element.27.at_vmem, bf16[18,32,128]{2,1,0:T(8,128)(2,1)S(1)} %get-tuple-element.28.rim_ref, ...), custom_call_target="tpu_custom_call" | custom-call | tf_op jit(solution)/shard_map/leaf/pallas_call | solution.py:364
  26.7 0.0 collective-permute-done.1.other_refs_0_
  26.7 0.0 collective-permute-done.2.other_refs_1_
  26.7 2.8 %down.1 = bf16[32,2048]{1,0:T(8,128)(2,1)} custom-call(s32[16,16]{1,0:T(8,128)S(1)} %get-tuple-element.21.at_ref.at_vmem, bf16[32,32,128]{2,1,0:T(8,128)(2,1)S(1)} %all-to-all-done.whole_ref.same_ref, bf16[8,32,128]{2,1,0:T(8,128)(2,1)S(1)} %collective-permute-done.own_ref.other_own_ref, bf16[12,32,128]{2,1,0:T(8,128)(2,1)S(1)} %collective-permute-done.1.other_refs_0_, ...), custom_call_target="tpu_custom_call" | custom-call | tf_op jit(solution)/shard_map/down/pallas_call | solution.py:386
  (1 shorter events, 0.0 us)
Async XLA Ops:
  2.6 17.8 %all-to-all-start = ((bf16[32,32,128]{2,1,0:T(8,128)(2,1)}), bf16[32,32,128]{2,1,0:T(8,128)(2,1)S(1)}, u32[]{:S(2)}, u32[]{:S(2)}) async-start(bf16[32,32,128]{2,1,0:T(8,128)(2,1)} %get-tuple-element.22), calls=%async_computation | async-start | bytes 524288 | tf_op jit(solution)/shard_map/all_to_all | solution.py:330
  8.0 12.4 %collective-permute-start = (bf16[8,32,128]{2,1,0:T(8,128)(2,1)S(1)}, bf16[8,32,128]{2,1,0:T(8,128)(2,1)S(1)}, u32[]{:S(2)}, u32[]{:S(2)}) collective-permute-start(bf16[8,32,128]{2,1,0:T(8,128)(2,1)S(1)} %get-tuple-element.23), channel_id=1, source_target_pairs={{0,1},{1,0},{2,3},{3,2},{4,5},{5,4},{6,7},{7,6},{8,9},{9,8},{10,11... | collective-permute-start | bytes 196616 | tf_op jit(solution)/shard_map/ppermute | solution.py:352
  9.2 12.7 %collective-permute-start.3 = (bf16[18,32,128]{2,1,0:T(8,128)(2,1)S(1)}, bf16[18,32,128]{2,1,0:T(8,128)(2,1)S(1)}, u32[]{:S(2)}, u32[]{:S(2)}) collective-permute-start(bf16[18,32,128]{2,1,0:T(8,128)(2,1)S(1)} %get-tuple-element.28.rim_ref), channel_id=1, source_target_pairs={{0,1},{1,0},{2,3},{3,2},{4,5},{5,4},{6,7},{7,6},{8,9},{9,8},{10,11... | collective-permute-start | bytes 442376 | tf_op jit(solution)/shard_map/ppermute | solution.py:327
  9.5 12.5 %collective-permute-start.4 = (bf16[18,32,128]{2,1,0:T(8,128)(2,1)S(1)}, bf16[18,32,128]{2,1,0:T(8,128)(2,1)S(1)}, u32[]{:S(2)}, u32[]{:S(2)}) collective-permute-start(bf16[18,32,128]{2,1,0:T(8,128)(2,1)S(1)} %get-tuple-element.28.rim_ref), channel_id=1, source_target_pairs={{1,2},{3,4},{5,6},{7,8},{9,10},{11,12},{13,14},{15,16},{17,18},{19... | collective-permute-start | bytes 442376 | tf_op jit(solution)/shard_map/ppermute | solution.py:329
  20.4 6.2 %collective-permute-start.1 = (bf16[12,32,128]{2,1,0:T(8,128)(2,1)S(1)}, bf16[12,32,128]{2,1,0:T(8,128)(2,1)S(1)}, u32[]{:S(2)}, u32[]{:S(2)}) collective-permute-start(bf16[12,32,128]{2,1,0:T(8,128)(2,1)S(1)} %get-tuple-element.24), channel_id=1, source_target_pairs={{0,1},{1,0},{2,3},{3,2},{4,5},{5,4},{6,7},{7,6},{8,9},{9,8},{10,11... | collective-permute-start | bytes 294920 | tf_op jit(solution)/shard_map/ppermute | solution.py:362
  20.5 6.2 %collective-permute-start.2 = (bf16[12,32,128]{2,1,0:T(8,128)(2,1)S(1)}, bf16[12,32,128]{2,1,0:T(8,128)(2,1)S(1)}, u32[]{:S(2)}, u32[]{:S(2)}) collective-permute-start(bf16[12,32,128]{2,1,0:T(8,128)(2,1)S(1)} %get-tuple-element.25), channel_id=1, source_target_pairs={{0,1},{1,0},{2,3},{3,2},{4,5},{5,4},{6,7},{7,6},{8,9},{9,8},{10,11... | collective-permute-start | bytes 294920 | tf_op jit(solution)/shard_map/ppermute | solution.py:362

commit v20 on v19

--- a/solution.py
+++ b/solution.py
@@ -55,8 +55,8 @@
 
 
 def up_kernel(
-    counts_hbm, charges_hbm, basis_hbm, transfer_hbm,
-    rim_ref, live_ref, parents_ref, sent_hbm,
+    axes, counts_hbm, charges_hbm, basis_hbm, transfer_hbm,
+    rim_ref, even_rim_ref, live_ref, parents_ref, sent_hbm,
     counts_ref, charges_ref, basis_ref, transfer_ref, sems, sent_sems,
 ):
     counts_in, charges_in, basis_in, transfer_in = start_all(
@@ -81,6 +81,7 @@
         lives.append(live)
     rim_ref[pairs] = lives[0]
     rim_ref[pairs + 1] = lives[-1]
+    even_rim_ref[pairs] = jnp.where(lax.rem(position(axes), 2) == 0, lives[-1], lives[0])
     basis_in.wait()
     none = jnp.zeros_like(lives[0])
     coefs = []
@@ -90,6 +91,7 @@
         coef = dot(both, basis_ref[2 * a : 2 * a + 2].reshape(2 * width, rank), NN)
         coef = jnp.concatenate([coef[:sides], coef[sides:]], axis=1).astype(jnp.bfloat16)
         rim_ref[a] = coef
+        even_rim_ref[a] = coef
         coefs.append(coef)
     transfer_in.wait()
     sums = [
@@ -199,7 +201,7 @@
     ):
         for a in range(pairs):
             spread_pair(table_ref, base + 2 * a, ref[a], rank)
-    before = jnp.where(parity == 1, even_ref[pairs + 1], odd_ref[pairs + 1])
+    before = jnp.where(parity == 1, even_ref[pairs], odd_ref[pairs + 1])
     after = jnp.where(parity == 1, odd_ref[pairs], even_ref[pairs])
     low = dot(before[:, width:], rim_near_ref[0], NT)
     high = dot(after[:, :width], rim_near_ref[1], NT)
@@ -302,17 +304,18 @@
     dma = lambda count: pltpu.SemaphoreType.DMA((count,))
     params = lambda mib: pltpu.CompilerParams(vmem_limit_bytes=mib * 2**20)
 
-    rim, live, parent_coef, sent = pl.pallas_call(
-        up_kernel,
+    rim, even_rim, live, parent_coef, sent = pl.pallas_call(
+        functools.partial(up_kernel, axes),
         name="up",
         out_shape=[
             shape((pairs + 2, sides, 2 * rank), bf16),
+            shape((pairs + 1, sides, 2 * rank), bf16),
             shape((pairs, sides, 2 * width), bf16),
             shape((own, sides, 2 * rank), bf16),
             pltpu.HBM((n // 2 * own, sides, 2 * rank), bf16),
         ],
         in_specs=[HBM] * 4,
-        out_specs=[VMEM, VMEM, VMEM, HBM],
+        out_specs=[VMEM] * 4 + [HBM],
         scratch_shapes=[
             pltpu.SMEM((leaves,), jnp.int32),
             pltpu.VMEM((sides, leaves * width), bf16),
@@ -324,7 +327,7 @@
         compiler_params=params(8),
     )(*keep(panel_counts, charges.T, basis, transfer))
 
-    even = lax.ppermute(rim, axes, [(i, i ^ 1) for i in range(total)])
+    even = lax.ppermute(even_rim, axes, [(i, i ^ 1) for i in range(total)])
     steps = [(i, i + 1) for i in range(1, total - 1, 2)]
     odd = lax.ppermute(rim, axes, steps + [(b, a) for a, b in steps])
     same = lax.all_to_all(sent, "gz", 0, 0, tiled=True)

time: 29.7 us -> 31.2 us (1.051)
  the two profiles are of different devices: /device:TPU:1 before, /device:TPU:3 now
where the time goes in v20:
time: 31.2 us; the launch traced here: 30.9 us
  starting transfers between devices  14 us (45%)
  Pallas kernels  13.1 us (42%)
  waiting for transfers between devices  3.7 us (12%)
    ppermute x1, starting transfers between devices, per_device(): odd = lax.ppermute(rim, axes, steps + [(b, a) for a, b in steps])  6.5 us
    pallas_call x1, Pallas kernels, per_device(): pl.pallas_call(functools.partial(leaf_kernel, axes), name='leaf', out_sha...  4.65 us
    all_to_all x1, starting transfers between devices, per_device(): same = lax.all_to_all(sent, 'gz', 0, 0, tiled=True)  4.6 us
    ppermute x1, waiting for transfers between devices, per_device(): even = lax.ppermute(even_rim, axes, [(i, i ^ 1) for i in range(total)])  3.68 us
    pallas_call x1, Pallas kernels, per_device(): pl.pallas_call(functools.partial(mid_kernel, axes), name='mid', out_shape...  3.1 us
    pallas_call x1, Pallas kernels, per_device(): pl.pallas_call(functools.partial(down_kernel, axes[1:]), name='down', out...  2.8 us
    pallas_call x1, Pallas kernels, per_device(): pl.pallas_call(functools.partial(up_kernel, axes), name='up', out_shape=[...  2.56 us
    ppermute x2, starting transfers between devices, per_device(): other = [lax.ppermute(piece, 'gp', [(0, 1), (1, 0)]) for piece in pieces]  1.59 us
  transfers between devices with their start and end apart: 6, of which 1 were waited for; matrix products, arithmetic and copies ran while one was open for 0% of the time, Pallas kernels for 25%

profile of v20, /device:TPU:3, one launch (start us, length us, event | category | flops | bytes accessed | tf_op | source)
XLA Modules:
  0.0 30.9 jit_solution(15357145743312194863)
XLA Ops:
  0.0 2.6 %up.1 = (bf16[18,32,128]{2,1,0:T(8,128)(2,1)S(1)}, bf16[17,32,128]{2,1,0:T(8,128)(2,1)S(1)}, bf16[16,32,128]{2,1,0:T(8,128)(2,1)S(1)}, bf16[8,32,128]{2,1,0:T(8,128)(2,1)S(1)}, bf16[32,32,128]{2,1,0:T(8,128)(2,1)}) custom-call(s32[32]{0:T(128)} %counts_hbm.3, bf16[32,2048]{1,0:T(8,128)(2,1)} %bitcast.3, bf16[32,64,64]{2,1,0:T(8,128)(2,1)} %basis_hbm.3, ...), custom_call_target="tpu_custom_call" | custom-call | tf_op jit(solution)/shard_map/up/pallas_call | solution.py:307
  2.6 4.6 %all-to-all-start = ((bf16[32,32,128]{2,1,0:T(8,128)(2,1)}), bf16[32,32,128]{2,1,0:T(8,128)(2,1)S(1)}, u32[]{:S(2)}, u32[]{:S(2)}) async-start(bf16[32,32,128]{2,1,0:T(8,128)(2,1)} %get-tuple-element.23), calls=%async_computation | async-start | bytes 524288 | tf_op jit(solution)/shard_map/all_to_all | solution.py:333
  7.2 1.2 %collective-permute-start = (bf16[8,32,128]{2,1,0:T(8,128)(2,1)S(1)}, bf16[8,32,128]{2,1,0:T(8,128)(2,1)S(1)}, u32[]{:S(2)}, u32[]{:S(2)}) collective-permute-start(bf16[8,32,128]{2,1,0:T(8,128)(2,1)S(1)} %get-tuple-element.24), channel_id=1, source_target_pairs={{0,1},{1,0},{2,3},{3,2},{4,5},{5,4},{6,7},{7,6},{8,9},{9,8},{10,11... | collective-permute-start | bytes 196616 | tf_op jit(solution)/shard_map/ppermute | solution.py:355
  8.4 6.5 %collective-permute-start.4 = (bf16[18,32,128]{2,1,0:T(8,128)(2,1)S(1)}, bf16[18,32,128]{2,1,0:T(8,128)(2,1)S(1)}, u32[]{:S(2)}, u32[]{:S(2)}) collective-permute-start(bf16[18,32,128]{2,1,0:T(8,128)(2,1)S(1)} %get-tuple-element.29.rim_ref), channel_id=1, source_target_pairs={{1,2},{3,4},{5,6},{7,8},{9,10},{11,12},{13,14},{15,16},{17,18},{19... | collective-permute-start | bytes 442376 | tf_op jit(solution)/shard_map/ppermute | solution.py:332
  14.9 0.1 collective-permute-start.3
  15.0 3.1 %mid.1 = (bf16[16,64,1024]{2,1,0:T(8,128)(2,1)S(1)}, f32[16,32,128]{2,1,0:T(8,128)S(1)}, bf16[2,64,64]{2,1,0:T(8,128)(2,1)S(1)}, s32[16,32]{1,0:T(8,128)S(1)}, s32[16,16]{1,0:T(8,128)S(1)}) custom-call(bf16[16,32,128]{2,1,0:T(8,128)(2,1)S(1)} %get-tuple-element.21.live_ref, bf16[32,3,64,64]{3,2,1,0:T(8,128)(2,1)} %near_hbm.1, ...), custom_call_target="tpu_custom_call" | custom-call | tf_op jit(solution)/shard_map/mid/pallas_call | solution.py:335
  18.1 0.0 collective-permute-done.own_ref.other_own_ref
  18.1 0.0 all-to-all-done.whole_ref.same_ref
  18.2 1.5 %collective-permute-start.1 = (bf16[12,32,128]{2,1,0:T(8,128)(2,1)S(1)}, bf16[12,32,128]{2,1,0:T(8,128)(2,1)S(1)}, u32[]{:S(2)}, u32[]{:S(2)}) collective-permute-start(bf16[12,32,128]{2,1,0:T(8,128)(2,1)S(1)} %get-tuple-element.25), channel_id=1, source_target_pairs={{0,1},{1,0},{2,3},{3,2},{4,5},{5,4},{6,7},{7,6},{8,9},{9,8},{10,11... | collective-permute-start | bytes 294920 | tf_op jit(solution)/shard_map/ppermute | solution.py:365
  19.7 0.1 collective-permute-start.2
  19.8 3.7 %collective-permute-done.3.even_ref = bf16[17,32,128]{2,1,0:T(8,128)(2,1)S(1)} collective-permute-done((bf16[17,32,128]{2,1,0:T(8,128)(2,1)S(1)}, bf16[17,32,128]{2,1,0:T(8,128)(2,1)S(1)}, u32[]{:S(2)}, u32[]{:S(2)}) %collective-permute-start.3) | collective-permute-done | bytes 139296 | tf_op jit(solution)/shard_map/ppermute | solution.py:330
  23.4 0.0 collective-permute-done.4.odd_ref
  23.4 4.6 %leaf.1 = (f32[16,32,128]{2,1,0:T(8,128)S(1)}, f32[2,32,128]{2,1,0:T(8,128)S(1)}, bf16[32,64,64]{2,1,0:T(8,128)(2,1)S(1)}, bf16[16,64,128]{2,1,0:T(8,128)(2,1)S(1)}) custom-call(s32[16,32]{1,0:T(8,128)S(1)} %get-tuple-element.28.at_vmem, bf16[18,32,128]{2,1,0:T(8,128)(2,1)S(1)} %get-tuple-element.29.rim_ref, ...), custom_call_target="tpu_custom_call" | custom-call | tf_op jit(solution)/shard_map/leaf/pallas_call | solution.py:367
  28.1 0.0 collective-permute-done.1.other_refs_0_
  28.1 0.0 collective-permute-done.2.other_refs_1_
  28.1 2.8 %down.1 = bf16[32,2048]{1,0:T(8,128)(2,1)} custom-call(s32[16,16]{1,0:T(8,128)S(1)} %get-tuple-element.22.at_ref.at_vmem, bf16[32,32,128]{2,1,0:T(8,128)(2,1)S(1)} %all-to-all-done.whole_ref.same_ref, bf16[8,32,128]{2,1,0:T(8,128)(2,1)S(1)} %collective-permute-done.own_ref.other_own_ref, bf16[12,32,128]{2,1,0:T(8,128)(2,1)S(1)} %collective-permute-done.1.other_refs_0_, ...), custom_call_target="tpu_custom_call" | custom-call | tf_op jit(solution)/shard_map/down/pallas_call | solution.py:389
  (1 shorter events, 0.0 us)
Async XLA Ops:
  2.6 15.6 %all-to-all-start = ((bf16[32,32,128]{2,1,0:T(8,128)(2,1)}), bf16[32,32,128]{2,1,0:T(8,128)(2,1)S(1)}, u32[]{:S(2)}, u32[]{:S(2)}) async-start(bf16[32,32,128]{2,1,0:T(8,128)(2,1)} %get-tuple-element.23), calls=%async_computation | async-start | bytes 524288 | tf_op jit(solution)/shard_map/all_to_all | solution.py:333
  7.2 10.9 %collective-permute-start = (bf16[8,32,128]{2,1,0:T(8,128)(2,1)S(1)}, bf16[8,32,128]{2,1,0:T(8,128)(2,1)S(1)}, u32[]{:S(2)}, u32[]{:S(2)}) collective-permute-start(bf16[8,32,128]{2,1,0:T(8,128)(2,1)S(1)} %get-tuple-element.24), channel_id=1, source_target_pairs={{0,1},{1,0},{2,3},{3,2},{4,5},{5,4},{6,7},{7,6},{8,9},{9,8},{10,11... | collective-permute-start | bytes 196616 | tf_op jit(solution)/shard_map/ppermute | solution.py:355
  8.4 15.0 %collective-permute-start.4 = (bf16[18,32,128]{2,1,0:T(8,128)(2,1)S(1)}, bf16[18,32,128]{2,1,0:T(8,128)(2,1)S(1)}, u32[]{:S(2)}, u32[]{:S(2)}) collective-permute-start(bf16[18,32,128]{2,1,0:T(8,128)(2,1)S(1)} %get-tuple-element.29.rim_ref), channel_id=1, source_target_pairs={{1,2},{3,4},{5,6},{7,8},{9,10},{11,12},{13,14},{15,16},{17,18},{19... | collective-permute-start | bytes 442376 | tf_op jit(solution)/shard_map/ppermute | solution.py:332
  14.9 8.5 %collective-permute-start.3 = (bf16[17,32,128]{2,1,0:T(8,128)(2,1)S(1)}, bf16[17,32,128]{2,1,0:T(8,128)(2,1)S(1)}, u32[]{:S(2)}, u32[]{:S(2)}) collective-permute-start(bf16[17,32,128]{2,1,0:T(8,128)(2,1)S(1)} %get-tuple-element.30), channel_id=1, source_target_pairs={{0,1},{1,0},{2,3},{3,2},{4,5},{5,4},{6,7},{7,6},{8,9},{9,8},{10,11... | collective-permute-start | bytes 417800 | tf_op jit(solution)/shard_map/ppermute | solution.py:330
  18.2 9.9 %collective-permute-start.1 = (bf16[12,32,128]{2,1,0:T(8,128)(2,1)S(1)}, bf16[12,32,128]{2,1,0:T(8,128)(2,1)S(1)}, u32[]{:S(2)}, u32[]{:S(2)}) collective-permute-start(bf16[12,32,128]{2,1,0:T(8,128)(2,1)S(1)} %get-tuple-element.25), channel_id=1, source_target_pairs={{0,1},{1,0},{2,3},{3,2},{4,5},{5,4},{6,7},{7,6},{8,9},{9,8},{10,11... | collective-permute-start | bytes 294920 | tf_op jit(solution)/shard_map/ppermute | solution.py:365
  19.7 8.4 %collective-permute-start.2 = (bf16[12,32,128]{2,1,0:T(8,128)(2,1)S(1)}, bf16[12,32,128]{2,1,0:T(8,128)(2,1)S(1)}, u32[]{:S(2)}, u32[]{:S(2)}) collective-permute-start(bf16[12,32,128]{2,1,0:T(8,128)(2,1)S(1)} %get-tuple-element.26), channel_id=1, source_target_pairs={{0,1},{1,0},{2,3},{3,2},{4,5},{5,4},{6,7},{7,6},{8,9},{9,8},{10,11... | collective-permute-start | bytes 294920 | tf_op jit(solution)/shard_map/ppermute | solution.py:365

commit v21 on v19

--- a/solution.py
+++ b/solution.py
@@ -56,7 +56,7 @@
 
 def up_kernel(
     counts_hbm, charges_hbm, basis_hbm, transfer_hbm,
-    rim_ref, live_ref, parents_ref, sent_hbm,
+    rim_ref, even_rim_ref, live_ref, sent_hbm,
     counts_ref, charges_ref, basis_ref, transfer_ref, sems, sent_sems,
 ):
     counts_in, charges_in, basis_in, transfer_in = start_all(
@@ -79,8 +79,9 @@
         live = jnp.where(pair_mask(counts_ref, a, sides, width), charge, jnp.zeros_like(charge))
         live_ref[a] = live
         lives.append(live)
-    rim_ref[pairs] = lives[0]
-    rim_ref[pairs + 1] = lives[-1]
+    for ref in (rim_ref, even_rim_ref):
+        ref[pairs] = lives[0]
+        ref[pairs + 1] = lives[-1]
     basis_in.wait()
     none = jnp.zeros_like(lives[0])
     coefs = []
@@ -90,6 +91,7 @@
         coef = dot(both, basis_ref[2 * a : 2 * a + 2].reshape(2 * width, rank), NN)
         coef = jnp.concatenate([coef[:sides], coef[sides:]], axis=1).astype(jnp.bfloat16)
         rim_ref[a] = coef
+        even_rim_ref[a] = coef
         coefs.append(coef)
     transfer_in.wait()
     sums = [
@@ -97,9 +99,10 @@
         for a in range(pairs)
     ]
     for a in range(own):
-        parents_ref[a] = jnp.concatenate(sums[2 * a : 2 * a + 2], axis=1).astype(jnp.bfloat16)
+        even_rim_ref[pairs + 2 + a] = jnp.concatenate(sums[2 * a : 2 * a + 2], axis=1).astype(jnp.bfloat16)
     copies = sent_hbm.shape[0] // own
-    for copy in start_all([(parents_ref, sent_hbm.at[pl.ds(own * c, own)]) for c in range(copies)], sent_sems):
+    block = even_rim_ref.at[pl.ds(pairs + 2, own)]
+    for copy in start_all([(block, sent_hbm.at[pl.ds(own * c, own)]) for c in range(copies)], sent_sems):
         copy.wait()
 
 
@@ -153,10 +156,10 @@
     parent_at_ref[...] = wanted ^ (lax.broadcasted_iota(jnp.int32, wanted.shape, 1) & 1)
 
 
-def halves_kernel(axis, whole_ref, own_ref, at_ref, first_ref, second_ref):
+def halves_kernel(axis, whole_ref, at_ref, first_ref, second_ref):
     del at_ref
-    own, half = own_ref.shape[0], first_ref.shape[0]
-    count = lax.axis_size(axis)
+    count, half = lax.axis_size(axis), first_ref.shape[0]
+    own = whole_ref.shape[0] // count
     for t in range(2 * half):
         source = lax.rem(lax.axis_index(axis) + 1 + t // own, count) * own + t % own
         (first_ref if t < half else second_ref)[t % half] = whole_ref[source]
@@ -227,7 +230,7 @@
 
 
 def down_kernel(
-    axes, at_vmem, same_ref, other_own_ref, other_refs, packed_ref, counts_hbm,
+    axes, at_vmem, same_ref, even_ref, other_refs, packed_ref, counts_hbm,
     far_ref, near_ref, edge_ref, transfer_ref, basis_ref,
     out_hbm, table_ref, at_ref, local_ref, down_ref, counts_ref, out_ref, sems, out_sems,
 ):
@@ -239,11 +242,12 @@
     half = 2 * same_ref.shape[0]
     left = left_half(sides, rank)
     parity, mine, count = lax.axis_index(axes[1]), lax.axis_index(axes[0]), lax.axis_size(axes[0])
-    own, piece = other_own_ref.shape[0], other_refs[0].shape[0]
+    own, piece = same_ref.shape[0] // count, other_refs[0].shape[0]
+    start = even_ref.shape[0] - own
     for t in range(count * own):
         spread_pair(table_ref, half * parity + 2 * t, same_ref[t], rank)
     for t in range(own):
-        spread_pair(table_ref, half * (1 - parity) + 2 * (mine * own + t), other_own_ref[t], rank)
+        spread_pair(table_ref, half * (1 - parity) + 2 * (mine * own + t), even_ref[start + t], rank)
     for t in range(2 * piece):
         place = lax.rem(mine + 1 + t // own, count) * own + t % own
         spread_pair(table_ref, half * (1 - parity) + 2 * place, other_refs[t // piece][t % piece], rank)
@@ -302,13 +306,13 @@
     dma = lambda count: pltpu.SemaphoreType.DMA((count,))
     params = lambda mib: pltpu.CompilerParams(vmem_limit_bytes=mib * 2**20)
 
-    rim, live, parent_coef, sent = pl.pallas_call(
+    rim, even_rim, live, sent = pl.pallas_call(
         up_kernel,
         name="up",
         out_shape=[
             shape((pairs + 2, sides, 2 * rank), bf16),
+            shape((pairs + 2 + own, sides, 2 * rank), bf16),
             shape((pairs, sides, 2 * width), bf16),
-            shape((own, sides, 2 * rank), bf16),
             pltpu.HBM((n // 2 * own, sides, 2 * rank), bf16),
         ],
         in_specs=[HBM] * 4,
@@ -324,7 +328,7 @@
         compiler_params=params(8),
     )(*keep(panel_counts, charges.T, basis, transfer))
 
-    even = lax.ppermute(rim, axes, [(i, i ^ 1) for i in range(total)])
+    even = lax.ppermute(even_rim, axes, [(i, i ^ 1) for i in range(total)])
     steps = [(i, i + 1) for i in range(1, total - 1, 2)]
     odd = lax.ppermute(rim, axes, steps + [(b, a) for a, b in steps])
     same = lax.all_to_all(sent, "gz", 0, 0, tiled=True)
@@ -349,16 +353,15 @@
         compiler_params=params(12),
     )(live, *keep(near_blocks, parent_coupling, leaf_partners.T, parent_partners))
 
-    other_own = lax.ppermute(parent_coef, "gp", [(0, 1), (1, 0)])
     piece = shape(((n // 2 - 1) * own // 2, sides, 2 * rank), bf16)
     pieces = pl.pallas_call(
         functools.partial(halves_kernel, "gz"),
         name="halves",
         out_shape=[piece, piece],
-        in_specs=[VMEM, VMEM, VMEM],
+        in_specs=[VMEM, VMEM],
         out_specs=[VMEM, VMEM],
         compiler_params=params(4),
-    )(same, other_own, parent_at)
+    )(same, parent_at)
     other = [lax.ppermute(piece, "gp", [(0, 1), (1, 0)]) for piece in pieces]
 
     far, edge, transfer_in, basis_in = pl.pallas_call(
@@ -400,7 +403,7 @@
             dma(parents // 4),
         ],
         compiler_params=params(12),
-    )(parent_at, same, other_own, other, parent_packed, *keep(panel_counts), far, near, edge, transfer_in, basis_in)
+    )(parent_at, same, even, other, parent_packed, *keep(panel_counts), far, near, edge, transfer_in, basis_in)
     return out.T
 
 

time: 29.7 us -> 30.4 us (1.024)
  the two profiles are of different devices: /device:TPU:1 before, /device:TPU:0 now
where the time goes in v21:
time: 30.4 us; the launch traced here: 30.2 us
  Pallas kernels  13.1 us (43%)
  starting transfers between devices  12.3 us (40%)
  waiting for transfers between devices  4.69 us (15%)
    all_to_all x1, starting transfers between devices, per_device(): same = lax.all_to_all(sent, 'gz', 0, 0, tiled=True)  6.33 us
    all_to_all x1, waiting for transfers between devices, per_device(): same = lax.all_to_all(sent, 'gz', 0, 0, tiled=True)  4.68 us
    pallas_call x1, Pallas kernels, per_device(): pl.pallas_call(functools.partial(leaf_kernel, axes), name='leaf', out_sha...  4.67 us
    ppermute x2, starting transfers between devices, per_device(): other = [lax.ppermute(piece, 'gp', [(0, 1), (1, 0)]) for piece in pieces]  3.77 us
    pallas_call x1, Pallas kernels, per_device(): pl.pallas_call(functools.partial(mid_kernel, axes), name='mid', out_shape...  3.09 us
    pallas_call x1, Pallas kernels, per_device(): pl.pallas_call(functools.partial(down_kernel, axes[1:]), name='down', out...  2.81 us
    pallas_call x1, Pallas kernels, per_device(): pl.pallas_call(up_kernel, name='up', out_shape=[shape((pairs + 2, sides,...  2.55 us
    ppermute x1, starting transfers between devices, per_device(): even = lax.ppermute(even_rim, axes, [(i, i ^ 1) for i in range(total)])  1.52 us
  transfers between devices with their start and end apart: 5, of which 1 were waited for; matrix products, arithmetic and copies ran while one was open for 0% of the time, Pallas kernels for 26%

profile of v21, /device:TPU:0, one launch (start us, length us, event | category | flops | bytes accessed | tf_op | source)
XLA Modules:
  0.0 30.2 jit_solution(7848825408215353209)
XLA Ops:
  0.0 2.6 %up.1 = (bf16[18,32,128]{2,1,0:T(8,128)(2,1)S(1)}, bf16[26,32,128]{2,1,0:T(8,128)(2,1)S(1)}, bf16[16,32,128]{2,1,0:T(8,128)(2,1)S(1)}, bf16[32,32,128]{2,1,0:T(8,128)(2,1)}) custom-call(s32[32]{0:T(128)} %counts_hbm.3, bf16[32,2048]{1,0:T(8,128)(2,1)} %bitcast.3, bf16[32,64,64]{2,1,0:T(8,128)(2,1)} %basis_hbm.3, bf16[32,64,64]{2,1,0:T(8,128)(2,1)} %transfer_hbm.3), custom_call_target="tpu_custom_call" | custom-call | tf_op jit(solution)/shard_map/up/pallas_call | solution.py:309
  2.6 6.3 %all-to-all-start = ((bf16[32,32,128]{2,1,0:T(8,128)(2,1)}), bf16[32,32,128]{2,1,0:T(8,128)(2,1)S(1)}, u32[]{:S(2)}, u32[]{:S(2)}) async-start(bf16[32,32,128]{2,1,0:T(8,128)(2,1)} %get-tuple-element.22), calls=%async_computation | async-start | bytes 524288 | tf_op jit(solution)/shard_map/all_to_all | solution.py:334
  8.9 1.5 %collective-permute-start = (bf16[26,32,128]{2,1,0:T(8,128)(2,1)S(1)}, bf16[26,32,128]{2,1,0:T(8,128)(2,1)S(1)}, u32[]{:S(2)}, u32[]{:S(2)}) collective-permute-start(bf16[26,32,128]{2,1,0:T(8,128)(2,1)S(1)} %get-tuple-element.23), channel_id=1, source_target_pairs={{0,1},{1,0},{2,3},{3,2},{4,5},{5,4},{6,7},{7,6},{8,9},{9,8},{10,11... | collective-permute-start | bytes 638984 | tf_op jit(solution)/shard_map/ppermute | solution.py:331
  10.4 0.7 %collective-permute-start.3 = (bf16[18,32,128]{2,1,0:T(8,128)(2,1)S(1)}, bf16[18,32,128]{2,1,0:T(8,128)(2,1)S(1)}, u32[]{:S(2)}, u32[]{:S(2)}) collective-permute-start(bf16[18,32,128]{2,1,0:T(8,128)(2,1)S(1)} %get-tuple-element.28.rim_ref), channel_id=1, source_target_pairs={{1,2},{3,4},{5,6},{7,8},{9,10},{11,12},{13,14},{15,16},{17,18},{19... | collective-permute-start | bytes 442376 | tf_op jit(solution)/shard_map/ppermute | solution.py:333
  11.1 3.1 %mid.1 = (bf16[16,64,1024]{2,1,0:T(8,128)(2,1)S(1)}, f32[16,32,128]{2,1,0:T(8,128)S(1)}, bf16[2,64,64]{2,1,0:T(8,128)(2,1)S(1)}, s32[16,32]{1,0:T(8,128)S(1)}, s32[16,16]{1,0:T(8,128)S(1)}) custom-call(bf16[16,32,128]{2,1,0:T(8,128)(2,1)S(1)} %get-tuple-element.20.live_ref, bf16[32,3,64,64]{3,2,1,0:T(8,128)(2,1)} %near_hbm.1, ...), custom_call_target="tpu_custom_call" | custom-call | tf_op jit(solution)/shard_map/mid/pallas_call | solution.py:336
  14.2 4.7 %all-to-all-done.whole_ref.same_ref = bf16[32,32,128]{2,1,0:T(8,128)(2,1)S(1)} async-done(((bf16[32,32,128]{2,1,0:T(8,128)(2,1)}), bf16[32,32,128]{2,1,0:T(8,128)(2,1)S(1)}, u32[]{:S(2)}, u32[]{:S(2)}) %all-to-all-start) | async-done | bytes 262176 | tf_op jit(solution)/shard_map/all_to_all | solution.py:334
  18.9 3.7 %collective-permute-start.1 = (bf16[12,32,128]{2,1,0:T(8,128)(2,1)S(1)}, bf16[12,32,128]{2,1,0:T(8,128)(2,1)S(1)}, u32[]{:S(2)}, u32[]{:S(2)}) collective-permute-start(bf16[12,32,128]{2,1,0:T(8,128)(2,1)S(1)} %get-tuple-element.24), channel_id=1, source_target_pairs={{0,1},{1,0},{2,3},{3,2},{4,5},{5,4},{6,7},{7,6},{8,9},{9,8},{10,11... | collective-permute-start | bytes 294920 | tf_op jit(solution)/shard_map/ppermute | solution.py:365
  22.6 0.1 collective-permute-start.2
  22.6 0.0 collective-permute-done.3.odd_ref
  22.7 0.0 collective-permute-done.even_ref
  22.7 4.7 %leaf.1 = (f32[16,32,128]{2,1,0:T(8,128)S(1)}, f32[2,32,128]{2,1,0:T(8,128)S(1)}, bf16[32,64,64]{2,1,0:T(8,128)(2,1)S(1)}, bf16[16,64,128]{2,1,0:T(8,128)(2,1)S(1)}) custom-call(s32[16,32]{1,0:T(8,128)S(1)} %get-tuple-element.27.at_vmem, bf16[18,32,128]{2,1,0:T(8,128)(2,1)S(1)} %get-tuple-element.28.rim_ref, ...), custom_call_target="tpu_custom_call" | custom-call | tf_op jit(solution)/shard_map/leaf/pallas_call | solution.py:367
  27.3 0.0 collective-permute-done.1.other_refs_0_
  27.3 0.0 collective-permute-done.2.other_refs_1_
  27.4 2.8 %down.1 = bf16[32,2048]{1,0:T(8,128)(2,1)} custom-call(s32[16,16]{1,0:T(8,128)S(1)} %get-tuple-element.21.at_ref.at_vmem, bf16[32,32,128]{2,1,0:T(8,128)(2,1)S(1)} %all-to-all-done.whole_ref.same_ref, bf16[26,32,128]{2,1,0:T(8,128)(2,1)S(1)} %collective-permute-done.even_ref, bf16[12,32,128]{2,1,0:T(8,128)(2,1)S(1)} %collective-permute-done.1.other_refs_0_, ...), custom_call_target="tpu_custom_call" | custom-call | tf_op jit(solution)/shard_map/down/pallas_call | solution.py:389
  (1 shorter events, 0.0 us)
Async XLA Ops:
  2.6 16.3 %all-to-all-start = ((bf16[32,32,128]{2,1,0:T(8,128)(2,1)}), bf16[32,32,128]{2,1,0:T(8,128)(2,1)S(1)}, u32[]{:S(2)}, u32[]{:S(2)}) async-start(bf16[32,32,128]{2,1,0:T(8,128)(2,1)} %get-tuple-element.22), calls=%async_computation | async-start | bytes 524288 | tf_op jit(solution)/shard_map/all_to_all | solution.py:334
  8.9 13.8 %collective-permute-start = (bf16[26,32,128]{2,1,0:T(8,128)(2,1)S(1)}, bf16[26,32,128]{2,1,0:T(8,128)(2,1)S(1)}, u32[]{:S(2)}, u32[]{:S(2)}) collective-permute-start(bf16[26,32,128]{2,1,0:T(8,128)(2,1)S(1)} %get-tuple-element.23), channel_id=1, source_target_pairs={{0,1},{1,0},{2,3},{3,2},{4,5},{5,4},{6,7},{7,6},{8,9},{9,8},{10,11... | collective-permute-start | bytes 638984 | tf_op jit(solution)/shard_map/ppermute | solution.py:331
  10.4 12.2 %collective-permute-start.3 = (bf16[18,32,128]{2,1,0:T(8,128)(2,1)S(1)}, bf16[18,32,128]{2,1,0:T(8,128)(2,1)S(1)}, u32[]{:S(2)}, u32[]{:S(2)}) collective-permute-start(bf16[18,32,128]{2,1,0:T(8,128)(2,1)S(1)} %get-tuple-element.28.rim_ref), channel_id=1, source_target_pairs={{1,2},{3,4},{5,6},{7,8},{9,10},{11,12},{13,14},{15,16},{17,18},{19... | collective-permute-start | bytes 442376 | tf_op jit(solution)/shard_map/ppermute | solution.py:333
  18.9 8.5 %collective-permute-start.1 = (bf16[12,32,128]{2,1,0:T(8,128)(2,1)S(1)}, bf16[12,32,128]{2,1,0:T(8,128)(2,1)S(1)}, u32[]{:S(2)}, u32[]{:S(2)}) collective-permute-start(bf16[12,32,128]{2,1,0:T(8,128)(2,1)S(1)} %get-tuple-element.24), channel_id=1, source_target_pairs={{0,1},{1,0},{2,3},{3,2},{4,5},{5,4},{6,7},{7,6},{8,9},{9,8},{10,11... | collective-permute-start | bytes 294920 | tf_op jit(solution)/shard_map/ppermute | solution.py:365
  22.6 4.8 %collective-permute-start.2 = (bf16[12,32,128]{2,1,0:T(8,128)(2,1)S(1)}, bf16[12,32,128]{2,1,0:T(8,128)(2,1)S(1)}, u32[]{:S(2)}, u32[]{:S(2)}) collective-permute-start(bf16[12,32,128]{2,1,0:T(8,128)(2,1)S(1)} %get-tuple-element.25), channel_id=1, source_target_pairs={{0,1},{1,0},{2,3},{3,2},{4,5},{5,4},{6,7},{7,6},{8,9},{9,8},{10,11... | collective-permute-start | bytes 294920 | tf_op jit(solution)/shard_map/ppermute | solution.py:365

commit v22 on v21

--- a/solution.py
+++ b/solution.py
@@ -55,8 +55,8 @@
 
 
 def up_kernel(
-    counts_hbm, charges_hbm, basis_hbm, transfer_hbm,
-    rim_ref, even_rim_ref, live_ref, sent_hbm,
+    axes, counts_hbm, charges_hbm, basis_hbm, transfer_hbm,
+    rim_ref, even_rim_ref, odd_rim_ref, live_ref, sent_hbm,
     counts_ref, charges_ref, basis_ref, transfer_ref, sems, sent_sems,
 ):
     counts_in, charges_in, basis_in, transfer_in = start_all(
@@ -82,6 +82,7 @@
     for ref in (rim_ref, even_rim_ref):
         ref[pairs] = lives[0]
         ref[pairs + 1] = lives[-1]
+    odd_rim_ref[pairs] = jnp.where(lax.rem(position(axes), 2) == 1, lives[-1], lives[0])
     basis_in.wait()
     none = jnp.zeros_like(lives[0])
     coefs = []
@@ -92,6 +93,7 @@
         coef = jnp.concatenate([coef[:sides], coef[sides:]], axis=1).astype(jnp.bfloat16)
         rim_ref[a] = coef
         even_rim_ref[a] = coef
+        odd_rim_ref[a] = coef
         coefs.append(coef)
     transfer_in.wait()
     sums = [
@@ -181,11 +183,11 @@
 
 
 def leaf_kernel(
-    axes, at_vmem, rim_ref, even_ref, odd_ref, rim_near_ref, coupling_hbm, transfer_hbm, basis_hbm,
+    axes, at_vmem, rim_ref, even_ref, ends_ref, odd_ref, rim_near_ref, coupling_hbm, transfer_hbm, basis_hbm,
     far_ref, edge_ref, transfer_ref, basis_packed_ref, table_ref, at_ref, coupling_ref, packed_ref, basis_ref, sems,
 ):
     leaves, many, rank, _ = coupling_ref.shape
-    chunks = [(at, 4) for at in range(0, leaves - 4, 4)] + [(leaves - 4, 2), (leaves - 2, 2)]
+    chunks = [(at, 4) for at in range(0, leaves, 4)]
     at_in, *coupling_in, transfer_in, basis_in = start_all(
         [(at_vmem, at_ref)]
         + [(coupling_hbm.at[pl.ds(at, size)], coupling_ref.at[pl.ds(at, size)]) for at, size in chunks]
@@ -197,13 +199,16 @@
     sides = rim_ref.shape[1]
     left = left_half(sides, rank)
     parity = lax.rem(position(axes), 2)
-    for ref, base in (
-        (rim_ref, leaves), (even_ref, 2 * leaves * (1 - parity)), (odd_ref, 2 * leaves * parity),
-    ):
-        for a in range(pairs):
-            spread_pair(table_ref, base + 2 * a, ref[a], rank)
-    before = jnp.where(parity == 1, even_ref[pairs + 1], odd_ref[pairs + 1])
-    after = jnp.where(parity == 1, odd_ref[pairs], even_ref[pairs])
+    row = lax.axis_size(axes[1]) * lax.axis_size(axes[2])
+    at_end = lax.rem(position(axes) + 1, row) < 2
+    for a in range(pairs):
+        spread_pair(table_ref, leaves + 2 * a, rim_ref[a], rank)
+        spread_pair(table_ref, 2 * leaves * (1 - parity) + 2 * a, even_ref[a], rank)
+        odd = jnp.where(at_end, ends_ref[a], odd_ref[a])
+        spread_pair(table_ref, 2 * leaves * parity + 2 * a, odd, rank)
+    edge = jnp.where(at_end, jnp.where(parity == 1, ends_ref[pairs], ends_ref[pairs + 1]), odd_ref[pairs])
+    before = jnp.where(parity == 1, even_ref[pairs + 1], edge)
+    after = jnp.where(parity == 1, edge, even_ref[pairs])
     low = dot(before[:, width:], rim_near_ref[0], NT)
     high = dot(after[:, :width], rim_near_ref[1], NT)
     edge_ref[0] = jnp.concatenate([low, jnp.zeros_like(low)], axis=1)
@@ -232,7 +237,7 @@
 def down_kernel(
     axes, at_vmem, same_ref, even_ref, other_refs, packed_ref, counts_hbm,
     far_ref, near_ref, edge_ref, transfer_ref, basis_ref,
-    out_hbm, table_ref, at_ref, local_ref, down_ref, counts_ref, out_ref, sems, out_sems,
+    out_ref, table_ref, at_ref, local_ref, down_ref, counts_ref, sems,
 ):
     at_in, counts_in = start_all([(at_vmem, at_ref), (counts_hbm, counts_ref)], sems)
     parents, many = at_ref.shape
@@ -260,7 +265,6 @@
         local = far_ref[q] + dot(down_ref[q], transfer_ref[2 * q : 2 * q + 2].reshape(2 * rank, rank), NT)
         local_ref[q] = local.astype(jnp.bfloat16)
     counts_in.wait()
-    sent = []
     for q in range(parents):
         local = local_ref[q]
         none = jnp.zeros_like(local)
@@ -273,12 +277,6 @@
             total = total + edge_ref[1]
         total = jnp.where(pair_mask(counts_ref, q, sides, width), total, jnp.zeros_like(total))
         out_ref[:, 2 * width * q : 2 * width * (q + 1)] = total.astype(out_ref.dtype)
-        if (q + 1) % 4 == 0:
-            lanes = pl.ds(2 * width * (q - 3), 8 * width)
-            sent.append(pltpu.make_async_copy(out_ref.at[:, lanes], out_hbm.at[:, lanes], out_sems.at[q // 4]))
-            sent[-1].start()
-    for copy in sent:
-        copy.wait()
 
 
 def per_device(
@@ -306,17 +304,18 @@
     dma = lambda count: pltpu.SemaphoreType.DMA((count,))
     params = lambda mib: pltpu.CompilerParams(vmem_limit_bytes=mib * 2**20)
 
-    rim, even_rim, live, sent = pl.pallas_call(
-        up_kernel,
+    rim, even_rim, odd_rim, live, sent = pl.pallas_call(
+        functools.partial(up_kernel, axes),
         name="up",
         out_shape=[
             shape((pairs + 2, sides, 2 * rank), bf16),
             shape((pairs + 2 + own, sides, 2 * rank), bf16),
+            shape((pairs + 1, sides, 2 * rank), bf16),
             shape((pairs, sides, 2 * width), bf16),
             pltpu.HBM((n // 2 * own, sides, 2 * rank), bf16),
         ],
         in_specs=[HBM] * 4,
-        out_specs=[VMEM, VMEM, VMEM, HBM],
+        out_specs=[VMEM] * 4 + [HBM],
         scratch_shapes=[
             pltpu.SMEM((leaves,), jnp.int32),
             pltpu.VMEM((sides, leaves * width), bf16),
@@ -330,7 +329,9 @@
 
     even = lax.ppermute(even_rim, axes, [(i, i ^ 1) for i in range(total)])
     steps = [(i, i + 1) for i in range(1, total - 1, 2)]
-    odd = lax.ppermute(rim, axes, steps + [(b, a) for a, b in steps])
+    both_ways = lambda pairs: pairs + [(b, a) for a, b in pairs]
+    ends = lax.ppermute(rim, axes, both_ways([s for s in steps if s[1] % n == 0]))
+    odd = lax.ppermute(odd_rim, axes, both_ways([s for s in steps if s[1] % n]))
     same = lax.all_to_all(sent, "gz", 0, 0, tiled=True)
 
     parent_packed, near, rim_near, leaf_at, parent_at = pl.pallas_call(
@@ -373,7 +374,7 @@
             shape(transfer.shape, bf16),
             shape((pairs, width, 2 * rank), bf16),
         ],
-        in_specs=[VMEM] * 5 + [HBM] * 3,
+        in_specs=[VMEM] * 6 + [HBM] * 3,
         out_specs=[VMEM] * 4,
         scratch_shapes=[
             pltpu.VMEM((3 * leaves, sides, 2 * rank), bf16),
@@ -381,26 +382,24 @@
             pltpu.VMEM(leaf_coupling.shape, bf16),
             pltpu.VMEM((leaves, rank, many * rank), bf16),
             pltpu.VMEM(basis.shape, bf16),
-            dma(4 + leaves // 4),
+            dma(3 + leaves // 4),
         ],
         compiler_params=params(20),
-    )(leaf_at, rim, even, odd, rim_near, *keep(leaf_coupling, transfer, basis))
+    )(leaf_at, rim, even, ends, odd, rim_near, *keep(leaf_coupling, transfer, basis))
 
     out = pl.pallas_call(
         functools.partial(down_kernel, axes[1:]),
         name="down",
-        out_shape=pltpu.HBM((sides, leaves * width), bf16),
+        out_shape=jax.ShapeDtypeStruct((sides, leaves * width), bf16),
         in_specs=[VMEM, VMEM, VMEM, [VMEM] * 2, VMEM, HBM] + [VMEM] * 5,
-        out_specs=HBM,
+        out_specs=VMEM,
         scratch_shapes=[
             pltpu.VMEM((n * parents, sides, 2 * rank), bf16),
             pltpu.SMEM((parents, many), jnp.int32),
             pltpu.VMEM((pairs, sides, 2 * rank), bf16),
             pltpu.VMEM((parents, sides, rank), bf16),
             pltpu.SMEM((leaves,), jnp.int32),
-            pltpu.VMEM((sides, leaves * width), bf16),
             dma(2),
-            dma(parents // 4),
         ],
         compiler_params=params(12),
     )(parent_at, same, even, other, parent_packed, *keep(panel_counts), far, near, edge, transfer_in, basis_in)

time: 30.4 us -> 30.9 us (1.016)
  waiting for transfers between devices: 4.69 us -> 3.87 us
  starting transfers between devices: 12.3 us -> 13.1 us
  Pallas kernels: 13.1 us -> 13.6 us
    all_to_all x1, waiting for transfers between devices: 4.68 us -> 3.82 us  [per_device(): same = lax.all_to_all(sent, 'gz', 0, 0, tiled=True)]
    pallas_call x1, Pallas kernels: 2.55 us -> 3.3 us  [per_device(): pl.pallas_call(functools.partial(up_kernel, axes), name='up', out_shape=[...]
    ppermute x1 -> x2, starting transfers between devices: 0.66 us -> 1.33 us  [the longest x1 0.67 us: per_device(): odd = lax.ppermute(odd_rim, axes, both_ways([s for s in steps if s[1] % n]))]
  transfers between devices with their start and end apart: 5 -> 6, of which waited for: 1 -> 1; matrix products, arithmetic and copies ran while one was open for 0% -> 0% of each run, Pallas kernels for 26% -> 25%
where the time goes in v22:
time: 30.9 us; the launch traced here: 30.7 us
  Pallas kernels  13.6 us (44%)
  starting transfers between devices  13.1 us (42%)
  waiting for transfers between devices  3.87 us (13%)
    all_to_all x1, starting transfers between devices, per_device(): same = lax.all_to_all(sent, 'gz', 0, 0, tiled=True)  6.33 us
    pallas_call x1, Pallas kernels, per_device(): pl.pallas_call(functools.partial(leaf_kernel, axes), name='leaf', out_sha...  4.47 us
    ppermute x2, starting transfers between devices, per_device(): other = [lax.ppermute(piece, 'gp', [(0, 1), (1, 0)]) for piece in pieces]  3.96 us
    all_to_all x1, waiting for transfers between devices, per_device(): same = lax.all_to_all(sent, 'gz', 0, 0, tiled=True)  3.82 us
    pallas_call x1, Pallas kernels, per_device(): pl.pallas_call(functools.partial(up_kernel, axes), name='up', out_shape=[...  3.3 us
    pallas_call x1, Pallas kernels, per_device(): pl.pallas_call(functools.partial(mid_kernel, axes), name='mid', out_shape...  3.09 us
    pallas_call x1, Pallas kernels, per_device(): pl.pallas_call(functools.partial(down_kernel, axes[1:]), name='down', out...  2.72 us
    ppermute x1, starting transfers between devices, per_device(): even = lax.ppermute(even_rim, axes, [(i, i ^ 1) for i in range(total)])  1.52 us
  transfers between devices with their start and end apart: 6, of which 1 were waited for; matrix products, arithmetic and copies ran while one was open for 0% of the time, Pallas kernels for 25%

profile of v22, /device:TPU:0, one launch (start us, length us, event | category | flops | bytes accessed | tf_op | source)
XLA Modules:
  0.0 30.7 jit_solution(7425161436995092135)
XLA Ops:
  0.0 3.3 %up.1 = (bf16[18,32,128]{2,1,0:T(8,128)(2,1)S(1)}, bf16[26,32,128]{2,1,0:T(8,128)(2,1)}, bf16[17,32,128]{2,1,0:T(8,128)(2,1)}, bf16[16,32,128]{2,1,0:T(8,128)(2,1)S(1)}, bf16[32,32,128]{2,1,0:T(8,128)(2,1)}) custom-call(s32[32]{0:T(128)} %counts_hbm.3, bf16[32,2048]{1,0:T(8,128)(2,1)} %bitcast.3, bf16[32,64,64]{2,1,0:T(8,128)(2,1)} %basis_hbm.3, ...), custom_call_target="tpu_custom_call" | custom-call | tf_op jit(solution)/shard_map/up/pallas_call | solution.py:307
  3.3 6.3 %all-to-all-start = ((bf16[32,32,128]{2,1,0:T(8,128)(2,1)}), bf16[32,32,128]{2,1,0:T(8,128)(2,1)S(1)}, u32[]{:S(2)}, u32[]{:S(2)}) async-start(bf16[32,32,128]{2,1,0:T(8,128)(2,1)} %get-tuple-element.23), calls=%async_computation | async-start | bytes 524288 | tf_op jit(solution)/shard_map/all_to_all | solution.py:335
  9.6 1.5 %collective-permute-start = (bf16[26,32,128]{2,1,0:T(8,128)(2,1)}, bf16[26,32,128]{2,1,0:T(8,128)(2,1)S(1)}, u32[]{:S(2)}, u32[]{:S(2)}) collective-permute-start(bf16[26,32,128]{2,1,0:T(8,128)(2,1)} %get-tuple-element.24), channel_id=1, source_target_pairs={{0,1},{1,0},{2,3},{3,2},{4,5},{5,4},{6,7},{7,6},{8,9},{9,8},{10,11... | collective-permute-start | bytes 638984 | tf_op jit(solution)/shard_map/ppermute | solution.py:330
  11.2 0.7 %collective-permute-start.3 = (bf16[18,32,128]{2,1,0:T(8,128)(2,1)S(1)}, bf16[18,32,128]{2,1,0:T(8,128)(2,1)S(1)}, u32[]{:S(2)}, u32[]{:S(2)}) collective-permute-start(bf16[18,32,128]{2,1,0:T(8,128)(2,1)S(1)} %get-tuple-element.29.rim_ref), channel_id=1, source_target_pairs={{7,8},{15,16},{23,24},{8,7},{16,15},{24,23}} | collective-permute-start | bytes 442376 | tf_op jit(solution)/shard_map/ppermute | solution.py:333
  11.8 0.7 %collective-permute-start.4 = (bf16[17,32,128]{2,1,0:T(8,128)(2,1)}, bf16[17,32,128]{2,1,0:T(8,128)(2,1)S(1)}, u32[]{:S(2)}, u32[]{:S(2)}) collective-permute-start(bf16[17,32,128]{2,1,0:T(8,128)(2,1)} %get-tuple-element.30), channel_id=1, source_target_pairs={{1,2},{3,4},{5,6},{9,10},{11,12},{13,14},{17,18},{19,20},{21,22},{... | collective-permute-start | bytes 417800 | tf_op jit(solution)/shard_map/ppermute | solution.py:334
  12.5 3.1 %mid.1 = (bf16[16,64,1024]{2,1,0:T(8,128)(2,1)S(1)}, f32[16,32,128]{2,1,0:T(8,128)S(1)}, bf16[2,64,64]{2,1,0:T(8,128)(2,1)S(1)}, s32[16,32]{1,0:T(8,128)S(1)}, s32[16,16]{1,0:T(8,128)S(1)}) custom-call(bf16[16,32,128]{2,1,0:T(8,128)(2,1)S(1)} %get-tuple-element.21.live_ref, bf16[32,3,64,64]{3,2,1,0:T(8,128)(2,1)} %near_hbm.1, ...), custom_call_target="tpu_custom_call" | custom-call | tf_op jit(solution)/shard_map/mid/pallas_call | solution.py:337
  15.6 3.8 %all-to-all-done.whole_ref.same_ref = bf16[32,32,128]{2,1,0:T(8,128)(2,1)S(1)} async-done(((bf16[32,32,128]{2,1,0:T(8,128)(2,1)}), bf16[32,32,128]{2,1,0:T(8,128)(2,1)S(1)}, u32[]{:S(2)}, u32[]{:S(2)}) %all-to-all-start) | async-done | bytes 262176 | tf_op jit(solution)/shard_map/all_to_all | solution.py:335
  19.4 3.9 %collective-permute-start.1 = (bf16[12,32,128]{2,1,0:T(8,128)(2,1)S(1)}, bf16[12,32,128]{2,1,0:T(8,128)(2,1)S(1)}, u32[]{:S(2)}, u32[]{:S(2)}) collective-permute-start(bf16[12,32,128]{2,1,0:T(8,128)(2,1)S(1)} %get-tuple-element.25), channel_id=1, source_target_pairs={{0,1},{1,0},{2,3},{3,2},{4,5},{5,4},{6,7},{7,6},{8,9},{9,8},{10,11... | collective-permute-start | bytes 294920 | tf_op jit(solution)/shard_map/ppermute | solution.py:366
  23.3 0.1 collective-permute-start.2
  23.4 0.0 collective-permute-done.4.odd_ref
  23.4 0.0 collective-permute-done.3.ends_ref
  23.4 0.0 collective-permute-done.even_ref
  23.4 4.5 %leaf.1 = (f32[16,32,128]{2,1,0:T(8,128)S(1)}, f32[2,32,128]{2,1,0:T(8,128)S(1)}, bf16[32,64,64]{2,1,0:T(8,128)(2,1)S(1)}, bf16[16,64,128]{2,1,0:T(8,128)(2,1)S(1)}) custom-call(s32[16,32]{1,0:T(8,128)S(1)} %get-tuple-element.28.at_vmem, bf16[18,32,128]{2,1,0:T(8,128)(2,1)S(1)} %get-tuple-element.29.rim_ref, ...), custom_call_target="tpu_custom_call" | custom-call | tf_op jit(solution)/shard_map/leaf/pallas_call | solution.py:368
  27.9 0.0 collective-permute-done.1.other_refs_0_
  27.9 0.0 collective-permute-done.2.other_refs_1_
  27.9 2.7 %down.1 = bf16[32,2048]{1,0:T(8,128)(2,1)} custom-call(s32[16,16]{1,0:T(8,128)S(1)} %get-tuple-element.22.at_ref.at_vmem, bf16[32,32,128]{2,1,0:T(8,128)(2,1)S(1)} %all-to-all-done.whole_ref.same_ref, bf16[26,32,128]{2,1,0:T(8,128)(2,1)S(1)} %collective-permute-done.even_ref, bf16[12,32,128]{2,1,0:T(8,128)(2,1)S(1)} %collective-permute-done.1.other_refs_0_, ...), custom_call_target="tpu_custom_call" | custom-call | tf_op jit(solution)/shard_map/down/pallas_call | solution.py:390
  (1 shorter events, 0.0 us)
Async XLA Ops:
  3.3 16.1 %all-to-all-start = ((bf16[32,32,128]{2,1,0:T(8,128)(2,1)}), bf16[32,32,128]{2,1,0:T(8,128)(2,1)S(1)}, u32[]{:S(2)}, u32[]{:S(2)}) async-start(bf16[32,32,128]{2,1,0:T(8,128)(2,1)} %get-tuple-element.23), calls=%async_computation | async-start | bytes 524288 | tf_op jit(solution)/shard_map/all_to_all | solution.py:335
  9.6 13.8 %collective-permute-start = (bf16[26,32,128]{2,1,0:T(8,128)(2,1)}, bf16[26,32,128]{2,1,0:T(8,128)(2,1)S(1)}, u32[]{:S(2)}, u32[]{:S(2)}) collective-permute-start(bf16[26,32,128]{2,1,0:T(8,128)(2,1)} %get-tuple-element.24), channel_id=1, source_target_pairs={{0,1},{1,0},{2,3},{3,2},{4,5},{5,4},{6,7},{7,6},{8,9},{9,8},{10,11... | collective-permute-start | bytes 638984 | tf_op jit(solution)/shard_map/ppermute | solution.py:330
  11.2 12.2 %collective-permute-start.3 = (bf16[18,32,128]{2,1,0:T(8,128)(2,1)S(1)}, bf16[18,32,128]{2,1,0:T(8,128)(2,1)S(1)}, u32[]{:S(2)}, u32[]{:S(2)}) collective-permute-start(bf16[18,32,128]{2,1,0:T(8,128)(2,1)S(1)} %get-tuple-element.29.rim_ref), channel_id=1, source_target_pairs={{7,8},{15,16},{23,24},{8,7},{16,15},{24,23}} | collective-permute-start | bytes 442376 | tf_op jit(solution)/shard_map/ppermute | solution.py:333
  11.8 11.6 %collective-permute-start.4 = (bf16[17,32,128]{2,1,0:T(8,128)(2,1)}, bf16[17,32,128]{2,1,0:T(8,128)(2,1)S(1)}, u32[]{:S(2)}, u32[]{:S(2)}) collective-permute-start(bf16[17,32,128]{2,1,0:T(8,128)(2,1)} %get-tuple-element.30), channel_id=1, source_target_pairs={{1,2},{3,4},{5,6},{9,10},{11,12},{13,14},{17,18},{19,20},{21,22},{... | collective-permute-start | bytes 417800 | tf_op jit(solution)/shard_map/ppermute | solution.py:334
  19.4 8.5 %collective-permute-start.1 = (bf16[12,32,128]{2,1,0:T(8,128)(2,1)S(1)}, bf16[12,32,128]{2,1,0:T(8,128)(2,1)S(1)}, u32[]{:S(2)}, u32[]{:S(2)}) collective-permute-start(bf16[12,32,128]{2,1,0:T(8,128)(2,1)S(1)} %get-tuple-element.25), channel_id=1, source_target_pairs={{0,1},{1,0},{2,3},{3,2},{4,5},{5,4},{6,7},{7,6},{8,9},{9,8},{10,11... | collective-permute-start | bytes 294920 | tf_op jit(solution)/shard_map/ppermute | solution.py:366
  23.3 4.6 %collective-permute-start.2 = (bf16[12,32,128]{2,1,0:T(8,128)(2,1)S(1)}, bf16[12,32,128]{2,1,0:T(8,128)(2,1)S(1)}, u32[]{:S(2)}, u32[]{:S(2)}) collective-permute-start(bf16[12,32,128]{2,1,0:T(8,128)(2,1)S(1)} %get-tuple-element.26), channel_id=1, source_target_pairs={{0,1},{1,0},{2,3},{3,2},{4,5},{5,4},{6,7},{7,6},{8,9},{9,8},{10,11... | collective-permute-start | bytes 294920 | tf_op jit(solution)/shard_map/ppermute | solution.py:366

commit v23 on v19

--- a/solution.py
+++ b/solution.py
@@ -182,7 +182,7 @@
     far_ref, edge_ref, transfer_ref, basis_packed_ref, table_ref, at_ref, coupling_ref, packed_ref, basis_ref, sems,
 ):
     leaves, many, rank, _ = coupling_ref.shape
-    chunks = [(at, 4) for at in range(0, leaves - 4, 4)] + [(leaves - 4, 2), (leaves - 2, 2)]
+    chunks = [(at, 4) for at in range(0, leaves, 4)]
     at_in, *coupling_in, transfer_in, basis_in = start_all(
         [(at_vmem, at_ref)]
         + [(coupling_hbm.at[pl.ds(at, size)], coupling_ref.at[pl.ds(at, size)]) for at, size in chunks]
@@ -229,7 +229,7 @@
 def down_kernel(
     axes, at_vmem, same_ref, other_own_ref, other_refs, packed_ref, counts_hbm,
     far_ref, near_ref, edge_ref, transfer_ref, basis_ref,
-    out_hbm, table_ref, at_ref, local_ref, down_ref, counts_ref, out_ref, sems, out_sems,
+    out_ref, table_ref, at_ref, local_ref, down_ref, counts_ref, sems,
 ):
     at_in, counts_in = start_all([(at_vmem, at_ref), (counts_hbm, counts_ref)], sems)
     parents, many = at_ref.shape
@@ -256,7 +256,6 @@
         local = far_ref[q] + dot(down_ref[q], transfer_ref[2 * q : 2 * q + 2].reshape(2 * rank, rank), NT)
         local_ref[q] = local.astype(jnp.bfloat16)
     counts_in.wait()
-    sent = []
     for q in range(parents):
         local = local_ref[q]
         none = jnp.zeros_like(local)
@@ -269,12 +268,6 @@
             total = total + edge_ref[1]
         total = jnp.where(pair_mask(counts_ref, q, sides, width), total, jnp.zeros_like(total))
         out_ref[:, 2 * width * q : 2 * width * (q + 1)] = total.astype(out_ref.dtype)
-        if (q + 1) % 4 == 0:
-            lanes = pl.ds(2 * width * (q - 3), 8 * width)
-            sent.append(pltpu.make_async_copy(out_ref.at[:, lanes], out_hbm.at[:, lanes], out_sems.at[q // 4]))
-            sent[-1].start()
-    for copy in sent:
-        copy.wait()
 
 
 def per_device(
@@ -378,7 +371,7 @@
             pltpu.VMEM(leaf_coupling.shape, bf16),
             pltpu.VMEM((leaves, rank, many * rank), bf16),
             pltpu.VMEM(basis.shape, bf16),
-            dma(4 + leaves // 4),
+            dma(3 + leaves // 4),
         ],
         compiler_params=params(20),
     )(leaf_at, rim, even, odd, rim_near, *keep(leaf_coupling, transfer, basis))
@@ -386,18 +379,16 @@
     out = pl.pallas_call(
         functools.partial(down_kernel, axes[1:]),
         name="down",
-        out_shape=pltpu.HBM((sides, leaves * width), bf16),
+        out_shape=jax.ShapeDtypeStruct((sides, leaves * width), bf16),
         in_specs=[VMEM, VMEM, VMEM, [VMEM] * 2, VMEM, HBM] + [VMEM] * 5,
-        out_specs=HBM,
+        out_specs=VMEM,
         scratch_shapes=[
             pltpu.VMEM((n * parents, sides, 2 * rank), bf16),
             pltpu.SMEM((parents, many), jnp.int32),
             pltpu.VMEM((pairs, sides, 2 * rank), bf16),
             pltpu.VMEM((parents, sides, rank), bf16),
             pltpu.SMEM((leaves,), jnp.int32),
-            pltpu.VMEM((sides, leaves * width), bf16),
             dma(2),
-            dma(parents // 4),
         ],
         compiler_params=params(12),
     )(parent_at, same, other_own, other, parent_packed, *keep(panel_counts), far, near, edge, transfer_in, basis_in)

time: 29.7 us -> 29.4 us (0.990)
  Pallas kernels: 13.2 us -> 12.9 us
where the time goes in v23:
time: 29.4 us; the launch traced here: 29.2 us
  starting transfers between devices  16.2 us (55%)
  Pallas kernels  12.9 us (44%)
    ppermute x1, starting transfers between devices, per_device(): odd = lax.ppermute(rim, axes, steps + [(b, a) for a, b in steps])  7.8 us
    all_to_all x1, starting transfers between devices, per_device(): same = lax.all_to_all(sent, 'gz', 0, 0, tiled=True)  5.43 us
    pallas_call x1, Pallas kernels, per_device(): pl.pallas_call(functools.partial(leaf_kernel, axes), name='leaf', out_sha...  4.49 us
    pallas_call x1, Pallas kernels, per_device(): pl.pallas_call(functools.partial(mid_kernel, axes), name='mid', out_shape...  3.09 us
    pallas_call x1, Pallas kernels, per_device(): pl.pallas_call(functools.partial(down_kernel, axes[1:]), name='down', out...  2.72 us
    pallas_call x1, Pallas kernels, per_device(): pl.pallas_call(up_kernel, name='up', out_shape=[shape((pairs + 2, sides,...  2.56 us
    ppermute x2, starting transfers between devices, per_device(): other = [lax.ppermute(piece, 'gp', [(0, 1), (1, 0)]) for piece in pieces]  1.52 us
    ppermute x1, starting transfers between devices, per_device(): other_own = lax.ppermute(parent_coef, 'gp', [(0, 1), (1, 0)])  1.24 us
  transfers between devices with their start and end apart: 6, of which 0 were waited for; matrix products, arithmetic and copies ran while one was open for 0% of the time, Pallas kernels for 26%

profile of v23, /device:TPU:1, one launch (start us, length us, event | category | flops | bytes accessed | tf_op | source)
XLA Modules:
  0.0 29.2 jit_solution(13797146330168703174)
XLA Ops:
  0.0 2.6 %up.1 = (bf16[18,32,128]{2,1,0:T(8,128)(2,1)S(1)}, bf16[16,32,128]{2,1,0:T(8,128)(2,1)S(1)}, bf16[8,32,128]{2,1,0:T(8,128)(2,1)S(1)}, bf16[32,32,128]{2,1,0:T(8,128)(2,1)}) custom-call(s32[32]{0:T(128)} %counts_hbm.3, bf16[32,2048]{1,0:T(8,128)(2,1)} %bitcast.3, bf16[32,64,64]{2,1,0:T(8,128)(2,1)} %basis_hbm.3, bf16[32,64,64]{2,1,0:T(8,128)(2,1)} %transfer_hbm.3), custom_call_target="tpu_custom_call" | custom-call | tf_op jit(solution)/shard_map/up/pallas_call | solution.py:298
  2.6 5.4 %all-to-all-start = ((bf16[32,32,128]{2,1,0:T(8,128)(2,1)}), bf16[32,32,128]{2,1,0:T(8,128)(2,1)S(1)}, u32[]{:S(2)}, u32[]{:S(2)}) async-start(bf16[32,32,128]{2,1,0:T(8,128)(2,1)} %get-tuple-element.22), calls=%async_computation | async-start | bytes 524288 | tf_op jit(solution)/shard_map/all_to_all | solution.py:323
  8.0 1.2 %collective-permute-start = (bf16[8,32,128]{2,1,0:T(8,128)(2,1)S(1)}, bf16[8,32,128]{2,1,0:T(8,128)(2,1)S(1)}, u32[]{:S(2)}, u32[]{:S(2)}) collective-permute-start(bf16[8,32,128]{2,1,0:T(8,128)(2,1)S(1)} %get-tuple-element.23), channel_id=1, source_target_pairs={{0,1},{1,0},{2,3},{3,2},{4,5},{5,4},{6,7},{7,6},{8,9},{9,8},{10,11... | collective-permute-start | bytes 196616 | tf_op jit(solution)/shard_map/ppermute | solution.py:345
  9.2 0.2 collective-permute-start.3
  9.5 7.8 %collective-permute-start.4 = (bf16[18,32,128]{2,1,0:T(8,128)(2,1)S(1)}, bf16[18,32,128]{2,1,0:T(8,128)(2,1)S(1)}, u32[]{:S(2)}, u32[]{:S(2)}) collective-permute-start(bf16[18,32,128]{2,1,0:T(8,128)(2,1)S(1)} %get-tuple-element.28.rim_ref), channel_id=1, source_target_pairs={{1,2},{3,4},{5,6},{7,8},{9,10},{11,12},{13,14},{15,16},{17,18},{19... | collective-permute-start | bytes 442376 | tf_op jit(solution)/shard_map/ppermute | solution.py:322
  17.3 3.1 %mid.1 = (bf16[16,64,1024]{2,1,0:T(8,128)(2,1)S(1)}, f32[16,32,128]{2,1,0:T(8,128)S(1)}, bf16[2,64,64]{2,1,0:T(8,128)(2,1)S(1)}, s32[16,32]{1,0:T(8,128)S(1)}, s32[16,16]{1,0:T(8,128)S(1)}) custom-call(bf16[16,32,128]{2,1,0:T(8,128)(2,1)S(1)} %get-tuple-element.20.live_ref, bf16[32,3,64,64]{3,2,1,0:T(8,128)(2,1)} %near_hbm.1, ...), custom_call_target="tpu_custom_call" | custom-call | tf_op jit(solution)/shard_map/mid/pallas_call | solution.py:325
  20.4 0.0 collective-permute-done.own_ref.other_own_ref
  20.4 0.0 all-to-all-done.whole_ref.same_ref
  20.4 0.1 collective-permute-start.1
  20.5 1.5 %collective-permute-start.2 = (bf16[12,32,128]{2,1,0:T(8,128)(2,1)S(1)}, bf16[12,32,128]{2,1,0:T(8,128)(2,1)S(1)}, u32[]{:S(2)}, u32[]{:S(2)}) collective-permute-start(bf16[12,32,128]{2,1,0:T(8,128)(2,1)S(1)} %get-tuple-element.25), channel_id=1, source_target_pairs={{0,1},{1,0},{2,3},{3,2},{4,5},{5,4},{6,7},{7,6},{8,9},{9,8},{10,11... | collective-permute-start | bytes 294920 | tf_op jit(solution)/shard_map/ppermute | solution.py:355
  22.0 0.0 collective-permute-done.3.even_ref
  22.0 0.0 collective-permute-done.4.odd_ref
  22.0 4.5 %leaf.1 = (f32[16,32,128]{2,1,0:T(8,128)S(1)}, f32[2,32,128]{2,1,0:T(8,128)S(1)}, bf16[32,64,64]{2,1,0:T(8,128)(2,1)S(1)}, bf16[16,64,128]{2,1,0:T(8,128)(2,1)S(1)}) custom-call(s32[16,32]{1,0:T(8,128)S(1)} %get-tuple-element.27.at_vmem, bf16[18,32,128]{2,1,0:T(8,128)(2,1)S(1)} %get-tuple-element.28.rim_ref, ...), custom_call_target="tpu_custom_call" | custom-call | tf_op jit(solution)/shard_map/leaf/pallas_call | solution.py:357
  26.5 0.0 collective-permute-done.1.other_refs_0_
  26.5 0.0 collective-permute-done.2.other_refs_1_
  26.5 2.7 %down.1 = bf16[32,2048]{1,0:T(8,128)(2,1)} custom-call(s32[16,16]{1,0:T(8,128)S(1)} %get-tuple-element.21.at_ref.at_vmem, bf16[32,32,128]{2,1,0:T(8,128)(2,1)S(1)} %all-to-all-done.whole_ref.same_ref, bf16[8,32,128]{2,1,0:T(8,128)(2,1)S(1)} %collective-permute-done.own_ref.other_own_ref, bf16[12,32,128]{2,1,0:T(8,128)(2,1)S(1)} %collective-permute-done.1.other_refs_0_, ...), custom_call_target="tpu_custom_call" | custom-call | tf_op jit(solution)/shard_map/down/pallas_call | solution.py:379
  (1 shorter events, 0.0 us)
Async XLA Ops:
  2.6 17.8 %all-to-all-start = ((bf16[32,32,128]{2,1,0:T(8,128)(2,1)}), bf16[32,32,128]{2,1,0:T(8,128)(2,1)S(1)}, u32[]{:S(2)}, u32[]{:S(2)}) async-start(bf16[32,32,128]{2,1,0:T(8,128)(2,1)} %get-tuple-element.22), calls=%async_computation | async-start | bytes 524288 | tf_op jit(solution)/shard_map/all_to_all | solution.py:323
  8.0 12.4 %collective-permute-start = (bf16[8,32,128]{2,1,0:T(8,128)(2,1)S(1)}, bf16[8,32,128]{2,1,0:T(8,128)(2,1)S(1)}, u32[]{:S(2)}, u32[]{:S(2)}) collective-permute-start(bf16[8,32,128]{2,1,0:T(8,128)(2,1)S(1)} %get-tuple-element.23), channel_id=1, source_target_pairs={{0,1},{1,0},{2,3},{3,2},{4,5},{5,4},{6,7},{7,6},{8,9},{9,8},{10,11... | collective-permute-start | bytes 196616 | tf_op jit(solution)/shard_map/ppermute | solution.py:345
  9.2 12.7 %collective-permute-start.3 = (bf16[18,32,128]{2,1,0:T(8,128)(2,1)S(1)}, bf16[18,32,128]{2,1,0:T(8,128)(2,1)S(1)}, u32[]{:S(2)}, u32[]{:S(2)}) collective-permute-start(bf16[18,32,128]{2,1,0:T(8,128)(2,1)S(1)} %get-tuple-element.28.rim_ref), channel_id=1, source_target_pairs={{0,1},{1,0},{2,3},{3,2},{4,5},{5,4},{6,7},{7,6},{8,9},{9,8},{10,11... | collective-permute-start | bytes 442376 | tf_op jit(solution)/shard_map/ppermute | solution.py:320
  9.5 12.5 %collective-permute-start.4 = (bf16[18,32,128]{2,1,0:T(8,128)(2,1)S(1)}, bf16[18,32,128]{2,1,0:T(8,128)(2,1)S(1)}, u32[]{:S(2)}, u32[]{:S(2)}) collective-permute-start(bf16[18,32,128]{2,1,0:T(8,128)(2,1)S(1)} %get-tuple-element.28.rim_ref), channel_id=1, source_target_pairs={{1,2},{3,4},{5,6},{7,8},{9,10},{11,12},{13,14},{15,16},{17,18},{19... | collective-permute-start | bytes 442376 | tf_op jit(solution)/shard_map/ppermute | solution.py:322
  20.4 6.0 %collective-permute-start.1 = (bf16[12,32,128]{2,1,0:T(8,128)(2,1)S(1)}, bf16[12,32,128]{2,1,0:T(8,128)(2,1)S(1)}, u32[]{:S(2)}, u32[]{:S(2)}) collective-permute-start(bf16[12,32,128]{2,1,0:T(8,128)(2,1)S(1)} %get-tuple-element.24), channel_id=1, source_target_pairs={{0,1},{1,0},{2,3},{3,2},{4,5},{5,4},{6,7},{7,6},{8,9},{9,8},{10,11... | collective-permute-start | bytes 294920 | tf_op jit(solution)/shard_map/ppermute | solution.py:355
  20.5 6.0 %collective-permute-start.2 = (bf16[12,32,128]{2,1,0:T(8,128)(2,1)S(1)}, bf16[12,32,128]{2,1,0:T(8,128)(2,1)S(1)}, u32[]{:S(2)}, u32[]{:S(2)}) collective-permute-start(bf16[12,32,128]{2,1,0:T(8,128)(2,1)S(1)} %get-tuple-element.25), channel_id=1, source_target_pairs={{0,1},{1,0},{2,3},{3,2},{4,5},{5,4},{6,7},{7,6},{8,9},{9,8},{10,11... | collective-permute-start | bytes 294920 | tf_op jit(solution)/shard_map/ppermute | solution.py:355

commit v24 on v23

--- a/solution.py
+++ b/solution.py
@@ -178,8 +178,9 @@
 
 
 def leaf_kernel(
-    axes, at_vmem, rim_ref, even_ref, odd_ref, rim_near_ref, coupling_hbm, transfer_hbm, basis_hbm,
-    far_ref, edge_ref, transfer_ref, basis_packed_ref, table_ref, at_ref, coupling_ref, packed_ref, basis_ref, sems,
+    axes, at_vmem, rim_ref, even_ref, odd_ref, rim_near_ref, same_ref, other_own_ref,
+    coupling_hbm, transfer_hbm, basis_hbm,
+    far_ref, edge_ref, transfer_ref, basis_packed_ref, parent_table_ref, table_ref, at_ref, coupling_ref, packed_ref, basis_ref, sems,
 ):
     leaves, many, rank, _ = coupling_ref.shape
     chunks = [(at, 4) for at in range(0, leaves, 4)]
@@ -199,6 +200,12 @@
     ):
         for a in range(pairs):
             spread_pair(table_ref, base + 2 * a, ref[a], rank)
+    own, half = other_own_ref.shape[0], 2 * same_ref.shape[0]
+    for t in range(same_ref.shape[0]):
+        spread_pair(parent_table_ref, half * parity + 2 * t, same_ref[t], rank)
+    for t in range(own):
+        place = lax.axis_index(axes[1]) * own + t
+        spread_pair(parent_table_ref, half * (1 - parity) + 2 * place, other_own_ref[t], rank)
     before = jnp.where(parity == 1, even_ref[pairs + 1], odd_ref[pairs + 1])
     after = jnp.where(parity == 1, odd_ref[pairs], even_ref[pairs])
     low = dot(before[:, width:], rim_near_ref[0], NT)
@@ -227,23 +234,20 @@
 
 
 def down_kernel(
-    axes, at_vmem, same_ref, other_own_ref, other_refs, packed_ref, counts_hbm,
+    axes, at_vmem, table_in, other_refs, packed_ref, counts_hbm,
     far_ref, near_ref, edge_ref, transfer_ref, basis_ref,
     out_ref, table_ref, at_ref, local_ref, down_ref, counts_ref, sems,
 ):
+    del table_in
     at_in, counts_in = start_all([(at_vmem, at_ref), (counts_hbm, counts_ref)], sems)
     parents, many = at_ref.shape
     rank = packed_ref.shape[1]
     width = basis_ref.shape[1]
-    sides = same_ref.shape[1]
-    half = 2 * same_ref.shape[0]
+    sides = table_ref.shape[1]
+    half = table_ref.shape[0] // 2
     left = left_half(sides, rank)
     parity, mine, count = lax.axis_index(axes[1]), lax.axis_index(axes[0]), lax.axis_size(axes[0])
-    own, piece = other_own_ref.shape[0], other_refs[0].shape[0]
-    for t in range(count * own):
-        spread_pair(table_ref, half * parity + 2 * t, same_ref[t], rank)
-    for t in range(own):
-        spread_pair(table_ref, half * (1 - parity) + 2 * (mine * own + t), other_own_ref[t], rank)
+    own, piece = half // 2 // count, other_refs[0].shape[0]
     for t in range(2 * piece):
         place = lax.rem(mine + 1 + t // own, count) * own + t % own
         spread_pair(table_ref, half * (1 - parity) + 2 * place, other_refs[t // piece][t % piece], rank)
@@ -354,7 +358,7 @@
     )(same, other_own, parent_at)
     other = [lax.ppermute(piece, "gp", [(0, 1), (1, 0)]) for piece in pieces]
 
-    far, edge, transfer_in, basis_in = pl.pallas_call(
+    far, edge, transfer_in, basis_in, parent_table = pl.pallas_call(
         functools.partial(leaf_kernel, axes),
         name="leaf",
         out_shape=[
@@ -362,9 +366,10 @@
             shape((2, sides, 2 * width), f32),
             shape(transfer.shape, bf16),
             shape((pairs, width, 2 * rank), bf16),
-        ],
-        in_specs=[VMEM] * 5 + [HBM] * 3,
-        out_specs=[VMEM] * 4,
+            shape((n * parents, sides, 2 * rank), bf16),
+        ],
+        in_specs=[VMEM] * 7 + [HBM] * 3,
+        out_specs=[VMEM] * 5,
         scratch_shapes=[
             pltpu.VMEM((3 * leaves, sides, 2 * rank), bf16),
             pltpu.SMEM((many, leaves), jnp.int32),
@@ -374,16 +379,19 @@
             dma(3 + leaves // 4),
         ],
         compiler_params=params(20),
-    )(leaf_at, rim, even, odd, rim_near, *keep(leaf_coupling, transfer, basis))
-
-    out = pl.pallas_call(
+    )(leaf_at, rim, even, odd, rim_near, same, other_own, *keep(leaf_coupling, transfer, basis))
+
+    out, _ = pl.pallas_call(
         functools.partial(down_kernel, axes[1:]),
         name="down",
-        out_shape=jax.ShapeDtypeStruct((sides, leaves * width), bf16),
-        in_specs=[VMEM, VMEM, VMEM, [VMEM] * 2, VMEM, HBM] + [VMEM] * 5,
-        out_specs=VMEM,
+        out_shape=[
+            jax.ShapeDtypeStruct((sides, leaves * width), bf16),
+            shape((n * parents, sides, 2 * rank), bf16),
+        ],
+        in_specs=[VMEM, VMEM, [VMEM] * 2, VMEM, HBM] + [VMEM] * 5,
+        out_specs=[VMEM, VMEM],
+        input_output_aliases={1: 1},
         scratch_shapes=[
-            pltpu.VMEM((n * parents, sides, 2 * rank), bf16),
             pltpu.SMEM((parents, many), jnp.int32),
             pltpu.VMEM((pairs, sides, 2 * rank), bf16),
             pltpu.VMEM((parents, sides, rank), bf16),
@@ -391,7 +399,7 @@
             dma(2),
         ],
         compiler_params=params(12),
-    )(parent_at, same, other_own, other, parent_packed, *keep(panel_counts), far, near, edge, transfer_in, basis_in)
+    )(parent_at, parent_table, other, parent_packed, *keep(panel_counts), far, near, edge, transfer_in, basis_in)
     return out.T
 
 

time: 29.4 us -> 31.1 us (1.058)
  the two profiles are of different devices: /device:TPU:1 before, /device:TPU:3 now
where the time goes in v24:
time: 31.1 us; the launch traced here: 30.9 us
  starting transfers between devices  14 us (45%)
  Pallas kernels  12.9 us (41%)
  waiting for transfers between devices  3.87 us (12%)
    ppermute x1, starting transfers between devices, per_device(): odd = lax.ppermute(rim, axes, steps + [(b, a) for a, b in steps])  6.5 us
    all_to_all x1, starting transfers between devices, per_device(): same = lax.all_to_all(sent, 'gz', 0, 0, tiled=True)  4.6 us
    pallas_call x1, Pallas kernels, per_device(): pl.pallas_call(functools.partial(leaf_kernel, axes), name='leaf', out_sha...  4.52 us
    ppermute x1, waiting for transfers between devices, per_device(): even = lax.ppermute(rim, axes, [(i, i ^ 1) for i in range(total)])  3.86 us
    pallas_call x1, Pallas kernels, per_device(): pl.pallas_call(functools.partial(mid_kernel, axes), name='mid', out_shape...  3.09 us
    pallas_call x1, Pallas kernels, per_device(): pl.pallas_call(functools.partial(down_kernel, axes[1:]), name='down', out...  2.71 us
    pallas_call x1, Pallas kernels, per_device(): pl.pallas_call(up_kernel, name='up', out_shape=[shape((pairs + 2, sides,...  2.56 us
    ppermute x2, starting transfers between devices, per_device(): other = [lax.ppermute(piece, 'gp', [(0, 1), (1, 0)]) for piece in pieces]  1.59 us
  transfers between devices with their start and end apart: 6, of which 1 were waited for; matrix products, arithmetic and copies ran while one was open for 0% of the time, Pallas kernels for 25%

profile of v24, /device:TPU:3, one launch (start us, length us, event | category | flops | bytes accessed | tf_op | source)
XLA Modules:
  0.0 30.9 jit_solution(4557154629633255325)
XLA Ops:
  0.0 2.6 %up.1 = (bf16[18,32,128]{2,1,0:T(8,128)(2,1)S(1)}, bf16[16,32,128]{2,1,0:T(8,128)(2,1)S(1)}, bf16[8,32,128]{2,1,0:T(8,128)(2,1)S(1)}, bf16[32,32,128]{2,1,0:T(8,128)(2,1)}) custom-call(s32[32]{0:T(128)} %counts_hbm.3, bf16[32,2048]{1,0:T(8,128)(2,1)} %bitcast.3, bf16[32,64,64]{2,1,0:T(8,128)(2,1)} %basis_hbm.3, bf16[32,64,64]{2,1,0:T(8,128)(2,1)} %transfer_hbm.3), custom_call_target="tpu_custom_call" | custom-call | tf_op jit(solution)/shard_map/up/pallas_call | solution.py:302
  2.6 4.6 %all-to-all-start = ((bf16[32,32,128]{2,1,0:T(8,128)(2,1)}), bf16[32,32,128]{2,1,0:T(8,128)(2,1)S(1)}, u32[]{:S(2)}, u32[]{:S(2)}) async-start(bf16[32,32,128]{2,1,0:T(8,128)(2,1)} %get-tuple-element.27), calls=%async_computation | async-start | bytes 524288 | tf_op jit(solution)/shard_map/all_to_all | solution.py:327
  7.2 1.2 %collective-permute-start.2 = (bf16[8,32,128]{2,1,0:T(8,128)(2,1)S(1)}, bf16[8,32,128]{2,1,0:T(8,128)(2,1)S(1)}, u32[]{:S(2)}, u32[]{:S(2)}) collective-permute-start(bf16[8,32,128]{2,1,0:T(8,128)(2,1)S(1)} %get-tuple-element.28), channel_id=1, source_target_pairs={{0,1},{1,0},{2,3},{3,2},{4,5},{5,4},{6,7},{7,6},{8,9},{9,8},{10,11... | collective-permute-start | bytes 196616 | tf_op jit(solution)/shard_map/ppermute | solution.py:349
  8.4 6.5 %collective-permute-start.1 = (bf16[18,32,128]{2,1,0:T(8,128)(2,1)S(1)}, bf16[18,32,128]{2,1,0:T(8,128)(2,1)S(1)}, u32[]{:S(2)}, u32[]{:S(2)}) collective-permute-start(bf16[18,32,128]{2,1,0:T(8,128)(2,1)S(1)} %get-tuple-element.25.rim_ref), channel_id=1, source_target_pairs={{1,2},{3,4},{5,6},{7,8},{9,10},{11,12},{13,14},{15,16},{17,18},{19... | collective-permute-start | bytes 442376 | tf_op jit(solution)/shard_map/ppermute | solution.py:326
  14.9 0.1 collective-permute-start
  15.0 3.1 %mid.1 = (bf16[16,64,1024]{2,1,0:T(8,128)(2,1)S(1)}, f32[16,32,128]{2,1,0:T(8,128)S(1)}, bf16[2,64,64]{2,1,0:T(8,128)(2,1)S(1)}, s32[16,32]{1,0:T(8,128)S(1)}, s32[16,16]{1,0:T(8,128)S(1)}) custom-call(bf16[16,32,128]{2,1,0:T(8,128)(2,1)S(1)} %get-tuple-element.22.live_ref, bf16[32,3,64,64]{3,2,1,0:T(8,128)(2,1)} %near_hbm.1, ...), custom_call_target="tpu_custom_call" | custom-call | tf_op jit(solution)/shard_map/mid/pallas_call | solution.py:329
  18.1 0.0 collective-permute-done.2.other_own_ref.own_ref
  18.1 0.0 all-to-all-done.same_ref.whole_ref
  18.2 1.5 %collective-permute-start.3 = (bf16[12,32,128]{2,1,0:T(8,128)(2,1)S(1)}, bf16[12,32,128]{2,1,0:T(8,128)(2,1)S(1)}, u32[]{:S(2)}, u32[]{:S(2)}) collective-permute-start(bf16[12,32,128]{2,1,0:T(8,128)(2,1)S(1)} %get-tuple-element.30), channel_id=1, source_target_pairs={{0,1},{1,0},{2,3},{3,2},{4,5},{5,4},{6,7},{7,6},{8,9},{9,8},{10,11... | collective-permute-start | bytes 294920 | tf_op jit(solution)/shard_map/ppermute | solution.py:359
  19.7 0.1 collective-permute-start.4
  19.8 0.0 collective-permute-done.1.odd_ref
  19.8 3.9 %collective-permute-done.even_ref = bf16[18,32,128]{2,1,0:T(8,128)(2,1)S(1)} collective-permute-done((bf16[18,32,128]{2,1,0:T(8,128)(2,1)S(1)}, bf16[18,32,128]{2,1,0:T(8,128)(2,1)S(1)}, u32[]{:S(2)}, u32[]{:S(2)}) %collective-permute-start) | collective-permute-done | bytes 147488 | tf_op jit(solution)/shard_map/ppermute | solution.py:324
  23.6 4.5 %leaf.1 = (f32[16,32,128]{2,1,0:T(8,128)S(1)}, f32[2,32,128]{2,1,0:T(8,128)S(1)}, bf16[32,64,64]{2,1,0:T(8,128)(2,1)S(1)}, bf16[16,64,128]{2,1,0:T(8,128)(2,1)S(1)}, bf16[128,32,128]{2,1,0:T(8,128)(2,1)S(1)}) custom-call(s32[16,32]{1,0:T(8,128)S(1)} %get-tuple-element.24.at_vmem, bf16[18,32,128]{2,1,0:T(8,128)(2,1)S(1)} %get-tuple-element.25.rim_ref, ...), custom_call_target="tpu_custom_call" | custom-call | tf_op jit(solution)/shard_map/leaf/pallas_call | solution.py:361
  28.1 0.0 collective-permute-done.3.other_refs_0_
  28.2 0.0 collective-permute-done.4.other_refs_1_
  28.2 2.7 %down.1 = (bf16[32,2048]{1,0:T(8,128)(2,1)}, bf16[128,32,128]{2,1,0:T(8,128)(2,1)S(1)}) custom-call(s32[16,16]{1,0:T(8,128)S(1)} %get-tuple-element.23.at_ref.at_vmem, bf16[128,32,128]{2,1,0:T(8,128)(2,1)S(1)} %get-tuple-element.29.table_in, bf16[12,32,128]{2,1,0:T(8,128)(2,1)S(1)} %collective-permute-done.3.other_refs_0_, ...), custom_call_target="tpu_custom_call", output_to_operand_aliasing={{1}: (1, {})} | custom-call | tf_op jit(solution)/shard_map/down/pallas_call | solution.py:384
  (1 shorter events, 0.0 us)
Async XLA Ops:
  2.6 15.5 %all-to-all-start = ((bf16[32,32,128]{2,1,0:T(8,128)(2,1)}), bf16[32,32,128]{2,1,0:T(8,128)(2,1)S(1)}, u32[]{:S(2)}, u32[]{:S(2)}) async-start(bf16[32,32,128]{2,1,0:T(8,128)(2,1)} %get-tuple-element.27), calls=%async_computation | async-start | bytes 524288 | tf_op jit(solution)/shard_map/all_to_all | solution.py:327
  7.2 10.9 %collective-permute-start.2 = (bf16[8,32,128]{2,1,0:T(8,128)(2,1)S(1)}, bf16[8,32,128]{2,1,0:T(8,128)(2,1)S(1)}, u32[]{:S(2)}, u32[]{:S(2)}) collective-permute-start(bf16[8,32,128]{2,1,0:T(8,128)(2,1)S(1)} %get-tuple-element.28), channel_id=1, source_target_pairs={{0,1},{1,0},{2,3},{3,2},{4,5},{5,4},{6,7},{7,6},{8,9},{9,8},{10,11... | collective-permute-start | bytes 196616 | tf_op jit(solution)/shard_map/ppermute | solution.py:349
  8.4 11.3 %collective-permute-start.1 = (bf16[18,32,128]{2,1,0:T(8,128)(2,1)S(1)}, bf16[18,32,128]{2,1,0:T(8,128)(2,1)S(1)}, u32[]{:S(2)}, u32[]{:S(2)}) collective-permute-start(bf16[18,32,128]{2,1,0:T(8,128)(2,1)S(1)} %get-tuple-element.25.rim_ref), channel_id=1, source_target_pairs={{1,2},{3,4},{5,6},{7,8},{9,10},{11,12},{13,14},{15,16},{17,18},{19... | collective-permute-start | bytes 442376 | tf_op jit(solution)/shard_map/ppermute | solution.py:326
  14.9 8.7 %collective-permute-start = (bf16[18,32,128]{2,1,0:T(8,128)(2,1)S(1)}, bf16[18,32,128]{2,1,0:T(8,128)(2,1)S(1)}, u32[]{:S(2)}, u32[]{:S(2)}) collective-permute-start(bf16[18,32,128]{2,1,0:T(8,128)(2,1)S(1)} %get-tuple-element.25.rim_ref), channel_id=1, source_target_pairs={{0,1},{1,0},{2,3},{3,2},{4,5},{5,4},{6,7},{7,6},{8,9},{9,8},{10,11... | collective-permute-start | bytes 442376 | tf_op jit(solution)/shard_map/ppermute | solution.py:324
  18.2 10.0 %collective-permute-start.3 = (bf16[12,32,128]{2,1,0:T(8,128)(2,1)S(1)}, bf16[12,32,128]{2,1,0:T(8,128)(2,1)S(1)}, u32[]{:S(2)}, u32[]{:S(2)}) collective-permute-start(bf16[12,32,128]{2,1,0:T(8,128)(2,1)S(1)} %get-tuple-element.30), channel_id=1, source_target_pairs={{0,1},{1,0},{2,3},{3,2},{4,5},{5,4},{6,7},{7,6},{8,9},{9,8},{10,11... | collective-permute-start | bytes 294920 | tf_op jit(solution)/shard_map/ppermute | solution.py:359
  19.7 8.5 %collective-permute-start.4 = (bf16[12,32,128]{2,1,0:T(8,128)(2,1)S(1)}, bf16[12,32,128]{2,1,0:T(8,128)(2,1)S(1)}, u32[]{:S(2)}, u32[]{:S(2)}) collective-permute-start(bf16[12,32,128]{2,1,0:T(8,128)(2,1)S(1)} %get-tuple-element.31), channel_id=1, source_target_pairs={{0,1},{1,0},{2,3},{3,2},{4,5},{5,4},{6,7},{7,6},{8,9},{9,8},{10,11... | collective-permute-start | bytes 294920 | tf_op jit(solution)/shard_map/ppermute | solution.py:359

commit v25 on v23

--- a/solution.py
+++ b/solution.py
@@ -59,17 +59,17 @@
     rim_ref, live_ref, parents_ref, sent_hbm,
     counts_ref, charges_ref, basis_ref, transfer_ref, sems, sent_sems,
 ):
-    counts_in, charges_in, basis_in, transfer_in = start_all(
-        [
-            (counts_hbm, counts_ref), (charges_hbm, charges_ref),
-            (basis_hbm, basis_ref), (transfer_hbm, transfer_ref),
-        ],
-        sems,
-    )
     sides = charges_ref.shape[0]
     leaves, width, rank = basis_ref.shape
     pairs = leaves // 2
     own = pairs // 2
+    parts = [pl.ds(0, pairs), pl.ds(pairs, pairs)]
+    counts_in, charges_in, *halves_in = start_all(
+        [(counts_hbm, counts_ref), (charges_hbm, charges_ref)]
+        + [(basis_hbm.at[part], basis_ref.at[part]) for part in parts]
+        + [(transfer_hbm.at[part], transfer_ref.at[part]) for part in parts],
+        sems,
+    )
     left = left_half(sides, width)
     counts_in.wait()
     charges_in.wait()
@@ -81,25 +81,32 @@
         lives.append(live)
     rim_ref[pairs] = lives[0]
     rim_ref[pairs + 1] = lives[-1]
-    basis_in.wait()
     none = jnp.zeros_like(lives[0])
     coefs = []
     for a in range(pairs):
+        if a % own == 0:
+            halves_in[a // own].wait()
         live = lives[a]
         both = jnp.concatenate([jnp.where(left, live, none), jnp.where(left, none, live)], axis=0)
         coef = dot(both, basis_ref[2 * a : 2 * a + 2].reshape(2 * width, rank), NN)
         coef = jnp.concatenate([coef[:sides], coef[sides:]], axis=1).astype(jnp.bfloat16)
         rim_ref[a] = coef
         coefs.append(coef)
-    transfer_in.wait()
-    sums = [
-        dot(coefs[a], transfer_ref[2 * a : 2 * a + 2].reshape(2 * rank, rank), NN)
-        for a in range(pairs)
-    ]
-    for a in range(own):
-        parents_ref[a] = jnp.concatenate(sums[2 * a : 2 * a + 2], axis=1).astype(jnp.bfloat16)
     copies = sent_hbm.shape[0] // own
-    for copy in start_all([(parents_ref, sent_hbm.at[pl.ds(own * c, own)]) for c in range(copies)], sent_sems):
+    sent, few = [], own // 2
+    for h in range(2):
+        halves_in[2 + h].wait()
+        sums = [
+            dot(coefs[a], transfer_ref[2 * a : 2 * a + 2].reshape(2 * rank, rank), NN)
+            for a in range(own * h, own * (h + 1))
+        ]
+        for a in range(few):
+            parents_ref[few * h + a] = jnp.concatenate(sums[2 * a : 2 * a + 2], axis=1).astype(jnp.bfloat16)
+        part = parents_ref.at[pl.ds(few * h, few)]
+        sent += start_all(
+            [(part, sent_hbm.at[pl.ds(own * c + few * h, few)]) for c in range(copies)], sent_sems.at[h]
+        )
+    for copy in sent:
         copy.wait()
 
 
@@ -311,8 +318,8 @@
             pltpu.VMEM((sides, leaves * width), bf16),
             pltpu.VMEM((leaves, width, rank), bf16),
             pltpu.VMEM((leaves, rank, rank), bf16),
-            dma(4),
-            dma(n // 2),
+            dma(6),
+            pltpu.SemaphoreType.DMA((2, n // 2)),
         ],
         compiler_params=params(8),
     )(*keep(panel_counts, charges.T, basis, transfer))

time: 29.4 us -> 29.7 us (1.010)
  Pallas kernels: 12.9 us -> 13.2 us
    pallas_call x1, Pallas kernels: 2.56 us -> 2.88 us  [per_device(): pl.pallas_call(up_kernel, name='up', out_shape=[shape((pairs + 2, sides,...]
where the time goes in v25:
time: 29.7 us; the launch traced here: 29.5 us
  starting transfers between devices  16.2 us (55%)
  Pallas kernels  13.2 us (44%)
    ppermute x1, starting transfers between devices, per_device(): odd = lax.ppermute(rim, axes, steps + [(b, a) for a, b in steps])  7.8 us
    all_to_all x1, starting transfers between devices, per_device(): same = lax.all_to_all(sent, 'gz', 0, 0, tiled=True)  5.43 us
    pallas_call x1, Pallas kernels, per_device(): pl.pallas_call(functools.partial(leaf_kernel, axes), name='leaf', out_sha...  4.46 us
    pallas_call x1, Pallas kernels, per_device(): pl.pallas_call(functools.partial(mid_kernel, axes), name='mid', out_shape...  3.09 us
    pallas_call x1, Pallas kernels, per_device(): pl.pallas_call(up_kernel, name='up', out_shape=[shape((pairs + 2, sides,...  2.88 us
    pallas_call x1, Pallas kernels, per_device(): pl.pallas_call(functools.partial(down_kernel, axes[1:]), name='down', out...  2.72 us
    ppermute x2, starting transfers between devices, per_device(): other = [lax.ppermute(piece, 'gp', [(0, 1), (1, 0)]) for piece in pieces]  1.52 us
    ppermute x1, starting transfers between devices, per_device(): other_own = lax.ppermute(parent_coef, 'gp', [(0, 1), (1, 0)])  1.24 us
  transfers between devices with their start and end apart: 6, of which 0 were waited for; matrix products, arithmetic and copies ran while one was open for 0% of the time, Pallas kernels for 26%

profile of v25, /device:TPU:1, one launch (start us, length us, event | category | flops | bytes accessed | tf_op | source)
XLA Modules:
  0.0 29.5 jit_solution(1984480920599027992)
XLA Ops:
  0.0 2.9 %up.1 = (bf16[18,32,128]{2,1,0:T(8,128)(2,1)S(1)}, bf16[16,32,128]{2,1,0:T(8,128)(2,1)S(1)}, bf16[8,32,128]{2,1,0:T(8,128)(2,1)S(1)}, bf16[32,32,128]{2,1,0:T(8,128)(2,1)}) custom-call(s32[32]{0:T(128)} %counts_hbm.3, bf16[32,2048]{1,0:T(8,128)(2,1)} %bitcast.3, bf16[32,64,64]{2,1,0:T(8,128)(2,1)} %basis_hbm.3, bf16[32,64,64]{2,1,0:T(8,128)(2,1)} %transfer_hbm.3), custom_call_target="tpu_custom_call" | custom-call | tf_op jit(solution)/shard_map/up/pallas_call | solution.py:305
  2.9 5.4 %all-to-all-start = ((bf16[32,32,128]{2,1,0:T(8,128)(2,1)}), bf16[32,32,128]{2,1,0:T(8,128)(2,1)S(1)}, u32[]{:S(2)}, u32[]{:S(2)}) async-start(bf16[32,32,128]{2,1,0:T(8,128)(2,1)} %get-tuple-element.22), calls=%async_computation | async-start | bytes 524288 | tf_op jit(solution)/shard_map/all_to_all | solution.py:330
  8.3 1.2 %collective-permute-start = (bf16[8,32,128]{2,1,0:T(8,128)(2,1)S(1)}, bf16[8,32,128]{2,1,0:T(8,128)(2,1)S(1)}, u32[]{:S(2)}, u32[]{:S(2)}) collective-permute-start(bf16[8,32,128]{2,1,0:T(8,128)(2,1)S(1)} %get-tuple-element.23), channel_id=1, source_target_pairs={{0,1},{1,0},{2,3},{3,2},{4,5},{5,4},{6,7},{7,6},{8,9},{9,8},{10,11... | collective-permute-start | bytes 196616 | tf_op jit(solution)/shard_map/ppermute | solution.py:352
  9.6 0.2 collective-permute-start.3
  9.8 7.8 %collective-permute-start.4 = (bf16[18,32,128]{2,1,0:T(8,128)(2,1)S(1)}, bf16[18,32,128]{2,1,0:T(8,128)(2,1)S(1)}, u32[]{:S(2)}, u32[]{:S(2)}) collective-permute-start(bf16[18,32,128]{2,1,0:T(8,128)(2,1)S(1)} %get-tuple-element.28.rim_ref), channel_id=1, source_target_pairs={{1,2},{3,4},{5,6},{7,8},{9,10},{11,12},{13,14},{15,16},{17,18},{19... | collective-permute-start | bytes 442376 | tf_op jit(solution)/shard_map/ppermute | solution.py:329
  17.6 3.1 %mid.1 = (bf16[16,64,1024]{2,1,0:T(8,128)(2,1)S(1)}, f32[16,32,128]{2,1,0:T(8,128)S(1)}, bf16[2,64,64]{2,1,0:T(8,128)(2,1)S(1)}, s32[16,32]{1,0:T(8,128)S(1)}, s32[16,16]{1,0:T(8,128)S(1)}) custom-call(bf16[16,32,128]{2,1,0:T(8,128)(2,1)S(1)} %get-tuple-element.20.live_ref, bf16[32,3,64,64]{3,2,1,0:T(8,128)(2,1)} %near_hbm.1, ...), custom_call_target="tpu_custom_call" | custom-call | tf_op jit(solution)/shard_map/mid/pallas_call | solution.py:332
  20.7 0.0 collective-permute-done.own_ref.other_own_ref
  20.7 0.0 all-to-all-done.whole_ref.same_ref
  20.8 0.1 collective-permute-start.1
  20.8 1.5 %collective-permute-start.2 = (bf16[12,32,128]{2,1,0:T(8,128)(2,1)S(1)}, bf16[12,32,128]{2,1,0:T(8,128)(2,1)S(1)}, u32[]{:S(2)}, u32[]{:S(2)}) collective-permute-start(bf16[12,32,128]{2,1,0:T(8,128)(2,1)S(1)} %get-tuple-element.25), channel_id=1, source_target_pairs={{0,1},{1,0},{2,3},{3,2},{4,5},{5,4},{6,7},{7,6},{8,9},{9,8},{10,11... | collective-permute-start | bytes 294920 | tf_op jit(solution)/shard_map/ppermute | solution.py:362
  22.3 0.0 collective-permute-done.3.even_ref
  22.3 0.0 collective-permute-done.4.odd_ref
  22.3 4.5 %leaf.1 = (f32[16,32,128]{2,1,0:T(8,128)S(1)}, f32[2,32,128]{2,1,0:T(8,128)S(1)}, bf16[32,64,64]{2,1,0:T(8,128)(2,1)S(1)}, bf16[16,64,128]{2,1,0:T(8,128)(2,1)S(1)}) custom-call(s32[16,32]{1,0:T(8,128)S(1)} %get-tuple-element.27.at_vmem, bf16[18,32,128]{2,1,0:T(8,128)(2,1)S(1)} %get-tuple-element.28.rim_ref, ...), custom_call_target="tpu_custom_call" | custom-call | tf_op jit(solution)/shard_map/leaf/pallas_call | solution.py:364
  26.8 0.0 collective-permute-done.1.other_refs_0_
  26.8 0.0 collective-permute-done.2.other_refs_1_
  26.8 2.7 %down.1 = bf16[32,2048]{1,0:T(8,128)(2,1)} custom-call(s32[16,16]{1,0:T(8,128)S(1)} %get-tuple-element.21.at_ref.at_vmem, bf16[32,32,128]{2,1,0:T(8,128)(2,1)S(1)} %all-to-all-done.whole_ref.same_ref, bf16[8,32,128]{2,1,0:T(8,128)(2,1)S(1)} %collective-permute-done.own_ref.other_own_ref, bf16[12,32,128]{2,1,0:T(8,128)(2,1)S(1)} %collective-permute-done.1.other_refs_0_, ...), custom_call_target="tpu_custom_call" | custom-call | tf_op jit(solution)/shard_map/down/pallas_call | solution.py:386
  (1 shorter events, 0.0 us)
Async XLA Ops:
  2.9 17.8 %all-to-all-start = ((bf16[32,32,128]{2,1,0:T(8,128)(2,1)}), bf16[32,32,128]{2,1,0:T(8,128)(2,1)S(1)}, u32[]{:S(2)}, u32[]{:S(2)}) async-start(bf16[32,32,128]{2,1,0:T(8,128)(2,1)} %get-tuple-element.22), calls=%async_computation | async-start | bytes 524288 | tf_op jit(solution)/shard_map/all_to_all | solution.py:330
  8.3 12.4 %collective-permute-start = (bf16[8,32,128]{2,1,0:T(8,128)(2,1)S(1)}, bf16[8,32,128]{2,1,0:T(8,128)(2,1)S(1)}, u32[]{:S(2)}, u32[]{:S(2)}) collective-permute-start(bf16[8,32,128]{2,1,0:T(8,128)(2,1)S(1)} %get-tuple-element.23), channel_id=1, source_target_pairs={{0,1},{1,0},{2,3},{3,2},{4,5},{5,4},{6,7},{7,6},{8,9},{9,8},{10,11... | collective-permute-start | bytes 196616 | tf_op jit(solution)/shard_map/ppermute | solution.py:352
  9.6 12.7 %collective-permute-start.3 = (bf16[18,32,128]{2,1,0:T(8,128)(2,1)S(1)}, bf16[18,32,128]{2,1,0:T(8,128)(2,1)S(1)}, u32[]{:S(2)}, u32[]{:S(2)}) collective-permute-start(bf16[18,32,128]{2,1,0:T(8,128)(2,1)S(1)} %get-tuple-element.28.rim_ref), channel_id=1, source_target_pairs={{0,1},{1,0},{2,3},{3,2},{4,5},{5,4},{6,7},{7,6},{8,9},{9,8},{10,11... | collective-permute-start | bytes 442376 | tf_op jit(solution)/shard_map/ppermute | solution.py:327
  9.8 12.5 %collective-permute-start.4 = (bf16[18,32,128]{2,1,0:T(8,128)(2,1)S(1)}, bf16[18,32,128]{2,1,0:T(8,128)(2,1)S(1)}, u32[]{:S(2)}, u32[]{:S(2)}) collective-permute-start(bf16[18,32,128]{2,1,0:T(8,128)(2,1)S(1)} %get-tuple-element.28.rim_ref), channel_id=1, source_target_pairs={{1,2},{3,4},{5,6},{7,8},{9,10},{11,12},{13,14},{15,16},{17,18},{19... | collective-permute-start | bytes 442376 | tf_op jit(solution)/shard_map/ppermute | solution.py:329
  20.8 6.0 %collective-permute-start.1 = (bf16[12,32,128]{2,1,0:T(8,128)(2,1)S(1)}, bf16[12,32,128]{2,1,0:T(8,128)(2,1)S(1)}, u32[]{:S(2)}, u32[]{:S(2)}) collective-permute-start(bf16[12,32,128]{2,1,0:T(8,128)(2,1)S(1)} %get-tuple-element.24), channel_id=1, source_target_pairs={{0,1},{1,0},{2,3},{3,2},{4,5},{5,4},{6,7},{7,6},{8,9},{9,8},{10,11... | collective-permute-start | bytes 294920 | tf_op jit(solution)/shard_map/ppermute | solution.py:362
  20.8 5.9 %collective-permute-start.2 = (bf16[12,32,128]{2,1,0:T(8,128)(2,1)S(1)}, bf16[12,32,128]{2,1,0:T(8,128)(2,1)S(1)}, u32[]{:S(2)}, u32[]{:S(2)}) collective-permute-start(bf16[12,32,128]{2,1,0:T(8,128)(2,1)S(1)} %get-tuple-element.25), channel_id=1, source_target_pairs={{0,1},{1,0},{2,3},{3,2},{4,5},{5,4},{6,7},{7,6},{8,9},{9,8},{10,11... | collective-permute-start | bytes 294920 | tf_op jit(solution)/shard_map/ppermute | solution.py:362

commit v26 on v23

--- a/solution.py
+++ b/solution.py
@@ -82,6 +82,7 @@
     rim_ref[pairs] = lives[0]
     rim_ref[pairs + 1] = lives[-1]
     basis_in.wait()
+    transfer_in.wait()
     none = jnp.zeros_like(lives[0])
     coefs = []
     for a in range(pairs):
@@ -91,7 +92,6 @@
         coef = jnp.concatenate([coef[:sides], coef[sides:]], axis=1).astype(jnp.bfloat16)
         rim_ref[a] = coef
         coefs.append(coef)
-    transfer_in.wait()
     sums = [
         dot(coefs[a], transfer_ref[2 * a : 2 * a + 2].reshape(2 * rank, rank), NN)
         for a in range(pairs)
@@ -118,7 +118,7 @@
     pairs = leaves // 2
     started = start_all(
         [(near_hbm, near_ref)]
-        + [(parent_hbm.at[pl.ds(4 * i, 4)], parent_ref.at[pl.ds(4 * i, 4)]) for i in range(parents // 4)]
+        + [(parent_hbm.at[pl.ds(8 * i, 8)], parent_ref.at[pl.ds(8 * i, 8)]) for i in range(parents // 8)]
         + [(leaf_partners_hbm, leaf_at_ref), (parent_partners_hbm, parent_at_ref)],
         sems,
     )
@@ -139,7 +139,7 @@
 
     for i, copy in enumerate(parent_in):
         copy.wait()
-        for q in range(4 * i, 4 * i + 4):
+        for q in range(8 * i, 8 * i + 8):
             parent_packed_ref[q] = side_by_side(parent_ref, q)
     for copy in started[-2:]:
         copy.wait()
@@ -337,7 +337,7 @@
         scratch_shapes=[
             pltpu.VMEM(near_blocks.shape, bf16),
             pltpu.VMEM(parent_coupling.shape, bf16),
-            dma(3 + parents // 4),
+            dma(3 + parents // 8),
         ],
         compiler_params=params(12),
     )(live, *keep(near_blocks, parent_coupling, leaf_partners.T, parent_partners))

time: 29.4 us -> 29.5 us (level)
  no operation moved by 1% of the time
where the time goes in v26:
time: 29.5 us; the launch traced here: 29.2 us
  starting transfers between devices  16.2 us (55%)
  Pallas kernels  12.9 us (44%)
    ppermute x1, starting transfers between devices, per_device(): odd = lax.ppermute(rim, axes, steps + [(b, a) for a, b in steps])  7.79 us
    all_to_all x1, starting transfers between devices, per_device(): same = lax.all_to_all(sent, 'gz', 0, 0, tiled=True)  5.43 us
    pallas_call x1, Pallas kernels, per_device(): pl.pallas_call(functools.partial(leaf_kernel, axes), name='leaf', out_sha...  4.47 us
    pallas_call x1, Pallas kernels, per_device(): pl.pallas_call(functools.partial(mid_kernel, axes), name='mid', out_shape...  3.11 us
    pallas_call x1, Pallas kernels, per_device(): pl.pallas_call(functools.partial(down_kernel, axes[1:]), name='down', out...  2.72 us
    pallas_call x1, Pallas kernels, per_device(): pl.pallas_call(up_kernel, name='up', out_shape=[shape((pairs + 2, sides,...  2.59 us
    ppermute x2, starting transfers between devices, per_device(): other = [lax.ppermute(piece, 'gp', [(0, 1), (1, 0)]) for piece in pieces]  1.52 us
    ppermute x1, starting transfers between devices, per_device(): other_own = lax.ppermute(parent_coef, 'gp', [(0, 1), (1, 0)])  1.24 us
  transfers between devices with their start and end apart: 6, of which 0 were waited for; matrix products, arithmetic and copies ran while one was open for 0% of the time, Pallas kernels for 26%

profile of v26, /device:TPU:1, one launch (start us, length us, event | category | flops | bytes accessed | tf_op | source)
XLA Modules:
  0.0 29.2 jit_solution(12696087800519266135)
XLA Ops:
  0.0 2.6 %up.1 = (bf16[18,32,128]{2,1,0:T(8,128)(2,1)S(1)}, bf16[16,32,128]{2,1,0:T(8,128)(2,1)S(1)}, bf16[8,32,128]{2,1,0:T(8,128)(2,1)S(1)}, bf16[32,32,128]{2,1,0:T(8,128)(2,1)}) custom-call(s32[32]{0:T(128)} %counts_hbm.3, bf16[32,2048]{1,0:T(8,128)(2,1)} %bitcast.3, bf16[32,64,64]{2,1,0:T(8,128)(2,1)} %basis_hbm.3, bf16[32,64,64]{2,1,0:T(8,128)(2,1)} %transfer_hbm.3), custom_call_target="tpu_custom_call" | custom-call | tf_op jit(solution)/shard_map/up/pallas_call | solution.py:298
  2.6 5.4 %all-to-all-start = ((bf16[32,32,128]{2,1,0:T(8,128)(2,1)}), bf16[32,32,128]{2,1,0:T(8,128)(2,1)S(1)}, u32[]{:S(2)}, u32[]{:S(2)}) async-start(bf16[32,32,128]{2,1,0:T(8,128)(2,1)} %get-tuple-element.22), calls=%async_computation | async-start | bytes 524288 | tf_op jit(solution)/shard_map/all_to_all | solution.py:323
  8.0 1.2 %collective-permute-start = (bf16[8,32,128]{2,1,0:T(8,128)(2,1)S(1)}, bf16[8,32,128]{2,1,0:T(8,128)(2,1)S(1)}, u32[]{:S(2)}, u32[]{:S(2)}) collective-permute-start(bf16[8,32,128]{2,1,0:T(8,128)(2,1)S(1)} %get-tuple-element.23), channel_id=1, source_target_pairs={{0,1},{1,0},{2,3},{3,2},{4,5},{5,4},{6,7},{7,6},{8,9},{9,8},{10,11... | collective-permute-start | bytes 196616 | tf_op jit(solution)/shard_map/ppermute | solution.py:345
  9.3 0.2 collective-permute-start.3
  9.5 7.8 %collective-permute-start.4 = (bf16[18,32,128]{2,1,0:T(8,128)(2,1)S(1)}, bf16[18,32,128]{2,1,0:T(8,128)(2,1)S(1)}, u32[]{:S(2)}, u32[]{:S(2)}) collective-permute-start(bf16[18,32,128]{2,1,0:T(8,128)(2,1)S(1)} %get-tuple-element.28.rim_ref), channel_id=1, source_target_pairs={{1,2},{3,4},{5,6},{7,8},{9,10},{11,12},{13,14},{15,16},{17,18},{19... | collective-permute-start | bytes 442376 | tf_op jit(solution)/shard_map/ppermute | solution.py:322
  17.3 3.1 %mid.1 = (bf16[16,64,1024]{2,1,0:T(8,128)(2,1)S(1)}, f32[16,32,128]{2,1,0:T(8,128)S(1)}, bf16[2,64,64]{2,1,0:T(8,128)(2,1)S(1)}, s32[16,32]{1,0:T(8,128)S(1)}, s32[16,16]{1,0:T(8,128)S(1)}) custom-call(bf16[16,32,128]{2,1,0:T(8,128)(2,1)S(1)} %get-tuple-element.20.live_ref, bf16[32,3,64,64]{3,2,1,0:T(8,128)(2,1)} %near_hbm.1, ...), custom_call_target="tpu_custom_call" | custom-call | tf_op jit(solution)/shard_map/mid/pallas_call | solution.py:325
  20.4 0.0 collective-permute-done.own_ref.other_own_ref
  20.4 0.0 all-to-all-done.whole_ref.same_ref
  20.5 0.1 collective-permute-start.1
  20.5 1.5 %collective-permute-start.2 = (bf16[12,32,128]{2,1,0:T(8,128)(2,1)S(1)}, bf16[12,32,128]{2,1,0:T(8,128)(2,1)S(1)}, u32[]{:S(2)}, u32[]{:S(2)}) collective-permute-start(bf16[12,32,128]{2,1,0:T(8,128)(2,1)S(1)} %get-tuple-element.25), channel_id=1, source_target_pairs={{0,1},{1,0},{2,3},{3,2},{4,5},{5,4},{6,7},{7,6},{8,9},{9,8},{10,11... | collective-permute-start | bytes 294920 | tf_op jit(solution)/shard_map/ppermute | solution.py:355
  22.0 0.0 collective-permute-done.3.even_ref
  22.0 0.0 collective-permute-done.4.odd_ref
  22.0 4.5 %leaf.1 = (f32[16,32,128]{2,1,0:T(8,128)S(1)}, f32[2,32,128]{2,1,0:T(8,128)S(1)}, bf16[32,64,64]{2,1,0:T(8,128)(2,1)S(1)}, bf16[16,64,128]{2,1,0:T(8,128)(2,1)S(1)}) custom-call(s32[16,32]{1,0:T(8,128)S(1)} %get-tuple-element.27.at_vmem, bf16[18,32,128]{2,1,0:T(8,128)(2,1)S(1)} %get-tuple-element.28.rim_ref, ...), custom_call_target="tpu_custom_call" | custom-call | tf_op jit(solution)/shard_map/leaf/pallas_call | solution.py:357
  26.5 0.0 collective-permute-done.1.other_refs_0_
  26.5 0.0 collective-permute-done.2.other_refs_1_
  26.5 2.7 %down.1 = bf16[32,2048]{1,0:T(8,128)(2,1)} custom-call(s32[16,16]{1,0:T(8,128)S(1)} %get-tuple-element.21.at_ref.at_vmem, bf16[32,32,128]{2,1,0:T(8,128)(2,1)S(1)} %all-to-all-done.whole_ref.same_ref, bf16[8,32,128]{2,1,0:T(8,128)(2,1)S(1)} %collective-permute-done.own_ref.other_own_ref, bf16[12,32,128]{2,1,0:T(8,128)(2,1)S(1)} %collective-permute-done.1.other_refs_0_, ...), custom_call_target="tpu_custom_call" | custom-call | tf_op jit(solution)/shard_map/down/pallas_call | solution.py:379
  (1 shorter events, 0.0 us)
Async XLA Ops:
  2.6 17.8 %all-to-all-start = ((bf16[32,32,128]{2,1,0:T(8,128)(2,1)}), bf16[32,32,128]{2,1,0:T(8,128)(2,1)S(1)}, u32[]{:S(2)}, u32[]{:S(2)}) async-start(bf16[32,32,128]{2,1,0:T(8,128)(2,1)} %get-tuple-element.22), calls=%async_computation | async-start | bytes 524288 | tf_op jit(solution)/shard_map/all_to_all | solution.py:323
  8.0 12.4 %collective-permute-start = (bf16[8,32,128]{2,1,0:T(8,128)(2,1)S(1)}, bf16[8,32,128]{2,1,0:T(8,128)(2,1)S(1)}, u32[]{:S(2)}, u32[]{:S(2)}) collective-permute-start(bf16[8,32,128]{2,1,0:T(8,128)(2,1)S(1)} %get-tuple-element.23), channel_id=1, source_target_pairs={{0,1},{1,0},{2,3},{3,2},{4,5},{5,4},{6,7},{7,6},{8,9},{9,8},{10,11... | collective-permute-start | bytes 196616 | tf_op jit(solution)/shard_map/ppermute | solution.py:345
  9.3 12.7 %collective-permute-start.3 = (bf16[18,32,128]{2,1,0:T(8,128)(2,1)S(1)}, bf16[18,32,128]{2,1,0:T(8,128)(2,1)S(1)}, u32[]{:S(2)}, u32[]{:S(2)}) collective-permute-start(bf16[18,32,128]{2,1,0:T(8,128)(2,1)S(1)} %get-tuple-element.28.rim_ref), channel_id=1, source_target_pairs={{0,1},{1,0},{2,3},{3,2},{4,5},{5,4},{6,7},{7,6},{8,9},{9,8},{10,11... | collective-permute-start | bytes 442376 | tf_op jit(solution)/shard_map/ppermute | solution.py:320
  9.5 12.5 %collective-permute-start.4 = (bf16[18,32,128]{2,1,0:T(8,128)(2,1)S(1)}, bf16[18,32,128]{2,1,0:T(8,128)(2,1)S(1)}, u32[]{:S(2)}, u32[]{:S(2)}) collective-permute-start(bf16[18,32,128]{2,1,0:T(8,128)(2,1)S(1)} %get-tuple-element.28.rim_ref), channel_id=1, source_target_pairs={{1,2},{3,4},{5,6},{7,8},{9,10},{11,12},{13,14},{15,16},{17,18},{19... | collective-permute-start | bytes 442376 | tf_op jit(solution)/shard_map/ppermute | solution.py:322
  20.5 6.0 %collective-permute-start.1 = (bf16[12,32,128]{2,1,0:T(8,128)(2,1)S(1)}, bf16[12,32,128]{2,1,0:T(8,128)(2,1)S(1)}, u32[]{:S(2)}, u32[]{:S(2)}) collective-permute-start(bf16[12,32,128]{2,1,0:T(8,128)(2,1)S(1)} %get-tuple-element.24), channel_id=1, source_target_pairs={{0,1},{1,0},{2,3},{3,2},{4,5},{5,4},{6,7},{7,6},{8,9},{9,8},{10,11... | collective-permute-start | bytes 294920 | tf_op jit(solution)/shard_map/ppermute | solution.py:355
  20.5 6.0 %collective-permute-start.2 = (bf16[12,32,128]{2,1,0:T(8,128)(2,1)S(1)}, bf16[12,32,128]{2,1,0:T(8,128)(2,1)S(1)}, u32[]{:S(2)}, u32[]{:S(2)}) collective-permute-start(bf16[12,32,128]{2,1,0:T(8,128)(2,1)S(1)} %get-tuple-element.25), channel_id=1, source_target_pairs={{0,1},{1,0},{2,3},{3,2},{4,5},{5,4},{6,7},{7,6},{8,9},{9,8},{10,11... | collective-permute-start | bytes 294920 | tf_op jit(solution)/shard_map/ppermute | solution.py:355

commit v27 on v23

--- a/solution.py
+++ b/solution.py
@@ -183,9 +183,10 @@
 ):
     leaves, many, rank, _ = coupling_ref.shape
     chunks = [(at, 4) for at in range(0, leaves, 4)]
+    fetches = [(at, 2) for at in range(0, leaves, 2)]
     at_in, *coupling_in, transfer_in, basis_in = start_all(
         [(at_vmem, at_ref)]
-        + [(coupling_hbm.at[pl.ds(at, size)], coupling_ref.at[pl.ds(at, size)]) for at, size in chunks]
+        + [(coupling_hbm.at[pl.ds(at, size)], coupling_ref.at[pl.ds(at, size)]) for at, size in fetches]
         + [(transfer_hbm, transfer_ref), (basis_hbm, basis_ref)],
         sems,
     )
@@ -210,7 +211,8 @@
     for i in range(len(chunks) + 1):
         now, ready = ready, []
         if i < len(chunks):
-            coupling_in[i].wait()
+            coupling_in[2 * i].wait()
+            coupling_in[2 * i + 1].wait()
             ready = range(chunks[i][0], sum(chunks[i]))
             for g in ready:
                 packed_ref[g] = side_by_side(coupling_ref, g)
@@ -371,7 +373,7 @@
             pltpu.VMEM(leaf_coupling.shape, bf16),
             pltpu.VMEM((leaves, rank, many * rank), bf16),
             pltpu.VMEM(basis.shape, bf16),
-            dma(3 + leaves // 4),
+            dma(3 + leaves // 2),
         ],
         compiler_params=params(20),
     )(leaf_at, rim, even, odd, rim_near, *keep(leaf_coupling, transfer, basis))

time: 29.4 us -> 29.5 us (level)
  no operation moved by 1% of the time
where the time goes in v27:
time: 29.5 us; the launch traced here: 29.3 us
  starting transfers between devices  16.2 us (55%)
  Pallas kernels  12.9 us (44%)
    ppermute x1, starting transfers between devices, per_device(): odd = lax.ppermute(rim, axes, steps + [(b, a) for a, b in steps])  7.8 us
    all_to_all x1, starting transfers between devices, per_device(): same = lax.all_to_all(sent, 'gz', 0, 0, tiled=True)  5.43 us
    pallas_call x1, Pallas kernels, per_device(): pl.pallas_call(functools.partial(leaf_kernel, axes), name='leaf', out_sha...  4.52 us
    pallas_call x1, Pallas kernels, per_device(): pl.pallas_call(functools.partial(mid_kernel, axes), name='mid', out_shape...  3.09 us
    pallas_call x1, Pallas kernels, per_device(): pl.pallas_call(functools.partial(down_kernel, axes[1:]), name='down', out...  2.73 us
    pallas_call x1, Pallas kernels, per_device(): pl.pallas_call(up_kernel, name='up', out_shape=[shape((pairs + 2, sides,...  2.56 us
    ppermute x2, starting transfers between devices, per_device(): other = [lax.ppermute(piece, 'gp', [(0, 1), (1, 0)]) for piece in pieces]  1.52 us
    ppermute x1, starting transfers between devices, per_device(): other_own = lax.ppermute(parent_coef, 'gp', [(0, 1), (1, 0)])  1.24 us
  transfers between devices with their start and end apart: 6, of which 0 were waited for; matrix products, arithmetic and copies ran while one was open for 0% of the time, Pallas kernels for 26%

profile of v27, /device:TPU:1, one launch (start us, length us, event | category | flops | bytes accessed | tf_op | source)
XLA Modules:
  0.0 29.3 jit_solution(4186663650280313498)
XLA Ops:
  0.0 2.6 %up.1 = (bf16[18,32,128]{2,1,0:T(8,128)(2,1)S(1)}, bf16[16,32,128]{2,1,0:T(8,128)(2,1)S(1)}, bf16[8,32,128]{2,1,0:T(8,128)(2,1)S(1)}, bf16[32,32,128]{2,1,0:T(8,128)(2,1)}) custom-call(s32[32]{0:T(128)} %counts_hbm.3, bf16[32,2048]{1,0:T(8,128)(2,1)} %bitcast.3, bf16[32,64,64]{2,1,0:T(8,128)(2,1)} %basis_hbm.3, bf16[32,64,64]{2,1,0:T(8,128)(2,1)} %transfer_hbm.3), custom_call_target="tpu_custom_call" | custom-call | tf_op jit(solution)/shard_map/up/pallas_call | solution.py:300
  2.6 5.4 %all-to-all-start = ((bf16[32,32,128]{2,1,0:T(8,128)(2,1)}), bf16[32,32,128]{2,1,0:T(8,128)(2,1)S(1)}, u32[]{:S(2)}, u32[]{:S(2)}) async-start(bf16[32,32,128]{2,1,0:T(8,128)(2,1)} %get-tuple-element.22), calls=%async_computation | async-start | bytes 524288 | tf_op jit(solution)/shard_map/all_to_all | solution.py:325
  8.0 1.2 %collective-permute-start = (bf16[8,32,128]{2,1,0:T(8,128)(2,1)S(1)}, bf16[8,32,128]{2,1,0:T(8,128)(2,1)S(1)}, u32[]{:S(2)}, u32[]{:S(2)}) collective-permute-start(bf16[8,32,128]{2,1,0:T(8,128)(2,1)S(1)} %get-tuple-element.23), channel_id=1, source_target_pairs={{0,1},{1,0},{2,3},{3,2},{4,5},{5,4},{6,7},{7,6},{8,9},{9,8},{10,11... | collective-permute-start | bytes 196616 | tf_op jit(solution)/shard_map/ppermute | solution.py:347
  9.2 0.2 collective-permute-start.3
  9.5 7.8 %collective-permute-start.4 = (bf16[18,32,128]{2,1,0:T(8,128)(2,1)S(1)}, bf16[18,32,128]{2,1,0:T(8,128)(2,1)S(1)}, u32[]{:S(2)}, u32[]{:S(2)}) collective-permute-start(bf16[18,32,128]{2,1,0:T(8,128)(2,1)S(1)} %get-tuple-element.28.rim_ref), channel_id=1, source_target_pairs={{1,2},{3,4},{5,6},{7,8},{9,10},{11,12},{13,14},{15,16},{17,18},{19... | collective-permute-start | bytes 442376 | tf_op jit(solution)/shard_map/ppermute | solution.py:324
  17.3 3.1 %mid.1 = (bf16[16,64,1024]{2,1,0:T(8,128)(2,1)S(1)}, f32[16,32,128]{2,1,0:T(8,128)S(1)}, bf16[2,64,64]{2,1,0:T(8,128)(2,1)S(1)}, s32[16,32]{1,0:T(8,128)S(1)}, s32[16,16]{1,0:T(8,128)S(1)}) custom-call(bf16[16,32,128]{2,1,0:T(8,128)(2,1)S(1)} %get-tuple-element.20.live_ref, bf16[32,3,64,64]{3,2,1,0:T(8,128)(2,1)} %near_hbm.1, ...), custom_call_target="tpu_custom_call" | custom-call | tf_op jit(solution)/shard_map/mid/pallas_call | solution.py:327
  20.4 0.0 collective-permute-done.own_ref.other_own_ref
  20.4 0.0 all-to-all-done.whole_ref.same_ref
  20.4 0.1 collective-permute-start.1
  20.5 1.5 %collective-permute-start.2 = (bf16[12,32,128]{2,1,0:T(8,128)(2,1)S(1)}, bf16[12,32,128]{2,1,0:T(8,128)(2,1)S(1)}, u32[]{:S(2)}, u32[]{:S(2)}) collective-permute-start(bf16[12,32,128]{2,1,0:T(8,128)(2,1)S(1)} %get-tuple-element.25), channel_id=1, source_target_pairs={{0,1},{1,0},{2,3},{3,2},{4,5},{5,4},{6,7},{7,6},{8,9},{9,8},{10,11... | collective-permute-start | bytes 294920 | tf_op jit(solution)/shard_map/ppermute | solution.py:357
  22.0 0.0 collective-permute-done.3.even_ref
  22.0 0.0 collective-permute-done.4.odd_ref
  22.0 4.5 %leaf.1 = (f32[16,32,128]{2,1,0:T(8,128)S(1)}, f32[2,32,128]{2,1,0:T(8,128)S(1)}, bf16[32,64,64]{2,1,0:T(8,128)(2,1)S(1)}, bf16[16,64,128]{2,1,0:T(8,128)(2,1)S(1)}) custom-call(s32[16,32]{1,0:T(8,128)S(1)} %get-tuple-element.27.at_vmem, bf16[18,32,128]{2,1,0:T(8,128)(2,1)S(1)} %get-tuple-element.28.rim_ref, ...), custom_call_target="tpu_custom_call" | custom-call | tf_op jit(solution)/shard_map/leaf/pallas_call | solution.py:359
  26.5 0.0 collective-permute-done.1.other_refs_0_
  26.5 0.0 collective-permute-done.2.other_refs_1_
  26.5 2.7 %down.1 = bf16[32,2048]{1,0:T(8,128)(2,1)} custom-call(s32[16,16]{1,0:T(8,128)S(1)} %get-tuple-element.21.at_ref.at_vmem, bf16[32,32,128]{2,1,0:T(8,128)(2,1)S(1)} %all-to-all-done.whole_ref.same_ref, bf16[8,32,128]{2,1,0:T(8,128)(2,1)S(1)} %collective-permute-done.own_ref.other_own_ref, bf16[12,32,128]{2,1,0:T(8,128)(2,1)S(1)} %collective-permute-done.1.other_refs_0_, ...), custom_call_target="tpu_custom_call" | custom-call | tf_op jit(solution)/shard_map/down/pallas_call | solution.py:381
  (1 shorter events, 0.0 us)
Async XLA Ops:
  2.6 17.8 %all-to-all-start = ((bf16[32,32,128]{2,1,0:T(8,128)(2,1)}), bf16[32,32,128]{2,1,0:T(8,128)(2,1)S(1)}, u32[]{:S(2)}, u32[]{:S(2)}) async-start(bf16[32,32,128]{2,1,0:T(8,128)(2,1)} %get-tuple-element.22), calls=%async_computation | async-start | bytes 524288 | tf_op jit(solution)/shard_map/all_to_all | solution.py:325
  8.0 12.4 %collective-permute-start = (bf16[8,32,128]{2,1,0:T(8,128)(2,1)S(1)}, bf16[8,32,128]{2,1,0:T(8,128)(2,1)S(1)}, u32[]{:S(2)}, u32[]{:S(2)}) collective-permute-start(bf16[8,32,128]{2,1,0:T(8,128)(2,1)S(1)} %get-tuple-element.23), channel_id=1, source_target_pairs={{0,1},{1,0},{2,3},{3,2},{4,5},{5,4},{6,7},{7,6},{8,9},{9,8},{10,11... | collective-permute-start | bytes 196616 | tf_op jit(solution)/shard_map/ppermute | solution.py:347
  9.2 12.7 %collective-permute-start.3 = (bf16[18,32,128]{2,1,0:T(8,128)(2,1)S(1)}, bf16[18,32,128]{2,1,0:T(8,128)(2,1)S(1)}, u32[]{:S(2)}, u32[]{:S(2)}) collective-permute-start(bf16[18,32,128]{2,1,0:T(8,128)(2,1)S(1)} %get-tuple-element.28.rim_ref), channel_id=1, source_target_pairs={{0,1},{1,0},{2,3},{3,2},{4,5},{5,4},{6,7},{7,6},{8,9},{9,8},{10,11... | collective-permute-start | bytes 442376 | tf_op jit(solution)/shard_map/ppermute | solution.py:322
  9.5 12.5 %collective-permute-start.4 = (bf16[18,32,128]{2,1,0:T(8,128)(2,1)S(1)}, bf16[18,32,128]{2,1,0:T(8,128)(2,1)S(1)}, u32[]{:S(2)}, u32[]{:S(2)}) collective-permute-start(bf16[18,32,128]{2,1,0:T(8,128)(2,1)S(1)} %get-tuple-element.28.rim_ref), channel_id=1, source_target_pairs={{1,2},{3,4},{5,6},{7,8},{9,10},{11,12},{13,14},{15,16},{17,18},{19... | collective-permute-start | bytes 442376 | tf_op jit(solution)/shard_map/ppermute | solution.py:324
  20.4 6.1 %collective-permute-start.1 = (bf16[12,32,128]{2,1,0:T(8,128)(2,1)S(1)}, bf16[12,32,128]{2,1,0:T(8,128)(2,1)S(1)}, u32[]{:S(2)}, u32[]{:S(2)}) collective-permute-start(bf16[12,32,128]{2,1,0:T(8,128)(2,1)S(1)} %get-tuple-element.24), channel_id=1, source_target_pairs={{0,1},{1,0},{2,3},{3,2},{4,5},{5,4},{6,7},{7,6},{8,9},{9,8},{10,11... | collective-permute-start | bytes 294920 | tf_op jit(solution)/shard_map/ppermute | solution.py:357
  20.5 6.0 %collective-permute-start.2 = (bf16[12,32,128]{2,1,0:T(8,128)(2,1)S(1)}, bf16[12,32,128]{2,1,0:T(8,128)(2,1)S(1)}, u32[]{:S(2)}, u32[]{:S(2)}) collective-permute-start(bf16[12,32,128]{2,1,0:T(8,128)(2,1)S(1)} %get-tuple-element.25), channel_id=1, source_target_pairs={{0,1},{1,0},{2,3},{3,2},{4,5},{5,4},{6,7},{7,6},{8,9},{9,8},{10,11... | collective-permute-start | bytes 294920 | tf_op jit(solution)/shard_map/ppermute | solution.py:357

commit v28 on v23

--- a/solution.py
+++ b/solution.py
@@ -182,7 +182,7 @@
     far_ref, edge_ref, transfer_ref, basis_packed_ref, table_ref, at_ref, coupling_ref, packed_ref, basis_ref, sems,
 ):
     leaves, many, rank, _ = coupling_ref.shape
-    chunks = [(at, 4) for at in range(0, leaves, 4)]
+    chunks = [(at, 8) for at in range(0, leaves, 8)]
     at_in, *coupling_in, transfer_in, basis_in = start_all(
         [(at_vmem, at_ref)]
         + [(coupling_hbm.at[pl.ds(at, size)], coupling_ref.at[pl.ds(at, size)]) for at, size in chunks]
@@ -371,7 +371,7 @@
             pltpu.VMEM(leaf_coupling.shape, bf16),
             pltpu.VMEM((leaves, rank, many * rank), bf16),
             pltpu.VMEM(basis.shape, bf16),
-            dma(3 + leaves // 4),
+            dma(3 + leaves // 8),
         ],
         compiler_params=params(20),
     )(leaf_at, rim, even, odd, rim_near, *keep(leaf_coupling, transfer, basis))

time: 29.4 us -> 29.5 us (level)
  no operation moved by 1% of the time
where the time goes in v28:
time: 29.5 us; the launch traced here: 29.3 us
  starting transfers between devices  16.2 us (55%)
  Pallas kernels  13 us (44%)
    ppermute x1, starting transfers between devices, per_device(): odd = lax.ppermute(rim, axes, steps + [(b, a) for a, b in steps])  7.8 us
    all_to_all x1, starting transfers between devices, per_device(): same = lax.all_to_all(sent, 'gz', 0, 0, tiled=True)  5.43 us
    pallas_call x1, Pallas kernels, per_device(): pl.pallas_call(functools.partial(leaf_kernel, axes), name='leaf', out_sha...  4.56 us
    pallas_call x1, Pallas kernels, per_device(): pl.pallas_call(functools.partial(mid_kernel, axes), name='mid', out_shape...  3.09 us
    pallas_call x1, Pallas kernels, per_device(): pl.pallas_call(functools.partial(down_kernel, axes[1:]), name='down', out...  2.72 us
    pallas_call x1, Pallas kernels, per_device(): pl.pallas_call(up_kernel, name='up', out_shape=[shape((pairs + 2, sides,...  2.56 us
    ppermute x2, starting transfers between devices, per_device(): other = [lax.ppermute(piece, 'gp', [(0, 1), (1, 0)]) for piece in pieces]  1.52 us
    ppermute x1, starting transfers between devices, per_device(): other_own = lax.ppermute(parent_coef, 'gp', [(0, 1), (1, 0)])  1.24 us
  transfers between devices with their start and end apart: 6, of which 0 were waited for; matrix products, arithmetic and copies ran while one was open for 0% of the time, Pallas kernels for 26%

profile of v28, /device:TPU:1, one launch (start us, length us, event | category | flops | bytes accessed | tf_op | source)
XLA Modules:
  0.0 29.3 jit_solution(7841287470368452789)
XLA Ops:
  0.0 2.6 %up.1 = (bf16[18,32,128]{2,1,0:T(8,128)(2,1)S(1)}, bf16[16,32,128]{2,1,0:T(8,128)(2,1)S(1)}, bf16[8,32,128]{2,1,0:T(8,128)(2,1)S(1)}, bf16[32,32,128]{2,1,0:T(8,128)(2,1)}) custom-call(s32[32]{0:T(128)} %counts_hbm.3, bf16[32,2048]{1,0:T(8,128)(2,1)} %bitcast.3, bf16[32,64,64]{2,1,0:T(8,128)(2,1)} %basis_hbm.3, bf16[32,64,64]{2,1,0:T(8,128)(2,1)} %transfer_hbm.3), custom_call_target="tpu_custom_call" | custom-call | tf_op jit(solution)/shard_map/up/pallas_call | solution.py:298
  2.6 5.4 %all-to-all-start = ((bf16[32,32,128]{2,1,0:T(8,128)(2,1)}), bf16[32,32,128]{2,1,0:T(8,128)(2,1)S(1)}, u32[]{:S(2)}, u32[]{:S(2)}) async-start(bf16[32,32,128]{2,1,0:T(8,128)(2,1)} %get-tuple-element.22), calls=%async_computation | async-start | bytes 524288 | tf_op jit(solution)/shard_map/all_to_all | solution.py:323
  8.0 1.2 %collective-permute-start = (bf16[8,32,128]{2,1,0:T(8,128)(2,1)S(1)}, bf16[8,32,128]{2,1,0:T(8,128)(2,1)S(1)}, u32[]{:S(2)}, u32[]{:S(2)}) collective-permute-start(bf16[8,32,128]{2,1,0:T(8,128)(2,1)S(1)} %get-tuple-element.23), channel_id=1, source_target_pairs={{0,1},{1,0},{2,3},{3,2},{4,5},{5,4},{6,7},{7,6},{8,9},{9,8},{10,11... | collective-permute-start | bytes 196616 | tf_op jit(solution)/shard_map/ppermute | solution.py:345
  9.2 0.2 collective-permute-start.3
  9.5 7.8 %collective-permute-start.4 = (bf16[18,32,128]{2,1,0:T(8,128)(2,1)S(1)}, bf16[18,32,128]{2,1,0:T(8,128)(2,1)S(1)}, u32[]{:S(2)}, u32[]{:S(2)}) collective-permute-start(bf16[18,32,128]{2,1,0:T(8,128)(2,1)S(1)} %get-tuple-element.28.rim_ref), channel_id=1, source_target_pairs={{1,2},{3,4},{5,6},{7,8},{9,10},{11,12},{13,14},{15,16},{17,18},{19... | collective-permute-start | bytes 442376 | tf_op jit(solution)/shard_map/ppermute | solution.py:322
  17.3 3.1 %mid.1 = (bf16[16,64,1024]{2,1,0:T(8,128)(2,1)S(1)}, f32[16,32,128]{2,1,0:T(8,128)S(1)}, bf16[2,64,64]{2,1,0:T(8,128)(2,1)S(1)}, s32[16,32]{1,0:T(8,128)S(1)}, s32[16,16]{1,0:T(8,128)S(1)}) custom-call(bf16[16,32,128]{2,1,0:T(8,128)(2,1)S(1)} %get-tuple-element.20.live_ref, bf16[32,3,64,64]{3,2,1,0:T(8,128)(2,1)} %near_hbm.1, ...), custom_call_target="tpu_custom_call" | custom-call | tf_op jit(solution)/shard_map/mid/pallas_call | solution.py:325
  20.4 0.0 collective-permute-done.own_ref.other_own_ref
  20.4 0.0 all-to-all-done.whole_ref.same_ref
  20.4 0.1 collective-permute-start.1
  20.5 1.5 %collective-permute-start.2 = (bf16[12,32,128]{2,1,0:T(8,128)(2,1)S(1)}, bf16[12,32,128]{2,1,0:T(8,128)(2,1)S(1)}, u32[]{:S(2)}, u32[]{:S(2)}) collective-permute-start(bf16[12,32,128]{2,1,0:T(8,128)(2,1)S(1)} %get-tuple-element.25), channel_id=1, source_target_pairs={{0,1},{1,0},{2,3},{3,2},{4,5},{5,4},{6,7},{7,6},{8,9},{9,8},{10,11... | collective-permute-start | bytes 294920 | tf_op jit(solution)/shard_map/ppermute | solution.py:355
  22.0 0.0 collective-permute-done.3.even_ref
  22.0 0.0 collective-permute-done.4.odd_ref
  22.0 4.6 %leaf.1 = (f32[16,32,128]{2,1,0:T(8,128)S(1)}, f32[2,32,128]{2,1,0:T(8,128)S(1)}, bf16[32,64,64]{2,1,0:T(8,128)(2,1)S(1)}, bf16[16,64,128]{2,1,0:T(8,128)(2,1)S(1)}) custom-call(s32[16,32]{1,0:T(8,128)S(1)} %get-tuple-element.27.at_vmem, bf16[18,32,128]{2,1,0:T(8,128)(2,1)S(1)} %get-tuple-element.28.rim_ref, ...), custom_call_target="tpu_custom_call" | custom-call | tf_op jit(solution)/shard_map/leaf/pallas_call | solution.py:357
  26.5 0.0 collective-permute-done.1.other_refs_0_
  26.6 0.0 collective-permute-done.2.other_refs_1_
  26.6 2.7 %down.1 = bf16[32,2048]{1,0:T(8,128)(2,1)} custom-call(s32[16,16]{1,0:T(8,128)S(1)} %get-tuple-element.21.at_ref.at_vmem, bf16[32,32,128]{2,1,0:T(8,128)(2,1)S(1)} %all-to-all-done.whole_ref.same_ref, bf16[8,32,128]{2,1,0:T(8,128)(2,1)S(1)} %collective-permute-done.own_ref.other_own_ref, bf16[12,32,128]{2,1,0:T(8,128)(2,1)S(1)} %collective-permute-done.1.other_refs_0_, ...), custom_call_target="tpu_custom_call" | custom-call | tf_op jit(solution)/shard_map/down/pallas_call | solution.py:379
  (1 shorter events, 0.0 us)
Async XLA Ops:
  2.6 17.8 %all-to-all-start = ((bf16[32,32,128]{2,1,0:T(8,128)(2,1)}), bf16[32,32,128]{2,1,0:T(8,128)(2,1)S(1)}, u32[]{:S(2)}, u32[]{:S(2)}) async-start(bf16[32,32,128]{2,1,0:T(8,128)(2,1)} %get-tuple-element.22), calls=%async_computation | async-start | bytes 524288 | tf_op jit(solution)/shard_map/all_to_all | solution.py:323
  8.0 12.4 %collective-permute-start = (bf16[8,32,128]{2,1,0:T(8,128)(2,1)S(1)}, bf16[8,32,128]{2,1,0:T(8,128)(2,1)S(1)}, u32[]{:S(2)}, u32[]{:S(2)}) collective-permute-start(bf16[8,32,128]{2,1,0:T(8,128)(2,1)S(1)} %get-tuple-element.23), channel_id=1, source_target_pairs={{0,1},{1,0},{2,3},{3,2},{4,5},{5,4},{6,7},{7,6},{8,9},{9,8},{10,11... | collective-permute-start | bytes 196616 | tf_op jit(solution)/shard_map/ppermute | solution.py:345
  9.2 12.7 %collective-permute-start.3 = (bf16[18,32,128]{2,1,0:T(8,128)(2,1)S(1)}, bf16[18,32,128]{2,1,0:T(8,128)(2,1)S(1)}, u32[]{:S(2)}, u32[]{:S(2)}) collective-permute-start(bf16[18,32,128]{2,1,0:T(8,128)(2,1)S(1)} %get-tuple-element.28.rim_ref), channel_id=1, source_target_pairs={{0,1},{1,0},{2,3},{3,2},{4,5},{5,4},{6,7},{7,6},{8,9},{9,8},{10,11... | collective-permute-start | bytes 442376 | tf_op jit(solution)/shard_map/ppermute | solution.py:320
  9.5 12.5 %collective-permute-start.4 = (bf16[18,32,128]{2,1,0:T(8,128)(2,1)S(1)}, bf16[18,32,128]{2,1,0:T(8,128)(2,1)S(1)}, u32[]{:S(2)}, u32[]{:S(2)}) collective-permute-start(bf16[18,32,128]{2,1,0:T(8,128)(2,1)S(1)} %get-tuple-element.28.rim_ref), channel_id=1, source_target_pairs={{1,2},{3,4},{5,6},{7,8},{9,10},{11,12},{13,14},{15,16},{17,18},{19... | collective-permute-start | bytes 442376 | tf_op jit(solution)/shard_map/ppermute | solution.py:322
  20.4 6.1 %collective-permute-start.1 = (bf16[12,32,128]{2,1,0:T(8,128)(2,1)S(1)}, bf16[12,32,128]{2,1,0:T(8,128)(2,1)S(1)}, u32[]{:S(2)}, u32[]{:S(2)}) collective-permute-start(bf16[12,32,128]{2,1,0:T(8,128)(2,1)S(1)} %get-tuple-element.24), channel_id=1, source_target_pairs={{0,1},{1,0},{2,3},{3,2},{4,5},{5,4},{6,7},{7,6},{8,9},{9,8},{10,11... | collective-permute-start | bytes 294920 | tf_op jit(solution)/shard_map/ppermute | solution.py:355
  20.5 6.0 %collective-permute-start.2 = (bf16[12,32,128]{2,1,0:T(8,128)(2,1)S(1)}, bf16[12,32,128]{2,1,0:T(8,128)(2,1)S(1)}, u32[]{:S(2)}, u32[]{:S(2)}) collective-permute-start(bf16[12,32,128]{2,1,0:T(8,128)(2,1)S(1)} %get-tuple-element.25), channel_id=1, source_target_pairs={{0,1},{1,0},{2,3},{3,2},{4,5},{5,4},{6,7},{7,6},{8,9},{9,8},{10,11... | collective-permute-start | bytes 294920 | tf_op jit(solution)/shard_map/ppermute | solution.py:355
